TPU v7x, 32 devices: a whole 2x2x4 slice. The times are simulated.
32 devices in a mesh: dp: 8 (over z, y), shard: 4 (over x, core).
Axes of the slice: x: 2, y: 2, z: 4, core: 2. Of those that a mesh axis runs over, the one named last changes fastest.
Arguments:
- tokens: bfloat16 [32768, 512], P(('dp', 'shard')), may hold values from -6 to 6
- out_grad: bfloat16 [32768, 512], P(('dp', 'shard')), may hold values from -6 to 6
- domain_ids: int32 [32], P(('dp', 'shard')), may hold values from 0 to 7
- domain_weight: float32 [8], replicated, may hold values from 0.3 to 3
- attn_master: float32 [5, 512, 512], P(None, 'shard')
- attn_first: float32 [5, 512, 512], P(None, 'shard'), may hold values from -0.0078125 to 0.0078125
- attn_second: float32 [5, 512, 512], P(None, 'shard'), may hold values from 1.4663101e-07 to 1.1730481e-06
- up_master: float32 [512, 2048], P('shard'), may hold values from -0.25 to 0.25
- up_first: float32 [512, 2048], P('shard'), may hold values from -0.0078125 to 0.0078125
- up_second: float32 [512, 2048], P('shard'), may hold values from 1.4663101e-07 to 1.1730481e-06
- down_master: float32 [2048, 512], P('shard'), may hold values from -0.125 to 0.125
- down_first: float32 [2048, 512], P('shard'), may hold values from -0.0078125 to 0.0078125
- down_second: float32 [2048, 512], P('shard'), may hold values from 1.4663101e-07 to 1.1730481e-06
- norm_master: float32 [4, 512], P(None, 'shard')
- norm_first: float32 [4, 512], P(None, 'shard'), may hold values from -0.03125 to 0.03125
- norm_second: float32 [4, 512], P(None, 'shard'), may hold values from 2.3460962e-06 to 1.876877e-05
Outputs:
- block_out: bfloat16 [32768, 512], P(('dp', 'shard'))
- input_grad: float32 [32768, 512], P(('dp', 'shard'))
- attn_new: float32 [5, 512, 512], P(None, 'shard')
- attn_first_new: float32 [5, 512, 512], P(None, 'shard')
- attn_second_new: float32 [5, 512, 512], P(None, 'shard')
- up_new: float32 [512, 2048], P('shard')
- up_first_new: float32 [512, 2048], P('shard')
- up_second_new: float32 [512, 2048], P('shard')
- down_new: float32 [2048, 512], P('shard')
- down_first_new: float32 [2048, 512], P('shard')
- down_second_new: float32 [2048, 512], P('shard')
- norm_new: float32 [4, 512], P(None, 'shard')
- norm_first_new: float32 [4, 512], P(None, 'shard')
- norm_second_new: float32 [4, 512], P(None, 'shard')
- clip_norm: float32 [], replicated
- attn_copy: bfloat16 [5, 512, 512], replicated
- up_copy: bfloat16 [512, 2048], replicated
- down_copy: bfloat16 [2048, 512], replicated
- norm_copy: bfloat16 [4, 512], replicated
All inputs are finite; a program needn't handle non-finite values.
Results may differ from a plain program's by a relative error of at most 0.02.
The roundings to bfloat16 on the way count: a program that leaves them out, or rounds other values in their place, can miss the bound.
Values may be sent and summed in bfloat16 or wider, within the bound.
No kernel may reach another device: no remote copies, remote signals or barrier semaphores. Data moves between devices by JAX's collectives and lax.ppermute only.
A program may use at most 128 MiB of HBM per device.

v0:
```python
import math

import jax
import jax.numpy as jnp
from jax import lax
from jax.sharding import PartitionSpec as P

HEADS = 8
STEP = 10


def dot_low(left, right):
    return jnp.dot(
        left.astype(jnp.bfloat16), right.astype(jnp.bfloat16), preferred_element_type=jnp.float32
    )


def product_keep(left, right):
    left_low = left.astype(jnp.bfloat16)
    right_low = right.astype(jnp.bfloat16)
    return (jnp.dot(left_low, right_low, preferred_element_type=jnp.float32), (left_low, right_low))


def product_back(kept, grad):
    left_low, right_low = kept
    grad_low = grad.astype(jnp.bfloat16)
    return (
        jnp.dot(grad_low, right_low.T, preferred_element_type=jnp.float32),
        jnp.dot(left_low.T, grad_low, preferred_element_type=jnp.float32),
    )


def product(left, right):
    rounded = jax.custom_vjp(dot_low)
    rounded.defvjp(product_keep, product_back)
    return rounded(left, right)


def layer_norm(values, gain, shift):
    centred = values - jnp.mean(values, axis=-1, keepdims=True)
    spread = jnp.mean(centred * centred, axis=-1, keepdims=True)
    return centred * lax.rsqrt(spread + 1e-05) * gain + shift


def mix_head(operands):
    queries, key_rows, value_rows, slot_exp, slot_sum = operands
    length = queries.shape[0]
    causal = jnp.arange(length)[:, None] >= jnp.arange(length)[None, :]
    affinity = jnp.where(causal, product(queries, key_rows.T), 0.0)
    numerator = product(affinity, slot_exp)
    scores = numerator / (slot_sum * math.sqrt(queries.shape[1]))
    weights = jax.nn.softmax(scores, axis=-1)
    spreads = jnp.where(causal, product(weights / slot_sum, slot_exp.T), 0.0)
    return product(spreads, value_rows)


def forward(inputs, attn_w, up_w, down_w, norm_w):
    length = inputs.shape[0]
    normed = layer_norm(inputs, norm_w[0], norm_w[1])
    queries = product(normed, attn_w[0])
    key_rows = product(normed, attn_w[1])
    value_rows = product(normed, attn_w[2])
    control = product(normed, attn_w[3])
    slot_exp = jnp.exp(control)
    slot_sum = jnp.cumsum(slot_exp, axis=0)

    def split_heads(array):
        return array.reshape(length, HEADS, -1).transpose(1, 0, 2)

    mixed = lax.map(
        jax.checkpoint(mix_head),
        (
            split_heads(queries),
            split_heads(key_rows),
            split_heads(value_rows),
            split_heads(slot_exp),
            split_heads(slot_sum),
        ),
    )
    mixed = mixed.transpose(1, 0, 2).reshape(length, -1)
    branch = inputs + product(mixed, attn_w[4])
    normed_two = layer_norm(branch, norm_w[2], norm_w[3])
    hidden = jax.nn.gelu(product(normed_two, up_w), approximate=True)
    return branch + product(hidden, down_w)


def adam_step(master, first, second, grad, rate, decay):
    first_new = 0.5 * first + 0.5 * grad
    second_new = 0.5 * second + 0.5 * grad * grad
    correction = 1.0 - 0.5**STEP
    update = first_new / correction / (jnp.sqrt(second_new / correction) + 1e-08)
    return (master - rate * (update + decay * master), first_new, second_new)


def shards(
    tokens,
    out_grad,
    domain_ids,
    domain_weight,
    attn_master,
    attn_first,
    attn_second,
    up_master,
    up_first,
    up_second,
    down_master,
    down_first,
    down_second,
    norm_master,
    norm_first,
    norm_second,
):
    gathered = (
        lax.all_gather(attn_master.astype(jnp.bfloat16), "shard", axis=1, tiled=True),
        lax.all_gather(up_master.astype(jnp.bfloat16), "shard", axis=0, tiled=True),
        lax.all_gather(down_master.astype(jnp.bfloat16), "shard", axis=0, tiled=True),
        lax.all_gather(norm_master.astype(jnp.bfloat16), "shard", axis=1, tiled=True),
    )
    params = tuple((array.astype(jnp.float32) for array in gathered))
    domains = domain_weight.shape[0]
    onehot = (domain_ids[:, None] == jnp.arange(domains, dtype=jnp.int32)[None, :]).astype(
        jnp.float32
    )
    counts = lax.psum(jnp.sum(onehot, axis=0), ("dp", "shard"))
    total_seqs = lax.axis_size("dp") * lax.axis_size("shard") * domain_ids.shape[0]
    per_domain = domain_weight * total_seqs / (domains * jnp.maximum(counts, 1.0))
    seq_weight = jnp.sum(onehot * per_domain[None, :], axis=1)
    seqs = domain_ids.shape[0]
    width = tokens.shape[1]
    length = tokens.shape[0] // seqs
    inputs = tokens.reshape(seqs, length, width)
    cotangent = out_grad.reshape(seqs, length, width)

    def per_sequence(totals, item):
        seq_in, seq_cot, factor = item
        result, pull = jax.vjp(forward, seq_in.astype(jnp.float32), *params)
        grads = pull(seq_cot.astype(jnp.float32) * factor)
        totals = tuple((total + grad for total, grad in zip(totals, grads[1:])))
        return (totals, (result.astype(jnp.bfloat16), grads[0]))

    start = tuple((jnp.zeros_like(param) for param in params))
    totals, (outputs, in_grads) = lax.scan(per_sequence, start, (inputs, cotangent, seq_weight))
    parted = (
        lax.psum_scatter(
            totals[0].astype(jnp.bfloat16), "shard", scatter_dimension=1, tiled=True
        ).astype(jnp.float32),
        lax.psum_scatter(
            totals[1].astype(jnp.bfloat16), "shard", scatter_dimension=0, tiled=True
        ).astype(jnp.float32),
        lax.psum_scatter(
            totals[2].astype(jnp.bfloat16), "shard", scatter_dimension=0, tiled=True
        ).astype(jnp.float32),
        lax.psum_scatter(
            totals[3].astype(jnp.bfloat16), "shard", scatter_dimension=1, tiled=True
        ).astype(jnp.float32),
    )
    owned = lax.psum(parted, "dp")
    local_sq = sum((jnp.sum(grad * grad) for grad in owned))
    clip_norm = jnp.sqrt(lax.psum(local_sq, "shard"))
    factor = jnp.minimum(1.0, 1.0 / (clip_norm + 1e-06))
    attn_new = adam_step(attn_master, attn_first, attn_second, owned[0] * factor, 0.05, 0.01)
    up_new = adam_step(up_master, up_first, up_second, owned[1] * factor, 0.05, 0.01)
    down_new = adam_step(down_master, down_first, down_second, owned[2] * factor, 0.05, 0.01)
    norm_new = adam_step(norm_master, norm_first, norm_second, owned[3] * factor, 0.3, 0.0)
    copies = (
        lax.all_gather(attn_new[0].astype(jnp.bfloat16), "shard", axis=1, tiled=True),
        lax.all_gather(up_new[0].astype(jnp.bfloat16), "shard", axis=0, tiled=True),
        lax.all_gather(down_new[0].astype(jnp.bfloat16), "shard", axis=0, tiled=True),
        lax.all_gather(norm_new[0].astype(jnp.bfloat16), "shard", axis=1, tiled=True),
    )
    return (
        outputs.reshape(-1, width),
        in_grads.reshape(-1, width),
        attn_new[0],
        attn_new[1],
        attn_new[2],
        up_new[0],
        up_new[1],
        up_new[2],
        down_new[0],
        down_new[1],
        down_new[2],
        norm_new[0],
        norm_new[1],
        norm_new[2],
        clip_norm,
        copies[0],
        copies[1],
        copies[2],
        copies[3],
    )


def solution(mesh):
    placed = (
        P(("dp", "shard"), None),
        P(("dp", "shard"), None),
        P(("dp", "shard")),
        P(),
        P(None, "shard", None),
        P(None, "shard", None),
        P(None, "shard", None),
        P("shard", None),
        P("shard", None),
        P("shard", None),
        P("shard", None),
        P("shard", None),
        P("shard", None),
        P(None, "shard"),
        P(None, "shard"),
        P(None, "shard"),
    )
    return jax.shard_map(
        shards,
        mesh=mesh,
        in_specs=placed,
        out_specs=(
            P(("dp", "shard"), None),
            P(("dp", "shard"), None),
            P(None, "shard", None),
            P(None, "shard", None),
            P(None, "shard", None),
            P("shard", None),
            P("shard", None),
            P("shard", None),
            P("shard", None),
            P("shard", None),
            P("shard", None),
            P(None, "shard"),
            P(None, "shard"),
            P(None, "shard"),
            P(),
            P(),
            P(),
            P(),
            P(),
        ),
        check_vma=False,
    )
```

profile of v0, /device:TPU:0, one launch (start us, length us, event | category | flops | bytes accessed | tf_op | source)
XLA Modules:
  0.0 717.2 jit_solution(2334401235907258733)
XLA Ops:
  14.4 42.4 %psum.42 = f32[8]{0:T(128)S(1)} all-reduce(f32[8]{0:T(128)S(1)} %compare_convert_fusion), channel_id=1, replica_groups=mesh['dp'=8,'shard'=4] {'dp','shard'}, use_global_device_ids=true, to_apply=%region_10.11 | all-reduce | flops 8 | bytes 64 | tf_op jit(solution)/shard_map/psum | solution.py:124
  56.8 5.4 all_gather.24
  86.3 2.9 convolution_bitcast_fusion.5
  91.2 2.9 copy.148
  97.6 36.8 %while.56 = (s32[]{:T(128)}, bf16[8,1024,64]{1,2,0:T(8,128)(2,1)S(1)}, bf16[8,1024,64]{2,1,0:T(8,128)(2,1)}, bf16[8,1024,64]{2,1,0:T(8,128)(2,1)}, bf16[8,1024,6...) while((s32[]{:T(128)}, ...), condition=%wide.region_7.8_spmd.clone.clone, body=%wide.region_4.7_spmd.clone.clone.sunk | while | flops 543750144 | bytes 2908253 | solution.py:70
  137.9 7.7 %fusion.108 = f32[1024,2048]{1,0:T(8,128)} fusion(bf16[512,2048]{1,0:T(8,128)(2,1)} %all-gather.9.cloned.1.call-done, f32[1024,512]{0,1:T(8,128)S(1)} %get-tuple-element.700, f32[512]{0:T(512)S(1)} %bitcast.352, f32[512]{0:T(512)S(1)} %bitcast.336, f32[1024]{0:T(1024)S(1)} %fusion.105, f32[1024]{0:T(1024)S(1)} %broadcast_multiply_fusion), kind=kOutput, calls=%fused_computation.186 | convolution fusion | flops 2150105088 | bytes 12595200 | tf_op jit(solution)/shard_map/while/body/eval_jaxpr/jvp()/dot_general | solution.py:21
  145.6 11.0 %fusion.61 = bf16[1024,2048]{1,0:T(8,128)(2,1)S(1)} fusion(f32[1024,2048]{1,0:T(8,128)} %fusion.108, bf16[2048,512]{1,0:T(8,128)(2,1)} %all-gather.11.cloned.1.call-done, bf16[1024,512]{0,1:T(8,128)(2,1)} %copy.150, f32[]{:T(128)} %fusion.107), kind=kOutput, calls=%fused_computation.78 | convolution fusion | flops 2190999552 | bytes 15728644 | tf_op jit(solution)/shard_map/while/body/eval_jaxpr/transpose(jvp())/dot_general | solution.py:36
  156.7 4.3 fusion.136
  161.0 3.3 copy.151
  164.2 2.9 multiply_reduce_fusion.1
  174.6 136.6 %while.55 = (s32[]{:T(128)}, bf16[8,1024,64]{1,2,0:T(8,128)(2,1)S(1)}, bf16[8,1024,64]{1,2,0:T(8,128)(2,1)}, bf16[8,1024,64]{1,2,0:T(8,128)(2,1)}, f32[8,1024,64...) while((s32[]{:T(128)}, ...), condition=%wide.region_18.19_spmd, body=%wide.region_14.18_spmd.sunk | while | flops 1491992576 | bytes 30474504 | solution.py:70
  311.3 3.4 copy.158
  314.7 6.7 fusion.75
  327.1 2.9 copy.161
  330.0 3.6 fusion.74
  341.5 9.3 %convolution_convert_fusion = bf16[2048,512]{1,0:T(8,128)(2,1)} fusion(bf16[1024,512]{0,1:T(8,128)(2,1)S(1)} %copy-done.16, f32[]{:T(128)} %fusion.107, f32[1024,2048]{1,0:T(8,128)} %fusion.108), kind=kOutput, calls=%fused_computation.90 | convolution fusion | flops 2168979456 | bytes 11534340 | tf_op jit(solution)/shard_map/while/body/eval_jaxpr/transpose(jvp())/dot_general | solution.py:36
  352.3 5.9 convolution_convert_fusion.1
  367.8 27.4 %reduce-scatter.11.cloned.1.call-done = bf16[512,512]{1,0:T(8,128)(2,1)} async-done(((bf16[2048,512]{1,0:T(8,128)(2,1)}), bf16[512,512]{1,0:T(8,128)(2,1)}) %reduce-scatter.11.cloned.1.call-update) | async-done | bytes 524304 | tf_op jit(solution)/shard_map/reduce_scatter | solution.py:150
  395.2 34.4 %reduce-scatter.9.cloned.1.call-done = bf16[128,2048]{1,0:T(8,128)(2,1)} async-done(((bf16[512,2048]{1,0:T(8,128)(2,1)}), bf16[128,2048]{1,0:T(8,128)(2,1)}) %reduce-scatter.9.cloned.1.call-update) | async-done | bytes 524304 | tf_op jit(solution)/shard_map/reduce_scatter | solution.py:147
  429.6 38.0 %reduce-scatter.7.cloned.1.call-done = bf16[5,128,512]{2,1,0:T(8,128)(2,1)} async-done(((bf16[5,512,512]{2,1,0:T(8,128)(2,1)}), bf16[5,128,512]{2,1,0:T(8,128)(2,1)}) %reduce-scatter.7.cloned.1.call-update) | async-done | bytes 655376 | tf_op jit(solution)/shard_map/reduce_scatter | solution.py:144
  467.6 140.0 %all-reduce.11 = (f32[5,128,512]{2,1,0:T(8,128)}, f32[128,2048]{1,0:T(8,128)}, f32[512,512]{1,0:T(8,128)}, f32[4,128]{1,0:T(4,128)S(1)}) all-reduce(bf16[5,128,512]{2,1,0:T(8,128)(2,1)} %reduce-scatter.7.cloned.1.call-done, bf16[128,2048]{1,0:T(8,128)(2,1)} %reduce-scatter.9.cloned.1.call-done, ...), channel_id=1, replica_groups=mesh['dp'=8,'shard'=4] {'dp'}, use_global_device_ids=true, to_apply=%region_24.25 | all-reduce | flops 852480 | bytes 5114880 | tf_op jit(solution)/shard_map/psum | solution.py:157
  616.0 6.7 psum.47
  623.4 4.6 fusion.120
  628.1 4.6 fusion.122
  632.9 5.9 fusion.124
  638.8 8.4 %add_convert_fusion.1 = bf16[1024,512]{0,1:T(8,128)(2,1)} fusion(f32[1024,512]{0,1:T(8,128)S(1)} %copy-done.1, bf16[2048,512]{1,0:T(8,128)(2,1)} %all-gather.11.cloned.1.call-done, f32[1024,2048]{1,0:T(8,128)} %fusion.108), kind=kOutput, calls=%fused_computation.113 | convolution fusion | flops 2167406592 | bytes 13631488 | tf_op jit(solution)/shard_map/while/body/eval_jaxpr/jvp()/dot_general | solution.py:21
  649.6 4.9 add_add_fusion.2
  654.5 2.9 copy.168
  658.1 5.1 all_gather.31
  663.1 10.1 %all-gather.15.cloned.1.call-done = bf16[512,2048]{1,0:T(8,128)(2,1)} async-done(((bf16[128,2048]{1,0:T(8,128)(2,1)}), bf16[512,2048]{1,0:T(8,128)(2,1)}) %all-gather.15.cloned.1.call-update) | async-done | bytes 2097168 | tf_op jit(solution)/shard_map/all_gather | solution.py:167
  673.3 27.6 %all-gather.13.cloned.1.call-done = bf16[5,512,512]{2,1,0:T(8,128)(2,1)} async-done(((bf16[5,128,512]{2,1,0:T(8,128)(2,1)}), bf16[5,512,512]{2,1,0:T(8,128)(2,1)}) %all-gather.13.cloned.1.call-update) | async-done | bytes 2621456 | tf_op jit(solution)/shard_map/all_gather | solution.py:166
  700.8 3.7 copy.238
  (454 shorter events, 256.0 us)
Async XLA Ops:
  7.2 58.8 %all-gather.7.cloned.1.call-start = ((), (), s32[]{:S(2)}) async-start(), calls=%async_computation.4 | async-start | bytes 3276800 | tf_op jit(solution)/shard_map/all_gather | solution.py:114
  9.7 128.2 %all-gather.9.cloned.1.call-start = ((), (), s32[]{:S(2)}) async-start(), calls=%async_computation.5 | async-start | bytes 2621440 | tf_op jit(solution)/shard_map/all_gather | solution.py:115
  10.6 135.0 %all-gather.11.cloned.1.call-start = ((), (), s32[]{:S(2)}) async-start(), calls=%async_computation.6 | async-start | bytes 2621440 | tf_op jit(solution)/shard_map/all_gather | solution.py:116
  11.5 355.5 %reduce-scatter.13.cloned.1.call-start = ((), (), s32[]{:S(2)}) async-start(), calls=%async_computation.13 | async-start | bytes 163840
  11.7 53.6 %copy-start.2 = (bf16[8,1024,64]{1,2,0:T(8,128)(2,1)}, bf16[8,1024,64]{1,2,0:T(8,128)(2,1)S(1)}, u32[]{:S(2)}) copy-start(bf16[8,1024,64]{1,2,0:T(8,128)(2,1)S(1)} %fusion.133) | copy-start | bytes 3145732
  12.7 44.1 %copy-start.52 = (f32[4,128]{1,0:T(4,128)S(1)}, f32[4,128]{1,0:T(4,128)}, u32[]{:S(2)}) copy-start(f32[4,128]{1,0:T(4,128)} %param.33) | copy-start | bytes 6148
  12.7 49.5 %copy-start.35 = (bf16[1024,512]{1,0:T(8,128)(2,1)S(1)}, bf16[1024,512]{1,0:T(8,128)(2,1)}, u32[]{:S(2)}) copy-start(bf16[1024,512]{1,0:T(8,128)(2,1)} %param.20) | copy-start | bytes 3145732
  62.2 27.2 %copy-start.47 = (f32[1,512]{1,0:T(1,128)}, f32[1,512]{1,0:T(1,128)S(1)}, u32[]{:S(2)}) copy-start(f32[1,512]{1,0:T(1,128)S(1)} %get-tuple-element.697) | copy-start | bytes 6148
  62.2 27.2 %copy-start.57 = (f32[1,512]{1,0:T(1,128)}, f32[1,512]{1,0:T(1,128)S(1)}, u32[]{:S(2)}) copy-start(f32[1,512]{1,0:T(1,128)S(1)} %get-tuple-element.698) | copy-start | bytes 6148
  62.2 75.7 %copy-start.59 = (f32[1,512]{1,0:T(1,128)}, f32[1,512]{1,0:T(1,128)S(1)}, u32[]{:S(2)}) copy-start(f32[1,512]{1,0:T(1,128)S(1)} %get-tuple-element.696) | copy-start | bytes 6148
  62.2 105.0 %copy-start.49 = (f32[1,512]{1,0:T(1,128)}, f32[1,512]{1,0:T(1,128)S(1)}, u32[]{:S(2)}) copy-start(f32[1,512]{1,0:T(1,128)S(1)} %get-tuple-element.695) | copy-start | bytes 6148
  63.3 4.7 copy-start.43
  64.0 25.4 %copy-start.39 = (f32[1024]{0:T(1024)}, f32[1024]{0:T(1024)S(1)}, u32[]{:S(2)}) copy-start(f32[1024]{0:T(1024)S(1)} %fusion.104) | copy-start | bytes 12292
  68.0 4.4 copy-start.11
  137.5 29.7 %copy-start = (f32[1024,512]{0,1:T(8,128)}, f32[1024,512]{0,1:T(8,128)S(1)}, u32[]{:S(2)}) copy-start(f32[1024,512]{0,1:T(8,128)S(1)} %get-tuple-element.700) | copy-start | bytes 6291460
  137.5 29.7 %copy-start.37 = (f32[1024]{0:T(1024)}, f32[1024]{0:T(1024)S(1)}, u32[]{:S(2)}) copy-start(f32[1024]{0:T(1024)S(1)} %broadcast_multiply_fusion) | copy-start | bytes 12292
  137.8 29.4 %copy-start.45 = (f32[1024]{0:T(1024)}, f32[1024]{0:T(1024)S(1)}, u32[]{:S(2)}) copy-start(f32[1024]{0:T(1024)S(1)} %fusion.105) | copy-start | bytes 12292
  145.6 11.1 %copy-start.62 = (bf16[512,2048]{1,0:T(8,128)(2,1)S(1)}, bf16[512,2048]{1,0:T(8,128)(2,1)}, u32[]{:S(2)}) copy-start(bf16[512,2048]{1,0:T(8,128)(2,1)} %all-gather.9.cloned.1.call-done) | copy-start | bytes 6291460
  156.7 4.3 copy-start.63
  227.0 4.1 copy-start.20
  295.3 4.1 copy-start.20
  311.2 25.5 %copy-start.4 = (bf16[8,1024,64]{1,2,0:T(8,128)(2,1)}, bf16[8,1024,64]{1,2,0:T(8,128)(2,1)S(1)}, u32[]{:S(2)}) copy-start(bf16[8,1024,64]{1,2,0:T(8,128)(2,1)S(1)} %get-tuple-element.420) | copy-start | bytes 3145732
  341.2 54.0 %reduce-scatter.11.cloned.1.call-start = ((), (), s32[]{:S(2)}) async-start(), calls=%async_computation.9 | async-start | bytes 2621440 | tf_op jit(solution)/shard_map/reduce_scatter | solution.py:150
  341.4 9.4 %copy-start.38 = (f32[1024]{0:T(1024)S(1)}, f32[1024]{0:T(1024)}, u32[]{:S(2)}) copy-start(f32[1024]{0:T(1024)} %copy-done.37) | copy-start | bytes 12292
  341.4 9.4 %copy-start.46 = (f32[1024]{0:T(1024)S(1)}, f32[1024]{0:T(1024)}, u32[]{:S(2)}) copy-start(f32[1024]{0:T(1024)} %copy-done.45) | copy-start | bytes 12292
  341.5 9.4 %copy-start.60 = (f32[1,512]{1,0:T(1,128)S(1)}, f32[1,512]{1,0:T(1,128)}, u32[]{:S(2)}) copy-start(f32[1,512]{1,0:T(1,128)} %copy-done.59) | copy-start | bytes 6148
  350.8 78.9 %reduce-scatter.9.cloned.1.call-start = ((), (), s32[]{:S(2)}) async-start(), calls=%async_computation.8 | async-start | bytes 2621440 | tf_op jit(solution)/shard_map/reduce_scatter | solution.py:147
  358.3 109.3 %reduce-scatter.7.cloned.1.call-start = ((), (), s32[]{:S(2)}) async-start(), calls=%async_computation.7 | async-start | bytes 3276800 | tf_op jit(solution)/shard_map/reduce_scatter | solution.py:144
  366.9 296.2 %all-gather.17.cloned.1.call-start = ((), (), s32[]{:S(2)}) async-start(), calls=%async_computation.12 | async-start | bytes 2621440 | tf_op jit(solution)/shard_map/all_gather | solution.py:168
  607.6 4.8 copy-start.21
  628.1 45.2 %all-gather.15.cloned.1.call-start = ((), (), s32[]{:S(2)}) async-start(), calls=%async_computation.11 | async-start | bytes 2621440 | tf_op jit(solution)/shard_map/all_gather | solution.py:167
  632.8 68.0 %all-gather.13.cloned.1.call-start = ((), (), s32[]{:S(2)}) async-start(), calls=%async_computation.10 | async-start | bytes 3276800 | tf_op jit(solution)/shard_map/all_gather | solution.py:166
  (63 other events, 148.8 us)
Sparse Core Ops, SparseCore 0:
  10.2 28.8 all-gather.6
  41.3 22.9 all-gather.8
  66.4 22.4 all-gather.10
  341.3 19.3 reduce-scatter.12
  363.8 31.3 reduce-scatter.10
  398.2 31.4 reduce-scatter.8
  432.9 34.6 reduce-scatter.6
  628.2 20.8 all-gather.16
  650.6 22.5 all-gather.14
  675.3 25.5 all-gather.12
where the time goes:
time: 729 us; the launch traced here: 717 us
  blocking collectives  200 us (27%)
  matrix products  193 us (26%)
  waiting for transfers between devices  138 us (19%)
  local copies, waits for them, and re-layouts  99.2 us (14%)
  other arithmetic  64.5 us (9%)
  between operations  20.6 us (3%)
    dot_general x110, matrix products, product(): return rounded(left, right)  167 us
    psum x1, blocking collectives, shards(): owned = lax.psum(parted, 'dp')  140 us
    psum x1, blocking collectives, shards(): counts = lax.psum(jnp.sum(onehot, axis=0), ('dp', 'shard'))  42.4 us
    reduce_scatter x1, waiting for transfers between devices, shards(): lax.psum_scatter(totals[0].astype(jnp.bfloat16), 'shard', scatter_dimensi...  38 us
    unnamed x138, local copies, waits for them, and re-layouts  37.9 us
    reduce_scatter x1, waiting for transfers between devices, shards(): lax.psum_scatter(totals[1].astype(jnp.bfloat16), 'shard', scatter_dimensi...  34.4 us
    all_gather x1, waiting for transfers between devices, shards(): lax.all_gather(attn_new[0].astype(jnp.bfloat16), 'shard', axis=1, tiled=T...  27.6 us
    reduce_scatter x1, waiting for transfers between devices, shards(): lax.psum_scatter(totals[2].astype(jnp.bfloat16), 'shard', scatter_dimensi...  27.4 us
  transfers between devices with their start and end apart: 10, of which 5 were waited for; matrix products, arithmetic and copies ran while one was open for 19% of the time, Pallas kernels for 0%

commit v1 on v0

v1 whole, which is shorter than its diff:
```python
import functools
import jax
import jax.numpy as jnp
from jax import lax
from jax.experimental import pallas as pl
from jax.experimental.pallas import tpu as pltpu
from jax.sharding import PartitionSpec as P

BF = jnp.bfloat16
F32 = jnp.float32
VMEM_LIMIT = 56 * 1024 * 1024
CHUNK = 256
SLOT = 64
GROUP = 256
SMALL = 16
STEP = 10


def dot(a, b):
    return jnp.dot(a, b, preferred_element_type=F32)


def dot_nt(a, b):
    return lax.dot_general(a, b, (((1,), (1,)), ((), ())), preferred_element_type=F32)


def dot_tn(a, b):
    return lax.dot_general(a, b, (((0,), (0,)), ((), ())), preferred_element_type=F32)


def head_of(shape, dim):
    return lax.broadcasted_iota(jnp.int32, shape, dim) // SLOT


def block_diagonal(state):
    return jnp.where(head_of(state.shape, 0) == head_of(state.shape, 1), state, 0.0).astype(BF)


def only_head(rows, head):
    return jnp.where(head_of(rows.shape, 1) == head, rows, jnp.zeros_like(rows))


def lower(square):
    row = lax.broadcasted_iota(jnp.int32, square.shape, 0)
    col = lax.broadcasted_iota(jnp.int32, square.shape, 1)
    return jnp.where(row >= col, square, 0.0).astype(BF)


def upper(square):
    row = lax.broadcasted_iota(jnp.int32, square.shape, 0)
    col = lax.broadcasted_iota(jnp.int32, square.shape, 1)
    return jnp.where(row <= col, square, 0.0).astype(BF)


def split_dot(ones, values):
    high = values.astype(BF)
    low = (values - high.astype(F32)).astype(BF)
    return dot(ones, high) + dot(ones, low)


def head_sums(values):
    ones = jnp.where(
        head_of((GROUP, GROUP), 0) == head_of((GROUP, GROUP), 1), 1.0, 0.0
    ).astype(BF)
    high = values.astype(BF)
    low = (values - high.astype(F32)).astype(BF)
    return dot(high, ones) + dot(low, ones)


def head_max(values):
    top = None
    head = head_of(values.shape, 1)
    for index in range(GROUP // SLOT):
        mine = jnp.max(jnp.where(head == index, values, -jnp.inf), axis=1, keepdims=True)
        top = mine if top is None else jnp.where(head == index, mine, top)
    return top


def normalise(values):
    centred = values - jnp.mean(values, axis=-1, keepdims=True)
    inv = lax.rsqrt(jnp.mean(centred * centred, axis=-1, keepdims=True) + 1e-05)
    return centred * inv, inv


def normalise_back(grad, unit, inv, gain):
    scaled = grad * gain
    return inv * (
        scaled
        - jnp.mean(scaled, axis=-1, keepdims=True)
        - unit * jnp.mean(scaled * unit, axis=-1, keepdims=True)
    )


def project_kernel(
    pos_ref, x_ref, p0, p1, p2, p3, q_ref, k_ref, v_ref, n_ref, e_ref, eb_ref, z_ref, w_ref, norm_ref, carry
):
    width = x_ref.shape[1]
    part = width // 4

    @pl.when(pl.program_id(0) == 0)
    def _():
        for index, piece in enumerate((p0, p1, p2, p3)):
            rows = pl.ds(pl.multiple_of(pos_ref[index] * part, part), part)
            for m in range(4):
                w_ref[m, rows, :] = piece[m * part : (m + 1) * part, :]
            norm_ref[0:4, rows] = piece[4 * part : 4 * part + 4, 0:part].astype(F32)
        carry[...] = jnp.zeros_like(carry)

    unit, _ = normalise(x_ref[...].astype(F32))
    normed = (unit * norm_ref[0:1, :] + norm_ref[1:2, :]).astype(BF)
    n_ref[...] = normed
    q_ref[...] = dot(normed, w_ref[0]).astype(BF)
    k_ref[...] = dot(normed, w_ref[1]).astype(BF)
    v_ref[...] = dot(normed, w_ref[2]).astype(BF)
    e = jnp.exp(dot(normed, w_ref[3]))
    e_ref[...] = e
    eb_ref[...] = e.astype(BF)
    rows = e.shape[0]
    ones = lower(jnp.ones((rows, rows), F32))
    z = split_dot(ones, e) + carry[0:1, :]
    z_ref[...] = z
    carry[0:1, :] = z[rows - 1 : rows, :]


def project(pos, x, pieces):
    length, width = x.shape
    steps = length // CHUNK
    rows = lambda dtype: jax.ShapeDtypeStruct((length, width), dtype)
    block = pl.BlockSpec((CHUNK, width), lambda i: (i, 0))
    whole = lambda a: pl.BlockSpec(a.shape, lambda i: (0,) * len(a.shape))
    return pl.pallas_call(
        project_kernel,
        grid=(steps,),
        in_specs=[pl.BlockSpec(memory_space=pltpu.SMEM), block] + [whole(p) for p in pieces],
        out_specs=[block] * 7
        + [
            pl.BlockSpec((4, width, width), lambda i: (0, 0, 0)),
            pl.BlockSpec((8, width), lambda i: (0, 0)),
        ],
        out_shape=[rows(BF), rows(BF), rows(BF), rows(BF), rows(F32), rows(BF), rows(F32)]
        + [jax.ShapeDtypeStruct((4, width, width), BF), jax.ShapeDtypeStruct((8, width), F32)],
        scratch_shapes=[pltpu.VMEM((8, width), F32)],
        compiler_params=pltpu.CompilerParams(
            dimension_semantics=("arbitrary",), vmem_limit_bytes=VMEM_LIMIT
        ),
        name="project",
    )(pos, x, *pieces)


def mix_kernel(q_ref, k_ref, v_ref, e_ref, z_ref, o_ref, w_ref, s_ref, keys_ref, values_ref, keys, values):
    @pl.when(pl.program_id(1) == 0)
    def _():
        keys[...] = jnp.zeros_like(keys)
        values[...] = jnp.zeros_like(values)

    q, k, v, e = q_ref[...], k_ref[...], v_ref[...], e_ref[...]
    inv = 1.0 / z_ref[...]
    heads = GROUP // SLOT
    es = [only_head(e, h) for h in range(heads)]
    key_state = block_diagonal(keys[...])
    value_state = block_diagonal(values[...])
    keys_ref[0, 0] = key_state
    values_ref[0, 0] = value_state
    total = dot(q, key_state)
    for h in range(heads):
        total += dot(lower(dot_nt(q, only_head(k, h))), es[h])
    scores = total * inv * 0.125
    s_ref[...] = scores
    raised = jnp.exp(scores - head_max(scores))
    weights = raised / head_sums(raised)
    w_ref[...] = weights
    ratio = (weights * inv).astype(BF)
    out = dot(ratio, value_state)
    for h in range(heads):
        out += dot(lower(dot_nt(ratio, es[h])), only_head(v, h))
    o_ref[...] = out.astype(BF)
    keys[...] += dot_tn(k, e)
    values[...] += dot_tn(e, v)


def mix(q, k, v, e, z):
    length, width = q.shape
    steps, groups = length // CHUNK, width // GROUP
    block = pl.BlockSpec((CHUNK, GROUP), lambda g, i: (i, g))
    state = pl.BlockSpec((1, 1, GROUP, GROUP), lambda g, i: (g, i, 0, 0))
    rows = lambda dtype: jax.ShapeDtypeStruct((length, width), dtype)
    states = jax.ShapeDtypeStruct((groups, steps, GROUP, GROUP), BF)
    return pl.pallas_call(
        mix_kernel,
        grid=(groups, steps),
        in_specs=[block] * 5,
        out_specs=[block] * 3 + [state] * 2,
        out_shape=[rows(BF), rows(F32), rows(F32), states, states],
        scratch_shapes=[pltpu.VMEM((GROUP, GROUP), F32)] * 2,
        compiler_params=pltpu.CompilerParams(
            dimension_semantics=("arbitrary", "arbitrary"), vmem_limit_bytes=VMEM_LIMIT
        ),
        name="mix",
    )(q, k, v, e, z)


def mix_back_kernel(
    g_ref, q_ref, k_ref, v_ref, eb_ref, e_ref, z_ref, w_ref, s_ref, keys_ref, values_ref,
    dq_ref, dk_ref, dv_ref, dc_ref, later_v, later_k, carry
):
    @pl.when(pl.program_id(1) == 0)
    def _():
        later_v[...] = jnp.zeros_like(later_v)
        later_k[...] = jnp.zeros_like(later_k)
        carry[...] = jnp.zeros_like(carry)

    g, q, k, v, e = g_ref[...], q_ref[...], k_ref[...], v_ref[...], eb_ref[...]
    inv = 1.0 / z_ref[...]
    weights = w_ref[...]
    ratio = (weights * inv).astype(BF)
    heads = GROUP // SLOT
    es = [only_head(e, h) for h in range(heads)]
    state = block_diagonal(later_v[...])
    d_ratio = dot_nt(g, values_ref[0, 0])
    dv = dot(e, state)
    de = dot_nt(v, state)
    for h in range(heads):
        vh = only_head(v, h)
        d_ratio += dot(lower(dot_nt(g, vh)), es[h])
        de += dot(upper(dot_nt(vh, g)), only_head(ratio, h))
        dv += dot(upper(dot_nt(es[h], ratio)), only_head(g, h))
    dv_ref[...] = dv.astype(BF)
    d_weights = d_ratio * inv
    both = d_weights * weights
    d_scores = weights * (d_weights - head_sums(both))
    dn = (d_scores * inv * 0.125).astype(BF)
    dz = -(both + d_scores * s_ref[...]) * inv
    state = block_diagonal(later_k[...])
    dq = dot_nt(dn, keys_ref[0, 0])
    dk = dot(e, state)
    de += dot_nt(k, state)
    for h in range(heads):
        kh = only_head(k, h)
        dq += dot(lower(dot_nt(dn, es[h])), kh)
        dk += dot(upper(dot_nt(es[h], dn)), only_head(q, h))
        de += dot(upper(dot_nt(kh, q)), only_head(dn, h))
    dq_ref[...] = dq.astype(BF)
    dk_ref[...] = dk.astype(BF)
    rows = dz.shape[0]
    ones = upper(jnp.ones((rows, rows), F32))
    z_sum = split_dot(ones, dz) + carry[0:1, :]
    carry[0:1, :] = z_sum[0:1, :]
    dc_ref[...] = ((de + z_sum) * e_ref[...]).astype(BF)
    later_v[...] += dot_tn(ratio, g)
    later_k[...] += dot_tn(dn, q)


def mix_back(g, q, k, v, eb, e, z, w, s, keys, values):
    length, width = q.shape
    steps, groups = length // CHUNK, width // GROUP
    block = pl.BlockSpec((CHUNK, GROUP), lambda g, i: (steps - 1 - i, g))
    state = pl.BlockSpec((1, 1, GROUP, GROUP), lambda g, i: (g, steps - 1 - i, 0, 0))
    rows = jax.ShapeDtypeStruct((length, width), BF)
    return pl.pallas_call(
        mix_back_kernel,
        grid=(groups, steps),
        in_specs=[block] * 9 + [state] * 2,
        out_specs=[block] * 4,
        out_shape=[rows] * 4,
        scratch_shapes=[pltpu.VMEM((GROUP, GROUP), F32)] * 2 + [pltpu.VMEM((8, GROUP), F32)],
        compiler_params=pltpu.CompilerParams(
            dimension_semantics=("arbitrary", "arbitrary"), vmem_limit_bytes=VMEM_LIMIT
        ),
        name="mix_back",
    )(g, q, k, v, eb, e, z, w, s, keys, values)


def scatter_parts(pos_ref, grads, send_ref, keep_ref, half, offset, part):
    for index in range(4):
        pos = pos_ref[index]
        target = send_ref if index % 2 else keep_ref
        rows = pl.ds(pl.multiple_of((pos // 2) * half + offset, part), part)
        target[rows, :] = grads[pl.ds(pl.multiple_of(pos * part, part), part), :]


def feed_kernel(
    pos_ref, factor_ref, x_ref, g_ref, o_ref, norm_ref, p0, p1, p2, p3,
    y_ref, dh_ref, do_ref, send_ref, keep_ref, dnorm_ref,
    wo, w1, w2, branch, unit_ref, inv_ref, n2, gb, n2_t, gb_t, dn2, grads
):
    step = pl.program_id(0)
    last = pl.num_programs(0) - 1
    length, width = x_ref.shape
    part = width // 4
    block = w1.shape[2]
    tiles = length // 256

    @pl.when(step == 0)
    def _():
        for index, piece in enumerate((p0, p1, p2, p3)):
            pos = pos_ref[index]
            rows = pl.ds(pl.multiple_of(pos * part, part), part)
            wo[rows, :] = piece[0:part, :]
            for j in range(4):
                w1[j, rows, :] = piece[(j + 1) * part : (j + 2) * part, :]
            w2[pos] = piece[5 * part : 5 * part + block, :]

        def before(i, _):
            rows = pl.ds(pl.multiple_of(i * 256, 256), 256)
            h1 = x_ref[rows, :].astype(F32) + dot(o_ref[rows, :], wo[...])
            branch[rows, :] = h1
            unit, inv = normalise(h1)
            unit_ref[rows, :] = unit
            inv_ref[rows, :] = jnp.broadcast_to(inv, (256, 128))
            normed = (unit * norm_ref[2:3, :] + norm_ref[3:4, :]).astype(BF)
            n2[rows, :] = normed
            n2_t[:, rows] = normed.T
            grad = (g_ref[rows, :].astype(F32) * factor_ref[0]).astype(BF)
            gb[rows, :] = grad
            gb_t[:, rows] = grad.T
            dn2[rows, :] = jnp.zeros((256, width), F32)
            return 0

        lax.fori_loop(0, tiles, before, 0)

    up = w1[step]
    down = w2[step]
    up_grad = jnp.zeros((width, block), F32)
    down_grad = jnp.zeros((width, block), F32)
    for i in range(tiles):
        rows = slice(i * 256, (i + 1) * 256)
        a = dot(n2[rows, :], up)
        inner = 0.7978845608 * (a + 0.044715 * a * a * a)
        t = jnp.tanh(inner)
        u = (0.5 * a * (1.0 + t)).astype(BF)
        slope = 0.5 * (1.0 + t) + 0.5 * a * (1.0 - t * t) * (
            0.7978845608 + (3.0 * 0.044715 * 0.7978845608) * a * a
        )
        da = (dot_nt(gb[rows, :], down) * slope).astype(BF)
        branch[rows, :] += dot(u, down)
        dn2[rows, :] += dot_nt(da, up)
        up_grad += dot(n2_t[:, rows], da)
        down_grad += dot(gb_t[:, rows], u)
    half = send_ref.shape[0] // 2
    grads[...] = up_grad.astype(BF)
    scatter_parts(pos_ref, grads, send_ref, keep_ref, half, (step + 1) * part, part)
    place = pl.ds(pl.multiple_of((step // 2) * half + 5 * part, part), width)
    mine = (step ^ pos_ref[0]) & 1 == 0

    @pl.when(mine)
    def _():
        keep_ref[place, :] = down_grad.astype(BF)

    @pl.when(jnp.logical_not(mine))
    def _():
        send_ref[place, :] = down_grad.astype(BF)

    @pl.when(step == last)
    def _():
        gain = norm_ref[2:3, :]

        def after(i, sums):
            rows = pl.ds(pl.multiple_of(i * 256, 256), 256)
            y_ref[rows, :] = branch[rows, :].astype(BF)
            grad = dn2[rows, :]
            unit = unit_ref[rows, :]
            dh = g_ref[rows, :].astype(F32) * factor_ref[0] + normalise_back(
                grad, unit, inv_ref[rows, 0:1], gain
            )
            dh_ref[rows, :] = dh
            dh_low = dh.astype(BF)
            do_ref[rows, :] = dot_nt(dh_low, wo[...]).astype(BF)
            return (
                sums[0] + jnp.sum(grad * unit, axis=0, keepdims=True),
                sums[1] + jnp.sum(grad, axis=0, keepdims=True),
                sums[2] + dot_tn(o_ref[rows, :], dh_low),
            )

        empty = jnp.zeros((1, width), F32)
        sums = lax.fori_loop(0, tiles, after, (empty, empty, jnp.zeros((width, width), F32)))
        dnorm_ref[...] = jnp.zeros_like(dnorm_ref)
        dnorm_ref[0:1, :] = sums[0]
        dnorm_ref[1:2, :] = sums[1]
        grads[...] = sums[2].astype(BF)
        scatter_parts(pos_ref, grads, send_ref, keep_ref, half, 0, part)


def feed(pos, factor, x, g, o, norm, pieces):
    length, width = x.shape
    block = (pieces[0].shape[0] - 5 * (width // 4))
    rows = lambda dtype: jax.ShapeDtypeStruct((length, width), dtype)
    whole = lambda a: pl.BlockSpec(a.shape, lambda i: (0,) * len(a.shape))
    out = [
        rows(BF), rows(F32), rows(BF),
        jax.ShapeDtypeStruct((2 * pieces[0].shape[0], width), BF),
        jax.ShapeDtypeStruct((2 * pieces[0].shape[0], width), BF),
        jax.ShapeDtypeStruct((8, width), F32),
    ]
    args = (x, g, o, norm) + tuple(pieces)
    return pl.pallas_call(
        feed_kernel,
        grid=(4,),
        in_specs=[pl.BlockSpec(memory_space=pltpu.SMEM)] * 2 + [whole(a) for a in args],
        out_specs=[whole(a) for a in out],
        out_shape=out,
        scratch_shapes=[
            pltpu.VMEM((width, width), BF),
            pltpu.VMEM((4, width, block), BF),
            pltpu.VMEM((4, block, width), BF),
            pltpu.VMEM((length, width), F32),
            pltpu.VMEM((length, width), F32),
            pltpu.VMEM((length, 128), F32),
            pltpu.VMEM((length, width), BF),
            pltpu.VMEM((length, width), BF),
            pltpu.VMEM((width, length), BF),
            pltpu.VMEM((width, length), BF),
            pltpu.VMEM((length, width), F32),
            pltpu.VMEM((width, block), BF),
        ],
        compiler_params=pltpu.CompilerParams(
            dimension_semantics=("arbitrary",), vmem_limit_bytes=VMEM_LIMIT
        ),
        name="feed",
    )(pos, factor, *args)


def project_back_kernel(
    pos_ref, x_ref, n_ref, dq_ref, dk_ref, dv_ref, dc_ref, dh_ref, w_ref, norm_ref, dnorm_ref,
    dx_ref, send_ref, keep_ref, w_grad, sums
):
    step = pl.program_id(0)
    width = x_ref.shape[1]
    part = width // 4

    @pl.when(step == 0)
    def _():
        w_grad[...] = jnp.zeros_like(w_grad)
        sums[...] = jnp.zeros_like(sums)

    n_t = n_ref[...].T
    dn = None
    for m, ref in enumerate((dq_ref, dk_ref, dv_ref, dc_ref)):
        d = ref[...]
        w_grad[m] += dot(n_t, d)
        term = dot_nt(d, w_ref[m])
        dn = term if dn is None else dn + term
    unit, inv = normalise(x_ref[...].astype(F32))
    dx_ref[...] = dh_ref[...] + normalise_back(dn, unit, inv, norm_ref[0:1, :])
    sums[0:1, :] += jnp.sum(dn * unit, axis=0, keepdims=True)
    sums[1:2, :] += jnp.sum(dn, axis=0, keepdims=True)

    @pl.when(step == pl.num_programs(0) - 1)
    def _():
        for index in range(4):
            pos = pos_ref[index]
            target = send_ref if index % 2 else keep_ref
            for m in range(4):
                rows = pl.ds(pl.multiple_of((pos // 2) * width + m * part, part), part)
                target[rows, :] = w_grad[m, pl.ds(pl.multiple_of(pos * part, part), part), :].astype(BF)
        small = jnp.concatenate(
            [sums[0:2, :], dnorm_ref[0:2, :], jnp.zeros((SMALL - 4, width), F32)], axis=0
        ).astype(BF)
        send_ref[2 * width : 2 * width + SMALL, :] = small
        keep_ref[2 * width : 2 * width + SMALL, :] = small


def project_back(pos, x, n, dq, dk, dv, dc, dh, w, norm, dnorm):
    length, width = x.shape
    tile = 256
    block = pl.BlockSpec((tile, width), lambda i: (i, 0))
    whole = lambda a: pl.BlockSpec(a.shape, lambda i: (0,) * len(a.shape))
    out = [
        jax.ShapeDtypeStruct((2 * width + SMALL, width), BF),
        jax.ShapeDtypeStruct((2 * width + SMALL, width), BF),
    ]
    return pl.pallas_call(
        project_back_kernel,
        grid=(length // tile,),
        in_specs=[pl.BlockSpec(memory_space=pltpu.SMEM)]
        + [block] * 7
        + [whole(w), whole(norm), whole(dnorm)],
        out_specs=[block] + [whole(a) for a in out],
        out_shape=[jax.ShapeDtypeStruct((length, width), F32)] + out,
        scratch_shapes=[pltpu.VMEM((4, width, width), F32), pltpu.VMEM((8, width), F32)],
        compiler_params=pltpu.CompilerParams(
            dimension_semantics=("arbitrary",), vmem_limit_bytes=VMEM_LIMIT
        ),
        name="project_back",
    )(pos, x, n, dq, dk, dv, dc, dh, w, norm, dnorm)


def exchange(values, even, odd):
    dp, shard = lax.axis_size("dp"), lax.axis_size("shard")
    perm = []
    for d in range(dp):
        for s in range(shard):
            axis, bit = odd if s % 2 else even
            other = (d ^ bit, s) if axis == "dp" else (d, s ^ bit)
            perm.append((d * shard + s, other[0] * shard + other[1]))
    return lax.ppermute(values, ("dp", "shard"), perm)


def swap(values, axis, bit):
    return exchange(values, (axis, bit), (axis, bit))


def fold_kernel(index_ref, acc_ref, got_ref, send_ref, keep_ref, *, pieces, extra):
    half = pieces // 2
    rows = (send_ref.shape[0] - extra) // half
    for j in range(half):
        for target, index in ((send_ref, j), (keep_ref, half + j)):
            source = pl.ds(pl.multiple_of(index_ref[index] * rows, rows), rows)
            total = acc_ref[source, :].astype(F32) + got_ref[source, :].astype(F32)
            target[j * rows : (j + 1) * rows, :] = total.astype(BF)
    if extra:
        last = pieces * rows
        total = acc_ref[last : last + extra, :].astype(F32) + got_ref[last : last + extra, :].astype(F32)
        send_ref[half * rows : half * rows + extra, :] = total.astype(BF)
        keep_ref[half * rows : half * rows + extra, :] = total.astype(BF)


def fold(index, acc, got, pieces, extra):
    height, width = acc.shape
    rows = (height - extra) // pieces
    out = jax.ShapeDtypeStruct((rows * pieces // 2 + extra, width), BF)
    whole = pl.BlockSpec(memory_space=pltpu.VMEM)
    return pl.pallas_call(
        functools.partial(fold_kernel, pieces=pieces, extra=extra),
        in_specs=[pl.BlockSpec(memory_space=pltpu.SMEM), whole, whole],
        out_specs=[whole, whole],
        out_shape=[out, out],
        compiler_params=pltpu.CompilerParams(vmem_limit_bytes=VMEM_LIMIT),
        name="fold",
    )(index, acc, got)


def add_low(left, right):
    return (left.astype(F32) + right.astype(F32)).astype(BF)


def bits_of(size):
    return [1 << b for b in range(size.bit_length() - 1)]


def reduce_scatter(send, keep, extra):
    dp, shard = lax.axis_index("dp"), lax.axis_index("shard")
    dp_bits = bits_of(lax.axis_size("dp"))
    split = dp_bits[:3]
    odd = shard % 2
    even_plan = [("shard", 2)] + [("dp", b) for b in split]
    odd_plan = [("dp", b) for b in split] + [("shard", 2)]
    got = swap(send, "shard", 1)
    pieces = 2 ** (len(split) + 1)
    for phase, (even_dim, odd_dim) in enumerate(zip(even_plan, odd_plan)):
        def bit_of(dim):
            return (((dp if dim[0] == "dp" else shard) & dim[1]) != 0).astype(jnp.int32)

        bit = jnp.where(odd == 1, bit_of(odd_dim), bit_of(even_dim))
        rank = jnp.where((odd == 0) & (phase == 0), len(split), 0)
        j = jnp.arange(pieces // 2, dtype=jnp.int32)
        base = ((j >> rank) << (rank + 1)) | (j & ((1 << rank) - 1))
        index = jnp.concatenate([base | ((1 - bit) << rank), base | (bit << rank)]).astype(jnp.int32)
        send, keep = fold(index, keep, got, pieces, extra)
        got = exchange(send, even_dim, odd_dim)
        pieces //= 2
    total = add_low(keep, got)
    for b in dp_bits[3:]:
        total = add_low(total, swap(total, "dp", b))
    return total


def gather_dp(piece):
    split = bits_of(lax.axis_size("dp"))[:3]
    even_plan = [split[0]] + split[1:][::-1]
    odd_plan = split[::-1]
    odd = lax.axis_index("shard") % 2
    mask = jnp.zeros((1,), jnp.int32)
    for even_bit, odd_bit in zip(even_plan, odd_plan):
        piece = jnp.concatenate([piece, exchange(piece, ("dp", even_bit), ("dp", odd_bit))], axis=0)
        mask = jnp.concatenate([mask, mask | jnp.where(odd == 1, odd_bit, even_bit)])
    return piece, (lax.axis_index("dp") & (2 ** len(split) - 1)) ^ mask


def adam(master, first, second, grad, rate, decay):
    first_new = 0.5 * first + 0.5 * grad
    second_new = 0.5 * second + 0.5 * grad * grad
    correction = 1.0 - 0.5**STEP
    update = first_new / correction / (jnp.sqrt(second_new / correction) + 1e-08)
    return master - rate * (update + decay * master), first_new, second_new


def update_kernel(
    index_ref, factor_ref, early_ref, late_ref, gn_ref,
    am, af, as_, um, uf, us, dm, df, ds, nm, nf, ns,
    am2, af2, as2, um2, uf2, us2, dm2, df2, ds2, nm2, nf2, ns2, copy_ref, early, late
):
    step = pl.program_id(0)
    steps = pl.num_programs(0)
    factor = factor_ref[0]
    width = early.shape[1]
    part = late.shape[0] // 4

    @pl.when(step == 0)
    def _():
        count = index_ref.shape[0]
        for source, target in ((early_ref, early), (late_ref, late)):
            rows = target.shape[0] // count
            for j in range(count):
                place = pl.ds(pl.multiple_of(index_ref[j] * rows, rows), rows)
                target[place, :] = source[j * rows : (j + 1) * rows, :]
        new = adam(nm[...], nf[...], ns[...], gn_ref[...] * factor, 0.3, 0.0)
        nm2[...], nf2[...], ns2[...] = new
        copy_ref[copy_ref.shape[0] - SMALL :, :] = jnp.zeros((SMALL, width), BF)
        copy_ref[copy_ref.shape[0] - SMALL : copy_ref.shape[0] - SMALL + 4, 0 : nm.shape[1]] = new[0].astype(BF)

    height = part // steps

    def span(base, size):
        return pl.ds(pl.multiple_of(base + step * size, size), size)

    for m in range(5):
        source = late[span(m * part, height), :] if m < 4 else early[span(0, height), :]
        new = adam(am[m], af[m], as_[m], source.astype(F32) * factor, 0.05, 0.01)
        am2[m], af2[m], as2[m] = new
        copy_ref[span(m * part, height), :] = new[0].astype(BF)
    blocks = um.shape[1] // width
    for j in range(blocks):
        source = early[span((j + 1) * part, height), :]
        cols = slice(j * width, (j + 1) * width)
        new = adam(um[:, cols], uf[:, cols], us[:, cols], source.astype(F32) * factor, 0.05, 0.01)
        um2[:, cols], uf2[:, cols], us2[:, cols] = new
        copy_ref[span((5 + j) * part, height), :] = new[0].astype(BF)
    tall = dm.shape[0]
    source = early[(blocks + 1) * part : (blocks + 1) * part + width, span(0, tall)].astype(F32).T
    new = adam(dm[...], df[...], ds[...], source * factor, 0.05, 0.01)
    dm2[...], df2[...], ds2[...] = new
    copy_ref[span((5 + blocks) * part, tall), :] = new[0].astype(BF)


def update(index, factor, early, late, gn, attn, up, down, norm):
    steps = 4
    smem = pl.BlockSpec(memory_space=pltpu.SMEM)
    whole = lambda a: pl.BlockSpec(a.shape, lambda i: (0,) * len(a.shape))
    five, part, width = attn[0].shape
    specs = (
        [pl.BlockSpec((five, part // steps, width), lambda i: (0, i, 0))] * 3
        + [pl.BlockSpec((part // steps, up[0].shape[1]), lambda i: (i, 0))] * 3
        + [pl.BlockSpec((down[0].shape[0] // steps, width), lambda i: (i, 0))] * 3
        + [whole(norm[0])] * 3
    )
    states = tuple(attn) + tuple(up) + tuple(down) + tuple(norm)
    copy = jax.ShapeDtypeStruct((early.shape[0] + late.shape[0] + SMALL, width), BF)
    return pl.pallas_call(
        update_kernel,
        grid=(steps,),
        in_specs=[smem, smem, whole(early), whole(late), whole(gn)] + specs,
        out_specs=specs + [whole(copy)],
        out_shape=[jax.ShapeDtypeStruct(a.shape, F32) for a in states] + [copy],
        scratch_shapes=[pltpu.VMEM(early.shape, BF), pltpu.VMEM(late.shape, BF)],
        compiler_params=pltpu.CompilerParams(
            dimension_semantics=("arbitrary",), vmem_limit_bytes=VMEM_LIMIT
        ),
        name="update",
    )(index, factor, early, late, gn, *states)


def unpack_kernel(pos_ref, p0, p1, p2, p3, attn_ref, up_ref, down_ref, norm_ref):
    part = attn_ref.shape[1] // 4
    width = attn_ref.shape[2]
    blocks = up_ref.shape[1] // width
    tall = down_ref.shape[0] // 4
    for index, piece in enumerate((p0, p1, p2, p3)):
        pos = pos_ref[index]
        rows = pl.ds(pl.multiple_of(pos * part, part), part)
        for m in range(5):
            attn_ref[m, rows, :] = piece[m * part : (m + 1) * part, :]
        for j in range(blocks):
            up_ref[rows, j * width : (j + 1) * width] = piece[(5 + j) * part : (6 + j) * part, :]
        last = (5 + blocks) * part
        down_ref[pl.ds(pl.multiple_of(pos * tall, tall), tall), :] = piece[last : last + tall, :]
        norm_ref[0:4, rows] = piece[last + tall : last + tall + 4, 0:part]


def unpack(pos, pieces, width, hidden):
    whole = pl.BlockSpec(memory_space=pltpu.VMEM)
    return pl.pallas_call(
        unpack_kernel,
        in_specs=[pl.BlockSpec(memory_space=pltpu.SMEM)] + [whole] * 4,
        out_specs=[whole] * 4,
        out_shape=[
            jax.ShapeDtypeStruct((5, width, width), BF),
            jax.ShapeDtypeStruct((width, hidden), BF),
            jax.ShapeDtypeStruct((hidden, width), BF),
            jax.ShapeDtypeStruct((4, width), BF),
        ],
        compiler_params=pltpu.CompilerParams(vmem_limit_bytes=VMEM_LIMIT),
        name="unpack",
    )(pos, *pieces)


def gather_shard(own):
    across = swap(own, "shard", 2)
    return own, swap(own, "shard", 1), across, swap(across, "shard", 1)


def sum_all(values, axes):
    for axis in axes:
        for b in bits_of(lax.axis_size(axis)):
            values = values + swap(values, axis, b)
    return values


def shards(
    tokens, out_grad, domain_ids, domain_weight,
    attn_master, attn_first, attn_second,
    up_master, up_first, up_second,
    down_master, down_first, down_second,
    norm_master, norm_first, norm_second,
):
    width = tokens.shape[1]
    hidden = up_master.shape[1]
    part = width // 4
    blocks = hidden // width
    shard = lax.axis_index("shard").astype(jnp.int32)
    pos = shard ^ jnp.arange(4, dtype=jnp.int32)

    small = jnp.pad(norm_master.astype(BF), ((0, SMALL - 4), (0, width - part)))
    first = gather_shard(
        jnp.concatenate([attn_master[:4].astype(BF).reshape(4 * part, width), small])
    )
    second = gather_shard(
        jnp.concatenate(
            [attn_master[4].astype(BF)]
            + [up_master[:, j * width : (j + 1) * width].astype(BF) for j in range(blocks)]
            + [down_master.astype(BF)]
        )
    )

    domains = domain_weight.shape[0]
    onehot = (domain_ids[:, None] == jnp.arange(domains, dtype=jnp.int32)[None, :]).astype(F32)
    counts = sum_all(jnp.sum(onehot, axis=0), ("shard", "dp"))
    total_seqs = lax.axis_size("dp") * lax.axis_size("shard") * domain_ids.shape[0]
    per_domain = domain_weight * total_seqs / (domains * jnp.maximum(counts, 1.0))
    seq_weight = jnp.sum(onehot * per_domain[None, :], axis=1)

    q, k, v, n, e, eb, z, w, norm = project(pos, tokens, first)
    o, weights, scores, keys, values = mix(q, k, v, eb, z)
    y, dh, do, send, keep, dnorm = feed(pos, seq_weight, tokens, out_grad, o, norm, second)
    early = reduce_scatter(send, keep, 0)
    early, index = gather_dp(early)
    early_sq = jnp.sum(jnp.square(early.astype(F32)))
    dq, dk, dv, dc = mix_back(do, q, k, v, eb, e, z, weights, scores, keys, values)
    dx, send, keep = project_back(pos, tokens, n, dq, dk, dv, dc, dh, w, norm, dnorm)
    late = reduce_scatter(send, keep, SMALL)
    rows = late.shape[0] - SMALL
    norm_grad = lax.dynamic_slice(late[rows : rows + 4], (0, shard * part), (4, part)).astype(F32)
    late, _ = gather_dp(late[:rows])
    square = early_sq + jnp.sum(jnp.square(late.astype(F32))) + jnp.sum(jnp.square(norm_grad))
    clip_norm = jnp.sqrt(sum_all(square[None], ("shard",)))
    factor = jnp.minimum(1.0, 1.0 / (clip_norm + 1e-06))
    new = update(
        index, factor, early, late, norm_grad,
        (attn_master, attn_first, attn_second),
        (up_master, up_first, up_second),
        (down_master, down_first, down_second),
        (norm_master, norm_first, norm_second),
    )
    copies = unpack(pos, gather_shard(new[12]), width, hidden)
    return (y, dx) + tuple(new[:12]) + (clip_norm[0],) + tuple(copies)


def solution(mesh):
    rows = P(("dp", "shard"), None)
    attn = (P(None, "shard", None),) * 3
    tall = (P("shard", None),) * 6
    norm = (P(None, "shard"),) * 3
    return jax.shard_map(
        shards,
        mesh=mesh,
        in_specs=(rows, rows, P(("dp", "shard")), P()) + attn + tall + norm,
        out_specs=(rows, rows) + attn + tall + norm + (P(),) * 5,
        check_vma=False,
    )
```

time: 729 us -> 324 us (0.44); the launches traced: 717 us -> 324 us
  blocking collectives: 200 us -> 0 us
  matrix products: 193 us -> 0 us
  Pallas kernels: 0 us -> 128 us
  local copies, waits for them, and re-layouts: 99.2 us -> 10.4 us
  other arithmetic: 64.5 us -> 12.8 us
  starting transfers between devices: 0.63 us -> 47.2 us
  waiting for transfers between devices: 138 us -> 119 us
  between operations: 20.6 us -> 6.18 us
    dot_general x117 -> x0, matrix products: 193 us -> none  [the longest x110 167 us: product(): return rounded(left, right)]
    psum x3 -> x0, blocking collectives: 189 us -> none  [the longest x1 140 us: shards(): owned = lax.psum(parted, 'dp')]
    pallas_call x0 -> x15, Pallas kernels: none -> 128 us  [the longest x1 30.6 us: feed(): pl.pallas_call(feed_kernel, grid=(4,), in_specs=[pl.BlockSpec(memory_spac...]
    ppermute x0 -> x32, waiting for transfers between devices: none -> 119 us  [exchange(): return lax.ppermute(values, ('dp', 'shard'), perm)]
    reduce_scatter x3 -> x0, waiting for transfers between devices: 99.8 us -> none  [the longest x1 38 us: shards(): lax.psum_scatter(totals[0].astype(jnp.bfloat16), 'shard', scatter_dimensi...]
    ppermute x0 -> x32, starting transfers between devices: none -> 47.2 us  [exchange(): return lax.ppermute(values, ('dp', 'shard'), perm)]
    all_gather x6 -> x0, waiting for transfers between devices: 37.7 us -> none  [the longest x1 27.6 us: shards(): lax.all_gather(attn_new[0].astype(jnp.bfloat16), 'shard', axis=1, tiled=T...]
    unnamed x138 -> x43, local copies, waits for them, and re-layouts: 37.9 us -> 10.4 us
  transfers between devices with their start and end apart: 10 -> 32, of which waited for: 5 -> 19; matrix products, arithmetic and copies ran while one was open for 19% -> 3% of each run, Pallas kernels for 0% -> 23%
where the time goes in v1:
time: 324 us
  Pallas kernels  128 us (40%)
  waiting for transfers between devices  119 us (37%)
  starting transfers between devices  47.2 us (15%)
  other arithmetic  12.8 us (4%)
  local copies, waits for them, and re-layouts  10.4 us (3%)
  between operations  6.18 us (2%)
    ppermute x32, waiting for transfers between devices, exchange(): return lax.ppermute(values, ('dp', 'shard'), perm)  119 us
    ppermute x32, starting transfers between devices, exchange(): return lax.ppermute(values, ('dp', 'shard'), perm)  47.2 us
    pallas_call x1, Pallas kernels, feed(): pl.pallas_call(feed_kernel, grid=(4,), in_specs=[pl.BlockSpec(memory_spac...  30.6 us
    pallas_call x1, Pallas kernels, mix_back(): pl.pallas_call(mix_back_kernel, grid=(groups, steps), in_specs=[block] *...  25.9 us
    pallas_call x8, Pallas kernels, fold(): pl.pallas_call(functools.partial(fold_kernel, pieces=pieces, extra=extra)...  19.6 us
    pallas_call x1, Pallas kernels, mix(): pl.pallas_call(mix_kernel, grid=(groups, steps), in_specs=[block] * 5, ou...  14.9 us
    pallas_call x1, Pallas kernels, update(): pl.pallas_call(update_kernel, grid=(steps,), in_specs=[smem, smem, whole(...  11.1 us
    pallas_call x1, Pallas kernels, project_back(): pl.pallas_call(project_back_kernel, grid=(length // tile,), in_specs=[pl....  10.9 us
  transfers between devices with their start and end apart: 32, of which 19 were waited for; matrix products, arithmetic and copies ran while one was open for 3% of the time, Pallas kernels for 23%

profile of v1, /device:TPU:0, one launch (start us, length us, event | category | flops | bytes accessed | tf_op | source)
XLA Modules:
  0.0 323.7 jit_solution(7969744974721788604)
XLA Ops:
  3.6 3.0 collective-permute-start.9
  6.7 25.9 %collective-permute-done.9.p2 = bf16[1152,512]{1,0:T(8,128)(2,1)S(1)} collective-permute-done((bf16[1152,512]{1,0:T(8,128)(2,1)S(1)}, bf16[1152,512]{1,0:T(8,128)(2,1)S(1)}, u32[]{:S(2)}, u32[]{:S(2)}) %collective-permute-start.9) | collective-permute-done | bytes 1179680 | tf_op jit(solution)/shard_map/ppermute | solution.py:495
  36.3 11.2 %collective-permute-done.6.p2 = bf16[528,512]{1,0:T(8,128)(2,1)} collective-permute-done((bf16[528,512]{1,0:T(8,128)(2,1)S(1)}, bf16[528,512]{1,0:T(8,128)(2,1)}, u32[]{:S(2)}, u32[]{:S(2)}) %collective-permute-start.6) | collective-permute-done | bytes 540704 | tf_op jit(solution)/shard_map/ppermute | solution.py:495
  58.2 2.8 collective-permute-start.4
  64.1 8.4 %project.1 = (bf16[1024,512]{1,0:T(8,128)(2,1)}, bf16[1024,512]{1,0:T(8,128)(2,1)}, bf16[1024,512]{1,0:T(8,128)(2,1)}, bf16[1024,512]{1,0:T(8,128)(2,1)}, f32[10...) custom-call(s32[4]{0:T(128)} %iota_xor_fusion.pos_ref, ...), custom_call_target="tpu_custom_call" | custom-call | tf_op jit(solution)/shard_map/project/pallas_call | solution.py:131
  72.5 14.9 %mix.1 = (bf16[1024,512]{1,0:T(8,128)(2,1)}, f32[1024,512]{1,0:T(8,128)}, f32[1024,512]{1,0:T(8,128)}, bf16[2,4,256,256]{3,2,1,0:T(8,128)(2,1)}, bf16[2,4,256,256]{3,2,1,0:T(8,128)(2,1)}) custom-call(bf16[1024,512]{1,0:T(8,128)(2,1)} %get-tuple-element.79.q_ref, bf16[1024,512]{1,0:T(8,128)(2,1)} %get-tuple-element.80.k_ref, ...), custom_call_target="tpu_custom_call" | custom-call | tf_op jit(solution)/shard_map/mix/pallas_call | solution.py:188
  87.5 30.6 %feed.1 = (bf16[1024,512]{1,0:T(8,128)(2,1)}, f32[1024,512]{1,0:T(8,128)}, bf16[1024,512]{1,0:T(8,128)(2,1)}, bf16[2304,512]{1,0:T(8,128)(2,1)}, bf16[2304,512]{1,0:T(8,128)(2,1)}, /*index=5*/f32[8,512]{1,0:T(8,128)}) custom-call(s32[4]{0:T(128)} %iota_xor_fusion.pos_ref, f32[1]{0:T(128)} %bitcast.1.factor_ref, bf16[1024,512]{1,0:T(8,128)(2,1)} %x_ref.5, ...), custom_call_target="tpu_custom_call" | custom-call | tf_op jit(solution)/shard_map/feed/pallas_call | solution.py:395
  118.7 4.1 %collective-permute-done.11.got_ref = bf16[2304,512]{1,0:T(8,128)(2,1)S(1)} collective-permute-done((bf16[2304,512]{1,0:T(8,128)(2,1)}, bf16[2304,512]{1,0:T(8,128)(2,1)S(1)}, u32[]{:S(2)}, u32[]{:S(2)}) %collective-permute-start.11) | collective-permute-done | bytes 2359328 | tf_op jit(solution)/shard_map/ppermute | solution.py:495
  124.2 4.3 %fold.8 = (bf16[1152,512]{1,0:T(8,128)(2,1)}, bf16[1152,512]{1,0:T(8,128)(2,1)}) custom-call(s32[16]{0:T(128)} %pad_add_fusion.3.index_ref, bf16[2304,512]{1,0:T(8,128)(2,1)} %get-tuple-element.102.acc_ref, bf16[2304,512]{1,0:T(8,128)(2,1)} %copy-done.2), custom_call_target="tpu_custom_call" | custom-call | tf_op jit(solution)/shard_map/fold/pallas_call | solution.py:522
  130.2 25.9 %mix_back.1 = (bf16[1024,512]{1,0:T(8,128)(2,1)}, bf16[1024,512]{1,0:T(8,128)(2,1)}, bf16[1024,512]{1,0:T(8,128)(2,1)}, bf16[1024,512]{1,0:T(8,128)(2,1)}) custom-call(bf16[1024,512]{1,0:T(8,128)(2,1)} %get-tuple-element.88.g_ref, bf16[1024,512]{1,0:T(8,128)(2,1)} %get-tuple-element.79.q_ref, bf16[1024,512]{1,0:T(8,128)(2,1)} %get-tuple-element.80.k_ref, ...), custom_call_target="tpu_custom_call" | custom-call | tf_op jit(solution)/shard_map/mix_back/pallas_call | solution.py:259
  156.1 10.9 %project_back.1 = (f32[1024,512]{1,0:T(8,128)}, bf16[1040,512]{1,0:T(8,128)(2,1)}, bf16[1040,512]{1,0:T(8,128)(2,1)}) custom-call(s32[4]{0:T(128)} %iota_xor_fusion.pos_ref, bf16[1024,512]{1,0:T(8,128)(2,1)} %x_ref.5, bf16[1024,512]{1,0:T(8,128)(2,1)} %get-tuple-element.87.n_ref, bf16[1024,512]{1,0:T(8,128)(2,1)} %get-tuple-element.94.dq_ref, ...), custom_call_target="tpu_custom_call" | custom-call | tf_op jit(solution)/shard_map/project_back/pallas_call | solution.py:471
  168.7 2.9 fold.9
  174.1 2.8 fold.12
  178.0 5.4 %collective-permute-done.13.got_ref = bf16[576,512]{1,0:T(8,128)(2,1)S(1)} collective-permute-done((bf16[576,512]{1,0:T(8,128)(2,1)}, bf16[576,512]{1,0:T(8,128)(2,1)S(1)}, u32[]{:S(2)}, u32[]{:S(2)}) %collective-permute-start.13) | collective-permute-done | bytes 589856 | tf_op jit(solution)/shard_map/ppermute | solution.py:495
  184.1 2.2 fold.10
  186.3 2.7 collective-permute-start.14
  189.8 2.1 fold.13
  194.0 3.5 %collective-permute-done.14.got_ref = bf16[288,512]{1,0:T(8,128)(2,1)S(1)} collective-permute-done((bf16[288,512]{1,0:T(8,128)(2,1)}, bf16[288,512]{1,0:T(8,128)(2,1)S(1)}, u32[]{:S(2)}, u32[]{:S(2)}) %collective-permute-start.14) | collective-permute-done | bytes 294944 | tf_op jit(solution)/shard_map/ppermute | solution.py:495
  200.0 4.6 %collective-permute-start.15 = (bf16[144,512]{1,0:T(8,128)(2,1)}, bf16[144,512]{1,0:T(8,128)(2,1)S(1)}, u32[]{:S(2)}, u32[]{:S(2)}) collective-permute-start(bf16[144,512]{1,0:T(8,128)(2,1)} %get-tuple-element.111), channel_id=1, source_target_pairs={{0,16},{1,3},{2,18},{3,1},{4,20},{5,7},{6,22},{7,5},{8,24},{9,11},... | collective-permute-start | bytes 442376 | tf_op jit(solution)/shard_map/ppermute | solution.py:495
  207.2 2.4 collective-permute-start.22
  209.5 4.8 %collective-permute-done.15 = bf16[144,512]{1,0:T(8,128)(2,1)S(1)} collective-permute-done((bf16[144,512]{1,0:T(8,128)(2,1)}, bf16[144,512]{1,0:T(8,128)(2,1)S(1)}, u32[]{:S(2)}, u32[]{:S(2)}) %collective-permute-start.15) | collective-permute-done | bytes 147488 | tf_op jit(solution)/shard_map/ppermute | solution.py:495
  222.2 4.1 %collective-permute-done.23 = bf16[80,512]{1,0:T(8,128)(2,1)S(1)} collective-permute-done((bf16[80,512]{1,0:T(8,128)(2,1)}, bf16[80,512]{1,0:T(8,128)(2,1)S(1)}, u32[]{:S(2)}, u32[]{:S(2)}) %collective-permute-start.23) | collective-permute-done | bytes 81952 | tf_op jit(solution)/shard_map/ppermute | solution.py:495
  227.5 4.1 %collective-permute-done.24 = bf16[64,512]{1,0:T(8,128)(2,1)S(1)} collective-permute-done((bf16[64,512]{1,0:T(8,128)(2,1)S(1)}, bf16[64,512]{1,0:T(8,128)(2,1)S(1)}, u32[]{:S(2)}, u32[]{:S(2)}) %collective-permute-start.24) | collective-permute-done | bytes 65568 | tf_op jit(solution)/shard_map/ppermute | solution.py:495
  232.8 4.9 %collective-permute-start.18 = (bf16[576,512]{1,0:T(8,128)(2,1)S(1)}, bf16[576,512]{1,0:T(8,128)(2,1)S(1)}, u32[]{:S(2)}, u32[]{:S(2)}) collective-permute-start(bf16[576,512]{1,0:T(8,128)(2,1)S(1)} %pad_maximum_fusion.1), channel_id=1, source_target_pairs={{0,8},{1,5},{2,10},{3,7},{4,12},{5,1},{6,14},{7,3},{8,0},{9,13},{1... | collective-permute-start | bytes 1769480 | tf_op jit(solution)/shard_map/ppermute | solution.py:495
  237.8 2.8 collective-permute-start.26
  242.4 5.9 %collective-permute-done.26 = bf16[256,512]{1,0:T(8,128)(2,1)S(1)} collective-permute-done((bf16[256,512]{1,0:T(8,128)(2,1)S(1)}, bf16[256,512]{1,0:T(8,128)(2,1)S(1)}, u32[]{:S(2)}, u32[]{:S(2)}) %collective-permute-start.26) | collective-permute-done | bytes 262176 | tf_op jit(solution)/shard_map/ppermute | solution.py:495
  249.9 2.2 multiply_reduce_fusion
  255.9 4.3 %collective-permute-start.28 = (f32[1]{0:T(128)}, f32[1]{0:T(128)}, u32[]{:S(2)}, u32[]{:S(2)}) collective-permute-start(f32[1]{0:T(128)} %add.71), channel_id=1, source_target_pairs={{0,2},{1,3},{2,0},{3,1},{4,6},{5,7},{6,4},{7,5},{8,10},{9,11},{10,... | collective-permute-start | bytes 20 | tf_op jit(solution)/shard_map/ppermute | solution.py:495
  261.1 11.1 %update.1 = (f32[5,128,512]{2,1,0:T(8,128)}, f32[5,128,512]{2,1,0:T(8,128)}, f32[5,128,512]{2,1,0:T(8,128)}, f32[128,2048]{1,0:T(8,128)}, f32[128,2048]{1,0:T(8,...) custom-call(s32[8]{0:T(128)} %add_xor_fusion.index_ref, ...), custom_call_target="tpu_custom_call" | custom-call | tf_op jit(solution)/shard_map/update/pallas_call | solution.py:648
  274.3 37.2 %collective-permute-done.30.p2 = bf16[1680,512]{1,0:T(8,128)(2,1)S(1)} collective-permute-done((bf16[1680,512]{1,0:T(8,128)(2,1)}, bf16[1680,512]{1,0:T(8,128)(2,1)S(1)}, u32[]{:S(2)}, u32[]{:S(2)}) %collective-permute-start.30) | collective-permute-done | bytes 1720352 | tf_op jit(solution)/shard_map/ppermute | solution.py:495
  311.5 3.6 %collective-permute-done.31.p3 = bf16[1680,512]{1,0:T(8,128)(2,1)S(1)} collective-permute-done((bf16[1680,512]{1,0:T(8,128)(2,1)S(1)}, bf16[1680,512]{1,0:T(8,128)(2,1)S(1)}, u32[]{:S(2)}, u32[]{:S(2)}) %collective-permute-start.31) | collective-permute-done | bytes 1720352 | tf_op jit(solution)/shard_map/ppermute | solution.py:495
  316.3 6.3 %unpack.1 = (bf16[5,512,512]{2,1,0:T(8,128)(2,1)}, bf16[512,2048]{1,0:T(8,128)(2,1)}, bf16[2048,512]{1,0:T(8,128)(2,1)}, bf16[4,512]{1,0:T(4,128)(2,1)}) custom-call(s32[4]{0:T(128)} %iota_xor_fusion.pos_ref, bf16[1680,512]{1,0:T(8,128)(2,1)} %get-tuple-element.134.p0, bf16[1680,512]{1,0:T(8,128)(2,1)} %copy-done.5, bf16[1680,512]{1,0:T(8,128)(2,1)} %copy-done.4, ...), custom_call_target="tpu_custom_call" | custom-call | tf_op jit(solution)/shard_map/unpack/pallas_call | solution.py:681
  (125 shorter events, 55.8 us)
Async XLA Ops:
  3.6 29.0 %collective-permute-start.9 = (bf16[1152,512]{1,0:T(8,128)(2,1)S(1)}, bf16[1152,512]{1,0:T(8,128)(2,1)S(1)}, u32[]{:S(2)}, u32[]{:S(2)}) collective-permute-start(bf16[1152,512]{1,0:T(8,128)(2,1)S(1)} %convert_dynamic-update-slice_fusion.p0), channel_id=1, source_target_pairs={{0,2},{1,3},{2,0},{3,1},{4,6},{5,7},{6,4},{7,5},{8,10},{9,11},{10,... | collective-permute-start | bytes 3538952 | tf_op jit(solution)/shard_map/ppermute | solution.py:495
  6.6 80.8 %collective-permute-start.8 = (bf16[1152,512]{1,0:T(8,128)(2,1)S(1)}, bf16[1152,512]{1,0:T(8,128)(2,1)}, u32[]{:S(2)}, u32[]{:S(2)}) collective-permute-start(bf16[1152,512]{1,0:T(8,128)(2,1)S(1)} %convert_dynamic-update-slice_fusion.p0), channel_id=1, source_target_pairs={{0,1},{1,0},{2,3},{3,2},{4,5},{5,4},{6,7},{7,6},{8,9},{9,8},{10,11... | collective-permute-start | bytes 3538952 | tf_op jit(solution)/shard_map/ppermute | solution.py:495
  32.6 54.9 %collective-permute-start.10 = (bf16[1152,512]{1,0:T(8,128)(2,1)S(1)}, bf16[1152,512]{1,0:T(8,128)(2,1)}, u32[]{:S(2)}, u32[]{:S(2)}) collective-permute-start(bf16[1152,512]{1,0:T(8,128)(2,1)S(1)} %collective-permute-done.9.p2), channel_id=1, source_target_pairs={{0,1},{1,0},{2,3},{3,2},{4,5},{5,4},{6,7},{7,6},{8,9},{9,8},{10,11... | collective-permute-start | bytes 3538952 | tf_op jit(solution)/shard_map/ppermute | solution.py:495
  32.6 14.9 %collective-permute-start.6 = (bf16[528,512]{1,0:T(8,128)(2,1)S(1)}, bf16[528,512]{1,0:T(8,128)(2,1)}, u32[]{:S(2)}, u32[]{:S(2)}) collective-permute-start(bf16[528,512]{1,0:T(8,128)(2,1)S(1)} %fusion.1.p0), channel_id=1, source_target_pairs={{0,2},{1,3},{2,0},{3,1},{4,6},{5,7},{6,4},{7,5},{8,10},{9,11},{10,... | collective-permute-start | bytes 1622024 | tf_op jit(solution)/shard_map/ppermute | solution.py:495
  34.4 28.8 %collective-permute-start.5 = (bf16[528,512]{1,0:T(8,128)(2,1)S(1)}, bf16[528,512]{1,0:T(8,128)(2,1)}, u32[]{:S(2)}, u32[]{:S(2)}) collective-permute-start(bf16[528,512]{1,0:T(8,128)(2,1)S(1)} %fusion.1.p0), channel_id=1, source_target_pairs={{0,1},{1,0},{2,3},{3,2},{4,5},{5,4},{6,7},{7,6},{8,9},{9,8},{10,11... | collective-permute-start | bytes 1622024 | tf_op jit(solution)/shard_map/ppermute | solution.py:495
  35.3 12.2 %collective-permute-start = (f32[8]{0:T(128)S(1)}, f32[8]{0:T(128)S(1)}, u32[]{:S(2)}, u32[]{:S(2)}) collective-permute-start(f32[8]{0:T(128)S(1)} %compare_convert_fusion), channel_id=1, source_target_pairs={{0,1},{1,0},{2,3},{3,2},{4,5},{5,4},{6,7},{7,6},{8,9},{9,8},{10,11... | collective-permute-start | bytes 104 | tf_op jit(solution)/shard_map/ppermute | solution.py:495
  47.5 15.8 %collective-permute-start.7 = (bf16[528,512]{1,0:T(8,128)(2,1)}, bf16[528,512]{1,0:T(8,128)(2,1)S(1)}, u32[]{:S(2)}, u32[]{:S(2)}) collective-permute-start(bf16[528,512]{1,0:T(8,128)(2,1)} %collective-permute-done.6.p2), channel_id=1, source_target_pairs={{0,1},{1,0},{2,3},{3,2},{4,5},{5,4},{6,7},{7,6},{8,9},{9,8},{10,11... | collective-permute-start | bytes 1622024 | tf_op jit(solution)/shard_map/ppermute | solution.py:495
  47.5 3.6 %collective-permute-start.1 = (f32[8]{0:T(128)S(1)}, f32[8]{0:T(128)S(1)}, u32[]{:S(2)}, u32[]{:S(2)}) collective-permute-start(f32[8]{0:T(128)S(1)} %fusion.8), channel_id=1, source_target_pairs={{0,2},{1,3},{2,0},{3,1},{4,6},{5,7},{6,4},{7,5},{8,10},{9,11},{10,... | collective-permute-start | bytes 104 | tf_op jit(solution)/shard_map/ppermute | solution.py:495
  51.1 3.5 %collective-permute-start.2 = (f32[8]{0:T(128)S(1)}, f32[8]{0:T(128)S(1)}, u32[]{:S(2)}, u32[]{:S(2)}) collective-permute-start(f32[8]{0:T(128)S(1)} %fusion.9), channel_id=1, source_target_pairs={{0,4},{1,5},{2,6},{3,7},{4,0},{5,1},{6,2},{7,3},{8,12},{9,13},{10,... | collective-permute-start | bytes 104 | tf_op jit(solution)/shard_map/ppermute | solution.py:495
  54.7 3.5 %collective-permute-start.3 = (f32[8]{0:T(128)S(1)}, f32[8]{0:T(128)S(1)}, u32[]{:S(2)}, u32[]{:S(2)}) collective-permute-start(f32[8]{0:T(128)S(1)} %add.61), channel_id=1, source_target_pairs={{0,8},{1,9},{2,10},{3,11},{4,12},{5,13},{6,14},{7,15},{8,0},{9,1},... | collective-permute-start | bytes 104 | tf_op jit(solution)/shard_map/ppermute | solution.py:495
  58.2 4.4 %collective-permute-start.4 = (f32[8]{0:T(128)S(1)}, f32[8]{0:T(128)S(1)}, u32[]{:S(2)}, u32[]{:S(2)}) collective-permute-start(f32[8]{0:T(128)S(1)} %add.62), channel_id=1, source_target_pairs={{0,16},{1,17},{2,18},{3,19},{4,20},{5,21},{6,22},{7,23},{8,24},{9,... | collective-permute-start | bytes 104 | tf_op jit(solution)/shard_map/ppermute | solution.py:495
  118.0 4.7 %collective-permute-start.11 = (bf16[2304,512]{1,0:T(8,128)(2,1)}, bf16[2304,512]{1,0:T(8,128)(2,1)S(1)}, u32[]{:S(2)}, u32[]{:S(2)}) collective-permute-start(bf16[2304,512]{1,0:T(8,128)(2,1)} %get-tuple-element.103), channel_id=1, source_target_pairs={{0,1},{1,0},{2,3},{3,2},{4,5},{5,4},{6,7},{7,6},{8,9},{9,8},{10,11... | collective-permute-start | bytes 7077896 | tf_op jit(solution)/shard_map/ppermute | solution.py:495
  128.5 39.2 %collective-permute-start.12 = (bf16[1152,512]{1,0:T(8,128)(2,1)}, bf16[1152,512]{1,0:T(8,128)(2,1)S(1)}, u32[]{:S(2)}, u32[]{:S(2)}) collective-permute-start(bf16[1152,512]{1,0:T(8,128)(2,1)} %get-tuple-element.105), channel_id=1, source_target_pairs={{0,2},{1,5},{2,0},{3,7},{4,6},{5,1},{6,4},{7,3},{8,10},{9,13},{10,... | collective-permute-start | bytes 3538952 | tf_op jit(solution)/shard_map/ppermute | solution.py:495
  167.0 6.1 %collective-permute-start.19 = (bf16[1040,512]{1,0:T(8,128)(2,1)}, bf16[1040,512]{1,0:T(8,128)(2,1)S(1)}, u32[]{:S(2)}, u32[]{:S(2)}) collective-permute-start(bf16[1040,512]{1,0:T(8,128)(2,1)} %get-tuple-element.113), channel_id=1, source_target_pairs={{0,1},{1,0},{2,3},{3,2},{4,5},{5,4},{6,7},{7,6},{8,9},{9,8},{10,11... | collective-permute-start | bytes 3194888 | tf_op jit(solution)/shard_map/ppermute | solution.py:495
  171.6 11.8 %collective-permute-start.13 = (bf16[576,512]{1,0:T(8,128)(2,1)}, bf16[576,512]{1,0:T(8,128)(2,1)S(1)}, u32[]{:S(2)}, u32[]{:S(2)}) collective-permute-start(bf16[576,512]{1,0:T(8,128)(2,1)} %get-tuple-element.107), channel_id=1, source_target_pairs={{0,4},{1,9},{2,6},{3,11},{4,0},{5,13},{6,2},{7,15},{8,12},{9,1},{1... | collective-permute-start | bytes 1769480 | tf_op jit(solution)/shard_map/ppermute | solution.py:495
  176.9 12.2 %collective-permute-start.20 = (bf16[528,512]{1,0:T(8,128)(2,1)}, bf16[528,512]{1,0:T(8,128)(2,1)S(1)}, u32[]{:S(2)}, u32[]{:S(2)}) collective-permute-start(bf16[528,512]{1,0:T(8,128)(2,1)} %get-tuple-element.115), channel_id=1, source_target_pairs={{0,2},{1,5},{2,0},{3,7},{4,6},{5,1},{6,4},{7,3},{8,10},{9,13},{10,... | collective-permute-start | bytes 1622024 | tf_op jit(solution)/shard_map/ppermute | solution.py:495
  186.3 11.2 %collective-permute-start.14 = (bf16[288,512]{1,0:T(8,128)(2,1)}, bf16[288,512]{1,0:T(8,128)(2,1)S(1)}, u32[]{:S(2)}, u32[]{:S(2)}) collective-permute-start(bf16[288,512]{1,0:T(8,128)(2,1)} %get-tuple-element.109), channel_id=1, source_target_pairs={{0,8},{1,17},{2,10},{3,19},{4,12},{5,21},{6,14},{7,23},{8,0},{9,25... | collective-permute-start | bytes 884744 | tf_op jit(solution)/shard_map/ppermute | solution.py:495
  192.0 12.7 %collective-permute-start.21 = (bf16[272,512]{1,0:T(8,128)(2,1)}, bf16[272,512]{1,0:T(8,128)(2,1)S(1)}, u32[]{:S(2)}, u32[]{:S(2)}) collective-permute-start(bf16[272,512]{1,0:T(8,128)(2,1)} %get-tuple-element.117), channel_id=1, source_target_pairs={{0,4},{1,9},{2,6},{3,11},{4,0},{5,13},{6,2},{7,15},{8,12},{9,1},{1... | collective-permute-start | bytes 835592 | tf_op jit(solution)/shard_map/ppermute | solution.py:495
  200.0 14.3 %collective-permute-start.15 = (bf16[144,512]{1,0:T(8,128)(2,1)}, bf16[144,512]{1,0:T(8,128)(2,1)S(1)}, u32[]{:S(2)}, u32[]{:S(2)}) collective-permute-start(bf16[144,512]{1,0:T(8,128)(2,1)} %get-tuple-element.111), channel_id=1, source_target_pairs={{0,16},{1,3},{2,18},{3,1},{4,20},{5,7},{6,22},{7,5},{8,24},{9,11},... | collective-permute-start | bytes 442376 | tf_op jit(solution)/shard_map/ppermute | solution.py:495
  207.2 9.7 %collective-permute-start.22 = (bf16[144,512]{1,0:T(8,128)(2,1)}, bf16[144,512]{1,0:T(8,128)(2,1)S(1)}, u32[]{:S(2)}, u32[]{:S(2)}) collective-permute-start(bf16[144,512]{1,0:T(8,128)(2,1)} %get-tuple-element.119), channel_id=1, source_target_pairs={{0,8},{1,17},{2,10},{3,19},{4,12},{5,21},{6,14},{7,23},{8,0},{9,25... | collective-permute-start | bytes 442376 | tf_op jit(solution)/shard_map/ppermute | solution.py:495
  215.3 5.2 %collective-permute-start.16 = (bf16[144,512]{1,0:T(8,128)(2,1)S(1)}, bf16[144,512]{1,0:T(8,128)(2,1)S(1)}, u32[]{:S(2)}, u32[]{:S(2)}) collective-permute-start(bf16[144,512]{1,0:T(8,128)(2,1)S(1)} %add_convert_fusion), channel_id=1, source_target_pairs={{0,4},{1,17},{2,6},{3,19},{4,0},{5,21},{6,2},{7,23},{8,12},{9,25},... | collective-permute-start | bytes 442376 | tf_op jit(solution)/shard_map/ppermute | solution.py:495
  219.2 7.1 %collective-permute-start.23 = (bf16[80,512]{1,0:T(8,128)(2,1)}, bf16[80,512]{1,0:T(8,128)(2,1)S(1)}, u32[]{:S(2)}, u32[]{:S(2)}) collective-permute-start(bf16[80,512]{1,0:T(8,128)(2,1)} %get-tuple-element.121), channel_id=1, source_target_pairs={{0,16},{1,3},{2,18},{3,1},{4,20},{5,7},{6,22},{7,5},{8,24},{9,11},... | collective-permute-start | bytes 245768 | tf_op jit(solution)/shard_map/ppermute | solution.py:495
  220.5 12.2 %collective-permute-start.17 = (bf16[288,512]{1,0:T(8,128)(2,1)S(1)}, bf16[288,512]{1,0:T(8,128)(2,1)S(1)}, u32[]{:S(2)}, u32[]{:S(2)}) collective-permute-start(bf16[288,512]{1,0:T(8,128)(2,1)S(1)} %pad_maximum_fusion.3), channel_id=1, source_target_pairs={{0,16},{1,9},{2,18},{3,11},{4,20},{5,13},{6,22},{7,15},{8,24},{9,1... | collective-permute-start | bytes 884744 | tf_op jit(solution)/shard_map/ppermute | solution.py:495
  227.3 4.3 %collective-permute-start.24 = (bf16[64,512]{1,0:T(8,128)(2,1)S(1)}, bf16[64,512]{1,0:T(8,128)(2,1)S(1)}, u32[]{:S(2)}, u32[]{:S(2)}) collective-permute-start(bf16[64,512]{1,0:T(8,128)(2,1)S(1)} %slice.44), channel_id=1, source_target_pairs={{0,4},{1,17},{2,6},{3,19},{4,0},{5,21},{6,2},{7,23},{8,12},{9,25},... | collective-permute-start | bytes 196616 | tf_op jit(solution)/shard_map/ppermute | solution.py:495
  231.6 6.1 %collective-permute-start.25 = (bf16[128,512]{1,0:T(8,128)(2,1)S(1)}, bf16[128,512]{1,0:T(8,128)(2,1)S(1)}, u32[]{:S(2)}, u32[]{:S(2)}) collective-permute-start(bf16[128,512]{1,0:T(8,128)(2,1)S(1)} %pad_maximum_fusion.5), channel_id=1, source_target_pairs={{0,16},{1,9},{2,18},{3,11},{4,20},{5,13},{6,22},{7,15},{8,24},{9,1... | collective-permute-start | bytes 393224 | tf_op jit(solution)/shard_map/ppermute | solution.py:495
  232.8 17.1 %collective-permute-start.18 = (bf16[576,512]{1,0:T(8,128)(2,1)S(1)}, bf16[576,512]{1,0:T(8,128)(2,1)S(1)}, u32[]{:S(2)}, u32[]{:S(2)}) collective-permute-start(bf16[576,512]{1,0:T(8,128)(2,1)S(1)} %pad_maximum_fusion.1), channel_id=1, source_target_pairs={{0,8},{1,5},{2,10},{3,7},{4,12},{5,1},{6,14},{7,3},{8,0},{9,13},{1... | collective-permute-start | bytes 1769480 | tf_op jit(solution)/shard_map/ppermute | solution.py:495
  237.8 10.6 %collective-permute-start.26 = (bf16[256,512]{1,0:T(8,128)(2,1)S(1)}, bf16[256,512]{1,0:T(8,128)(2,1)S(1)}, u32[]{:S(2)}, u32[]{:S(2)}) collective-permute-start(bf16[256,512]{1,0:T(8,128)(2,1)S(1)} %pad_maximum_fusion.4), channel_id=1, source_target_pairs={{0,8},{1,5},{2,10},{3,7},{4,12},{5,1},{6,14},{7,3},{8,0},{9,13},{1... | collective-permute-start | bytes 786440 | tf_op jit(solution)/shard_map/ppermute | solution.py:495
  254.0 1.2 collective-permute-start.27
  255.9 4.5 %collective-permute-start.28 = (f32[1]{0:T(128)}, f32[1]{0:T(128)}, u32[]{:S(2)}, u32[]{:S(2)}) collective-permute-start(f32[1]{0:T(128)} %add.71), channel_id=1, source_target_pairs={{0,2},{1,3},{2,0},{3,1},{4,6},{5,7},{6,4},{7,5},{8,10},{9,11},{10,... | collective-permute-start | bytes 20 | tf_op jit(solution)/shard_map/ppermute | solution.py:495
  272.3 39.3 %collective-permute-start.30 = (bf16[1680,512]{1,0:T(8,128)(2,1)}, bf16[1680,512]{1,0:T(8,128)(2,1)S(1)}, u32[]{:S(2)}, u32[]{:S(2)}) collective-permute-start(bf16[1680,512]{1,0:T(8,128)(2,1)} %get-tuple-element.134.p0), channel_id=1, source_target_pairs={{0,2},{1,3},{2,0},{3,1},{4,6},{5,7},{6,4},{7,5},{8,10},{9,11},{10,... | collective-permute-start | bytes 5160968 | tf_op jit(solution)/shard_map/ppermute | solution.py:495
  274.3 37.2 %collective-permute-start.29 = (bf16[1680,512]{1,0:T(8,128)(2,1)}, bf16[1680,512]{1,0:T(8,128)(2,1)S(1)}, u32[]{:S(2)}, u32[]{:S(2)}) collective-permute-start(bf16[1680,512]{1,0:T(8,128)(2,1)} %get-tuple-element.134.p0), channel_id=1, source_target_pairs={{0,1},{1,0},{2,3},{3,2},{4,5},{5,4},{6,7},{7,6},{8,9},{9,8},{10,11... | collective-permute-start | bytes 5160968 | tf_op jit(solution)/shard_map/ppermute | solution.py:495
  311.5 3.6 %collective-permute-start.31 = (bf16[1680,512]{1,0:T(8,128)(2,1)S(1)}, bf16[1680,512]{1,0:T(8,128)(2,1)S(1)}, u32[]{:S(2)}, u32[]{:S(2)}) collective-permute-start(bf16[1680,512]{1,0:T(8,128)(2,1)S(1)} %collective-permute-done.30.p2), channel_id=1, source_target_pairs={{0,1},{1,0},{2,3},{3,2},{4,5},{5,4},{6,7},{7,6},{8,9},{9,8},{10,11... | collective-permute-start | bytes 5160968 | tf_op jit(solution)/shard_map/ppermute | solution.py:495
  (19 other events, 235.8 us)

commit v2 on v1

v2 whole, which is shorter than its diff:
```python
import functools
import jax
import jax.numpy as jnp
from jax import lax
from jax.experimental import pallas as pl
from jax.experimental.pallas import tpu as pltpu
from jax.sharding import PartitionSpec as P

BF = jnp.bfloat16
F32 = jnp.float32
VMEM_LIMIT = 56 * 1024 * 1024
VMEM_SMALL = 24 * 1024 * 1024
CHUNK = 256
SLOT = 64
GROUP = 256
LANES = 128
SMALL = 16
CHEAP = pl.CostEstimate(flops=1, bytes_accessed=1, transcendentals=0)
STEP = 10


def whole(a):
    return pl.BlockSpec(a.shape, lambda *_: (0,) * len(a.shape), pipeline_mode=pl.Buffered(1))


def dot(a, b):
    return jnp.dot(a, b, preferred_element_type=F32)


def dot_nt(a, b):
    return lax.dot_general(a, b, (((1,), (1,)), ((), ())), preferred_element_type=F32)


def dot_tn(a, b):
    return lax.dot_general(a, b, (((0,), (0,)), ((), ())), preferred_element_type=F32)


def head_of(shape, dim):
    return lax.broadcasted_iota(jnp.int32, shape, dim) // SLOT


def block_diagonal(state):
    return jnp.where(head_of(state.shape, 0) == head_of(state.shape, 1), state, 0.0).astype(BF)


def only_head(rows, head):
    return jnp.where(head_of(rows.shape, 1) == head, rows, jnp.zeros_like(rows))


def lower(square):
    row = lax.broadcasted_iota(jnp.int32, square.shape, 0)
    col = lax.broadcasted_iota(jnp.int32, square.shape, 1)
    return jnp.where(row >= col, square, 0.0).astype(BF)


def upper(square):
    row = lax.broadcasted_iota(jnp.int32, square.shape, 0)
    col = lax.broadcasted_iota(jnp.int32, square.shape, 1)
    return jnp.where(row <= col, square, 0.0).astype(BF)


def split_dot(ones, values):
    high = values.astype(BF)
    low = (values - high.astype(F32)).astype(BF)
    return dot(ones, high) + dot(ones, low)


def head_sums(values):
    ones = jnp.where(
        head_of((GROUP, GROUP), 0) == head_of((GROUP, GROUP), 1), 1.0, 0.0
    ).astype(BF)
    high = values.astype(BF)
    low = (values - high.astype(F32)).astype(BF)
    return dot(high, ones) + dot(low, ones)


def head_max(values):
    top = None
    head = head_of(values.shape, 1)
    for index in range(GROUP // SLOT):
        mine = jnp.max(jnp.where(head == index, values, -jnp.inf), axis=1, keepdims=True)
        top = mine if top is None else jnp.where(head == index, mine, top)
    return top


def normalise(values):
    centred = values - jnp.mean(values, axis=-1, keepdims=True)
    inv = lax.rsqrt(jnp.mean(centred * centred, axis=-1, keepdims=True) + 1e-05)
    return centred * inv, inv


def normalise_back(grad, unit, inv, gain):
    scaled = grad * gain
    return inv * (
        scaled
        - jnp.mean(scaled, axis=-1, keepdims=True)
        - unit * jnp.mean(scaled * unit, axis=-1, keepdims=True)
    )


def project_kernel(
    pos_ref, x_ref, p0, p1, p2, p3, q_ref, k_ref, v_ref, n_ref, e_ref, eb_ref, z_ref, w_ref, norm_ref, carry
):
    width = x_ref.shape[1]
    part = width // 4

    @pl.when(pl.program_id(0) == 0)
    def _():
        for index, piece in enumerate((p0, p1, p2, p3)):
            rows = pl.ds(pl.multiple_of(pos_ref[index] * part, part), part)
            for m in range(4):
                w_ref[m, rows, :] = piece[m * part : (m + 1) * part, :]
            norm_ref[0:4, rows] = piece[4 * part : 4 * part + 4, 0:part].astype(F32)
        carry[...] = jnp.zeros_like(carry)

    unit, _ = normalise(x_ref[...].astype(F32))
    normed = (unit * norm_ref[0:1, :] + norm_ref[1:2, :]).astype(BF)
    n_ref[...] = normed
    q_ref[...] = dot(normed, w_ref[0]).astype(BF)
    k_ref[...] = dot(normed, w_ref[1]).astype(BF)
    v_ref[...] = dot(normed, w_ref[2]).astype(BF)
    e = jnp.exp(dot(normed, w_ref[3]))
    e_ref[...] = e
    eb_ref[...] = e.astype(BF)
    rows = e.shape[0]
    ones = lower(jnp.ones((rows, rows), F32))
    z = split_dot(ones, e) + carry[0:1, :]
    z_ref[...] = z
    carry[0:1, :] = z[rows - 1 : rows, :]


def project(pos, x, pieces):
    length, width = x.shape
    steps = length // CHUNK
    rows = lambda dtype: jax.ShapeDtypeStruct((length, width), dtype)
    block = pl.BlockSpec((CHUNK, width), lambda i: (i, 0))
    return pl.pallas_call(
        project_kernel,
        grid=(steps,),
        in_specs=[pl.BlockSpec(memory_space=pltpu.SMEM), block] + [whole(p) for p in pieces],
        out_specs=[block] * 7
        + [
            whole(jax.ShapeDtypeStruct((4, width, width), BF)),
            whole(jax.ShapeDtypeStruct((8, width), F32)),
        ],
        out_shape=[rows(BF), rows(BF), rows(BF), rows(BF), rows(F32), rows(BF), rows(F32)]
        + [jax.ShapeDtypeStruct((4, width, width), BF), jax.ShapeDtypeStruct((8, width), F32)],
        scratch_shapes=[pltpu.VMEM((8, width), F32)],
        compiler_params=pltpu.CompilerParams(
            dimension_semantics=("arbitrary",), vmem_limit_bytes=VMEM_LIMIT
        ),
        name="project",
        cost_estimate=CHEAP,
    )(pos, x, *pieces)


def mix_kernel(q_ref, k_ref, v_ref, e_ref, z_ref, o_ref, w_ref, s_ref, keys_ref, values_ref, keys, values):
    @pl.when(pl.program_id(1) == 0)
    def _():
        keys[...] = jnp.zeros_like(keys)
        values[...] = jnp.zeros_like(values)

    q, k, v, e = q_ref[...], k_ref[...], v_ref[...], e_ref[...]
    inv = 1.0 / z_ref[...]
    heads = GROUP // SLOT
    es = [only_head(e, h) for h in range(heads)]
    key_state = block_diagonal(keys[...])
    value_state = block_diagonal(values[...])
    keys_ref[0, 0] = key_state
    values_ref[0, 0] = value_state
    total = dot(q, key_state)
    for h in range(heads):
        total += dot(lower(dot_nt(q, only_head(k, h))), es[h])
    scores = total * inv * 0.125
    s_ref[...] = scores
    raised = jnp.exp(scores - head_max(scores))
    weights = raised / head_sums(raised)
    w_ref[...] = weights
    ratio = (weights * inv).astype(BF)
    out = dot(ratio, value_state)
    for h in range(heads):
        out += dot(lower(dot_nt(ratio, es[h])), only_head(v, h))
    o_ref[...] = out.astype(BF)
    keys[...] += dot_tn(k, e)
    values[...] += dot_tn(e, v)


def mix(q, k, v, e, z):
    length, width = q.shape
    steps, groups = length // CHUNK, width // GROUP
    block = pl.BlockSpec((CHUNK, GROUP), lambda g, i: (i, g))
    state = pl.BlockSpec((1, 1, GROUP, GROUP), lambda g, i: (g, i, 0, 0))
    rows = lambda dtype: jax.ShapeDtypeStruct((length, width), dtype)
    states = jax.ShapeDtypeStruct((groups, steps, GROUP, GROUP), BF)
    return pl.pallas_call(
        mix_kernel,
        grid=(groups, steps),
        in_specs=[block] * 5,
        out_specs=[block] * 3 + [state] * 2,
        out_shape=[rows(BF), rows(F32), rows(F32), states, states],
        scratch_shapes=[pltpu.VMEM((GROUP, GROUP), F32)] * 2,
        compiler_params=pltpu.CompilerParams(
            dimension_semantics=("arbitrary", "arbitrary"), vmem_limit_bytes=VMEM_LIMIT
        ),
        name="mix",
        cost_estimate=CHEAP,
    )(q, k, v, e, z)


def mix_back_kernel(
    g_ref, q_ref, k_ref, v_ref, eb_ref, e_ref, z_ref, w_ref, s_ref, keys_ref, values_ref,
    dq_ref, dk_ref, dv_ref, dc_ref, later_v, later_k, carry
):
    @pl.when(pl.program_id(0) == 0)
    def _():
        later_v[...] = jnp.zeros_like(later_v)
        later_k[...] = jnp.zeros_like(later_k)
        carry[...] = jnp.zeros_like(carry)

    g, q, k, v, e = g_ref[...], q_ref[...], k_ref[...], v_ref[...], eb_ref[...]
    inv = 1.0 / z_ref[...]
    weights = w_ref[...]
    ratio = (weights * inv).astype(BF)
    heads = GROUP // SLOT
    es = [only_head(e, h) for h in range(heads)]
    state = block_diagonal(later_v[...])
    d_ratio = dot_nt(g, values_ref[0, 0])
    dv = dot(e, state)
    de = dot_nt(v, state)
    for h in range(heads):
        vh = only_head(v, h)
        d_ratio += dot(lower(dot_nt(g, vh)), es[h])
        de += dot(upper(dot_nt(vh, g)), only_head(ratio, h))
        dv += dot(upper(dot_nt(es[h], ratio)), only_head(g, h))
    dv_ref[...] = dv.astype(BF)
    d_weights = d_ratio * inv
    both = d_weights * weights
    d_scores = weights * (d_weights - head_sums(both))
    dn = (d_scores * inv * 0.125).astype(BF)
    dz = -(both + d_scores * s_ref[...]) * inv
    state = block_diagonal(later_k[...])
    dq = dot_nt(dn, keys_ref[0, 0])
    dk = dot(e, state)
    de += dot_nt(k, state)
    for h in range(heads):
        kh = only_head(k, h)
        dq += dot(lower(dot_nt(dn, es[h])), kh)
        dk += dot(upper(dot_nt(es[h], dn)), only_head(q, h))
        de += dot(upper(dot_nt(kh, q)), only_head(dn, h))
    dq_ref[...] = dq.astype(BF)
    dk_ref[...] = dk.astype(BF)
    rows = dz.shape[0]
    ones = upper(jnp.ones((rows, rows), F32))
    z_sum = split_dot(ones, dz) + carry[0:1, :]
    carry[0:1, :] = z_sum[0:1, :]
    dc_ref[...] = ((de + z_sum) * e_ref[...]).astype(BF)
    later_v[...] += dot_tn(ratio, g)
    later_k[...] += dot_tn(dn, q)


def mix_back(group, g, q, k, v, eb, e, z, w, s, keys, values):
    length, width = q.shape
    steps = length // CHUNK
    block = pl.BlockSpec((CHUNK, GROUP), lambda i: (steps - 1 - i, group))
    state = pl.BlockSpec((1, 1, GROUP, GROUP), lambda i: (group, steps - 1 - i, 0, 0))
    out = pl.BlockSpec((CHUNK, GROUP), lambda i: (steps - 1 - i, 0))
    rows = jax.ShapeDtypeStruct((length, GROUP), BF)
    return pl.pallas_call(
        mix_back_kernel,
        grid=(steps,),
        in_specs=[block] * 9 + [state] * 2,
        out_specs=[out] * 4,
        out_shape=[rows] * 4,
        scratch_shapes=[pltpu.VMEM((GROUP, GROUP), F32)] * 2 + [pltpu.VMEM((8, GROUP), F32)],
        compiler_params=pltpu.CompilerParams(
            dimension_semantics=("arbitrary",), vmem_limit_bytes=VMEM_LIMIT
        ),
        name="mix_back",
        cost_estimate=CHEAP,
    )(g, q, k, v, eb, e, z, w, s, keys, values)


def scatter_unit(place_ref, grads, first, unit, shard, target, table):
    count = place_ref.shape[1] // 2
    part = LANES
    rows = part // count
    height = target.shape[0] // (2 * count)
    for d in range(count):
        place = place_ref[table, (shard // 2) * count + d]
        where = pl.ds(pl.multiple_of(place * height + unit * rows, rows), rows)
        target[where, :] = grads[pl.ds(pl.multiple_of(first + d * rows, rows), rows), :]


def scatter_shards(pos_ref, place_ref, grads, send_ref, keep_ref, unit):
    for index in range(4):
        pos = pos_ref[index]
        target = send_ref if index % 2 else keep_ref
        scatter_unit(place_ref, grads, pos * LANES, unit, pos, target, index % 2)


def feed_kernel(
    pos_ref, place_ref, factor_ref, x_ref, g_ref, o_ref, norm_ref, p0, p1, p2, p3,
    y_ref, dh_ref, do_ref, send_ref, keep_ref, dnorm_ref,
    wo, w1, w2, branch, unit_ref, inv_ref, n2, gb, n2_t, gb_t, dn2, grads
):
    step = pl.program_id(0)
    last = pl.num_programs(0) - 1
    length, width = x_ref.shape
    part = width // 4
    block = w1.shape[2]
    tiles = length // 256

    @pl.when(step == 0)
    def _():
        for index, piece in enumerate((p0, p1, p2, p3)):
            pos = pos_ref[index]
            rows = pl.ds(pl.multiple_of(pos * part, part), part)
            wo[rows, :] = piece[0:part, :]
            for j in range(4):
                w1[j, rows, :] = piece[(j + 1) * part : (j + 2) * part, :]
            w2[pos] = piece[5 * part : 5 * part + block, :]

        def before(i, _):
            rows = pl.ds(pl.multiple_of(i * 256, 256), 256)
            h1 = x_ref[rows, :].astype(F32) + dot(o_ref[rows, :], wo[...])
            branch[rows, :] = h1
            unit, inv = normalise(h1)
            unit_ref[rows, :] = unit
            inv_ref[rows, :] = jnp.broadcast_to(inv, (256, 128))
            normed = (unit * norm_ref[2:3, :] + norm_ref[3:4, :]).astype(BF)
            n2[rows, :] = normed
            n2_t[:, rows] = normed.T
            grad = (g_ref[rows, :].astype(F32) * factor_ref[0]).astype(BF)
            gb[rows, :] = grad
            gb_t[:, rows] = grad.T
            dn2[rows, :] = jnp.zeros((256, width), F32)
            return 0

        lax.fori_loop(0, tiles, before, 0)

    up = w1[step]
    down = w2[step]
    up_grad = jnp.zeros((width, block), F32)
    down_grad = jnp.zeros((width, block), F32)
    for i in range(tiles):
        rows = slice(i * 256, (i + 1) * 256)
        a = dot(n2[rows, :], up)
        inner = 0.7978845608 * (a + 0.044715 * a * a * a)
        t = jnp.tanh(inner)
        u = (0.5 * a * (1.0 + t)).astype(BF)
        slope = 0.5 * (1.0 + t) + 0.5 * a * (1.0 - t * t) * (
            0.7978845608 + (3.0 * 0.044715 * 0.7978845608) * a * a
        )
        da = (dot_nt(gb[rows, :], down) * slope).astype(BF)
        branch[rows, :] += dot(u, down)
        dn2[rows, :] += dot_nt(da, up)
        up_grad += dot(n2_t[:, rows], da)
        down_grad += dot(gb_t[:, rows], u)
    grads[...] = up_grad.astype(BF)
    scatter_shards(pos_ref, place_ref, grads, send_ref, keep_ref, step + 1)
    grads[...] = down_grad.astype(BF)
    mine = (step ^ pos_ref[0]) & 1 == 0

    @pl.when(mine)
    def _():
        for u in range(4):
            scatter_unit(place_ref, grads, u * part, 5 + u, step, keep_ref, 0)

    @pl.when(jnp.logical_not(mine))
    def _():
        for u in range(4):
            scatter_unit(place_ref, grads, u * part, 5 + u, step, send_ref, 1)

    @pl.when(step == last)
    def _():
        gain = norm_ref[2:3, :]

        def after(i, sums):
            rows = pl.ds(pl.multiple_of(i * 256, 256), 256)
            y_ref[rows, :] = branch[rows, :].astype(BF)
            grad = dn2[rows, :]
            unit = unit_ref[rows, :]
            dh = g_ref[rows, :].astype(F32) * factor_ref[0] + normalise_back(
                grad, unit, inv_ref[rows, 0:1], gain
            )
            dh_ref[rows, :] = dh
            dh_low = dh.astype(BF)
            do_ref[rows, :] = dot_nt(dh_low, wo[...]).astype(BF)
            return (
                sums[0] + jnp.sum(grad * unit, axis=0, keepdims=True),
                sums[1] + jnp.sum(grad, axis=0, keepdims=True),
                sums[2] + dot_tn(o_ref[rows, :], dh_low),
            )

        empty = jnp.zeros((1, width), F32)
        sums = lax.fori_loop(0, tiles, after, (empty, empty, jnp.zeros((width, width), F32)))
        dnorm_ref[...] = jnp.zeros_like(dnorm_ref)
        dnorm_ref[0:1, :] = sums[0]
        dnorm_ref[1:2, :] = sums[1]
        grads[...] = sums[2].astype(BF)
        scatter_shards(pos_ref, place_ref, grads, send_ref, keep_ref, 0)


def feed(pos, place, factor, x, g, o, norm, pieces):
    length, width = x.shape
    block = width
    height = 5 * (width // 4) + block
    rows = lambda dtype: jax.ShapeDtypeStruct((length, width), dtype)
    out = [
        rows(BF), rows(F32), rows(BF),
        jax.ShapeDtypeStruct((2 * height, width), BF),
        jax.ShapeDtypeStruct((2 * height, width), BF),
        jax.ShapeDtypeStruct((8, width), F32),
    ]
    args = (x, g, o, norm) + tuple(pieces)
    return pl.pallas_call(
        feed_kernel,
        grid=(4,),
        in_specs=[pl.BlockSpec(memory_space=pltpu.SMEM)] * 3 + [whole(a) for a in args],
        out_specs=[whole(a) for a in out],
        out_shape=out,
        scratch_shapes=[
            pltpu.VMEM((width, width), BF),
            pltpu.VMEM((4, width, block), BF),
            pltpu.VMEM((4, block, width), BF),
            pltpu.VMEM((length, width), F32),
            pltpu.VMEM((length, width), F32),
            pltpu.VMEM((length, 128), F32),
            pltpu.VMEM((length, width), BF),
            pltpu.VMEM((length, width), BF),
            pltpu.VMEM((width, length), BF),
            pltpu.VMEM((width, length), BF),
            pltpu.VMEM((length, width), F32),
            pltpu.VMEM((width, block), BF),
        ],
        compiler_params=pltpu.CompilerParams(
            dimension_semantics=("arbitrary",), vmem_limit_bytes=VMEM_LIMIT
        ),
        name="feed",
        cost_estimate=CHEAP,
    )(pos, place, factor, *args)


def weight_back_kernel(pos_ref, place_ref, n_ref, *refs):
    grads_in, (send_ref, keep_ref, n_t, grads) = refs[:8], refs[8:]
    step = pl.program_id(0)

    @pl.when(step == 0)
    def _():
        n_t[...] = n_ref[...].T

    for m in range(4):
        @pl.when(step == m)
        def _():
            for half in range(2):
                cols = slice(half * GROUP, (half + 1) * GROUP)
                grads[:, cols] = dot(n_t[...], grads_in[half * 4 + m][...]).astype(BF)

    scatter_shards(pos_ref, place_ref, grads, send_ref, keep_ref, step)


def weight_back(pos, place, n, halves):
    length, width = n.shape
    out = jax.ShapeDtypeStruct((2 * width, width), BF)
    args = (n,) + tuple(halves)
    return pl.pallas_call(
        weight_back_kernel,
        grid=(4,),
        in_specs=[pl.BlockSpec(memory_space=pltpu.SMEM)] * 2 + [whole(a) for a in args],
        out_specs=[whole(out)] * 2,
        out_shape=[out] * 2,
        scratch_shapes=[pltpu.VMEM((width, length), BF), pltpu.VMEM((width, width), BF)],
        compiler_params=pltpu.CompilerParams(
            dimension_semantics=("arbitrary",), vmem_limit_bytes=VMEM_SMALL
        ),
        name="weight_back",
        cost_estimate=CHEAP,
    )(pos, place, *args)


def input_back_kernel(x_ref, dh_ref, w_ref, norm_ref, dnorm_ref, *refs):
    grads_in, (dx_ref, small_ref, sums) = refs[:8], refs[8:]
    step = pl.program_id(0)

    @pl.when(step == 0)
    def _():
        sums[...] = jnp.zeros_like(sums)

    dn = None
    for m in range(4):
        for half in range(2):
            cols = slice(half * GROUP, (half + 1) * GROUP)
            term = dot_nt(grads_in[half * 4 + m][...], w_ref[m, :, cols])
            dn = term if dn is None else dn + term
    unit, inv = normalise(x_ref[...].astype(F32))
    dx_ref[...] = dh_ref[...] + normalise_back(dn, unit, inv, norm_ref[0:1, :])
    sums[0:1, :] += jnp.sum(dn * unit, axis=0, keepdims=True)
    sums[1:2, :] += jnp.sum(dn, axis=0, keepdims=True)

    @pl.when(step == pl.num_programs(0) - 1)
    def _():
        small_ref[...] = jnp.concatenate(
            [sums[0:2, :], dnorm_ref[0:2, :], jnp.zeros((SMALL - 4, sums.shape[1]), F32)], axis=0
        ).astype(BF)


def input_back(x, dh, w, norm, dnorm, halves):
    length, width = x.shape
    tile = 256
    block = pl.BlockSpec((tile, width), lambda i: (i, 0))
    thin = pl.BlockSpec((tile, GROUP), lambda i: (i, 0))
    small = jax.ShapeDtypeStruct((SMALL, width), BF)
    return pl.pallas_call(
        input_back_kernel,
        grid=(length // tile,),
        in_specs=[block] * 2 + [whole(w), whole(norm), whole(dnorm)] + [thin] * 8,
        out_specs=[block, whole(small)],
        out_shape=[jax.ShapeDtypeStruct((length, width), F32), small],
        scratch_shapes=[pltpu.VMEM((8, width), F32)],
        compiler_params=pltpu.CompilerParams(
            dimension_semantics=("arbitrary",), vmem_limit_bytes=VMEM_SMALL
        ),
        name="input_back",
        cost_estimate=CHEAP,
    )(x, dh, w, norm, dnorm, *halves)


def bits_of(size):
    return [1 << b for b in range(size.bit_length() - 1)]


def split_bits():
    return bits_of(lax.axis_size("dp"))[:3]


def exchange(values, even, odd):
    dp, shard = lax.axis_size("dp"), lax.axis_size("shard")
    perm = []
    for d in range(dp):
        for s in range(shard):
            axis, bit = odd if s % 2 else even
            other = (d ^ bit, s) if axis == "dp" else (d, s ^ bit)
            perm.append((d * shard + s, other[0] * shard + other[1]))
    return lax.ppermute(values, ("dp", "shard"), perm)


def swap(values, axis, bit):
    return exchange(values, (axis, bit), (axis, bit))


def after(values, *others):
    return lax.optimization_barrier((values,) + others)[0]


def places():
    count = 2 ** len(split_bits())
    dp, shard = lax.axis_index("dp"), lax.axis_index("shard")
    piece = jnp.arange(2 * count, dtype=jnp.int32)
    far = (piece // count) ^ (shard // 2)
    along = (piece % count) ^ (dp % count)
    order = 0
    for b in range(len(split_bits())):
        order = order * 2 + ((along >> b) & 1)
    even, odd = far * count + order, order * 2 + far
    mine = shard % 2
    return jnp.stack(
        [jnp.where(mine == 0, even, odd), jnp.where(mine == 0, odd, even)]
    ).astype(jnp.int32)


def phases():
    split = [("dp", b) for b in split_bits()]
    return list(zip([("shard", 2)] + split, split + [("shard", 2)]))


def add_up(parts, low, high):
    total = parts[0][low:high].astype(F32)
    for part in parts[1:]:
        total = total + part[low:high].astype(F32)
    return total.astype(BF)


def add_rest(piece):
    for b in bits_of(lax.axis_size("dp"))[3:]:
        piece = add_up([piece, swap(piece, "dp", b)], 0, piece.shape[0])
    return piece


def gather_plan():
    split = split_bits()
    even = [split[0]] + split[1:][::-1]
    odd = split[::-1]
    return [(("dp", a), ("dp", b)) for a, b in zip(even, odd)]


def gather_index():
    odd = lax.axis_index("shard") % 2
    mask = jnp.zeros((1,), jnp.int32)
    for (_, even_bit), (_, odd_bit) in gather_plan():
        mask = jnp.concatenate([mask, mask | jnp.where(odd == 1, odd_bit, even_bit)])
    return (lax.axis_index("dp") % mask.shape[0]) ^ mask


def adam(master, first, second, grad, rate, decay):
    first_new = 0.5 * first + 0.5 * grad
    second_new = 0.5 * second + 0.5 * grad * grad
    correction = 1.0 - 0.5**STEP
    update = first_new / correction / (jnp.sqrt(second_new / correction) + 1e-08)
    return master - rate * (update + decay * master), first_new, second_new


def update_kernel(index_ref, factor_ref, early_ref, late_ref, gn_ref, *refs, states):
    am, af, as_, um, uf, us, dm, df, ds, nm, nf, ns = refs[:12]
    early, late = refs[-2:]
    outs = refs[12:-2]
    step = pl.program_id(0)
    factor = factor_ref[0]
    width = early.shape[1]
    part = late.shape[0] // 4
    blocks = um.shape[1] // width
    height = part // pl.num_programs(0)

    def keep(group, where, unit, size, new):
        if states:
            for target, value in zip(outs[3 * group : 3 * group + 3], new):
                target[where] = value
        else:
            rows = pl.ds(pl.multiple_of(unit * part + step * size, size), size)
            outs[0][rows, :] = new[0].astype(BF)

    @pl.when(step == 0)
    def _():
        count = index_ref.shape[0]
        rows = part // count
        for source, target in ((early_ref, early), (late_ref, late)):
            units = target.shape[0] // part
            for j in range(count):
                for u in range(units):
                    place = pl.ds(pl.multiple_of(u * part + index_ref[j] * rows, rows), rows)
                    first = (j * units + u) * rows
                    target[place, :] = source[first : first + rows, :]
        new = adam(nm[...], nf[...], ns[...], gn_ref[...] * factor, 0.3, 0.0)
        if states:
            outs[9][...], outs[10][...], outs[11][...] = new
        else:
            last = outs[0].shape[0] - SMALL
            outs[0][last:, :] = jnp.zeros((SMALL, width), BF)
            outs[0][last : last + 4, 0:part] = new[0].astype(BF)

    def span(base, size):
        return pl.ds(pl.multiple_of(base + step * size, size), size)

    for m in range(5):
        source = late[span(m * part, height), :] if m < 4 else early[span(0, height), :]
        new = adam(am[m], af[m], as_[m], source.astype(F32) * factor, 0.05, 0.01)
        keep(0, (m, slice(None), slice(None)), m, height, new)
    for j in range(blocks):
        source = early[span((j + 1) * part, height), :]
        cols = (slice(None), slice(j * width, (j + 1) * width))
        new = adam(um[cols], uf[cols], us[cols], source.astype(F32) * factor, 0.05, 0.01)
        keep(1, cols, 5 + j, height, new)
    tall = dm.shape[0]
    source = early[(blocks + 1) * part :, span(0, tall)].astype(F32).T
    new = adam(dm[...], df[...], ds[...], source * factor, 0.05, 0.01)
    keep(2, (slice(None), slice(None)), 5 + blocks, tall, new)


def update(states, index, factor, early, late, gn, attn, up, down, norm):
    steps = 4
    smem = pl.BlockSpec(memory_space=pltpu.SMEM)
    five, part, width = attn[0].shape
    specs = (
        [pl.BlockSpec((five, part // steps, width), lambda i: (0, i, 0))] * 3
        + [pl.BlockSpec((part // steps, up[0].shape[1]), lambda i: (i, 0))] * 3
        + [pl.BlockSpec((down[0].shape[0] // steps, width), lambda i: (i, 0))] * 3
        + [whole(norm[0])] * 3
    )
    arrays = tuple(attn) + tuple(up) + tuple(down) + tuple(norm)
    copy = jax.ShapeDtypeStruct((early.shape[0] + late.shape[0] + SMALL, width), BF)
    return pl.pallas_call(
        functools.partial(update_kernel, states=states),
        grid=(steps,),
        in_specs=[smem, smem, whole(early), whole(late), whole(gn)] + specs,
        out_specs=specs if states else [whole(copy)],
        out_shape=[jax.ShapeDtypeStruct(a.shape, F32) for a in arrays] if states else [copy],
        scratch_shapes=[pltpu.VMEM(early.shape, BF), pltpu.VMEM(late.shape, BF)],
        compiler_params=pltpu.CompilerParams(
            dimension_semantics=("arbitrary",), vmem_limit_bytes=VMEM_LIMIT
        ),
        name="update" if states else "renew",
        cost_estimate=CHEAP,
    )(index, factor, early, late, gn, *arrays)


def place_units(pos, piece, first, units, attn_ref, up_ref, down_ref, sems, start):
    width = attn_ref.shape[2]
    part = LANES
    blocks = up_ref.shape[1] // width
    tall = down_ref.shape[0] // 4
    found = []
    for j, unit in enumerate(units):
        source = piece.at[pl.ds(first + j * part, part), :]
        rows = pl.ds(pl.multiple_of(pos * part, part), part)
        if unit < 5:
            target = attn_ref.at[unit, rows, :]
        elif unit < 5 + blocks:
            target = up_ref.at[rows, pl.ds((unit - 5) * width, width)]
        else:
            base = pl.multiple_of(pos * tall + (unit - 5 - blocks) * part, part)
            target = down_ref.at[pl.ds(base, part), :]
        found.append(pltpu.make_async_copy(source, target, sems.at[start + j]))
    return found


def unpack_near_kernel(pos_ref, p0, p1, attn_ref, up_ref, down_ref, sems):
    units = list(range(p0.shape[0] // LANES))
    copies = place_units(pos_ref[0], p0, 0, units, attn_ref, up_ref, down_ref, sems, 0)
    copies += place_units(pos_ref[1], p1, 0, units, attn_ref, up_ref, down_ref, sems, len(units))
    for copy in copies:
        copy.start()
    for copy in copies:
        copy.wait()


def unpack_far_kernel(pos_ref, half_ref, *refs):
    pieces, (attn_ref, up_ref, down_ref, sems) = refs[:6], refs[9:]
    units = list(range((pieces[0].shape[0] * 2 + pieces[2].shape[0]) // LANES))
    low = pieces[0].shape[0] // LANES
    for side in range(2):
        @pl.when(half_ref[0] == side)
        def _():
            copies = []
            for shift in range(2):
                pos = pos_ref[2 + shift]
                group = pieces[3 * shift : 3 * shift + 3]
                for part, piece in zip((side, 1 - side), group[:2]):
                    copies += place_units(
                        pos, piece, 0, units[part * low : (part + 1) * low],
                        attn_ref, up_ref, down_ref, sems, len(copies),
                    )
                copies += place_units(
                    pos, group[2], 0, units[2 * low :],
                    attn_ref, up_ref, down_ref, sems, len(copies),
                )
            for copy in copies:
                copy.start()
            for copy in copies:
                copy.wait()


def share_copies(pos, own, other_work, width, hidden):
    units = own.shape[0] // LANES
    low = 4 * LANES
    half = (lax.axis_index("dp") % 2).astype(jnp.int32)[None]
    near = swap(own, "shard", 1)
    ours = lax.dynamic_slice(own, (half[0] * low, 0), (low, width))
    far_a = swap(ours, "shard", 2)
    far_c = swap(after(own[2 * low :], far_a), "shard", 2)
    far_b = swap(far_a, "dp", 1)
    hbm = pl.BlockSpec(memory_space=pl.ANY)
    vmem = pl.BlockSpec(memory_space=pltpu.VMEM)
    smem = pl.BlockSpec(memory_space=pltpu.SMEM)
    shapes = [
        jax.ShapeDtypeStruct((5, width, width), BF),
        jax.ShapeDtypeStruct((width, hidden), BF),
        jax.ShapeDtypeStruct((hidden, width), BF),
    ]
    params = pltpu.CompilerParams(vmem_limit_bytes=VMEM_SMALL)
    begun = list(pl.pallas_call(
        unpack_near_kernel,
        in_specs=[smem, vmem, vmem],
        out_specs=[hbm] * 3,
        out_shape=shapes,
        scratch_shapes=[pltpu.SemaphoreType.DMA((2 * units,))],
        compiler_params=params,
        name="unpack_near",
        cost_estimate=CHEAP,
    )(pos, own, near))
    far = [far_a, far_b, far_c]
    across = [swap(f, "shard", 1) for f in far[:2]]
    across.append(swap(after(far[2], other_work, *across), "shard", 1))
    done = pl.pallas_call(
        unpack_far_kernel,
        in_specs=[smem, smem] + [vmem] * 6 + [hbm] * 3,
        out_specs=[hbm] * 3,
        out_shape=shapes,
        scratch_shapes=[pltpu.SemaphoreType.DMA((2 * units,))],
        input_output_aliases={8: 0, 9: 1, 10: 2},
        compiler_params=params,
        name="unpack_far",
        cost_estimate=CHEAP,
    )(pos, half, *far, *across, *begun)
    last = units * LANES
    norms = [p[last : last + 4, :LANES] for p in (own, near)] + [
        p[p.shape[0] - SMALL : p.shape[0] - SMALL + 4, :LANES] for p in (far[2], across[2])
    ]
    low_bit, high_bit = pos[0] % 2 == 1, pos[0] // 2 == 1
    a, b, c, d = norms
    a, b, c, d = [jnp.where(low_bit, v, u) for u, v in ((a, b), (b, a), (c, d), (d, c))]
    a, b, c, d = [jnp.where(high_bit, v, u) for u, v in ((a, c), (b, d), (c, a), (d, b))]
    return tuple(done) + (jnp.concatenate([a, b, c, d], axis=1),)


def gather_shard(own):
    across = swap(own, "shard", 2)
    return own, swap(own, "shard", 1), across, swap(across, "shard", 1)


def shards(
    tokens, out_grad, domain_ids, domain_weight,
    attn_master, attn_first, attn_second,
    up_master, up_first, up_second,
    down_master, down_first, down_second,
    norm_master, norm_first, norm_second,
):
    width = tokens.shape[1]
    hidden = up_master.shape[1]
    part = width // 4
    blocks = hidden // width
    dp = lax.axis_index("dp")
    shard = lax.axis_index("shard").astype(jnp.int32)
    pos = shard ^ jnp.arange(4, dtype=jnp.int32)
    place = places()

    small = jnp.pad(norm_master.astype(BF), ((0, SMALL - 4), (0, width - part)))
    first = gather_shard(
        jnp.concatenate([attn_master[:4].astype(BF).reshape(4 * part, width), small])
    )

    domains = domain_weight.shape[0]
    onehot = (domain_ids[:, None] == jnp.arange(domains, dtype=jnp.int32)[None, :]).astype(F32)
    counts = jnp.sum(onehot, axis=0)
    for b in bits_of(lax.axis_size("dp")):
        counts = counts + swap(counts, "dp", b)
    counts_row = jnp.pad(counts.astype(BF)[None], ((0, SMALL - 1), (0, width - domains)))
    second = after(
        jnp.concatenate(
            [attn_master[4].astype(BF)]
            + [up_master[:, j * width : (j + 1) * width].astype(BF) for j in range(blocks)]
            + [down_master.astype(BF), counts_row]
        ),
        first[2],
    )
    across = swap(second, "shard", 2)
    q, k, v, n, e, eb, z, w, norm = project(pos, tokens, first)
    o, weights, scores, keys, values = mix(q, k, v, eb, z)
    second = (
        second, swap(second, "shard", 1), across, swap(after(across, o), "shard", 1)
    )
    total_seqs = lax.axis_size("dp") * lax.axis_size("shard") * domain_ids.shape[0]
    last = second[0].shape[0] - SMALL
    counts = sum(piece[last, :domains].astype(F32) for piece in second)
    per_domain = domain_weight * total_seqs / (domains * jnp.maximum(counts, 1.0))
    seq_weight = jnp.sum(onehot * per_domain[None, :], axis=1)

    y, dh, do, send, keep, dnorm = feed(pos, place, seq_weight, tokens, out_grad, o, norm, second)

    steps = phases()
    early = [keep, swap(send, "shard", 1)]
    pieces = 2 ** len(steps)
    rows = keep.shape[0] // pieces

    def forward_phase(parts, phase, rows):
        low = rows * pieces >> (phase + 1)
        return add_up(parts, low, 2 * low)

    saved = (q, k, v, eb, e, z, weights, scores, keys, values)
    back = list(mix_back(0, do, *saved))
    out = after(forward_phase(early, 0, rows), back[0])
    early.append(exchange(out, *steps[0]))
    back += mix_back(1, after(do, out), *saved)
    out = after(forward_phase(early, 1, rows), back[4])
    early.append(exchange(out, *steps[1]))
    send, keep = weight_back(pos, place, after(n, out), back)
    late = [keep, swap(send, "shard", 1)]
    out = forward_phase(early, 2, rows)
    early.append(exchange(out, *steps[2]))
    dx, small = input_back(tokens, after(dh, out), w, norm, dnorm, back)
    small = add_up([small, swap(small, "shard", 1)], 0, SMALL)
    thin = keep.shape[0] // pieces
    for phase in range(len(steps)):
        if phase >= 3:
            early.append(exchange(forward_phase(early, phase, rows), *steps[phase]))
        out = forward_phase(late, phase, thin)
        got = exchange(jnp.concatenate([out, small]), *steps[phase])
        late.append(got)
        small = add_up([small, got[out.shape[0] :]], 0, SMALL)
    early = add_rest(add_up(early, 0, rows))
    late = add_rest(jnp.concatenate([add_up(late, 0, thin), small]))
    late, small = late[:thin], late[thin:]
    norm_grad = lax.dynamic_slice(small[:4], (0, shard * part), (4, part)).astype(F32)
    for step in gather_plan():
        early = jnp.concatenate([early, exchange(early, *step)])
        late = jnp.concatenate([late, exchange(late, *step)])
    square = sum(jnp.sum(jnp.square(part.astype(F32))) for part in (early, late, norm_grad))[None]
    for b in (1, 2):
        square = square + swap(square, "shard", b)
    index = gather_index()
    clip_norm = jnp.sqrt(square)
    factor = jnp.minimum(1.0, 1.0 / (clip_norm + 1e-06))
    inputs = (
        index, factor, early, late, norm_grad,
        (attn_master, attn_first, attn_second),
        (up_master, up_first, up_second),
        (down_master, down_first, down_second),
        (norm_master, norm_first, norm_second),
    )
    (own,) = update(False, *inputs)
    new = update(True, *inputs)
    copies = share_copies(pos, own, new[0], width, hidden)
    return (y, dx) + tuple(new) + (clip_norm[0],) + tuple(copies)


def solution(mesh):
    rows = P(("dp", "shard"), None)
    attn = (P(None, "shard", None),) * 3
    tall = (P("shard", None),) * 6
    norm = (P(None, "shard"),) * 3
    return jax.shard_map(
        shards,
        mesh=mesh,
        in_specs=(rows, rows, P(("dp", "shard")), P()) + attn + tall + norm,
        out_specs=(rows, rows) + attn + tall + norm + (P(),) * 5,
        check_vma=False,
    )
```

time: 324 us -> 254 us (0.78)
  waiting for transfers between devices: 119 us -> 58 us
  Pallas kernels: 128 us -> 116 us
  other arithmetic: 12.8 us -> 17.4 us
  starting transfers between devices: 47.2 us -> 42.8 us
    ppermute x32 -> x35, waiting for transfers between devices: 119 us -> 58 us  [exchange(): return lax.ppermute(values, ('dp', 'shard'), perm)]
    pallas_call x12 -> x8, Pallas kernels: 73.7 us -> 61.7 us  [the longest x2 28.3 us: mix_back(): pl.pallas_call(mix_back_kernel, grid=(steps,), in_specs=[block] * 9 + [st...]
    ppermute x32 -> x35, starting transfers between devices: 47.2 us -> 42.8 us  [exchange(): return lax.ppermute(values, ('dp', 'shard'), perm)]
    unnamed x43 -> x79, local copies, waits for them, and re-layouts: 10.4 us -> 9.81 us
  transfers between devices with their start and end apart: 32 -> 35, of which waited for: 19 -> 21; matrix products, arithmetic and copies ran while one was open for 3% -> 6% of each run, Pallas kernels for 23% -> 29%
where the time goes in v2:
time: 254 us; the launch traced here: 253 us
  Pallas kernels  116 us (46%)
  waiting for transfers between devices  58 us (23%)
  starting transfers between devices  42.8 us (17%)
  other arithmetic  17.4 us (7%)
  local copies, waits for them, and re-layouts  12.7 us (5%)
  between operations  6.37 us (3%)
    ppermute x35, waiting for transfers between devices, exchange(): return lax.ppermute(values, ('dp', 'shard'), perm)  58 us
    ppermute x35, starting transfers between devices, exchange(): return lax.ppermute(values, ('dp', 'shard'), perm)  42.8 us
    pallas_call x1, Pallas kernels, feed(): pl.pallas_call(feed_kernel, grid=(4,), in_specs=[pl.BlockSpec(memory_spac...  31 us
    pallas_call x2, Pallas kernels, mix_back(): pl.pallas_call(mix_back_kernel, grid=(steps,), in_specs=[block] * 9 + [st...  28.3 us
    pallas_call x2, Pallas kernels, update(): pl.pallas_call(functools.partial(update_kernel, states=states), grid=(ste...  18.9 us
    pallas_call x1, Pallas kernels, mix(): pl.pallas_call(mix_kernel, grid=(groups, steps), in_specs=[block] * 5, ou...  14.9 us
    unnamed x79, local copies, waits for them, and re-layouts  9.81 us
    pallas_call x1, Pallas kernels, project(): pl.pallas_call(project_kernel, grid=(steps,), in_specs=[pl.BlockSpec(memo...  8.43 us
  transfers between devices with their start and end apart: 35, of which 21 were waited for; matrix products, arithmetic and copies ran while one was open for 6% of the time, Pallas kernels for 29%

profile of v2, /device:TPU:0, one launch (start us, length us, event | category | flops | bytes accessed | tf_op | source)
XLA Modules:
  0.0 253.5 jit_solution(1124025703331651308)
XLA Ops:
  2.2 3.0 %collective-permute-start.3 = (bf16[528,512]{1,0:T(8,128)(2,1)S(1)}, bf16[528,512]{1,0:T(8,128)(2,1)S(1)}, u32[]{:S(2)}, u32[]{:S(2)}) collective-permute-start(bf16[528,512]{1,0:T(8,128)(2,1)S(1)} %fusion.1.p0), channel_id=1, source_target_pairs={{0,2},{1,3},{2,0},{3,1},{4,6},{5,7},{6,4},{7,5},{8,10},{9,11},{10,... | collective-permute-start | bytes 1622024 | tf_op jit(solution)/shard_map/ppermute | solution.py:544
  13.3 2.0 collective-permute-done.1
  15.3 2.6 %collective-permute-start.2 = (f32[8]{0:T(128)S(1)}, f32[8]{0:T(128)S(1)}, u32[]{:S(2)}, u32[]{:S(2)}) collective-permute-start(f32[8]{0:T(128)S(1)} %fusion.13), channel_id=1, source_target_pairs={{0,16},{1,17},{2,18},{3,19},{4,20},{5,21},{6,22},{7,23},{8,24},{9,... | collective-permute-start | bytes 104 | tf_op jit(solution)/shard_map/ppermute | solution.py:544
  17.9 1.9 collective-permute-done.2
  21.9 1.6 collective-permute-done.6.p1
  24.4 8.4 %project.1 = (bf16[1024,512]{1,0:T(8,128)(2,1)}, bf16[1024,512]{1,0:T(8,128)(2,1)}, bf16[1024,512]{1,0:T(8,128)(2,1)}, bf16[1024,512]{1,0:T(8,128)(2,1)}, f32[10...) custom-call(s32[4]{0:T(128)} %iota_xor_fusion.pos_ref, ...), custom_call_target="tpu_custom_call" | custom-call | flops 1 | bytes 1 | tf_op jit(solution)/shard_map/project/pallas_call | solution.py:137
  32.8 14.9 %mix.1 = (bf16[1024,512]{1,0:T(8,128)(2,1)}, f32[1024,512]{1,0:T(8,128)}, f32[1024,512]{1,0:T(8,128)}, bf16[2,4,256,256]{3,2,1,0:T(8,128)(2,1)}, bf16[2,4,256,256]{3,2,1,0:T(8,128)(2,1)}) custom-call(bf16[1024,512]{1,0:T(8,128)(2,1)} %get-tuple-element.79.q_ref, bf16[1024,512]{1,0:T(8,128)(2,1)} %get-tuple-element.80.k_ref, ...), custom_call_target="tpu_custom_call" | custom-call | flops 1 | bytes 1 | tf_op jit(solution)/shard_map/mix/pallas_call | solution.py:195
  48.7 2.0 collective-permute-done.8.p3
  52.0 31.0 %feed.1 = (bf16[1024,512]{1,0:T(8,128)(2,1)}, f32[1024,512]{1,0:T(8,128)}, bf16[1024,512]{1,0:T(8,128)(2,1)}, bf16[2304,512]{1,0:T(8,128)(2,1)}, bf16[2304,512]{1,0:T(8,128)(2,1)}, /*index=5*/f32[8,512]{1,0:T(8,128)}) custom-call(s32[4]{0:T(128)} %iota_xor_fusion.pos_ref, s32[2,16]{1,0:T(2,128)} %pad_add_fusion.place_ref, f32[1]{0:T(128)} %bitcast.5.factor_ref, ...), custom_call_target="tpu_custom_call" | custom-call | flops 1 | bytes 1 | tf_op jit(solution)/shard_map/feed/pallas_call | solution.py:416
  83.2 14.1 %mix_back.2 = (bf16[1024,256]{1,0:T(8,128)(2,1)}, bf16[1024,256]{1,0:T(8,128)(2,1)}, bf16[1024,256]{1,0:T(8,128)(2,1)}, bf16[1024,256]{1,0:T(8,128)(2,1)}) custom-call(bf16[1024,512]{1,0:T(8,128)(2,1)} %get-tuple-element.99.g_ref, bf16[1024,512]{1,0:T(8,128)(2,1)} %get-tuple-element.79.q_ref, bf16[1024,512]{1,0:T(8,128)(2,1)} %get-tuple-element.80.k_ref, ...), custom_call_target="tpu_custom_call" | custom-call | flops 1 | bytes 1 | tf_op jit(solution)/shard_map/mix_back/pallas_call | solution.py:268
  99.2 14.2 %mix_back.3 = (bf16[1024,256]{1,0:T(8,128)(2,1)}, bf16[1024,256]{1,0:T(8,128)(2,1)}, bf16[1024,256]{1,0:T(8,128)(2,1)}, bf16[1024,256]{1,0:T(8,128)(2,1)}) custom-call(bf16[1024,512]{1,0:T(8,128)(2,1)} %get-tuple-element.99.g_ref, bf16[1024,512]{1,0:T(8,128)(2,1)} %get-tuple-element.79.q_ref, bf16[1024,512]{1,0:T(8,128)(2,1)} %get-tuple-element.80.k_ref, ...), custom_call_target="tpu_custom_call" | custom-call | flops 1 | bytes 1 | tf_op jit(solution)/shard_map/mix_back/pallas_call | solution.py:268
  120.0 4.2 %weight_back.1 = (bf16[1024,512]{1,0:T(8,128)(2,1)S(1)}, bf16[1024,512]{1,0:T(8,128)(2,1)S(1)}) custom-call(s32[4]{0:T(128)S(1)} %copy-done.23, s32[2,16]{1,0:T(2,128)S(1)} %copy-done.25, bf16[1024,512]{1,0:T(8,128)(2,1)S(1)} %copy-done.13, bf16[1024,256]{1,0:T(8,128)(2,1)S(1)} %copy-done.2, bf16[1024,256]{1,0:T(8,128)(2,1)S(1)} %copy-done.3, ...), custom_call_target="tpu_custom_call" | custom-call | flops 1 | bytes 1 | tf_op jit(solution)/shard_map/weight_back/pallas_call | solution.py:466
  126.5 4.5 %input_back.1 = (f32[1024,512]{1,0:T(8,128)}, bf16[16,512]{1,0:T(8,128)(2,1)S(1)}) custom-call(bf16[1024,512]{1,0:T(8,128)(2,1)S(1)} %copy-done.1, f32[1024,512]{1,0:T(8,128)S(1)} %copy-done.12, bf16[4,512,512]{2,1,0:T(8,128)(2,1)S(1)} %copy-done.11, f32[8,512]{1,0:T(8,128)S(1)} %copy-done.22, f32[8,512]{1,0:T(8,128)S(1)} %copy-done.24, ...), custom_call_target="tpu_custom_call" | custom-call | flops 1 | bytes 1 | tf_op jit(solution)/shard_map/input_back/pallas_call | solution.py:513
  135.5 6.3 %collective-permute-done.19 = bf16[528,512]{1,0:T(8,128)(2,1)S(1)} collective-permute-done((bf16[528,512]{1,0:T(8,128)(2,1)S(1)}, bf16[528,512]{1,0:T(8,128)(2,1)S(1)}, u32[]{:S(2)}, u32[]{:S(2)}) %collective-permute-start.19) | collective-permute-done | bytes 540704 | tf_op jit(solution)/shard_map/ppermute | solution.py:544
  143.9 2.7 %collective-permute-start.13 = (bf16[144,512]{1,0:T(8,128)(2,1)S(1)}, bf16[144,512]{1,0:T(8,128)(2,1)S(1)}, u32[]{:S(2)}, u32[]{:S(2)}) collective-permute-start(bf16[144,512]{1,0:T(8,128)(2,1)S(1)} %add_convert_fusion.6), channel_id=1, source_target_pairs={{0,16},{1,3},{2,18},{3,1},{4,20},{5,7},{6,22},{7,5},{8,24},{9,11},... | collective-permute-start | bytes 442376 | tf_op jit(solution)/shard_map/ppermute | solution.py:544
  146.6 2.1 collective-permute-done.20
  148.7 1.7 collective-permute-start.21
  152.6 3.1 %collective-permute-start.14 = (bf16[144,512]{1,0:T(8,128)(2,1)S(1)}, bf16[144,512]{1,0:T(8,128)(2,1)S(1)}, u32[]{:S(2)}, u32[]{:S(2)}) collective-permute-start(bf16[144,512]{1,0:T(8,128)(2,1)S(1)} %add_convert_fusion.5), channel_id=1, source_target_pairs={{0,4},{1,17},{2,6},{3,19},{4,0},{5,21},{6,2},{7,23},{8,12},{9,25},... | collective-permute-start | bytes 442376 | tf_op jit(solution)/shard_map/ppermute | solution.py:544
  159.3 2.4 collective-permute-done.22
  162.5 8.7 %collective-permute-done.15 = bf16[288,512]{1,0:T(8,128)(2,1)S(1)} collective-permute-done((bf16[288,512]{1,0:T(8,128)(2,1)S(1)}, bf16[288,512]{1,0:T(8,128)(2,1)S(1)}, u32[]{:S(2)}, u32[]{:S(2)}) %collective-permute-start.15) | collective-permute-done | bytes 294944 | tf_op jit(solution)/shard_map/ppermute | solution.py:544
  171.4 3.5 %collective-permute-start.24 = (bf16[128,512]{1,0:T(8,128)(2,1)S(1)}, bf16[128,512]{1,0:T(8,128)(2,1)S(1)}, u32[]{:S(2)}, u32[]{:S(2)}) collective-permute-start(bf16[128,512]{1,0:T(8,128)(2,1)S(1)} %pad_maximum_fusion.8), channel_id=1, source_target_pairs={{0,16},{1,9},{2,18},{3,11},{4,20},{5,13},{6,22},{7,15},{8,24},{9,1... | collective-permute-start | bytes 393224 | tf_op jit(solution)/shard_map/ppermute | solution.py:544
  175.1 5.1 %collective-permute-done.24 = bf16[128,512]{1,0:T(8,128)(2,1)S(1)} collective-permute-done((bf16[128,512]{1,0:T(8,128)(2,1)S(1)}, bf16[128,512]{1,0:T(8,128)(2,1)S(1)}, u32[]{:S(2)}, u32[]{:S(2)}) %collective-permute-start.24) | collective-permute-done | bytes 131104 | tf_op jit(solution)/shard_map/ppermute | solution.py:544
  180.2 4.0 %collective-permute-start.25 = (bf16[256,512]{1,0:T(8,128)(2,1)S(1)}, bf16[256,512]{1,0:T(8,128)(2,1)S(1)}, u32[]{:S(2)}, u32[]{:S(2)}) collective-permute-start(bf16[256,512]{1,0:T(8,128)(2,1)S(1)} %pad_maximum_fusion.6), channel_id=1, source_target_pairs={{0,8},{1,5},{2,10},{3,7},{4,12},{5,1},{6,14},{7,3},{8,0},{9,13},{1... | collective-permute-start | bytes 786440 | tf_op jit(solution)/shard_map/ppermute | solution.py:544
  184.9 2.2 multiply_reduce_fusion
  194.0 3.1 %collective-permute-start.27 = (f32[1]{0:T(128)}, f32[1]{0:T(128)}, u32[]{:S(2)}, u32[]{:S(2)}) collective-permute-start(f32[1]{0:T(128)} %add.307), channel_id=1, source_target_pairs={{0,2},{1,3},{2,0},{3,1},{4,6},{5,7},{6,4},{7,5},{8,10},{9,11},{10,... | collective-permute-start | bytes 20 | tf_op jit(solution)/shard_map/ppermute | solution.py:544
  198.3 8.3 %renew.1.p0 = bf16[1680,512]{1,0:T(8,128)(2,1)} custom-call(s32[8]{0:T(128)} %add_xor_fusion.index_ref, f32[1]{0:T(128)S(6)} %min.3.factor_ref, bf16[1152,512]{1,0:T(8,128)(2,1)} %get-tuple-element.142.early_ref, bf16[512,512]{1,0:T(8,128)(2,1)} %get-tuple-element.140.late_ref, f32[4,128]{1,0:T(4,128)} %get-tuple-element.138.gn_ref, f32[5,128,512]{2,1,0:T(8,128)} %refs_0_.3, ...), custom_call_target="tpu_custom_call" | custom-call | flops 1 | bytes 1 | tf_op jit(solution)/shard_map/renew/pallas_call | solution.py:680
  207.8 1.8 collective-permute-start.28
  209.5 11.0 %collective-permute-done.28.refs_0_ = bf16[512,512]{1,0:T(8,128)(2,1)S(1)} collective-permute-done((bf16[512,512]{1,0:T(8,128)(2,1)S(1)}, bf16[512,512]{1,0:T(8,128)(2,1)S(1)}, u32[]{:S(2)}, u32[]{:S(2)}) %collective-permute-start.28) | collective-permute-done | bytes 524320 | tf_op jit(solution)/shard_map/ppermute | solution.py:544
  224.2 8.1 %collective-permute-done.29.refs_1_ = bf16[512,512]{1,0:T(8,128)(2,1)S(1)} collective-permute-done((bf16[512,512]{1,0:T(8,128)(2,1)S(1)}, bf16[512,512]{1,0:T(8,128)(2,1)S(1)}, u32[]{:S(2)}, u32[]{:S(2)}) %collective-permute-start.29) | collective-permute-done | bytes 524320 | tf_op jit(solution)/shard_map/ppermute | solution.py:544
  232.4 10.6 %update.1 = (f32[5,128,512]{2,1,0:T(8,128)}, f32[5,128,512]{2,1,0:T(8,128)}, f32[5,128,512]{2,1,0:T(8,128)}, f32[128,2048]{1,0:T(8,128)}, f32[128,2048]{1,0:T(8,...) custom-call(s32[8]{0:T(128)} %add_xor_fusion.index_ref, ...), custom_call_target="tpu_custom_call" | custom-call | flops 1 | bytes 1 | tf_op jit(solution)/shard_map/update/pallas_call | solution.py:680
  245.2 2.5 unpack_near.1
  249.1 3.3 %unpack_far.1 = (bf16[5,512,512]{2,1,0:T(8,128)(2,1)}, bf16[512,2048]{1,0:T(8,128)(2,1)}, bf16[2048,512]{1,0:T(8,128)(2,1)}) custom-call(s32[4]{0:T(128)S(1)} %copy-done.23, s32[1]{0:T(128)} %bitcast.9.half_ref, bf16[512,512]{1,0:T(8,128)(2,1)S(1)} %copy-done.15, ...), custom_call_target="tpu_custom_call", output_to_operand_aliasing={{0}: (8, {}), {1}: (9, {}), {2}: (10, {})} | custom-call | flops 1 | bytes 1 | tf_op jit(solution)/shard_map/unpack_far/pallas_call | solution.py:782
  (178 shorter events, 52.1 us)
Async XLA Ops:
  2.2 18.1 %collective-permute-start.3 = (bf16[528,512]{1,0:T(8,128)(2,1)S(1)}, bf16[528,512]{1,0:T(8,128)(2,1)S(1)}, u32[]{:S(2)}, u32[]{:S(2)}) collective-permute-start(bf16[528,512]{1,0:T(8,128)(2,1)S(1)} %fusion.1.p0), channel_id=1, source_target_pairs={{0,2},{1,3},{2,0},{3,1},{4,6},{5,7},{6,4},{7,5},{8,10},{9,11},{10,... | collective-permute-start | bytes 1622024 | tf_op jit(solution)/shard_map/ppermute | solution.py:544
  5.9 5.8 %collective-permute-start = (f32[8]{0:T(128)S(1)}, f32[8]{0:T(128)S(1)}, u32[]{:S(2)}, u32[]{:S(2)}) collective-permute-start(f32[8]{0:T(128)S(1)} %compare_convert_fusion), channel_id=1, source_target_pairs={{0,4},{1,5},{2,6},{3,7},{4,0},{5,1},{6,2},{7,3},{8,12},{9,13},{10,... | collective-permute-start | bytes 104 | tf_op jit(solution)/shard_map/ppermute | solution.py:544
  11.7 3.5 %collective-permute-start.1 = (f32[8]{0:T(128)S(1)}, f32[8]{0:T(128)S(1)}, u32[]{:S(2)}, u32[]{:S(2)}) collective-permute-start(f32[8]{0:T(128)S(1)} %fusion.11), channel_id=1, source_target_pairs={{0,8},{1,9},{2,10},{3,11},{4,12},{5,13},{6,14},{7,15},{8,0},{9,1},... | collective-permute-start | bytes 104 | tf_op jit(solution)/shard_map/ppermute | solution.py:544
  15.3 4.4 %collective-permute-start.2 = (f32[8]{0:T(128)S(1)}, f32[8]{0:T(128)S(1)}, u32[]{:S(2)}, u32[]{:S(2)}) collective-permute-start(f32[8]{0:T(128)S(1)} %fusion.13), channel_id=1, source_target_pairs={{0,16},{1,17},{2,18},{3,19},{4,20},{5,21},{6,22},{7,23},{8,24},{9,... | collective-permute-start | bytes 104 | tf_op jit(solution)/shard_map/ppermute | solution.py:544
  20.3 27.4 %collective-permute-start.5 = (bf16[1168,512]{1,0:T(8,128)(2,1)}, bf16[1168,512]{1,0:T(8,128)(2,1)S(1)}, u32[]{:S(2)}, u32[]{:S(2)}) collective-permute-start(bf16[1168,512]{1,0:T(8,128)(2,1)} %constant_dynamic-update-slice_fusion.p0), channel_id=1, source_target_pairs={{0,2},{1,3},{2,0},{3,1},{4,6},{5,7},{6,4},{7,5},{8,10},{9,11},{10,... | collective-permute-start | bytes 3588104 | tf_op jit(solution)/shard_map/ppermute | solution.py:544
  20.9 2.9 %collective-permute-start.7 = (bf16[528,512]{1,0:T(8,128)(2,1)S(1)}, bf16[528,512]{1,0:T(8,128)(2,1)}, u32[]{:S(2)}, u32[]{:S(2)}) collective-permute-start(bf16[528,512]{1,0:T(8,128)(2,1)S(1)} %collective-permute-done.3.p2), channel_id=1, source_target_pairs={{0,1},{1,0},{2,3},{3,2},{4,5},{5,4},{6,7},{7,6},{8,9},{9,8},{10,11... | collective-permute-start | bytes 1622024 | tf_op jit(solution)/shard_map/ppermute | solution.py:544
  21.9 26.8 %collective-permute-start.4 = (bf16[1168,512]{1,0:T(8,128)(2,1)}, bf16[1168,512]{1,0:T(8,128)(2,1)}, u32[]{:S(2)}, u32[]{:S(2)}) collective-permute-start(bf16[1168,512]{1,0:T(8,128)(2,1)} %constant_dynamic-update-slice_fusion.p0), channel_id=1, source_target_pairs={{0,1},{1,0},{2,3},{3,2},{4,5},{5,4},{6,7},{7,6},{8,9},{9,8},{10,11... | collective-permute-start | bytes 3588104 | tf_op jit(solution)/shard_map/ppermute | solution.py:544
  47.8 2.9 %collective-permute-start.8 = (bf16[1168,512]{1,0:T(8,128)(2,1)S(1)}, bf16[1168,512]{1,0:T(8,128)(2,1)S(1)}, u32[]{:S(2)}, u32[]{:S(2)}) collective-permute-start(bf16[1168,512]{1,0:T(8,128)(2,1)S(1)} %collective-permute-done.5.p2), channel_id=1, source_target_pairs={{0,1},{1,0},{2,3},{3,2},{4,5},{5,4},{6,7},{7,6},{8,9},{9,8},{10,11... | collective-permute-start | bytes 3588104 | tf_op jit(solution)/shard_map/ppermute | solution.py:544
  83.0 14.3 %collective-permute-start.9 = (bf16[2304,512]{1,0:T(8,128)(2,1)}, bf16[2304,512]{1,0:T(8,128)(2,1)S(1)}, u32[]{:S(2)}, u32[]{:S(2)}) collective-permute-start(bf16[2304,512]{1,0:T(8,128)(2,1)} %get-tuple-element.90), channel_id=1, source_target_pairs={{0,1},{1,0},{2,3},{3,2},{4,5},{5,4},{6,7},{7,6},{8,9},{9,8},{10,11... | collective-permute-start | bytes 7077896 | tf_op jit(solution)/shard_map/ppermute | solution.py:544
  97.6 16.4 %collective-permute-start.10 = (bf16[1152,512]{1,0:T(8,128)(2,1)S(1)}, bf16[1152,512]{1,0:T(8,128)(2,1)}, u32[]{:S(2)}, u32[]{:S(2)}) collective-permute-start(bf16[1152,512]{1,0:T(8,128)(2,1)S(1)} %add_convert_fusion), channel_id=1, source_target_pairs={{0,2},{1,5},{2,0},{3,7},{4,6},{5,1},{6,4},{7,3},{8,10},{9,13},{10,... | collective-permute-start | bytes 3538952 | tf_op jit(solution)/shard_map/ppermute | solution.py:544
  115.4 9.9 %collective-permute-start.11 = (bf16[576,512]{1,0:T(8,128)(2,1)S(1)}, bf16[576,512]{1,0:T(8,128)(2,1)S(1)}, u32[]{:S(2)}, u32[]{:S(2)}) collective-permute-start(bf16[576,512]{1,0:T(8,128)(2,1)S(1)} %add_convert_fusion.1), channel_id=1, source_target_pairs={{0,4},{1,9},{2,6},{3,11},{4,0},{5,13},{6,2},{7,15},{8,12},{9,1},{1... | collective-permute-start | bytes 1769480 | tf_op jit(solution)/shard_map/ppermute | solution.py:544
  124.3 8.0 %collective-permute-start.17 = (bf16[1024,512]{1,0:T(8,128)(2,1)S(1)}, bf16[1024,512]{1,0:T(8,128)(2,1)S(1)}, u32[]{:S(2)}, u32[]{:S(2)}) collective-permute-start(bf16[1024,512]{1,0:T(8,128)(2,1)S(1)} %get-tuple-element.115), channel_id=1, source_target_pairs={{0,1},{1,0},{2,3},{3,2},{4,5},{5,4},{6,7},{7,6},{8,9},{9,8},{10,11... | collective-permute-start | bytes 3145736 | tf_op jit(solution)/shard_map/ppermute | solution.py:544
  132.4 9.4 %collective-permute-start.19 = (bf16[528,512]{1,0:T(8,128)(2,1)S(1)}, bf16[528,512]{1,0:T(8,128)(2,1)S(1)}, u32[]{:S(2)}, u32[]{:S(2)}) collective-permute-start(bf16[528,512]{1,0:T(8,128)(2,1)S(1)} %pad_maximum_fusion.2), channel_id=1, source_target_pairs={{0,2},{1,5},{2,0},{3,7},{4,6},{5,1},{6,4},{7,3},{8,10},{9,13},{10,... | collective-permute-start | bytes 1622024 | tf_op jit(solution)/shard_map/ppermute | solution.py:544
  133.9 9.0 %collective-permute-start.12 = (bf16[288,512]{1,0:T(8,128)(2,1)S(1)}, bf16[288,512]{1,0:T(8,128)(2,1)S(1)}, u32[]{:S(2)}, u32[]{:S(2)}) collective-permute-start(bf16[288,512]{1,0:T(8,128)(2,1)S(1)} %add_convert_fusion.3), channel_id=1, source_target_pairs={{0,8},{1,17},{2,10},{3,19},{4,12},{5,21},{6,14},{7,23},{8,0},{9,25... | collective-permute-start | bytes 884744 | tf_op jit(solution)/shard_map/ppermute | solution.py:544
  142.0 6.6 %collective-permute-start.20 = (bf16[272,512]{1,0:T(8,128)(2,1)S(1)}, bf16[272,512]{1,0:T(8,128)(2,1)S(1)}, u32[]{:S(2)}, u32[]{:S(2)}) collective-permute-start(bf16[272,512]{1,0:T(8,128)(2,1)S(1)} %pad_maximum_fusion.5), channel_id=1, source_target_pairs={{0,4},{1,9},{2,6},{3,11},{4,0},{5,13},{6,2},{7,15},{8,12},{9,1},{1... | collective-permute-start | bytes 835592 | tf_op jit(solution)/shard_map/ppermute | solution.py:544
  143.9 7.7 %collective-permute-start.13 = (bf16[144,512]{1,0:T(8,128)(2,1)S(1)}, bf16[144,512]{1,0:T(8,128)(2,1)S(1)}, u32[]{:S(2)}, u32[]{:S(2)}) collective-permute-start(bf16[144,512]{1,0:T(8,128)(2,1)S(1)} %add_convert_fusion.6), channel_id=1, source_target_pairs={{0,16},{1,3},{2,18},{3,1},{4,20},{5,7},{6,22},{7,5},{8,24},{9,11},... | collective-permute-start | bytes 442376 | tf_op jit(solution)/shard_map/ppermute | solution.py:544
  148.7 7.4 %collective-permute-start.21 = (bf16[144,512]{1,0:T(8,128)(2,1)S(1)}, bf16[144,512]{1,0:T(8,128)(2,1)S(1)}, u32[]{:S(2)}, u32[]{:S(2)}) collective-permute-start(bf16[144,512]{1,0:T(8,128)(2,1)S(1)} %pad_maximum_fusion.7), channel_id=1, source_target_pairs={{0,8},{1,17},{2,10},{3,19},{4,12},{5,21},{6,14},{7,23},{8,0},{9,25... | collective-permute-start | bytes 442376 | tf_op jit(solution)/shard_map/ppermute | solution.py:544
  152.6 6.2 %collective-permute-start.14 = (bf16[144,512]{1,0:T(8,128)(2,1)S(1)}, bf16[144,512]{1,0:T(8,128)(2,1)S(1)}, u32[]{:S(2)}, u32[]{:S(2)}) collective-permute-start(bf16[144,512]{1,0:T(8,128)(2,1)S(1)} %add_convert_fusion.5), channel_id=1, source_target_pairs={{0,4},{1,17},{2,6},{3,19},{4,0},{5,21},{6,2},{7,23},{8,12},{9,25},... | collective-permute-start | bytes 442376 | tf_op jit(solution)/shard_map/ppermute | solution.py:544
  156.3 5.5 %collective-permute-start.22 = (bf16[80,512]{1,0:T(8,128)(2,1)S(1)}, bf16[80,512]{1,0:T(8,128)(2,1)S(1)}, u32[]{:S(2)}, u32[]{:S(2)}) collective-permute-start(bf16[80,512]{1,0:T(8,128)(2,1)S(1)} %pad_maximum_fusion.9), channel_id=1, source_target_pairs={{0,16},{1,3},{2,18},{3,1},{4,20},{5,7},{6,22},{7,5},{8,24},{9,11},... | collective-permute-start | bytes 245768 | tf_op jit(solution)/shard_map/ppermute | solution.py:544
  158.9 12.4 %collective-permute-start.15 = (bf16[288,512]{1,0:T(8,128)(2,1)S(1)}, bf16[288,512]{1,0:T(8,128)(2,1)S(1)}, u32[]{:S(2)}, u32[]{:S(2)}) collective-permute-start(bf16[288,512]{1,0:T(8,128)(2,1)S(1)} %pad_maximum_fusion.4), channel_id=1, source_target_pairs={{0,16},{1,9},{2,18},{3,11},{4,20},{5,13},{6,22},{7,15},{8,24},{9,1... | collective-permute-start | bytes 884744 | tf_op jit(solution)/shard_map/ppermute | solution.py:544
  161.8 9.6 %collective-permute-start.23 = (bf16[64,512]{1,0:T(8,128)(2,1)S(1)}, bf16[64,512]{1,0:T(8,128)(2,1)S(1)}, u32[]{:S(2)}, u32[]{:S(2)}) collective-permute-start(bf16[64,512]{1,0:T(8,128)(2,1)S(1)} %add_convert_fusion.8), channel_id=1, source_target_pairs={{0,4},{1,17},{2,6},{3,19},{4,0},{5,21},{6,2},{7,23},{8,12},{9,25},... | collective-permute-start | bytes 196616 | tf_op jit(solution)/shard_map/ppermute | solution.py:544
  171.3 13.6 %collective-permute-start.16 = (bf16[576,512]{1,0:T(8,128)(2,1)S(1)}, bf16[576,512]{1,0:T(8,128)(2,1)S(1)}, u32[]{:S(2)}, u32[]{:S(2)}) collective-permute-start(bf16[576,512]{1,0:T(8,128)(2,1)S(1)} %pad_maximum_fusion.1), channel_id=1, source_target_pairs={{0,8},{1,5},{2,10},{3,7},{4,12},{5,1},{6,14},{7,3},{8,0},{9,13},{1... | collective-permute-start | bytes 1769480 | tf_op jit(solution)/shard_map/ppermute | solution.py:544
  171.4 8.8 %collective-permute-start.24 = (bf16[128,512]{1,0:T(8,128)(2,1)S(1)}, bf16[128,512]{1,0:T(8,128)(2,1)S(1)}, u32[]{:S(2)}, u32[]{:S(2)}) collective-permute-start(bf16[128,512]{1,0:T(8,128)(2,1)S(1)} %pad_maximum_fusion.8), channel_id=1, source_target_pairs={{0,16},{1,9},{2,18},{3,11},{4,20},{5,13},{6,22},{7,15},{8,24},{9,1... | collective-permute-start | bytes 393224 | tf_op jit(solution)/shard_map/ppermute | solution.py:544
  180.2 8.3 %collective-permute-start.25 = (bf16[256,512]{1,0:T(8,128)(2,1)S(1)}, bf16[256,512]{1,0:T(8,128)(2,1)S(1)}, u32[]{:S(2)}, u32[]{:S(2)}) collective-permute-start(bf16[256,512]{1,0:T(8,128)(2,1)S(1)} %pad_maximum_fusion.6), channel_id=1, source_target_pairs={{0,8},{1,5},{2,10},{3,7},{4,12},{5,1},{6,14},{7,3},{8,0},{9,13},{1... | collective-permute-start | bytes 786440 | tf_op jit(solution)/shard_map/ppermute | solution.py:544
  194.0 3.7 %collective-permute-start.27 = (f32[1]{0:T(128)}, f32[1]{0:T(128)}, u32[]{:S(2)}, u32[]{:S(2)}) collective-permute-start(f32[1]{0:T(128)} %add.307), channel_id=1, source_target_pairs={{0,2},{1,3},{2,0},{3,1},{4,6},{5,7},{6,4},{7,5},{8,10},{9,11},{10,... | collective-permute-start | bytes 20 | tf_op jit(solution)/shard_map/ppermute | solution.py:544
  207.8 12.8 %collective-permute-start.28 = (bf16[512,512]{1,0:T(8,128)(2,1)S(1)}, bf16[512,512]{1,0:T(8,128)(2,1)S(1)}, u32[]{:S(2)}, u32[]{:S(2)}) collective-permute-start(bf16[512,512]{1,0:T(8,128)(2,1)S(1)} %constant_dynamic-slice_fusion), channel_id=1, source_target_pairs={{0,2},{1,3},{2,0},{3,1},{4,6},{5,7},{6,4},{7,5},{8,10},{9,11},{10,... | collective-permute-start | bytes 1572872 | tf_op jit(solution)/shard_map/ppermute | solution.py:544
  220.6 11.8 %collective-permute-start.29 = (bf16[512,512]{1,0:T(8,128)(2,1)S(1)}, bf16[512,512]{1,0:T(8,128)(2,1)S(1)}, u32[]{:S(2)}, u32[]{:S(2)}) collective-permute-start(bf16[512,512]{1,0:T(8,128)(2,1)S(1)} %collective-permute-done.28.refs_0_), channel_id=1, source_target_pairs={{0,4},{1,5},{2,6},{3,7},{4,0},{5,1},{6,2},{7,3},{8,12},{9,13},{10,... | collective-permute-start | bytes 1572872 | tf_op jit(solution)/shard_map/ppermute | solution.py:544
  221.3 23.9 %collective-permute-start.34 = (bf16[1680,512]{1,0:T(8,128)(2,1)}, bf16[1680,512]{1,0:T(8,128)(2,1)S(1)}, u32[]{:S(2)}, u32[]{:S(2)}) collective-permute-start(bf16[1680,512]{1,0:T(8,128)(2,1)} %renew.1.p0), channel_id=1, source_target_pairs={{0,1},{1,0},{2,3},{3,2},{4,5},{5,4},{6,7},{7,6},{8,9},{9,8},{10,11... | collective-permute-start | bytes 5160968 | tf_op jit(solution)/shard_map/ppermute | solution.py:544
  222.5 21.4 %collective-permute-start.30 = (bf16[656,512]{1,0:T(8,128)(2,1)S(1)}, bf16[656,512]{1,0:T(8,128)(2,1)}, u32[]{:S(2)}, u32[]{:S(2)}) collective-permute-start(bf16[656,512]{1,0:T(8,128)(2,1)S(1)} %slice.291), channel_id=1, source_target_pairs={{0,2},{1,3},{2,0},{3,1},{4,6},{5,7},{6,4},{7,5},{8,10},{9,11},{10,... | collective-permute-start | bytes 2015240 | tf_op jit(solution)/shard_map/ppermute | solution.py:544
  224.0 19.0 %collective-permute-start.31 = (bf16[512,512]{1,0:T(8,128)(2,1)S(1)}, bf16[512,512]{1,0:T(8,128)(2,1)S(1)}, u32[]{:S(2)}, u32[]{:S(2)}) collective-permute-start(bf16[512,512]{1,0:T(8,128)(2,1)S(1)} %collective-permute-done.28.refs_0_), channel_id=1, source_target_pairs={{0,1},{1,0},{2,3},{3,2},{4,5},{5,4},{6,7},{7,6},{8,9},{9,8},{10,11... | collective-permute-start | bytes 1572872 | tf_op jit(solution)/shard_map/ppermute | solution.py:544
  232.4 11.5 %collective-permute-start.32 = (bf16[512,512]{1,0:T(8,128)(2,1)S(1)}, bf16[512,512]{1,0:T(8,128)(2,1)S(1)}, u32[]{:S(2)}, u32[]{:S(2)}) collective-permute-start(bf16[512,512]{1,0:T(8,128)(2,1)S(1)} %collective-permute-done.29.refs_1_), channel_id=1, source_target_pairs={{0,1},{1,0},{2,3},{3,2},{4,5},{5,4},{6,7},{7,6},{8,9},{9,8},{10,11... | collective-permute-start | bytes 1572872 | tf_op jit(solution)/shard_map/ppermute | solution.py:544
  244.6 3.1 %collective-permute-start.33 = (bf16[656,512]{1,0:T(8,128)(2,1)}, bf16[656,512]{1,0:T(8,128)(2,1)}, u32[]{:S(2)}, u32[]{:S(2)}) collective-permute-start(bf16[656,512]{1,0:T(8,128)(2,1)} %collective-permute-done.30.refs_2_), channel_id=1, source_target_pairs={{0,1},{1,0},{2,3},{3,2},{4,5},{5,4},{6,7},{7,6},{8,9},{9,8},{10,11... | collective-permute-start | bytes 2015240 | tf_op jit(solution)/shard_map/ppermute | solution.py:544
  (41 other events, 230.9 us)

commit v3 on v2

v3 whole, which is shorter than its diff:
```python
import functools
import jax
import jax.numpy as jnp
from jax import lax
from jax.experimental import pallas as pl
from jax.experimental.pallas import tpu as pltpu
from jax.sharding import PartitionSpec as P

BF = jnp.bfloat16
F32 = jnp.float32
VMEM_LIMIT = 56 * 1024 * 1024
VMEM_SMALL = 24 * 1024 * 1024
CHUNK = 256
SLOT = 64
GROUP = 256
LANES = 128
SMALL = 16
CHEAP = pl.CostEstimate(flops=1, bytes_accessed=1, transcendentals=0)
STEP = 10
TILE = 512
COUNTS = (1, 2, 1)


def whole(a):
    return pl.BlockSpec(a.shape, lambda *_: (0,) * len(a.shape), pipeline_mode=pl.Buffered(1))


def dot(a, b):
    return jnp.dot(a, b, preferred_element_type=F32)


def dot_nt(a, b):
    return lax.dot_general(a, b, (((1,), (1,)), ((), ())), preferred_element_type=F32)


def dot_tn(a, b):
    return lax.dot_general(a, b, (((0,), (0,)), ((), ())), preferred_element_type=F32)


def head_of(shape, dim):
    return lax.broadcasted_iota(jnp.int32, shape, dim) // SLOT


def block_diagonal(state):
    return jnp.where(head_of(state.shape, 0) == head_of(state.shape, 1), state, 0.0).astype(BF)


def only_head(rows, head):
    return jnp.where(head_of(rows.shape, 1) == head, rows, jnp.zeros_like(rows))


def by_head(rows):
    return jnp.concatenate([only_head(rows, h) for h in range(GROUP // SLOT)], axis=0)


def lower(square):
    size = square.shape[0]
    row = lax.broadcasted_iota(jnp.int16, (size, size), 0)
    col = lax.broadcasted_iota(jnp.int16, (size, size), 1)
    return jnp.concatenate(
        [
            jnp.where(row >= col, square[:, first : first + size].astype(BF), jnp.zeros((), BF))
            for first in range(0, square.shape[1], size)
        ],
        axis=1,
    )


def upper(square):
    size = square.shape[1]
    row = lax.broadcasted_iota(jnp.int16, (size, size), 0)
    col = lax.broadcasted_iota(jnp.int16, (size, size), 1)
    return jnp.concatenate(
        [
            jnp.where(row <= col, square[first : first + size, :].astype(BF), jnp.zeros((), BF))
            for first in range(0, square.shape[0], size)
        ],
        axis=1,
    )


def split_dot(ones, values):
    high = values.astype(BF)
    low = (values - high.astype(F32)).astype(BF)
    return dot(ones, high) + dot(ones, low)


def head_ones():
    return jnp.where(
        head_of((GROUP, GROUP), 0) == head_of((GROUP, GROUP), 1), 1.0, 0.0
    ).astype(BF)


def head_sums(values):
    ones = head_ones()
    high = values.astype(BF)
    low = (values - high.astype(F32)).astype(BF)
    return dot(high, ones) + dot(low, ones)


def head_max(values):
    top = None
    head = head_of(values.shape, 1)
    for index in range(GROUP // SLOT):
        mine = jnp.max(jnp.where(head == index, values, -jnp.inf), axis=1, keepdims=True)
        top = mine if top is None else jnp.where(head == index, mine, top)
    return top


def normalise(values):
    centred = values - jnp.mean(values, axis=-1, keepdims=True)
    inv = lax.rsqrt(jnp.mean(centred * centred, axis=-1, keepdims=True) + 1e-05)
    return centred * inv, inv


def normalise_back(grad, unit, inv, gain):
    scaled = grad * gain
    return inv * (
        scaled
        - jnp.mean(scaled, axis=-1, keepdims=True)
        - unit * jnp.mean(scaled * unit, axis=-1, keepdims=True)
    )


def attend_kernel(
    pos_ref, half_ref, x_ref, near0, near1, far0, far1, far2, far3,
    q_ref, k_ref, v_ref, n_ref, e_ref, eb_ref, z_ref, o_ref, w_ref, s_ref, keys_ref, values_ref,
    weights_ref, norm_ref, keys, values, carry
):
    width = x_ref.shape[1]
    part = width // 4

    @pl.when(pl.program_id(0) == 0)
    def _():
        low = far0.shape[0]

        def rows_of(index, first, count):
            if index < 2:
                return (near0, near1)[index][first : first + count, :]
            a, b = ((far0, far1), (far2, far3))[index - 2]
            if first >= low:
                a, b, first = b, a, first - low
            return jnp.where(half_ref[0] == 0, a[first : first + count, :], b[first : first + count, :])

        for index in range(4):
            rows = pl.ds(pl.multiple_of(pos_ref[index] * part, part), part)
            for m in range(4):
                weights_ref[m, rows, :] = rows_of(index, m * part + SMALL * (m > 1), part)
            norm_ref[:, rows] = rows_of(index, 2 * part, SMALL)[0:8, 0:part].astype(F32)
        carry[...] = jnp.zeros_like(carry)
        keys[...] = jnp.zeros_like(keys)
        values[...] = jnp.zeros_like(values)

    heads = range(GROUP // SLOT)
    groups = range(keys.shape[0])
    cols = [slice(i * GROUP, (i + 1) * GROUP) for i in groups]
    unit, _ = normalise(x_ref[...].astype(F32))
    normed = (unit * norm_ref[0:1, :] + norm_ref[1:2, :]).astype(BF)
    n_ref[...] = normed
    rows = normed.shape[0]
    ones = lower(jnp.ones((rows, rows), F32))
    q, k, v, e, inv = [], [], [], [], []
    for c in cols:
        raised = jnp.exp(dot(normed, weights_ref[3, :, c]))
        z = split_dot(ones, raised) + carry[0:1, c]
        carry[0:1, c] = z[rows - 1 : rows, :]
        e_ref[:, c] = raised
        z_ref[:, c] = z
        e.append(raised.astype(BF))
        inv.append(1.0 / z)
        for m, part_of in enumerate((q, k, v)):
            part_of.append(dot(normed, weights_ref[m, :, c]).astype(BF))
    for i in groups:
        q_ref[:, cols[i]], k_ref[:, cols[i]], v_ref[:, cols[i]] = q[i], k[i], v[i]
        eb_ref[:, cols[i]] = e[i]
    total, value_state = [], []
    for i in groups:
        state = block_diagonal(keys[i])
        keys_ref[i, 0] = state
        total.append(dot(q[i], state))
        state = block_diagonal(values[i])
        values_ref[i, 0] = state
        value_state.append(state)
    es = [by_head(e[i]) for i in groups]
    for i in groups:
        total[i] += dot(lower(dot_nt(q[i], by_head(k[i]))), es[i])
    scores = [total[i] * inv[i] * 0.125 for i in groups]
    raised = [jnp.exp(scores[i] - head_max(scores[i])) for i in groups]
    weights = [raised[i] / head_sums(raised[i]) for i in groups]
    ratio = [(weights[i] * inv[i]).astype(BF) for i in groups]
    out = [dot(ratio[i], value_state[i]) for i in groups]
    for i in groups:
        out[i] += dot(lower(dot_nt(ratio[i], es[i])), by_head(v[i]))
    for i in groups:
        s_ref[:, cols[i]] = scores[i]
        w_ref[:, cols[i]] = weights[i]
        o_ref[:, cols[i]] = out[i].astype(BF)
        keys[i] += dot_tn(k[i], e[i])
        values[i] += dot_tn(e[i], v[i])


def attend(pos, half, x, pieces):
    length, width = x.shape
    steps, groups = length // CHUNK, width // GROUP
    rows = lambda dtype: jax.ShapeDtypeStruct((length, width), dtype)
    block = pl.BlockSpec((CHUNK, width), lambda i: (i, 0))
    state = pl.BlockSpec((groups, 1, GROUP, GROUP), lambda i: (0, i, 0, 0))
    states = jax.ShapeDtypeStruct((groups, steps, GROUP, GROUP), BF)
    full = [jax.ShapeDtypeStruct((4, width, width), BF), jax.ShapeDtypeStruct((8, width), F32)]
    return pl.pallas_call(
        attend_kernel,
        grid=(steps,),
        in_specs=[pl.BlockSpec(memory_space=pltpu.SMEM)] * 2 + [block] + [whole(p) for p in pieces],
        out_specs=[block] * 10 + [state] * 2 + [whole(a) for a in full],
        out_shape=[rows(BF)] * 4
        + [rows(F32), rows(BF), rows(F32), rows(BF), rows(F32), rows(F32), states, states]
        + full,
        scratch_shapes=[pltpu.VMEM((groups, GROUP, GROUP), F32)] * 2 + [pltpu.VMEM((8, width), F32)],
        compiler_params=pltpu.CompilerParams(
            dimension_semantics=("arbitrary",), vmem_limit_bytes=VMEM_LIMIT
        ),
        name="attend",
        cost_estimate=CHEAP,
    )(pos, half, x, *pieces)


def mix_back_kernel(*refs, begun):
    g_ref, q_ref, k_ref, v_ref, eb_ref, e_ref, z_ref, w_ref, s_ref, keys_ref, values_ref = refs[:11]
    before, (dq_ref, dk_ref, dv_ref, dc_ref, later_v, later_k, carry) = refs[11:-7], refs[-7:]

    @pl.when(pl.program_id(0) == 0)
    def _():
        if begun:
            later_v[...], later_k[...], carry[...] = [ref[...] for ref in before]
        else:
            later_v[...] = jnp.zeros_like(later_v)
            later_k[...] = jnp.zeros_like(later_k)
            carry[...] = jnp.zeros_like(carry)

    heads = range(GROUP // SLOT)
    groups = range(later_v.shape[0])
    cols = [slice(i * GROUP, (i + 1) * GROUP) for i in groups]
    g, q, k, v, e = [[ref[:, c] for c in cols] for ref in (g_ref, q_ref, k_ref, v_ref, eb_ref)]
    inv = [1.0 / z_ref[:, c] for c in cols]
    weights = [w_ref[:, c] for c in cols]
    ratio = [(weights[i] * inv[i]).astype(BF) for i in groups]
    es = [by_head(e[i]) for i in groups]
    state = [block_diagonal(later_v[i]) for i in groups]
    d_ratio = [dot_nt(g[i], values_ref[i, 0]) for i in groups]
    dv = [dot(e[i], state[i]) for i in groups]
    de = [dot_nt(v[i], state[i]) for i in groups]
    for i in groups:
        vs = by_head(v[i])
        d_ratio[i] += dot(lower(dot_nt(g[i], vs)), es[i])
        de[i] += dot(upper(dot_nt(vs, g[i])), by_head(ratio[i]))
        dv[i] += dot(upper(dot_nt(es[i], ratio[i])), by_head(g[i]))
    d_weights = [d_ratio[i] * inv[i] for i in groups]
    both = [d_weights[i] * weights[i] for i in groups]
    d_scores = [weights[i] * (d_weights[i] - head_sums(both[i])) for i in groups]
    dn = [(d_scores[i] * inv[i] * 0.125).astype(BF) for i in groups]
    dz = [-(both[i] + d_scores[i] * s_ref[:, cols[i]]) * inv[i] for i in groups]
    state = [block_diagonal(later_k[i]) for i in groups]
    dq = [dot_nt(dn[i], keys_ref[i, 0]) for i in groups]
    dk = [dot(e[i], state[i]) for i in groups]
    de = [de[i] + dot_nt(k[i], state[i]) for i in groups]
    for i in groups:
        ks = by_head(k[i])
        dq[i] += dot(lower(dot_nt(dn[i], es[i])), ks)
        dk[i] += dot(upper(dot_nt(es[i], dn[i])), by_head(q[i]))
        de[i] += dot(upper(dot_nt(ks, q[i])), by_head(dn[i]))
    rows = dz[0].shape[0]
    ones = upper(jnp.ones((rows, rows), F32))
    for i in groups:
        dv_ref[:, cols[i]] = dv[i].astype(BF)
        dq_ref[:, cols[i]] = dq[i].astype(BF)
        dk_ref[:, cols[i]] = dk[i].astype(BF)
        z_sum = split_dot(ones, dz[i]) + carry[0:1, cols[i]]
        carry[0:1, cols[i]] = z_sum[0:1, :]
        dc_ref[:, cols[i]] = ((de[i] + z_sum) * e_ref[:, cols[i]]).astype(BF)
        later_v[i] += dot_tn(ratio[i], g[i])
        later_k[i] += dot_tn(dn[i], q[i])


def mix_back(last, count, before, g, q, k, v, eb, e, z, w, s, keys, values):
    length, width = q.shape
    groups = width // GROUP
    block = pl.BlockSpec((CHUNK, width), lambda i: (last - i, 0))
    state = pl.BlockSpec((groups, 1, GROUP, GROUP), lambda i: (0, last - i, 0, 0))
    out = pl.BlockSpec((CHUNK, width), lambda i: (count - 1 - i, 0))
    rows = jax.ShapeDtypeStruct((count * CHUNK, width), BF)
    sums = [jax.ShapeDtypeStruct((groups, GROUP, GROUP), F32)] * 2
    sums += [jax.ShapeDtypeStruct((8, width), F32)]
    return pl.pallas_call(
        functools.partial(mix_back_kernel, begun=bool(before)),
        grid=(count,),
        in_specs=[block] * 9 + [state] * 2 + [whole(a) for a in before],
        out_specs=[out] * 4 + [whole(a) for a in sums],
        out_shape=[rows] * 4 + sums,
        compiler_params=pltpu.CompilerParams(
            dimension_semantics=("arbitrary",), vmem_limit_bytes=VMEM_LIMIT
        ),
        name="mix_back",
        cost_estimate=CHEAP,
    )(g, q, k, v, eb, e, z, w, s, keys, values, *before)


def scatter_unit(place_ref, grads, first, unit, shard, target, table):
    count = place_ref.shape[1] // 2
    part = LANES
    rows = part // count
    height = target.shape[0] // LANES * LANES // (2 * count)
    for d in range(count):
        place = place_ref[table, (shard // 2) * count + d]
        where = pl.ds(pl.multiple_of(place * height + unit * rows, rows), rows)
        target[where, :] = grads[pl.ds(pl.multiple_of(first + d * rows, rows), rows), :]


def scatter_shards(pos_ref, place_ref, grads, send_ref, keep_ref, unit):
    for index in range(4):
        pos = pos_ref[index]
        target = send_ref if index % 2 else keep_ref
        scatter_unit(place_ref, grads, pos * LANES, unit, pos, target, index % 2)


def feed_kernel(
    pos_ref, place_ref, factor_ref, x_ref, g_ref, o_ref, norm_ref, p0, p1, p2, p3, t0, t1, t2, t3,
    y_ref, dh_ref, do_ref, send_ref, keep_ref, dnorm_ref,
    wo, w1, w2, branch, unit_ref, inv_ref, n2, gb, n2_t, gb_t, dn2, grads, u_all, da_all
):
    step = pl.program_id(0)
    last = pl.num_programs(0) - 1
    length, width = x_ref.shape
    part = width // 4
    block = w1.shape[2]
    tiles = length // 256

    @pl.when(step == 0)
    def _():
        for index, (piece, tall) in enumerate(((p0, t0), (p1, t1), (p2, t2), (p3, t3))):
            pos = pos_ref[index]
            rows = pl.ds(pl.multiple_of(pos * part, part), part)
            wo[rows, :] = piece[0:part, :]
            for j in range(4):
                w1[j, rows, :] = piece[(j + 1) * part : (j + 2) * part, :]
            w2[pos] = tall[0:block, :]

        def before(i, _):
            rows = pl.ds(pl.multiple_of(i * 256, 256), 256)
            h1 = x_ref[rows, :].astype(F32) + dot(o_ref[rows, :], wo[...])
            branch[rows, :] = h1
            unit, inv = normalise(h1)
            unit_ref[rows, :] = unit
            inv_ref[rows, :] = jnp.broadcast_to(inv, (256, 128))
            normed = (unit * norm_ref[2:3, :] + norm_ref[3:4, :]).astype(BF)
            n2[rows, :] = normed
            n2_t[:, rows] = normed.T
            grad = (g_ref[rows, :].astype(F32) * factor_ref[0]).astype(BF)
            gb[rows, :] = grad
            gb_t[:, rows] = grad.T
            dn2[rows, :] = jnp.zeros((256, width), F32)
            return 0

        lax.fori_loop(0, tiles, before, 0)

    up = w1[step]
    down = w2[step]
    tile = TILE
    for i in range(length // tile):
        rows = slice(i * tile, (i + 1) * tile)
        a = dot(n2[rows, :], up)
        square = a * a
        half = 0.5 + 0.5 * jnp.tanh(a * (0.7978845608 + (0.044715 * 0.7978845608) * square))
        u = a * half
        slope = half + u * (1.0 - half) * (
            2.0 * 0.7978845608 + (6.0 * 0.044715 * 0.7978845608) * square
        )
        u = u.astype(BF)
        da = (dot_nt(gb[rows, :], down) * slope).astype(BF)
        u_all[rows, :] = u
        da_all[rows, :] = da
        branch[rows, :] += dot(u, down)
        dn2[rows, :] += dot_nt(da, up)
    up_grad = dot(n2_t[...], da_all[...])
    down_grad = dot(gb_t[...], u_all[...])
    grads[...] = up_grad.astype(BF)
    scatter_shards(pos_ref, place_ref, grads, send_ref, keep_ref, step + 1)
    grads[...] = down_grad.astype(BF)
    mine = (step ^ pos_ref[0]) & 1 == 0

    @pl.when(mine)
    def _():
        for u in range(4):
            scatter_unit(place_ref, grads, u * part, 5 + u, step, keep_ref, 0)

    @pl.when(jnp.logical_not(mine))
    def _():
        for u in range(4):
            scatter_unit(place_ref, grads, u * part, 5 + u, step, send_ref, 1)

    @pl.when(step == last)
    def _():
        gain = norm_ref[2:3, :]

        def after(i, sums):
            rows = pl.ds(pl.multiple_of(i * 256, 256), 256)
            y_ref[rows, :] = branch[rows, :].astype(BF)
            grad = dn2[rows, :]
            unit = unit_ref[rows, :]
            dh = g_ref[rows, :].astype(F32) * factor_ref[0] + normalise_back(
                grad, unit, inv_ref[rows, 0:1], gain
            )
            dh_ref[rows, :] = dh
            dh_low = dh.astype(BF)
            do_ref[rows, :] = dot_nt(dh_low, wo[...]).astype(BF)
            return (
                sums[0] + jnp.sum(grad * unit, axis=0, keepdims=True),
                sums[1] + jnp.sum(grad, axis=0, keepdims=True),
                sums[2] + dot_tn(o_ref[rows, :], dh_low),
            )

        empty = jnp.zeros((1, width), F32)
        sums = lax.fori_loop(0, tiles, after, (empty, empty, jnp.zeros((width, width), F32)))
        dnorm_ref[...] = jnp.zeros_like(dnorm_ref)
        dnorm_ref[0:1, :] = sums[0]
        dnorm_ref[1:2, :] = sums[1]
        grads[...] = sums[2].astype(BF)
        scatter_shards(pos_ref, place_ref, grads, send_ref, keep_ref, 0)


def feed(pos, place, factor, x, g, o, norm, pieces, talls):
    length, width = x.shape
    block = width
    height = 5 * (width // 4) + block
    rows = lambda dtype: jax.ShapeDtypeStruct((length, width), dtype)
    out = [
        rows(BF), rows(F32), rows(BF),
        jax.ShapeDtypeStruct((2 * height, width), BF),
        jax.ShapeDtypeStruct((2 * height, width), BF),
        jax.ShapeDtypeStruct((8, width), F32),
    ]
    args = (x, g, o, norm) + tuple(pieces) + tuple(talls)
    return pl.pallas_call(
        feed_kernel,
        grid=(4,),
        in_specs=[pl.BlockSpec(memory_space=pltpu.SMEM)] * 3 + [whole(a) for a in args],
        out_specs=[whole(a) for a in out],
        out_shape=out,
        scratch_shapes=[
            pltpu.VMEM((width, width), BF),
            pltpu.VMEM((4, width, block), BF),
            pltpu.VMEM((4, block, width), BF),
            pltpu.VMEM((length, width), F32),
            pltpu.VMEM((length, width), F32),
            pltpu.VMEM((length, 128), F32),
            pltpu.VMEM((length, width), BF),
            pltpu.VMEM((length, width), BF),
            pltpu.VMEM((width, length), BF),
            pltpu.VMEM((width, length), BF),
            pltpu.VMEM((length, width), F32),
            pltpu.VMEM((width, block), BF),
            pltpu.VMEM((length, block), BF),
            pltpu.VMEM((length, block), BF),
        ],
        compiler_params=pltpu.CompilerParams(
            dimension_semantics=("arbitrary",), vmem_limit_bytes=VMEM_LIMIT
        ),
        name="feed",
        cost_estimate=CHEAP,
    )(pos, place, factor, *args)


def weight_back_kernel(pos_ref, place_ref, small_ref, n_ref, *refs):
    grads_in, (send_ref, keep_ref, n_t, grads) = refs[:-4], refs[-4:]
    step = pl.program_id(0)

    @pl.when(step == 0)
    def _():
        n_t[...] = n_ref[...].T
        for target in (send_ref, keep_ref):
            target[target.shape[0] - SMALL :, :] = small_ref[...]

    for m in range(4):
        @pl.when(step == m)
        def _():
            total = None
            first = 0
            for j in range(len(grads_in) // 4):
                part = grads_in[4 * j + m]
                last = first + part.shape[0]
                term = dot(n_t[:, first:last], part[...])
                total = term if total is None else total + term
                first = last
            grads[...] = total.astype(BF)

    scatter_shards(pos_ref, place_ref, grads, send_ref, keep_ref, step)


def weight_back(pos, place, small, n, halves):
    length, width = n.shape
    out = jax.ShapeDtypeStruct((2 * width + SMALL, width), BF)
    args = (small, n) + tuple(halves)
    return pl.pallas_call(
        weight_back_kernel,
        grid=(4,),
        in_specs=[pl.BlockSpec(memory_space=pltpu.SMEM)] * 2 + [whole(a) for a in args],
        out_specs=[whole(out)] * 2,
        out_shape=[out] * 2,
        scratch_shapes=[pltpu.VMEM((width, length), BF), pltpu.VMEM((width, width), BF)],
        compiler_params=pltpu.CompilerParams(
            dimension_semantics=("arbitrary",), vmem_limit_bytes=VMEM_SMALL
        ),
        name="weight_back",
        cost_estimate=CHEAP,
    )(pos, place, *args)


def input_back_kernel(x_ref, dh_ref, w_ref, norm_ref, dnorm_ref, *refs):
    grads_in, (dx_ref, small_ref, sums, dn_ref) = refs[:-4], refs[-4:]
    step = pl.program_id(0)
    tile = x_ref.shape[0]

    @pl.when(step == 0)
    def _():
        sums[...] = jnp.zeros_like(sums)

    first = 0
    for j in range(len(grads_in) // 4):
        count = grads_in[4 * j].shape[0] // tile
        begin = first

        @pl.when((step >= begin) & (step < begin + count))
        def _():
            rows = pl.ds(pl.multiple_of((step - begin) * tile, tile), tile)
            dn = None
            for m in range(4):
                term = dot_nt(grads_in[4 * j + m][rows, :], w_ref[m])
                dn = term if dn is None else dn + term
            dn_ref[...] = dn

        first += count

    dn = dn_ref[...]
    unit, inv = normalise(x_ref[...].astype(F32))
    dx_ref[...] = dh_ref[...] + normalise_back(dn, unit, inv, norm_ref[0:1, :])
    sums[0:1, :] += jnp.sum(dn * unit, axis=0, keepdims=True)
    sums[1:2, :] += jnp.sum(dn, axis=0, keepdims=True)

    @pl.when(step == pl.num_programs(0) - 1)
    def _():
        small_ref[...] = jnp.concatenate(
            [sums[0:2, :], dnorm_ref[0:2, :], jnp.zeros((SMALL - 4, sums.shape[1]), F32)], axis=0
        ).astype(BF)


def input_back(x, dh, w, norm, dnorm, halves):
    length, width = x.shape
    tile = 256
    block = pl.BlockSpec((tile, width), lambda i: (i, 0))
    small = jax.ShapeDtypeStruct((SMALL, width), BF)
    return pl.pallas_call(
        input_back_kernel,
        grid=(length // tile,),
        in_specs=[block] * 2 + [whole(w), whole(norm), whole(dnorm)] + [whole(a) for a in halves],
        out_specs=[block, whole(small)],
        out_shape=[jax.ShapeDtypeStruct((length, width), F32), small],
        scratch_shapes=[pltpu.VMEM((8, width), F32), pltpu.VMEM((tile, width), F32)],
        compiler_params=pltpu.CompilerParams(
            dimension_semantics=("arbitrary",), vmem_limit_bytes=VMEM_SMALL
        ),
        name="input_back",
        cost_estimate=CHEAP,
    )(x, dh, w, norm, dnorm, *halves)


def bits_of(size):
    return [1 << b for b in range(size.bit_length() - 1)]


def split_bits():
    return bits_of(lax.axis_size("dp"))[:3]


def exchange(values, even, odd):
    dp, shard = lax.axis_size("dp"), lax.axis_size("shard")
    perm = []
    for d in range(dp):
        for s in range(shard):
            axis, bit = odd if s % 2 else even
            other = (d ^ bit, s) if axis == "dp" else (d, s ^ bit)
            perm.append((d * shard + s, other[0] * shard + other[1]))
    return lax.ppermute(values, ("dp", "shard"), perm)


def swap(values, axis, bit):
    return exchange(values, (axis, bit), (axis, bit))


def after(values, *others):
    return lax.optimization_barrier((values,) + others)[0]


def places():
    count = 2 ** len(split_bits())
    dp, shard = lax.axis_index("dp"), lax.axis_index("shard")
    piece = jnp.arange(2 * count, dtype=jnp.int32)
    far = (piece // count) ^ (shard // 2)
    along = (piece % count) ^ (dp % count)
    order = 0
    for b in range(len(split_bits())):
        order = order * 2 + ((along >> b) & 1)
    even, odd = far * count + order, order * 2 + far
    mine = shard % 2
    return jnp.stack(
        [jnp.where(mine == 0, even, odd), jnp.where(mine == 0, odd, even)]
    ).astype(jnp.int32)


def phases():
    split = [("dp", b) for b in split_bits()]
    return list(zip([("shard", 2)] + split, split + [("shard", 2)]))


def add_up(parts, low, high):
    total = parts[0][low:high].astype(F32)
    for part in parts[1:]:
        total = total + part[low:high].astype(F32)
    return total.astype(BF)


def add_rest(piece):
    for b in bits_of(lax.axis_size("dp"))[3:]:
        piece = add_up([piece, swap(piece, "dp", b)], 0, piece.shape[0])
    return piece


def gather_plan():
    split = split_bits()
    even = [split[0]] + split[1:][::-1]
    odd = split[::-1]
    return [(("dp", a), ("dp", b)) for a, b in zip(even, odd)]


def gather_index():
    odd = lax.axis_index("shard") % 2
    mask = jnp.zeros((1,), jnp.int32)
    for (_, even_bit), (_, odd_bit) in gather_plan():
        mask = jnp.concatenate([mask, mask | jnp.where(odd == 1, odd_bit, even_bit)])
    return (lax.axis_index("dp") % mask.shape[0]) ^ mask


def adam(master, first, second, grad, rate, decay):
    first_new = 0.5 * first + 0.5 * grad
    second_new = 0.5 * second + 0.5 * grad * grad
    correction = 1.0 - 0.5**STEP
    update = first_new / correction / (jnp.sqrt(second_new / correction) + 1e-08)
    return master - rate * (update + decay * master), first_new, second_new


def gather_rows(index_ref, sources, targets):
    count = index_ref.shape[0]
    rows = LANES // count
    for source, target in zip(sources, targets):
        units = target.shape[0] // LANES
        for j in range(count):
            for u in range(units):
                place = pl.ds(pl.multiple_of(u * LANES + index_ref[j] * rows, rows), rows)
                first = (j * units + u) * rows
                target[place, :] = source[first : first + rows, :]


def renew_first_kernel(
    side_ref, index_ref, factor_ref, early_ref, late_ref, gn_ref, nm, nf, ns,
    am, af, as_, um, uf, us, copy_ref, early, late
):
    factor = factor_ref[0]
    width = early.shape[1]
    height = am.shape[1]
    gather_rows(index_ref, (early_ref, late_ref), (early, late))

    def span(unit):
        return pl.ds(pl.multiple_of(unit * LANES + side_ref[0] * height, height), height)

    for unit in range(8):
        if unit < 5:
            source = late[span(unit), :] if unit < 4 else early[span(0), :]
            state = am[unit], af[unit], as_[unit]
        else:
            source = early[span(unit - 4), :]
            cols = slice((unit - 5) * width, (unit - 4) * width)
            state = um[:, cols], uf[:, cols], us[:, cols]
        new = adam(*state, source.astype(F32) * factor, 0.05, 0.01)
        copy_ref[unit * height : (unit + 1) * height, :] = new[0].astype(BF)
    new = adam(nm[...], nf[...], ns[...], gn_ref[...] * factor, 0.3, 0.0)
    last = copy_ref.shape[0] - SMALL
    copy_ref[last:, :] = jnp.zeros((SMALL, width), BF)
    copy_ref[last : last + 4, 0:LANES] = new[0].astype(BF)


def renew_first(side, index, factor, early, late, gn, attn, up, norm):
    five, part, width = attn[0].shape
    hidden = up[0].shape[1]
    smem = pl.BlockSpec(memory_space=pltpu.SMEM)
    copy = jax.ShapeDtypeStruct((8 * part // 2 + SMALL, width), BF)
    return pl.pallas_call(
        renew_first_kernel,
        grid_spec=pltpu.PrefetchScalarGridSpec(
            num_scalar_prefetch=1,
            grid=(1,),
            in_specs=[smem, smem, whole(early), whole(late), whole(gn)]
            + [whole(a) for a in norm]
            + [pl.BlockSpec((five, part // 2, width), lambda i, side: (0, side[0], 0))] * 3
            + [pl.BlockSpec((part // 2, hidden), lambda i, side: (side[0], 0))] * 3,
            out_specs=whole(copy),
            scratch_shapes=[pltpu.VMEM(early.shape, BF), pltpu.VMEM(late.shape, BF)],
        ),
        out_shape=copy,
        compiler_params=pltpu.CompilerParams(
            dimension_semantics=("arbitrary",), vmem_limit_bytes=VMEM_LIMIT
        ),
        name="renew_first",
        cost_estimate=CHEAP,
    )(side, index, factor, early, late, gn, *norm, *attn, *up)


def update_kernel(index_ref, factor_ref, early_ref, late_ref, gn_ref, *refs):
    am, af, as_, um, uf, us, dm, df, ds, nm, nf, ns = refs[:12]
    early, late = refs[-2:]
    outs, copy_low, copy_high = refs[12:-4], refs[-4], refs[-3]
    step = pl.program_id(0)
    factor = factor_ref[0]
    width = early.shape[1]
    part = late.shape[0] // 4
    blocks = um.shape[1] // width
    height = part // pl.num_programs(0)

    def keep(group, where, unit, size, new):
        for target, value in zip(outs[3 * group : 3 * group + 3], new):
            target[where] = value
        target, unit = (copy_low, unit) if unit < 8 else (copy_high, unit - 8)
        rows = pl.ds(pl.multiple_of(unit * part + step * size, size), size)
        target[rows, :] = new[0].astype(BF)

    @pl.when(step == 0)
    def _():
        gather_rows(index_ref, (early_ref, late_ref), (early, late))
        new = adam(nm[...], nf[...], ns[...], gn_ref[...] * factor, 0.3, 0.0)
        outs[9][...], outs[10][...], outs[11][...] = new

    def span(base, size):
        return pl.ds(pl.multiple_of(base + step * size, size), size)

    for m in range(5):
        source = late[span(m * part, height), :] if m < 4 else early[span(0, height), :]
        new = adam(am[m], af[m], as_[m], source.astype(F32) * factor, 0.05, 0.01)
        keep(0, (m, slice(None), slice(None)), m, height, new)
    for j in range(blocks):
        source = early[span((j + 1) * part, height), :]
        cols = (slice(None), slice(j * width, (j + 1) * width))
        new = adam(um[cols], uf[cols], us[cols], source.astype(F32) * factor, 0.05, 0.01)
        keep(1, cols, 5 + j, height, new)
    tall = dm.shape[0]
    source = early[(blocks + 1) * part :, span(0, tall)].astype(F32).T
    new = adam(dm[...], df[...], ds[...], source * factor, 0.05, 0.01)
    keep(2, (slice(None), slice(None)), 5 + blocks, tall, new)


def update(index, factor, early, late, gn, attn, up, down, norm):
    steps = 4
    smem = pl.BlockSpec(memory_space=pltpu.SMEM)
    five, part, width = attn[0].shape
    specs = (
        [pl.BlockSpec((five, part // steps, width), lambda i: (0, i, 0))] * 3
        + [pl.BlockSpec((part // steps, up[0].shape[1]), lambda i: (i, 0))] * 3
        + [pl.BlockSpec((down[0].shape[0] // steps, width), lambda i: (i, 0))] * 3
        + [whole(norm[0])] * 3
    )
    arrays = tuple(attn) + tuple(up) + tuple(down) + tuple(norm)
    low = jax.ShapeDtypeStruct((8 * part, width), BF)
    high = jax.ShapeDtypeStruct((early.shape[0] + late.shape[0] - 8 * part, width), BF)
    return pl.pallas_call(
        update_kernel,
        grid=(steps,),
        in_specs=[smem, smem, whole(early), whole(late), whole(gn)] + specs,
        out_specs=specs + [whole(low), whole(high)],
        out_shape=[jax.ShapeDtypeStruct(a.shape, F32) for a in arrays] + [low, high],
        scratch_shapes=[pltpu.VMEM(early.shape, BF), pltpu.VMEM(late.shape, BF)],
        compiler_params=pltpu.CompilerParams(
            dimension_semantics=("arbitrary",), vmem_limit_bytes=VMEM_LIMIT
        ),
        name="update",
        cost_estimate=CHEAP,
    )(index, factor, early, late, gn, *arrays)


def place_unit(pos, source, unit, first, count, attn_ref, up_ref, down_ref, sem):
    width = attn_ref.shape[2]
    blocks = up_ref.shape[1] // width
    tall = down_ref.shape[0] // 4
    rows = pl.ds(pl.multiple_of(pos * LANES + first, count), count)
    if unit < 5:
        target = attn_ref.at[unit, rows, :]
    elif unit < 5 + blocks:
        target = up_ref.at[rows, pl.ds((unit - 5) * width, width)]
    else:
        base = pl.multiple_of(pos * tall + (unit - 5 - blocks) * LANES + first, count)
        target = down_ref.at[pl.ds(base, count), :]
    return pltpu.make_async_copy(source, target, sem)


def run_copies(copies):
    for copy in copies:
        copy.start()
    for copy in copies:
        copy.wait()


def place_whole(pos, piece, unit, outs, sems, copies):
    for j in range(piece.shape[0] // LANES):
        source = piece.at[pl.ds(j * LANES, LANES), :]
        copies.append(place_unit(pos, source, unit + j, 0, LANES, *outs, sems.at[len(copies)]))


def place_half(pos, side, piece, outs, sems, copies):
    half = LANES // 2
    for unit in range(8):
        source = piece.at[pl.ds(unit * half, half), :]
        copies.append(place_unit(pos, source, unit, half * side, half, *outs, sems.at[len(copies)]))


def unpack_near_kernel(pos_ref, side_ref, p0, p1, p2, p3, p4, p5, attn_ref, up_ref, down_ref, sems):
    copies = []
    outs = attn_ref, up_ref, down_ref
    for index, parts in enumerate(((p0, p1), (p2, p3))):
        place_whole(pos_ref[index], parts[0], 0, outs, sems, copies)
        place_whole(pos_ref[index], parts[1], 8, outs, sems, copies)
    for index, piece in enumerate((p4, p5)):
        place_half(pos_ref[2 + index], side_ref[0], piece, outs, sems, copies)
    run_copies(copies)


def unpack_far_kernel(pos_ref, side_ref, p0, p1, p2, p3, *refs):
    outs, sems = refs[3:6], refs[6]
    copies = []
    for index, piece in enumerate((p0, p1)):
        place_half(pos_ref[2 + index], side_ref[0] ^ 1, piece, outs, sems, copies)
    for index, piece in enumerate((p2, p3)):
        place_whole(pos_ref[2 + index], piece, 8, outs, sems, copies)
    run_copies(copies)


def share_copies(pos, side, low, high, first, width, hidden):
    units = (low.shape[0] + high.shape[0]) // LANES
    ours = swap(first, "shard", 2)
    other = swap(after(ours, low), "dp", 1)
    rest = swap(after(high, ours), "shard", 2)
    near = [swap(after(part, ours), "shard", 1) for part in (low, high)]
    ours_too = swap(after(ours, low), "shard", 1)
    first_too = swap(after(first[8 * LANES // 2 :], ours), "shard", 1)
    hbm = pl.BlockSpec(memory_space=pl.ANY)
    vmem = pl.BlockSpec(memory_space=pltpu.VMEM)
    smem = pl.BlockSpec(memory_space=pltpu.SMEM)
    shapes = [
        jax.ShapeDtypeStruct((5, width, width), BF),
        jax.ShapeDtypeStruct((width, hidden), BF),
        jax.ShapeDtypeStruct((hidden, width), BF),
    ]
    params = pltpu.CompilerParams(vmem_limit_bytes=VMEM_SMALL)
    begun = pl.pallas_call(
        unpack_near_kernel,
        in_specs=[smem, smem] + [vmem] * 6,
        out_specs=[hbm] * 3,
        out_shape=shapes,
        scratch_shapes=[pltpu.SemaphoreType.DMA((2 * (units + 8),))],
        compiler_params=params,
        name="unpack_near",
        cost_estimate=CHEAP,
    )(pos, side, low, high, *near, ours, ours_too)
    a, b, c, d = [
        p[p.shape[0] - SMALL : p.shape[0] - SMALL + 4, :LANES]
        for p in (first, first_too, ours, ours_too)
    ]
    low_bit, high_bit = pos[0] % 2 == 1, pos[0] // 2 == 1
    a, b, c, d = [jnp.where(low_bit, v, u) for u, v in ((a, b), (b, a), (c, d), (d, c))]
    a, b, c, d = [jnp.where(high_bit, v, u) for u, v in ((a, c), (b, d), (c, a), (d, b))]
    norms = jnp.concatenate([a, b, c, d], axis=1)
    far = [other, swap(after(other, begun[0], norms), "shard", 1)]
    far += [rest, swap(after(rest, begun[0], norms), "shard", 1)]
    done = pl.pallas_call(
        unpack_far_kernel,
        in_specs=[smem, smem] + [vmem] * 4 + [hbm] * 3,
        out_specs=[hbm] * 3,
        out_shape=shapes,
        scratch_shapes=[pltpu.SemaphoreType.DMA((2 * units,))],
        input_output_aliases={6: 0, 7: 1, 8: 2},
        compiler_params=params,
        name="unpack_far",
        cost_estimate=CHEAP,
    )(pos, side, *far, *begun)
    return tuple(done) + (norms,)


def shards(
    tokens, out_grad, domain_ids, domain_weight,
    attn_master, attn_first, attn_second,
    up_master, up_first, up_second,
    down_master, down_first, down_second,
    norm_master, norm_first, norm_second,
):
    length, width = tokens.shape
    hidden = up_master.shape[1]
    part = width // 4
    blocks = hidden // width
    dp = lax.axis_index("dp")
    shard = lax.axis_index("shard").astype(jnp.int32)
    pos = shard ^ jnp.arange(4, dtype=jnp.int32)
    half = (dp % 2).astype(jnp.int32)[None]
    place = places()

    small = jnp.pad(norm_master.astype(BF), ((0, SMALL - 4), (0, width - part)))
    rows = attn_master[:4].astype(BF).reshape(4 * part, width)
    own = jnp.concatenate([rows[: 2 * part], small, rows[2 * part :], jnp.zeros_like(small)])
    middle = own.shape[0] // 2
    near = swap(own, "shard", 1)
    ours = lax.dynamic_slice(own, (half[0] * middle, 0), (middle, width))
    far_a = swap(ours, "shard", 2)

    domains = domain_weight.shape[0]
    onehot = (domain_ids[:, None] == jnp.arange(domains, dtype=jnp.int32)[None, :]).astype(F32)
    counts = jnp.sum(onehot, axis=0)
    dp_bits = bits_of(lax.axis_size("dp"))
    for b in dp_bits[:2]:
        counts = counts + swap(counts, "dp", b)
    far_b = swap(after(far_a, counts), "dp", 1)
    second = jnp.concatenate(
        [attn_master[4].astype(BF)]
        + [up_master[:, j * width : (j + 1) * width].astype(BF) for j in range(blocks)]
    )
    second_far = swap(after(second, counts), "shard", 2)
    for b in dp_bits[2:]:
        counts = counts + after(swap(counts, "dp", b), far_b)
    counts_row = jnp.pad(counts.astype(BF)[None], ((0, SMALL - 1), (0, width - domains)))
    third = jnp.concatenate([down_master.astype(BF), counts_row])
    third_far = swap(third, "shard", 2)
    far = [far_a, far_b, swap(far_a, "shard", 1), swap(far_b, "shard", 1)]
    q, k, v, n, e, eb, z, o, weights, scores, keys, values, w, norm = attend(
        pos, half, after(tokens, third), [own, near] + far
    )
    second = [second, swap(second, "shard", 1), second_far, swap(after(second_far, o), "shard", 1)]
    third = [third, swap(third, "shard", 1), third_far, swap(after(third_far, o), "shard", 1)]
    total_seqs = lax.axis_size("dp") * lax.axis_size("shard") * domain_ids.shape[0]
    counts = sum(piece[piece.shape[0] - SMALL, :domains].astype(F32) for piece in third)
    per_domain = domain_weight * total_seqs / (domains * jnp.maximum(counts, 1.0))
    seq_weight = jnp.sum(onehot * per_domain[None, :], axis=1)
    y, dh, do, send, keep, dnorm = feed(
        pos, place, seq_weight, tokens, out_grad, o, norm, second, third
    )

    steps, plan = phases(), gather_plan()
    pieces = 2 ** len(steps)
    rows = keep.shape[0] // pieces

    def forward_phase(parts, phase, rows):
        low = rows * pieces >> (phase + 1)
        return add_up(parts, low, 2 * low)

    saved = (q, k, v, eb, e, z, weights, scores, keys, values)
    chunks = length // CHUNK
    early = [keep, swap(send, "shard", 1)]
    later = mix_back(chunks - 1, 1, (), do, *saved)
    out = after(forward_phase(early, 0, rows), later[0])
    early.append(exchange(out, *steps[0]))
    sooner = mix_back(chunks - 2, chunks - 1, later[4:], after(do, out), *saved)
    back = list(sooner[:4]) + list(later[:4])
    out = after(forward_phase(early, 1, rows), back[0])
    early.append(exchange(out, *steps[1]))
    dx, small = input_back(tokens, after(dh, out), w, norm, dnorm, back)
    send, keep = weight_back(pos, place, small, n, back)
    turn = forward_phase(early, 2, rows)
    got = exchange(turn, *steps[2])
    late = [keep, swap(after(send, turn), "shard", 1)]
    height = keep.shape[0] - SMALL
    thin = height // pieces
    small = add_up(late, height, height + SMALL)

    def late_phase(phase):
        out = jnp.concatenate([forward_phase(late, phase, thin), small])
        return out, exchange(out, *steps[phase])

    def late_sum(got):
        late.append(got)
        return add_up([small, got[got.shape[0] - SMALL :]], 0, SMALL)

    turn, late_got = late_phase(0)
    small = late_sum(late_got)
    turn, late_got = late_phase(1)
    early.append(after(got, turn))
    got = exchange(forward_phase(early, 3, rows), *steps[3])
    small = late_sum(late_got)
    turn, late_got = late_phase(2)
    early.append(after(got, turn))
    early = add_rest(add_up(early, 0, rows))
    got = exchange(early, *plan[0])
    small = late_sum(late_got)
    turn, late_got = late_phase(3)
    early = jnp.concatenate([early, after(got, turn)])
    got = exchange(early, *plan[1])
    small = late_sum(late_got)
    late = add_rest(jnp.concatenate([add_up(late, 0, thin), small]))
    late, small = late[:thin], late[thin:]
    late_got = exchange(late, *plan[0])
    norm_grad = lax.dynamic_slice(small[:4], (0, shard * part), (4, part)).astype(F32)
    late = jnp.concatenate([late, late_got])
    late = jnp.concatenate([late, exchange(late, *plan[1])])
    early = jnp.concatenate([early, after(got, late)])
    got = exchange(early, *plan[2])
    late_got = exchange(late, *plan[2])
    early = jnp.concatenate([early, after(got, late)])
    square = jnp.sum(jnp.square(norm_grad)) + jnp.sum(jnp.square(early.astype(F32)))
    late = jnp.concatenate([late, after(late_got, square)])
    square = (square + jnp.sum(jnp.square(late.astype(F32))))[None]
    for b in (1, 2):
        square = square + swap(square, "shard", b)
    index = gather_index()
    clip_norm = jnp.sqrt(square)
    factor = jnp.minimum(1.0, 1.0 / (clip_norm + 1e-06))
    attn = (attn_master, attn_first, attn_second)
    up = (up_master, up_first, up_second)
    down = (down_master, down_first, down_second)
    norms = (norm_master, norm_first, norm_second)
    leaving = renew_first(half, index, factor, early, late, norm_grad, attn, up, norms)
    *new, low, high = update(index, factor, early, after(late, leaving), norm_grad, attn, up, down, norms)
    copies = share_copies(pos, half, low, high, leaving, width, hidden)
    return (y, dx) + tuple(new) + (clip_norm[0],) + tuple(copies)


def solution(mesh):
    rows = P(("dp", "shard"), None)
    attn = (P(None, "shard", None),) * 3
    tall = (P("shard", None),) * 6
    norm = (P(None, "shard"),) * 3
    return jax.shard_map(
        shards,
        mesh=mesh,
        in_specs=(rows, rows, P(("dp", "shard")), P()) + attn + tall + norm,
        out_specs=(rows, rows) + attn + tall + norm + (P(),) * 5,
        check_vma=False,
    )
```

time: 254 us -> 238 us (0.937)
  Pallas kernels: 116 us -> 103 us
  local copies, waits for them, and re-layouts: 12.7 us -> 7.79 us
  waiting for transfers between devices: 58 us -> 62.7 us
  starting transfers between devices: 42.8 us -> 38.5 us
    pallas_call x8 -> x7, Pallas kernels: 76.4 us -> 63.9 us  [the longest x2 24.7 us: mix_back(): pl.pallas_call(functools.partial(mix_back_kernel, begun=bool(before)), gr...]
    ppermute x35 -> x41, waiting for transfers between devices: 58 us -> 62.7 us  [exchange(): return lax.ppermute(values, ('dp', 'shard'), perm)]
    ppermute x35 -> x41, starting transfers between devices: 42.8 us -> 38.5 us  [exchange(): return lax.ppermute(values, ('dp', 'shard'), perm)]
    unnamed x79 -> x68, local copies, waits for them, and re-layouts: 9.81 us -> 6.91 us
  transfers between devices with their start and end apart: 35 -> 41, of which waited for: 21 -> 25; matrix products, arithmetic and copies ran while one was open for 6% -> 5% of each run, Pallas kernels for 29% -> 28%
where the time goes in v3:
time: 238 us; the launch traced here: 237 us
  Pallas kernels  103 us (43%)
  waiting for transfers between devices  62.7 us (26%)
  starting transfers between devices  38.5 us (16%)
  other arithmetic  18.5 us (8%)
  local copies, waits for them, and re-layouts  7.79 us (3%)
  between operations  6.44 us (3%)
    ppermute x41, waiting for transfers between devices, exchange(): return lax.ppermute(values, ('dp', 'shard'), perm)  62.7 us
    ppermute x41, starting transfers between devices, exchange(): return lax.ppermute(values, ('dp', 'shard'), perm)  38.5 us
    pallas_call x1, Pallas kernels, feed(): pl.pallas_call(feed_kernel, grid=(4,), in_specs=[pl.BlockSpec(memory_spac...  29.2 us
    pallas_call x2, Pallas kernels, mix_back(): pl.pallas_call(functools.partial(mix_back_kernel, begun=bool(before)), gr...  24.7 us
    pallas_call x1, Pallas kernels, attend(): pl.pallas_call(attend_kernel, grid=(steps,), in_specs=[pl.BlockSpec(memor...  17.9 us
    pallas_call x1, Pallas kernels, update(): pl.pallas_call(update_kernel, grid=(steps,), in_specs=[smem, smem, whole(...  11 us
    convert_element_type x14, other arithmetic, add_up(): return total.astype(BF)  7.05 us
    unnamed x68, local copies, waits for them, and re-layouts  6.91 us
  transfers between devices with their start and end apart: 41, of which 25 were waited for; matrix products, arithmetic and copies ran while one was open for 5% of the time, Pallas kernels for 28%

profile of v3, /device:TPU:0, one launch (start us, length us, event | category | flops | bytes accessed | tf_op | source)
XLA Modules:
  0.0 236.9 jit_solution(925189860682254016)
XLA Ops:
  3.0 2.6 %collective-permute-start.3 = (bf16[272,512]{1,0:T(8,128)(2,1)S(1)}, bf16[272,512]{1,0:T(8,128)(2,1)}, u32[]{:S(2)}, u32[]{:S(2)}) collective-permute-start(bf16[272,512]{1,0:T(8,128)(2,1)S(1)} %constant_dynamic-slice_fusion), channel_id=1, source_target_pairs={{0,2},{1,3},{2,0},{3,1},{4,6},{5,7},{6,4},{7,5},{8,10},{9,11},{10,... | collective-permute-start | bytes 835592 | tf_op jit(solution)/shard_map/ppermute | solution.py:591
  11.4 2.0 collective-permute-done.1
  15.1 2.7 %collective-permute-start.2 = (f32[8]{0:T(128)S(1)}, f32[8]{0:T(128)S(1)}, u32[]{:S(2)}, u32[]{:S(2)}) collective-permute-start(f32[8]{0:T(128)S(1)} %fusion.22), channel_id=1, source_target_pairs={{0,16},{1,17},{2,18},{3,19},{4,20},{5,21},{6,22},{7,23},{8,24},{9,... | collective-permute-start | bytes 104 | tf_op jit(solution)/shard_map/ppermute | solution.py:591
  19.6 2.1 collective-permute-done.4.far1
  25.7 17.9 %attend.1 = (bf16[1024,512]{1,0:T(8,128)(2,1)}, bf16[1024,512]{1,0:T(8,128)(2,1)}, bf16[1024,512]{1,0:T(8,128)(2,1)}, bf16[1024,512]{1,0:T(8,128)(2,1)}, f32[102...) custom-call(s32[4]{0:T(128)} %iota_xor_fusion.pos_ref, ...), custom_call_target="tpu_custom_call" | custom-call | flops 1 | bytes 1 | tf_op jit(solution)/shard_map/attend/pallas_call | solution.py:210
  50.1 29.2 %feed.1 = (bf16[1024,512]{1,0:T(8,128)(2,1)}, f32[1024,512]{1,0:T(8,128)}, bf16[1024,512]{1,0:T(8,128)(2,1)}, bf16[2304,512]{1,0:T(8,128)(2,1)}, bf16[2304,512]{1,0:T(8,128)(2,1)}, /*index=5*/f32[8,512]{1,0:T(8,128)}) custom-call(s32[4]{0:T(128)} %iota_xor_fusion.pos_ref, s32[2,16]{1,0:T(2,128)} %pad_add_fusion.place_ref, f32[1]{0:T(128)} %bitcast.8.factor_ref, ...), custom_call_target="tpu_custom_call" | custom-call | flops 1 | bytes 1 | tf_op jit(solution)/shard_map/feed/pallas_call | solution.py:442
  79.4 7.7 %mix_back.2 = (bf16[256,512]{1,0:T(8,128)(2,1)}, bf16[256,512]{1,0:T(8,128)(2,1)}, bf16[256,512]{1,0:T(8,128)(2,1)}, bf16[256,512]{1,0:T(8,128)(2,1)}, f32[2,256...) custom-call(bf16[1024,512]{1,0:T(8,128)(2,1)} %get-tuple-element.123.refs_0_, ...), custom_call_target="tpu_custom_call" | custom-call | flops 1 | bytes 1 | tf_op jit(solution)/shard_map/mix_back/pallas_call | solution.py:293
  89.8 17.0 %mix_back.3 = (bf16[768,512]{1,0:T(8,128)(2,1)}, bf16[768,512]{1,0:T(8,128)(2,1)}, bf16[768,512]{1,0:T(8,128)(2,1)}, bf16[768,512]{1,0:T(8,128)(2,1)}, f32[2,256...) custom-call(bf16[1024,512]{1,0:T(8,128)(2,1)} %get-tuple-element.123.refs_0_, ...), custom_call_target="tpu_custom_call" | custom-call | flops 1 | bytes 1 | tf_op jit(solution)/shard_map/mix_back/pallas_call | solution.py:293
  113.1 5.5 %input_back.1 = (f32[1024,512]{1,0:T(8,128)}, bf16[16,512]{1,0:T(8,128)(2,1)S(1)}) custom-call(bf16[1024,512]{1,0:T(8,128)(2,1)S(1)} %copy-done, f32[1024,512]{1,0:T(8,128)S(1)} %copy-done.8, bf16[4,512,512]{2,1,0:T(8,128)(2,1)S(1)} %copy-done.7, f32[8,512]{1,0:T(8,128)S(1)} %copy-done.16, f32[8,512]{1,0:T(8,128)S(1)} %copy-done.18, ...), custom_call_target="tpu_custom_call" | custom-call | flops 1 | bytes 1 | tf_op jit(solution)/shard_map/input_back/pallas_call | solution.py:560
  118.6 4.4 %weight_back.1 = (bf16[1040,512]{1,0:T(8,128)(2,1)S(1)}, bf16[1040,512]{1,0:T(8,128)(2,1)S(1)}) custom-call(s32[4]{0:T(128)S(1)} %copy-done.17, s32[2,16]{1,0:T(2,128)S(1)} %copy-done.19, bf16[16,512]{1,0:T(8,128)(2,1)S(1)} %get-tuple-element.139.small_ref, bf16[1024,512]{1,0:T(8,128)(2,1)S(1)} %copy-done.14, bf16[768,512]{1,0:T(8,128)(2,1)S(1)} %copy-done.1, ...), custom_call_target="tpu_custom_call" | custom-call | flops 1 | bytes 1 | tf_op jit(solution)/shard_map/weight_back/pallas_call | solution.py:502
  125.2 2.3 collective-permute-done.17
  130.3 6.8 %collective-permute-done.18 = bf16[528,512]{1,0:T(8,128)(2,1)S(1)} collective-permute-done((bf16[528,512]{1,0:T(8,128)(2,1)S(1)}, bf16[528,512]{1,0:T(8,128)(2,1)S(1)}, u32[]{:S(2)}, u32[]{:S(2)}) %collective-permute-start.18) | collective-permute-done | bytes 540704 | tf_op jit(solution)/shard_map/ppermute | solution.py:591
  138.9 2.6 %collective-permute-start.23 = (bf16[144,512]{1,0:T(8,128)(2,1)S(1)}, bf16[144,512]{1,0:T(8,128)(2,1)S(1)}, u32[]{:S(2)}, u32[]{:S(2)}) collective-permute-start(bf16[144,512]{1,0:T(8,128)(2,1)S(1)} %add_convert_fusion.6), channel_id=1, source_target_pairs={{0,16},{1,3},{2,18},{3,1},{4,20},{5,7},{6,22},{7,5},{8,24},{9,11},... | collective-permute-start | bytes 442376 | tf_op jit(solution)/shard_map/ppermute | solution.py:591
  141.5 2.3 collective-permute-done.19
  145.1 3.2 %collective-permute-done.23 = bf16[144,512]{1,0:T(8,128)(2,1)S(1)} collective-permute-done((bf16[144,512]{1,0:T(8,128)(2,1)S(1)}, bf16[144,512]{1,0:T(8,128)(2,1)S(1)}, u32[]{:S(2)}, u32[]{:S(2)}) %collective-permute-start.23) | collective-permute-done | bytes 147488 | tf_op jit(solution)/shard_map/ppermute | solution.py:591
  149.4 2.7 %collective-permute-start.24 = (bf16[144,512]{1,0:T(8,128)(2,1)S(1)}, bf16[144,512]{1,0:T(8,128)(2,1)S(1)}, u32[]{:S(2)}, u32[]{:S(2)}) collective-permute-start(bf16[144,512]{1,0:T(8,128)(2,1)S(1)} %add_convert_fusion.5), channel_id=1, source_target_pairs={{0,4},{1,17},{2,6},{3,19},{4,0},{5,21},{6,2},{7,23},{8,12},{9,25},... | collective-permute-start | bytes 442376 | tf_op jit(solution)/shard_map/ppermute | solution.py:591
  153.2 2.0 collective-permute-done.24
  155.2 3.1 %collective-permute-done.21 = bf16[80,512]{1,0:T(8,128)(2,1)S(1)} collective-permute-done((bf16[80,512]{1,0:T(8,128)(2,1)S(1)}, bf16[80,512]{1,0:T(8,128)(2,1)S(1)}, u32[]{:S(2)}, u32[]{:S(2)}) %collective-permute-start.21) | collective-permute-done | bytes 81952 | tf_op jit(solution)/shard_map/ppermute | solution.py:591
  159.3 3.4 %collective-permute-done.26 = bf16[64,512]{1,0:T(8,128)(2,1)S(1)} collective-permute-done((bf16[64,512]{1,0:T(8,128)(2,1)S(1)}, bf16[64,512]{1,0:T(8,128)(2,1)S(1)}, u32[]{:S(2)}, u32[]{:S(2)}) %collective-permute-start.26) | collective-permute-done | bytes 65568 | tf_op jit(solution)/shard_map/ppermute | solution.py:591
  163.3 8.8 %collective-permute-done.27 = bf16[128,512]{1,0:T(8,128)(2,1)S(1)} collective-permute-done((bf16[128,512]{1,0:T(8,128)(2,1)S(1)}, bf16[128,512]{1,0:T(8,128)(2,1)S(1)}, u32[]{:S(2)}, u32[]{:S(2)}) %collective-permute-start.27) | collective-permute-done | bytes 131104 | tf_op jit(solution)/shard_map/ppermute | solution.py:591
  172.6 1.9 collective-permute-start.29
  176.3 5.8 %collective-permute-done.28 = bf16[576,512]{1,0:T(8,128)(2,1)S(1)} collective-permute-done((bf16[576,512]{1,0:T(8,128)(2,1)S(1)}, bf16[576,512]{1,0:T(8,128)(2,1)S(1)}, u32[]{:S(2)}, u32[]{:S(2)}) %collective-permute-start.28) | collective-permute-done | bytes 589856 | tf_op jit(solution)/shard_map/ppermute | solution.py:591
  182.1 2.2 multiply_reduce_fusion
  191.5 2.0 collective-permute-done.31
  194.2 4.7 %renew_first.1 = bf16[528,512]{1,0:T(8,128)(2,1)} custom-call(s32[1]{0:T(128)} %bitcast.6.half_ref.side_ref, s32[8]{0:T(128)} %add_xor_fusion.index_ref, f32[1]{0:T(128)S(6)} %min.3.factor_ref, bf16[1152,512]{1,0:T(8,128)(2,1)} %get-tuple-element.180.early_ref, bf16[512,512]{1,0:T(8,128)(2,1)} %get-tuple-element.150.late_ref, ...), custom_call_target="tpu_custom_call" | custom-call | flops 1 | bytes 1 | tf_op jit(solution)/shard_map/renew_first/pallas_call | solution.py:704
  199.2 11.0 %update.1 = (f32[5,128,512]{2,1,0:T(8,128)}, f32[5,128,512]{2,1,0:T(8,128)}, f32[5,128,512]{2,1,0:T(8,128)}, f32[128,2048]{1,0:T(8,128)}, f32[128,2048]{1,0:T(8,...) custom-call(s32[8]{0:T(128)} %add_xor_fusion.index_ref, ...), custom_call_target="tpu_custom_call" | custom-call | flops 1 | bytes 1 | tf_op jit(solution)/shard_map/update/pallas_call | solution.py:780
  214.0 2.0 collective-permute-done.37
  216.0 2.0 collective-permute-start.33
  221.9 3.0 %unpack_near.1 = (bf16[5,512,512]{2,1,0:T(8,128)(2,1)}, bf16[512,2048]{1,0:T(8,128)(2,1)}, bf16[2048,512]{1,0:T(8,128)(2,1)}) custom-call(s32[4]{0:T(128)S(1)} %copy-done.17, s32[1]{0:T(128)} %bitcast.6.half_ref.side_ref, bf16[1024,512]{1,0:T(8,128)(2,1)S(1)} %copy-done.9, bf16[640,512]{1,0:T(8,128)(2,1)S(1)} %copy-done.15, ...), custom_call_target="tpu_custom_call" | custom-call | flops 1 | bytes 1 | tf_op jit(solution)/shard_map/unpack_near/pallas_call | solution.py:868
  224.8 5.2 %collective-permute-done.39.p2 = bf16[640,512]{1,0:T(8,128)(2,1)S(1)} collective-permute-done((bf16[640,512]{1,0:T(8,128)(2,1)}, bf16[640,512]{1,0:T(8,128)(2,1)S(1)}, u32[]{:S(2)}, u32[]{:S(2)}) %collective-permute-start.39) | collective-permute-done | bytes 655392 | tf_op jit(solution)/shard_map/ppermute | solution.py:591
  231.0 2.1 collective-permute-done.38.p1
  233.1 2.7 %unpack_far.1 = (bf16[5,512,512]{2,1,0:T(8,128)(2,1)}, bf16[512,2048]{1,0:T(8,128)(2,1)}, bf16[2048,512]{1,0:T(8,128)(2,1)}) custom-call(s32[4]{0:T(128)S(1)} %copy-done.17, s32[1]{0:T(128)} %bitcast.6.half_ref.side_ref, bf16[528,512]{1,0:T(8,128)(2,1)} %collective-permute-done.33.p0, ...), custom_call_target="tpu_custom_call", output_to_operand_aliasing={{0}: (6, {}), {1}: (7, {}), {2}: (8, {})} | custom-call | flops 1 | bytes 1 | tf_op jit(solution)/shard_map/unpack_far/pallas_call | solution.py:888
  (180 shorter events, 57.8 us)
Async XLA Ops:
  2.4 23.0 %collective-permute-start.7 = (bf16[544,512]{1,0:T(8,128)(2,1)S(1)}, bf16[544,512]{1,0:T(8,128)(2,1)}, u32[]{:S(2)}, u32[]{:S(2)}) collective-permute-start(bf16[544,512]{1,0:T(8,128)(2,1)S(1)} %fusion.5.near0), channel_id=1, source_target_pairs={{0,1},{1,0},{2,3},{3,2},{4,5},{5,4},{6,7},{7,6},{8,9},{9,8},{10,11... | collective-permute-start | bytes 1671176 | tf_op jit(solution)/shard_map/ppermute | solution.py:591
  3.0 10.4 %collective-permute-start.3 = (bf16[272,512]{1,0:T(8,128)(2,1)S(1)}, bf16[272,512]{1,0:T(8,128)(2,1)}, u32[]{:S(2)}, u32[]{:S(2)}) collective-permute-start(bf16[272,512]{1,0:T(8,128)(2,1)S(1)} %constant_dynamic-slice_fusion), channel_id=1, source_target_pairs={{0,2},{1,3},{2,0},{3,1},{4,6},{5,7},{6,4},{7,5},{8,10},{9,11},{10,... | collective-permute-start | bytes 835592 | tf_op jit(solution)/shard_map/ppermute | solution.py:591
  6.2 3.6 %collective-permute-start = (f32[8]{0:T(128)S(1)}, f32[8]{0:T(128)S(1)}, u32[]{:S(2)}, u32[]{:S(2)}) collective-permute-start(f32[8]{0:T(128)S(1)} %compare_convert_fusion), channel_id=1, source_target_pairs={{0,4},{1,5},{2,6},{3,7},{4,0},{5,1},{6,2},{7,3},{8,12},{9,13},{10,... | collective-permute-start | bytes 104 | tf_op jit(solution)/shard_map/ppermute | solution.py:591
  9.8 3.5 %collective-permute-start.1 = (f32[8]{0:T(128)S(1)}, f32[8]{0:T(128)S(1)}, u32[]{:S(2)}, u32[]{:S(2)}) collective-permute-start(f32[8]{0:T(128)S(1)} %fusion.19), channel_id=1, source_target_pairs={{0,8},{1,9},{2,10},{3,11},{4,12},{5,13},{6,14},{7,15},{8,0},{9,1},... | collective-permute-start | bytes 104 | tf_op jit(solution)/shard_map/ppermute | solution.py:591
  13.4 8.3 %collective-permute-start.4 = (bf16[272,512]{1,0:T(8,128)(2,1)}, bf16[272,512]{1,0:T(8,128)(2,1)}, u32[]{:S(2)}, u32[]{:S(2)}) collective-permute-start(bf16[272,512]{1,0:T(8,128)(2,1)} %collective-permute-done.3.far0), channel_id=1, source_target_pairs={{0,4},{1,5},{2,6},{3,7},{4,0},{5,1},{6,2},{7,3},{8,12},{9,13},{10,... | collective-permute-start | bytes 835592 | tf_op jit(solution)/shard_map/ppermute | solution.py:591
  15.1 4.5 %collective-permute-start.2 = (f32[8]{0:T(128)S(1)}, f32[8]{0:T(128)S(1)}, u32[]{:S(2)}, u32[]{:S(2)}) collective-permute-start(f32[8]{0:T(128)S(1)} %fusion.22), channel_id=1, source_target_pairs={{0,16},{1,17},{2,18},{3,19},{4,20},{5,21},{6,22},{7,23},{8,24},{9,... | collective-permute-start | bytes 104 | tf_op jit(solution)/shard_map/ppermute | solution.py:591
  17.8 25.8 %collective-permute-start.12 = (bf16[640,512]{1,0:T(8,128)(2,1)S(1)}, bf16[640,512]{1,0:T(8,128)(2,1)S(1)}, u32[]{:S(2)}, u32[]{:S(2)}) collective-permute-start(bf16[640,512]{1,0:T(8,128)(2,1)S(1)} %slice_dynamic-update-slice_fusion.p0), channel_id=1, source_target_pairs={{0,2},{1,3},{2,0},{3,1},{4,6},{5,7},{6,4},{7,5},{8,10},{9,11},{10,... | collective-permute-start | bytes 1966088 | tf_op jit(solution)/shard_map/ppermute | solution.py:591
  21.8 23.2 %collective-permute-start.6 = (bf16[528,512]{1,0:T(8,128)(2,1)S(1)}, bf16[528,512]{1,0:T(8,128)(2,1)}, u32[]{:S(2)}, u32[]{:S(2)}) collective-permute-start(bf16[528,512]{1,0:T(8,128)(2,1)S(1)} %fusion.6.t0), channel_id=1, source_target_pairs={{0,2},{1,3},{2,0},{3,1},{4,6},{5,7},{6,4},{7,5},{8,10},{9,11},{10,... | collective-permute-start | bytes 1622024 | tf_op jit(solution)/shard_map/ppermute | solution.py:591
  25.3 23.7 %collective-permute-start.11 = (bf16[640,512]{1,0:T(8,128)(2,1)S(1)}, bf16[640,512]{1,0:T(8,128)(2,1)S(1)}, u32[]{:S(2)}, u32[]{:S(2)}) collective-permute-start(bf16[640,512]{1,0:T(8,128)(2,1)S(1)} %slice_dynamic-update-slice_fusion.p0), channel_id=1, source_target_pairs={{0,1},{1,0},{2,3},{3,2},{4,5},{5,4},{6,7},{7,6},{8,9},{9,8},{10,11... | collective-permute-start | bytes 1966088 | tf_op jit(solution)/shard_map/ppermute | solution.py:591
  43.6 5.4 %collective-permute-start.13 = (bf16[640,512]{1,0:T(8,128)(2,1)S(1)}, bf16[640,512]{1,0:T(8,128)(2,1)S(1)}, u32[]{:S(2)}, u32[]{:S(2)}) collective-permute-start(bf16[640,512]{1,0:T(8,128)(2,1)S(1)} %collective-permute-done.12.p2), channel_id=1, source_target_pairs={{0,1},{1,0},{2,3},{3,2},{4,5},{5,4},{6,7},{7,6},{8,9},{9,8},{10,11... | collective-permute-start | bytes 1966088 | tf_op jit(solution)/shard_map/ppermute | solution.py:591
  79.3 7.9 %collective-permute-start.14 = (bf16[2304,512]{1,0:T(8,128)(2,1)}, bf16[2304,512]{1,0:T(8,128)(2,1)S(1)}, u32[]{:S(2)}, u32[]{:S(2)}) collective-permute-start(bf16[2304,512]{1,0:T(8,128)(2,1)} %get-tuple-element.109), channel_id=1, source_target_pairs={{0,1},{1,0},{2,3},{3,2},{4,5},{5,4},{6,7},{7,6},{8,9},{9,8},{10,11... | collective-permute-start | bytes 7077896 | tf_op jit(solution)/shard_map/ppermute | solution.py:591
  88.8 18.1 %collective-permute-start.15 = (bf16[1152,512]{1,0:T(8,128)(2,1)}, bf16[1152,512]{1,0:T(8,128)(2,1)}, u32[]{:S(2)}, u32[]{:S(2)}) collective-permute-start(bf16[1152,512]{1,0:T(8,128)(2,1)} %add_convert_fusion), channel_id=1, source_target_pairs={{0,2},{1,5},{2,0},{3,7},{4,6},{5,1},{6,4},{7,3},{8,10},{9,13},{10,... | collective-permute-start | bytes 3538952 | tf_op jit(solution)/shard_map/ppermute | solution.py:591
  108.5 14.5 %collective-permute-start.16 = (bf16[576,512]{1,0:T(8,128)(2,1)S(1)}, bf16[576,512]{1,0:T(8,128)(2,1)S(1)}, u32[]{:S(2)}, u32[]{:S(2)}) collective-permute-start(bf16[576,512]{1,0:T(8,128)(2,1)S(1)} %add_convert_fusion.1), channel_id=1, source_target_pairs={{0,4},{1,9},{2,6},{3,11},{4,0},{5,13},{6,2},{7,15},{8,12},{9,1},{1... | collective-permute-start | bytes 1769480 | tf_op jit(solution)/shard_map/ppermute | solution.py:591
  127.7 9.4 %collective-permute-start.18 = (bf16[528,512]{1,0:T(8,128)(2,1)S(1)}, bf16[528,512]{1,0:T(8,128)(2,1)S(1)}, u32[]{:S(2)}, u32[]{:S(2)}) collective-permute-start(bf16[528,512]{1,0:T(8,128)(2,1)S(1)} %pad_maximum_fusion.2), channel_id=1, source_target_pairs={{0,2},{1,5},{2,0},{3,7},{4,6},{5,1},{6,4},{7,3},{8,10},{9,13},{10,... | collective-permute-start | bytes 1622024 | tf_op jit(solution)/shard_map/ppermute | solution.py:591
  128.7 9.1 %collective-permute-start.22 = (bf16[288,512]{1,0:T(8,128)(2,1)S(1)}, bf16[288,512]{1,0:T(8,128)(2,1)S(1)}, u32[]{:S(2)}, u32[]{:S(2)}) collective-permute-start(bf16[288,512]{1,0:T(8,128)(2,1)S(1)} %add_convert_fusion.3), channel_id=1, source_target_pairs={{0,8},{1,17},{2,10},{3,19},{4,12},{5,21},{6,14},{7,23},{8,0},{9,25... | collective-permute-start | bytes 884744 | tf_op jit(solution)/shard_map/ppermute | solution.py:591
  137.2 6.6 %collective-permute-start.19 = (bf16[272,512]{1,0:T(8,128)(2,1)S(1)}, bf16[272,512]{1,0:T(8,128)(2,1)S(1)}, u32[]{:S(2)}, u32[]{:S(2)}) collective-permute-start(bf16[272,512]{1,0:T(8,128)(2,1)S(1)} %pad_maximum_fusion.5), channel_id=1, source_target_pairs={{0,4},{1,9},{2,6},{3,11},{4,0},{5,13},{6,2},{7,15},{8,12},{9,1},{1... | collective-permute-start | bytes 835592 | tf_op jit(solution)/shard_map/ppermute | solution.py:591
  138.9 9.4 %collective-permute-start.23 = (bf16[144,512]{1,0:T(8,128)(2,1)S(1)}, bf16[144,512]{1,0:T(8,128)(2,1)S(1)}, u32[]{:S(2)}, u32[]{:S(2)}) collective-permute-start(bf16[144,512]{1,0:T(8,128)(2,1)S(1)} %add_convert_fusion.6), channel_id=1, source_target_pairs={{0,16},{1,3},{2,18},{3,1},{4,20},{5,7},{6,22},{7,5},{8,24},{9,11},... | collective-permute-start | bytes 442376 | tf_op jit(solution)/shard_map/ppermute | solution.py:591
  144.0 8.1 %collective-permute-start.20 = (bf16[144,512]{1,0:T(8,128)(2,1)S(1)}, bf16[144,512]{1,0:T(8,128)(2,1)S(1)}, u32[]{:S(2)}, u32[]{:S(2)}) collective-permute-start(bf16[144,512]{1,0:T(8,128)(2,1)S(1)} %pad_maximum_fusion.7), channel_id=1, source_target_pairs={{0,8},{1,17},{2,10},{3,19},{4,12},{5,21},{6,14},{7,23},{8,0},{9,25... | collective-permute-start | bytes 442376 | tf_op jit(solution)/shard_map/ppermute | solution.py:591
  149.4 5.8 %collective-permute-start.24 = (bf16[144,512]{1,0:T(8,128)(2,1)S(1)}, bf16[144,512]{1,0:T(8,128)(2,1)S(1)}, u32[]{:S(2)}, u32[]{:S(2)}) collective-permute-start(bf16[144,512]{1,0:T(8,128)(2,1)S(1)} %add_convert_fusion.5), channel_id=1, source_target_pairs={{0,4},{1,17},{2,6},{3,19},{4,0},{5,21},{6,2},{7,23},{8,12},{9,25},... | collective-permute-start | bytes 442376 | tf_op jit(solution)/shard_map/ppermute | solution.py:591
  152.1 6.1 %collective-permute-start.21 = (bf16[80,512]{1,0:T(8,128)(2,1)S(1)}, bf16[80,512]{1,0:T(8,128)(2,1)S(1)}, u32[]{:S(2)}, u32[]{:S(2)}) collective-permute-start(bf16[80,512]{1,0:T(8,128)(2,1)S(1)} %pad_maximum_fusion.9), channel_id=1, source_target_pairs={{0,16},{1,3},{2,18},{3,1},{4,20},{5,7},{6,22},{7,5},{8,24},{9,11},... | collective-permute-start | bytes 245768 | tf_op jit(solution)/shard_map/ppermute | solution.py:591
  158.3 4.3 %collective-permute-start.26 = (bf16[64,512]{1,0:T(8,128)(2,1)S(1)}, bf16[64,512]{1,0:T(8,128)(2,1)S(1)}, u32[]{:S(2)}, u32[]{:S(2)}) collective-permute-start(bf16[64,512]{1,0:T(8,128)(2,1)S(1)} %add_convert_fusion.8), channel_id=1, source_target_pairs={{0,4},{1,17},{2,6},{3,19},{4,0},{5,21},{6,2},{7,23},{8,12},{9,25},... | collective-permute-start | bytes 196616 | tf_op jit(solution)/shard_map/ppermute | solution.py:591
  158.4 13.7 %collective-permute-start.25 = (bf16[288,512]{1,0:T(8,128)(2,1)S(1)}, bf16[288,512]{1,0:T(8,128)(2,1)S(1)}, u32[]{:S(2)}, u32[]{:S(2)}) collective-permute-start(bf16[288,512]{1,0:T(8,128)(2,1)S(1)} %pad_maximum_fusion.4), channel_id=1, source_target_pairs={{0,16},{1,9},{2,18},{3,11},{4,20},{5,13},{6,22},{7,15},{8,24},{9,1... | collective-permute-start | bytes 884744 | tf_op jit(solution)/shard_map/ppermute | solution.py:591
  162.6 9.5 %collective-permute-start.27 = (bf16[128,512]{1,0:T(8,128)(2,1)S(1)}, bf16[128,512]{1,0:T(8,128)(2,1)S(1)}, u32[]{:S(2)}, u32[]{:S(2)}) collective-permute-start(bf16[128,512]{1,0:T(8,128)(2,1)S(1)} %pad_maximum_fusion.8), channel_id=1, source_target_pairs={{0,16},{1,9},{2,18},{3,11},{4,20},{5,13},{6,22},{7,15},{8,24},{9,1... | collective-permute-start | bytes 393224 | tf_op jit(solution)/shard_map/ppermute | solution.py:591
  172.2 9.9 %collective-permute-start.28 = (bf16[576,512]{1,0:T(8,128)(2,1)S(1)}, bf16[576,512]{1,0:T(8,128)(2,1)S(1)}, u32[]{:S(2)}, u32[]{:S(2)}) collective-permute-start(bf16[576,512]{1,0:T(8,128)(2,1)S(1)} %pad_maximum_fusion.1), channel_id=1, source_target_pairs={{0,8},{1,5},{2,10},{3,7},{4,12},{5,1},{6,14},{7,3},{8,0},{9,13},{1... | collective-permute-start | bytes 1769480 | tf_op jit(solution)/shard_map/ppermute | solution.py:591
  172.6 13.0 %collective-permute-start.29 = (bf16[256,512]{1,0:T(8,128)(2,1)S(1)}, bf16[256,512]{1,0:T(8,128)(2,1)S(1)}, u32[]{:S(2)}, u32[]{:S(2)}) collective-permute-start(bf16[256,512]{1,0:T(8,128)(2,1)S(1)} %pad_maximum_fusion.6), channel_id=1, source_target_pairs={{0,8},{1,5},{2,10},{3,7},{4,12},{5,1},{6,14},{7,3},{8,0},{9,13},{1... | collective-permute-start | bytes 786440 | tf_op jit(solution)/shard_map/ppermute | solution.py:591
  189.8 3.7 %collective-permute-start.31 = (f32[1]{0:T(128)}, f32[1]{0:T(128)}, u32[]{:S(2)}, u32[]{:S(2)}) collective-permute-start(f32[1]{0:T(128)} %add.303), channel_id=1, source_target_pairs={{0,2},{1,3},{2,0},{3,1},{4,6},{5,7},{6,4},{7,5},{8,10},{9,11},{10,... | collective-permute-start | bytes 20 | tf_op jit(solution)/shard_map/ppermute | solution.py:591
  198.9 13.3 %collective-permute-start.32 = (bf16[528,512]{1,0:T(8,128)(2,1)}, bf16[528,512]{1,0:T(8,128)(2,1)S(1)}, u32[]{:S(2)}, u32[]{:S(2)}) collective-permute-start(bf16[528,512]{1,0:T(8,128)(2,1)} %renew_first.1), channel_id=1, source_target_pairs={{0,2},{1,3},{2,0},{3,1},{4,6},{5,7},{6,4},{7,5},{8,10},{9,11},{10,... | collective-permute-start | bytes 1622024 | tf_op jit(solution)/shard_map/ppermute | solution.py:591
  212.2 7.4 %collective-permute-start.34 = (bf16[1024,512]{1,0:T(8,128)(2,1)}, bf16[1024,512]{1,0:T(8,128)(2,1)S(1)}, u32[]{:S(2)}, u32[]{:S(2)}) collective-permute-start(bf16[1024,512]{1,0:T(8,128)(2,1)} %get-tuple-element.166.p0), channel_id=1, source_target_pairs={{0,1},{1,0},{2,3},{3,2},{4,5},{5,4},{6,7},{7,6},{8,9},{9,8},{10,11... | collective-permute-start | bytes 3145736 | tf_op jit(solution)/shard_map/ppermute | solution.py:591
  212.2 6.1 %collective-permute-start.36 = (bf16[528,512]{1,0:T(8,128)(2,1)S(1)}, bf16[528,512]{1,0:T(8,128)(2,1)S(1)}, u32[]{:S(2)}, u32[]{:S(2)}) collective-permute-start(bf16[528,512]{1,0:T(8,128)(2,1)S(1)} %collective-permute-done.32.p4), channel_id=1, source_target_pairs={{0,1},{1,0},{2,3},{3,2},{4,5},{5,4},{6,7},{7,6},{8,9},{9,8},{10,11... | collective-permute-start | bytes 1622024 | tf_op jit(solution)/shard_map/ppermute | solution.py:591
  212.7 6.9 %collective-permute-start.35 = (bf16[640,512]{1,0:T(8,128)(2,1)}, bf16[640,512]{1,0:T(8,128)(2,1)S(1)}, u32[]{:S(2)}, u32[]{:S(2)}) collective-permute-start(bf16[640,512]{1,0:T(8,128)(2,1)} %get-tuple-element.167.p1), channel_id=1, source_target_pairs={{0,1},{1,0},{2,3},{3,2},{4,5},{5,4},{6,7},{7,6},{8,9},{9,8},{10,11... | collective-permute-start | bytes 1966088 | tf_op jit(solution)/shard_map/ppermute | solution.py:591
  212.7 17.4 %collective-permute-start.39 = (bf16[640,512]{1,0:T(8,128)(2,1)}, bf16[640,512]{1,0:T(8,128)(2,1)S(1)}, u32[]{:S(2)}, u32[]{:S(2)}) collective-permute-start(bf16[640,512]{1,0:T(8,128)(2,1)} %get-tuple-element.167.p1), channel_id=1, source_target_pairs={{0,2},{1,3},{2,0},{3,1},{4,6},{5,7},{6,4},{7,5},{8,10},{9,11},{10,... | collective-permute-start | bytes 1966088 | tf_op jit(solution)/shard_map/ppermute | solution.py:591
  216.0 14.9 %collective-permute-start.33 = (bf16[528,512]{1,0:T(8,128)(2,1)S(1)}, bf16[528,512]{1,0:T(8,128)(2,1)}, u32[]{:S(2)}, u32[]{:S(2)}) collective-permute-start(bf16[528,512]{1,0:T(8,128)(2,1)S(1)} %collective-permute-done.32.p4), channel_id=1, source_target_pairs={{0,4},{1,5},{2,6},{3,7},{4,0},{5,1},{6,2},{7,3},{8,12},{9,13},{10,... | collective-permute-start | bytes 1622024 | tf_op jit(solution)/shard_map/ppermute | solution.py:591
  (41 other events, 278.0 us)

commit v4 on v3

--- a/solution.py
+++ b/solution.py
@@ -8,8 +8,13 @@
 
 BF = jnp.bfloat16
 F32 = jnp.float32
-VMEM_LIMIT = 56 * 1024 * 1024
-VMEM_SMALL = 24 * 1024 * 1024
+MIB = 1024 * 1024
+VMEM_ATTEND = 40 * MIB
+VMEM_MIX = 44 * MIB
+VMEM_FEED = 44 * MIB
+VMEM_BACK = 24 * MIB
+VMEM_UPDATE = 56 * MIB
+VMEM_UNPACK = 24 * MIB
 CHUNK = 256
 SLOT = 64
 GROUP = 256
@@ -217,7 +222,7 @@
         + full,
         scratch_shapes=[pltpu.VMEM((groups, GROUP, GROUP), F32)] * 2 + [pltpu.VMEM((8, width), F32)],
         compiler_params=pltpu.CompilerParams(
-            dimension_semantics=("arbitrary",), vmem_limit_bytes=VMEM_LIMIT
+            dimension_semantics=("arbitrary",), vmem_limit_bytes=VMEM_ATTEND
         ),
         name="attend",
         cost_estimate=CHEAP,
@@ -297,7 +302,7 @@
         out_specs=[out] * 4 + [whole(a) for a in sums],
         out_shape=[rows] * 4 + sums,
         compiler_params=pltpu.CompilerParams(
-            dimension_semantics=("arbitrary",), vmem_limit_bytes=VMEM_LIMIT
+            dimension_semantics=("arbitrary",), vmem_limit_bytes=VMEM_MIX
         ),
         name="mix_back",
         cost_estimate=CHEAP,
@@ -323,9 +328,9 @@
 
 
 def feed_kernel(
-    pos_ref, place_ref, factor_ref, x_ref, g_ref, o_ref, norm_ref, p0, p1, p2, p3, t0, t1, t2, t3,
+    pos_ref, place_ref, domain_ref, x_ref, g_ref, o_ref, norm_ref, p0, p1, p2, p3, t0, t1, t2, t3,
     y_ref, dh_ref, do_ref, send_ref, keep_ref, dnorm_ref,
-    wo, w1, w2, branch, unit_ref, inv_ref, n2, gb, n2_t, gb_t, dn2, grads, u_all, da_all
+    wo, w1, w2, branch, unit_ref, inv_ref, n2, gb, n2_t, gb_t, dn2, grads, u_all, da_all, factor_ref
 ):
     step = pl.program_id(0)
     last = pl.num_programs(0) - 1
@@ -343,6 +348,9 @@
             for j in range(4):
                 w1[j, rows, :] = piece[(j + 1) * part : (j + 2) * part, :]
             w2[pos] = tall[0:block, :]
+        count = sum(t[block : block + SMALL, 0:LANES].astype(F32) for t in (t0, t1, t2, t3))
+        share = domain_ref[0:1, :] * domain_ref[1:2, :] / jnp.maximum(count[0:1, :], 1.0)
+        factor_ref[...] = jnp.broadcast_to(jnp.sum(share, axis=1, keepdims=True), factor_ref.shape)
 
         def before(i, _):
             rows = pl.ds(pl.multiple_of(i * 256, 256), 256)
@@ -354,7 +362,7 @@
             normed = (unit * norm_ref[2:3, :] + norm_ref[3:4, :]).astype(BF)
             n2[rows, :] = normed
             n2_t[:, rows] = normed.T
-            grad = (g_ref[rows, :].astype(F32) * factor_ref[0]).astype(BF)
+            grad = (g_ref[rows, :].astype(F32) * factor_ref[0:1, 0:1]).astype(BF)
             gb[rows, :] = grad
             gb_t[:, rows] = grad.T
             dn2[rows, :] = jnp.zeros((256, width), F32)
@@ -406,7 +414,7 @@
             y_ref[rows, :] = branch[rows, :].astype(BF)
             grad = dn2[rows, :]
             unit = unit_ref[rows, :]
-            dh = g_ref[rows, :].astype(F32) * factor_ref[0] + normalise_back(
+            dh = g_ref[rows, :].astype(F32) * factor_ref[0:1, 0:1] + normalise_back(
                 grad, unit, inv_ref[rows, 0:1], gain
             )
             dh_ref[rows, :] = dh
@@ -427,7 +435,7 @@
         scatter_shards(pos_ref, place_ref, grads, send_ref, keep_ref, 0)
 
 
-def feed(pos, place, factor, x, g, o, norm, pieces, talls):
+def feed(pos, place, domain_rows, x, g, o, norm, pieces, talls):
     length, width = x.shape
     block = width
     height = 5 * (width // 4) + block
@@ -438,11 +446,11 @@
         jax.ShapeDtypeStruct((2 * height, width), BF),
         jax.ShapeDtypeStruct((8, width), F32),
     ]
-    args = (x, g, o, norm) + tuple(pieces) + tuple(talls)
+    args = (domain_rows, x, g, o, norm) + tuple(pieces) + tuple(talls)
     return pl.pallas_call(
         feed_kernel,
         grid=(4,),
-        in_specs=[pl.BlockSpec(memory_space=pltpu.SMEM)] * 3 + [whole(a) for a in args],
+        in_specs=[pl.BlockSpec(memory_space=pltpu.SMEM)] * 2 + [whole(a) for a in args],
         out_specs=[whole(a) for a in out],
         out_shape=out,
         scratch_shapes=[
@@ -460,13 +468,14 @@
             pltpu.VMEM((width, block), BF),
             pltpu.VMEM((length, block), BF),
             pltpu.VMEM((length, block), BF),
+            pltpu.VMEM((8, LANES), F32),
         ],
         compiler_params=pltpu.CompilerParams(
-            dimension_semantics=("arbitrary",), vmem_limit_bytes=VMEM_LIMIT
+            dimension_semantics=("arbitrary",), vmem_limit_bytes=VMEM_FEED
         ),
         name="feed",
         cost_estimate=CHEAP,
-    )(pos, place, factor, *args)
+    )(pos, place, *args)
 
 
 def weight_back_kernel(pos_ref, place_ref, small_ref, n_ref, *refs):
@@ -507,7 +516,7 @@
         out_shape=[out] * 2,
         scratch_shapes=[pltpu.VMEM((width, length), BF), pltpu.VMEM((width, width), BF)],
         compiler_params=pltpu.CompilerParams(
-            dimension_semantics=("arbitrary",), vmem_limit_bytes=VMEM_SMALL
+            dimension_semantics=("arbitrary",), vmem_limit_bytes=VMEM_BACK
         ),
         name="weight_back",
         cost_estimate=CHEAP,
@@ -565,7 +574,7 @@
         out_shape=[jax.ShapeDtypeStruct((length, width), F32), small],
         scratch_shapes=[pltpu.VMEM((8, width), F32), pltpu.VMEM((tile, width), F32)],
         compiler_params=pltpu.CompilerParams(
-            dimension_semantics=("arbitrary",), vmem_limit_bytes=VMEM_SMALL
+            dimension_semantics=("arbitrary",), vmem_limit_bytes=VMEM_BACK
         ),
         name="input_back",
         cost_estimate=CHEAP,
@@ -659,23 +668,50 @@
 def gather_rows(index_ref, sources, targets):
     count = index_ref.shape[0]
     rows = LANES // count
-    for source, target in zip(sources, targets):
+    for parts, target in zip(sources, targets):
         units = target.shape[0] // LANES
         for j in range(count):
+            source = parts[2 * j // count]
             for u in range(units):
                 place = pl.ds(pl.multiple_of(u * LANES + index_ref[j] * rows, rows), rows)
-                first = (j * units + u) * rows
+                first = (j % (count // 2) * units + u) * rows
                 target[place, :] = source[first : first + rows, :]
 
 
+def squares_kernel(e0, e1, l0, l1, gn_ref, out_ref):
+    total = jnp.sum(jnp.square(gn_ref[...]))
+    for ref in (e0, e1, l0, l1):
+        values = ref[...].astype(F32)
+        total += jnp.sum(values * values)
+    out_ref[...] = jnp.full(out_ref.shape, total, F32)
+
+
+def squares(early, late, gn):
+    vmem = pl.BlockSpec(memory_space=pltpu.VMEM)
+    return pl.pallas_call(
+        squares_kernel,
+        in_specs=[vmem] * 5,
+        out_specs=vmem,
+        out_shape=jax.ShapeDtypeStruct((8, LANES), F32),
+        compiler_params=pltpu.CompilerParams(vmem_limit_bytes=VMEM_UNPACK),
+        name="squares",
+        cost_estimate=CHEAP,
+    )(*early, *late, gn)
+
+
+def clip_factor(square_ref, other_ref):
+    norm = jnp.sqrt(square_ref[0:1, 0:1] + other_ref[0:1, 0:1])
+    return jnp.minimum(1.0, 1.0 / (norm + 1e-06))
+
+
 def renew_first_kernel(
-    side_ref, index_ref, factor_ref, early_ref, late_ref, gn_ref, nm, nf, ns,
+    side_ref, index_ref, square_ref, other_ref, e0, e1, l0, l1, gn_ref, nm, nf, ns,
     am, af, as_, um, uf, us, copy_ref, early, late
 ):
-    factor = factor_ref[0]
+    factor = clip_factor(square_ref, other_ref)
     width = early.shape[1]
     height = am.shape[1]
-    gather_rows(index_ref, (early_ref, late_ref), (early, late))
+    gather_rows(index_ref, ((e0, e1), (l0, l1)), (early, late))
 
     def span(unit):
         return pl.ds(pl.multiple_of(unit * LANES + side_ref[0] * height, height), height)
@@ -696,7 +732,7 @@
     copy_ref[last : last + 4, 0:LANES] = new[0].astype(BF)
 
 
-def renew_first(side, index, factor, early, late, gn, attn, up, norm):
+def renew_first(side, index, square, early, late, gn, attn, up, norm):
     five, part, width = attn[0].shape
     hidden = up[0].shape[1]
     smem = pl.BlockSpec(memory_space=pltpu.SMEM)
@@ -706,28 +742,30 @@
         grid_spec=pltpu.PrefetchScalarGridSpec(
             num_scalar_prefetch=1,
             grid=(1,),
-            in_specs=[smem, smem, whole(early), whole(late), whole(gn)]
-            + [whole(a) for a in norm]
+            in_specs=[smem] + [whole(a) for a in (*square, *early, *late, gn, *norm)]
             + [pl.BlockSpec((five, part // 2, width), lambda i, side: (0, side[0], 0))] * 3
             + [pl.BlockSpec((part // 2, hidden), lambda i, side: (side[0], 0))] * 3,
             out_specs=whole(copy),
-            scratch_shapes=[pltpu.VMEM(early.shape, BF), pltpu.VMEM(late.shape, BF)],
+            scratch_shapes=[
+                pltpu.VMEM((2 * early[0].shape[0], width), BF),
+                pltpu.VMEM((2 * late[0].shape[0], width), BF),
+            ],
         ),
         out_shape=copy,
         compiler_params=pltpu.CompilerParams(
-            dimension_semantics=("arbitrary",), vmem_limit_bytes=VMEM_LIMIT
+            dimension_semantics=("arbitrary",), vmem_limit_bytes=VMEM_UPDATE
         ),
         name="renew_first",
         cost_estimate=CHEAP,
-    )(side, index, factor, early, late, gn, *norm, *attn, *up)
-
-
-def update_kernel(index_ref, factor_ref, early_ref, late_ref, gn_ref, *refs):
+    )(side, index, *square, *early, *late, gn, *norm, *attn, *up)
+
+
+def update_kernel(index_ref, square_ref, other_ref, e0, e1, l0, l1, gn_ref, *refs):
     am, af, as_, um, uf, us, dm, df, ds, nm, nf, ns = refs[:12]
     early, late = refs[-2:]
     outs, copy_low, copy_high = refs[12:-4], refs[-4], refs[-3]
     step = pl.program_id(0)
-    factor = factor_ref[0]
+    factor = clip_factor(square_ref, other_ref)
     width = early.shape[1]
     part = late.shape[0] // 4
     blocks = um.shape[1] // width
@@ -742,7 +780,7 @@
 
     @pl.when(step == 0)
     def _():
-        gather_rows(index_ref, (early_ref, late_ref), (early, late))
+        gather_rows(index_ref, ((e0, e1), (l0, l1)), (early, late))
         new = adam(nm[...], nf[...], ns[...], gn_ref[...] * factor, 0.3, 0.0)
         outs[9][...], outs[10][...], outs[11][...] = new
 
@@ -764,7 +802,7 @@
     keep(2, (slice(None), slice(None)), 5 + blocks, tall, new)
 
 
-def update(index, factor, early, late, gn, attn, up, down, norm):
+def update(index, square, early, late, gn, attn, up, down, norm):
     steps = 4
     smem = pl.BlockSpec(memory_space=pltpu.SMEM)
     five, part, width = attn[0].shape
@@ -776,20 +814,21 @@
     )
     arrays = tuple(attn) + tuple(up) + tuple(down) + tuple(norm)
     low = jax.ShapeDtypeStruct((8 * part, width), BF)
-    high = jax.ShapeDtypeStruct((early.shape[0] + late.shape[0] - 8 * part, width), BF)
+    tall, short = 2 * early[0].shape[0], 2 * late[0].shape[0]
+    high = jax.ShapeDtypeStruct((tall + short - 8 * part, width), BF)
     return pl.pallas_call(
         update_kernel,
         grid=(steps,),
-        in_specs=[smem, smem, whole(early), whole(late), whole(gn)] + specs,
+        in_specs=[smem] + [whole(a) for a in (*square, *early, *late, gn)] + specs,
         out_specs=specs + [whole(low), whole(high)],
         out_shape=[jax.ShapeDtypeStruct(a.shape, F32) for a in arrays] + [low, high],
-        scratch_shapes=[pltpu.VMEM(early.shape, BF), pltpu.VMEM(late.shape, BF)],
+        scratch_shapes=[pltpu.VMEM((tall, width), BF), pltpu.VMEM((short, width), BF)],
         compiler_params=pltpu.CompilerParams(
-            dimension_semantics=("arbitrary",), vmem_limit_bytes=VMEM_LIMIT
+            dimension_semantics=("arbitrary",), vmem_limit_bytes=VMEM_UPDATE
         ),
         name="update",
         cost_estimate=CHEAP,
-    )(index, factor, early, late, gn, *arrays)
+    )(index, *square, *early, *late, gn, *arrays)
 
 
 def place_unit(pos, source, unit, first, count, attn_ref, up_ref, down_ref, sem):
@@ -864,7 +903,7 @@
         jax.ShapeDtypeStruct((width, hidden), BF),
         jax.ShapeDtypeStruct((hidden, width), BF),
     ]
-    params = pltpu.CompilerParams(vmem_limit_bytes=VMEM_SMALL)
+    params = pltpu.CompilerParams(vmem_limit_bytes=VMEM_UNPACK)
     begun = pl.pallas_call(
         unpack_near_kernel,
         in_specs=[smem, smem] + [vmem] * 6,
@@ -925,6 +964,7 @@
     far_a = swap(ours, "shard", 2)
 
     domains = domain_weight.shape[0]
+    devices = lax.axis_size("dp") * lax.axis_size("shard") * domain_ids.shape[0]
     onehot = (domain_ids[:, None] == jnp.arange(domains, dtype=jnp.int32)[None, :]).astype(F32)
     counts = jnp.sum(onehot, axis=0)
     dp_bits = bits_of(lax.axis_size("dp"))
@@ -941,18 +981,21 @@
     counts_row = jnp.pad(counts.astype(BF)[None], ((0, SMALL - 1), (0, width - domains)))
     third = jnp.concatenate([down_master.astype(BF), counts_row])
     third_far = swap(third, "shard", 2)
-    far = [far_a, far_b, swap(far_a, "shard", 1), swap(far_b, "shard", 1)]
+    second = [second, swap(second, "shard", 1), second_far]
+    third = [third, swap(third, "shard", 1), third_far]
+    domain_rows = jnp.pad(
+        jnp.stack([onehot[0], domain_weight * devices / domains]),
+        ((0, 6), (0, LANES - domains)),
+    )
+    far_c = swap(far_a, "shard", 1)
+    far = [far_a, far_b, far_c, swap(far_b, "shard", 1)]
     q, k, v, n, e, eb, z, o, weights, scores, keys, values, w, norm = attend(
-        pos, half, after(tokens, third), [own, near] + far
+        pos, half, tokens, [own, near] + far
     )
-    second = [second, swap(second, "shard", 1), second_far, swap(after(second_far, o), "shard", 1)]
-    third = [third, swap(third, "shard", 1), third_far, swap(after(third_far, o), "shard", 1)]
-    total_seqs = lax.axis_size("dp") * lax.axis_size("shard") * domain_ids.shape[0]
-    counts = sum(piece[piece.shape[0] - SMALL, :domains].astype(F32) for piece in third)
-    per_domain = domain_weight * total_seqs / (domains * jnp.maximum(counts, 1.0))
-    seq_weight = jnp.sum(onehot * per_domain[None, :], axis=1)
+    for pieces in (second, third):
+        pieces.append(swap(after(pieces[2], o), "shard", 1))
     y, dh, do, send, keep, dnorm = feed(
-        pos, place, seq_weight, tokens, out_grad, o, norm, second, third
+        pos, place, domain_rows, tokens, out_grad, o, norm, second, third
     )
 
     steps, plan = phases(), gather_plan()
@@ -1013,24 +1056,23 @@
     late = jnp.concatenate([late, exchange(late, *plan[1])])
     early = jnp.concatenate([early, after(got, late)])
     got = exchange(early, *plan[2])
-    late_got = exchange(late, *plan[2])
-    early = jnp.concatenate([early, after(got, late)])
-    square = jnp.sum(jnp.square(norm_grad)) + jnp.sum(jnp.square(early.astype(F32)))
-    late = jnp.concatenate([late, after(late_got, square)])
-    square = (square + jnp.sum(jnp.square(late.astype(F32))))[None]
-    for b in (1, 2):
-        square = square + swap(square, "shard", b)
+    late = (late, exchange(late, *plan[2]))
+    early = (early, got)
+    square = squares(early, late, norm_grad)
+    square = square + swap(square, "shard", 1)
+    square = (square, swap(square, "shard", 2))
     index = gather_index()
-    clip_norm = jnp.sqrt(square)
-    factor = jnp.minimum(1.0, 1.0 / (clip_norm + 1e-06))
+    clip_norm = jnp.sqrt(square[0][0, 0] + square[1][0, 0])
     attn = (attn_master, attn_first, attn_second)
     up = (up_master, up_first, up_second)
     down = (down_master, down_first, down_second)
     norms = (norm_master, norm_first, norm_second)
-    leaving = renew_first(half, index, factor, early, late, norm_grad, attn, up, norms)
-    *new, low, high = update(index, factor, early, after(late, leaving), norm_grad, attn, up, down, norms)
+    leaving = renew_first(half, index, square, early, late, norm_grad, attn, up, norms)
+    *new, low, high = update(
+        index, square, early, after(late, leaving), norm_grad, attn, up, down, norms
+    )
     copies = share_copies(pos, half, low, high, leaving, width, hidden)
-    return (y, dx) + tuple(new) + (clip_norm[0],) + tuple(copies)
+    return (y, dx) + tuple(new) + (clip_norm,) + tuple(copies)
 
 
 def solution(mesh):

time: 238 us -> 224 us (0.941)
  other arithmetic: 18.5 us -> 11.1 us
  Pallas kernels: 103 us -> 96.6 us
  waiting for transfers between devices: 62.7 us -> 65.7 us
    reduce_sum x4 -> x0, other arithmetic: 6.28 us -> none  [the longest x1 2.15 us: shards(): jnp.sum(jnp.square(early.astype(F32)))]
    pallas_call x1, Pallas kernels: 29.2 us -> 26 us  [feed(): pl.pallas_call(feed_kernel, grid=(4,), in_specs=[pl.BlockSpec(memory_spac...]
    ppermute x41, waiting for transfers between devices: 62.7 us -> 65.7 us  [exchange(): return lax.ppermute(values, ('dp', 'shard'), perm)]
    unnamed x68 -> x50, local copies, waits for them, and re-layouts: 6.91 us -> 4.33 us
    pallas_call x2, Pallas kernels: 24.7 us -> 22.2 us  [mix_back(): pl.pallas_call(functools.partial(mix_back_kernel, begun=bool(before)), gr...]
    pallas_call x1 -> x2, Pallas kernels: 11 us -> 11.6 us  [the longest x1 11 us: update(): pl.pallas_call(update_kernel, grid=(steps,), in_specs=[smem] + [whole(a)...]
  transfers between devices with their start and end apart: 41 -> 41, of which waited for: 25 -> 24; matrix products, arithmetic and copies ran while one was open for 5% -> 4% of each run, Pallas kernels for 28% -> 28%
where the time goes in v4:
time: 224 us; the launch traced here: 223 us
  Pallas kernels  96.6 us (43%)
  waiting for transfers between devices  65.7 us (29%)
  starting transfers between devices  37.9 us (17%)
  other arithmetic  11.1 us (5%)
  local copies, waits for them, and re-layouts  7.56 us (3%)
  between operations  4.44 us (2%)
    ppermute x41, waiting for transfers between devices, exchange(): return lax.ppermute(values, ('dp', 'shard'), perm)  65.7 us
    ppermute x41, starting transfers between devices, exchange(): return lax.ppermute(values, ('dp', 'shard'), perm)  37.9 us
    pallas_call x1, Pallas kernels, feed(): pl.pallas_call(feed_kernel, grid=(4,), in_specs=[pl.BlockSpec(memory_spac...  26 us
    pallas_call x2, Pallas kernels, mix_back(): pl.pallas_call(functools.partial(mix_back_kernel, begun=bool(before)), gr...  22.2 us
    pallas_call x1, Pallas kernels, attend(): pl.pallas_call(attend_kernel, grid=(steps,), in_specs=[pl.BlockSpec(memor...  16.9 us
    pallas_call x1, Pallas kernels, update(): pl.pallas_call(update_kernel, grid=(steps,), in_specs=[smem] + [whole(a)...  11 us
    convert_element_type x14, other arithmetic, add_up(): return total.astype(BF)  7.03 us
    pallas_call x1, Pallas kernels, input_back(): pl.pallas_call(input_back_kernel, grid=(length // tile,), in_specs=[block...  5.45 us
  transfers between devices with their start and end apart: 41, of which 24 were waited for; matrix products, arithmetic and copies ran while one was open for 4% of the time, Pallas kernels for 28%

profile of v4, /device:TPU:0, one launch (start us, length us, event | category | flops | bytes accessed | tf_op | source)
XLA Modules:
  0.0 223.3 jit_solution(1718510251652006399)
XLA Ops:
  3.0 2.6 %collective-permute-start.1 = (bf16[272,512]{1,0:T(8,128)(2,1)S(1)}, bf16[272,512]{1,0:T(8,128)(2,1)}, u32[]{:S(2)}, u32[]{:S(2)}) collective-permute-start(bf16[272,512]{1,0:T(8,128)(2,1)S(1)} %constant_dynamic-slice_fusion), channel_id=1, source_target_pairs={{0,2},{1,3},{2,0},{3,1},{4,6},{5,7},{6,4},{7,5},{8,10},{9,11},{10,... | collective-permute-start | bytes 835592 | tf_op jit(solution)/shard_map/ppermute | solution.py:600
  7.9 1.9 collective-permute-done.2
  11.4 2.0 collective-permute-done.3
  15.1 2.7 %collective-permute-start.10 = (f32[8]{0:T(128)S(1)}, f32[8]{0:T(128)S(1)}, u32[]{:S(2)}, u32[]{:S(2)}) collective-permute-start(f32[8]{0:T(128)S(1)} %fusion.13), channel_id=1, source_target_pairs={{0,16},{1,17},{2,18},{3,19},{4,20},{5,21},{6,22},{7,23},{8,24},{9,... | collective-permute-start | bytes 104 | tf_op jit(solution)/shard_map/ppermute | solution.py:600
  19.6 2.1 collective-permute-done.4.far1
  25.7 16.9 %attend.1 = (bf16[1024,512]{1,0:T(8,128)(2,1)S(1)}, bf16[1024,512]{1,0:T(8,128)(2,1)S(1)}, bf16[1024,512]{1,0:T(8,128)(2,1)S(1)}, bf16[1024,512]{1,0:T(8,128)(2,...) custom-call(s32[4]{0:T(128)S(1)} %iota_xor_fusion.pos_ref, ...), custom_call_target="tpu_custom_call" | custom-call | flops 1 | bytes 1 | tf_op jit(solution)/shard_map/attend/pallas_call | solution.py:215
  45.0 2.4 %collective-permute-done.11.t1 = bf16[528,512]{1,0:T(8,128)(2,1)S(1)} collective-permute-done((bf16[528,512]{1,0:T(8,128)(2,1)S(1)}, bf16[528,512]{1,0:T(8,128)(2,1)S(1)}, u32[]{:S(2)}, u32[]{:S(2)}) %collective-permute-start.11) | collective-permute-done | bytes 540704 | tf_op jit(solution)/shard_map/ppermute | solution.py:600
  47.9 26.0 %feed.1 = (bf16[1024,512]{1,0:T(8,128)(2,1)}, f32[1024,512]{1,0:T(8,128)}, bf16[1024,512]{1,0:T(8,128)(2,1)S(1)}, bf16[2304,512]{1,0:T(8,128)(2,1)}, bf16[2304,512]{1,0:T(8,128)(2,1)}, /*index=5*/f32[8,512]{1,0:T(8,128)S(1)}) custom-call(s32[4]{0:T(128)S(1)} %iota_xor_fusion.pos_ref, s32[2,16]{1,0:T(2,128)S(1)} %pad_add_fusion.place_ref, ...), custom_call_target="tpu_custom_call" | custom-call | flops 1 | bytes 1 | tf_op jit(solution)/shard_map/feed/pallas_call | solution.py:450
  74.0 6.0 %mix_back.2 = (bf16[256,512]{1,0:T(8,128)(2,1)S(1)}, bf16[256,512]{1,0:T(8,128)(2,1)S(1)}, bf16[256,512]{1,0:T(8,128)(2,1)S(1)}, bf16[256,512]{1,0:T(8,128)(2,1)...) custom-call(bf16[1024,512]{1,0:T(8,128)(2,1)S(1)} %get-tuple-element.120.refs_0_, ...), custom_call_target="tpu_custom_call" | custom-call | flops 1 | bytes 1 | tf_op jit(solution)/shard_map/mix_back/pallas_call | solution.py:298
  82.4 16.2 %mix_back.3 = (bf16[768,512]{1,0:T(8,128)(2,1)S(1)}, bf16[768,512]{1,0:T(8,128)(2,1)S(1)}, bf16[768,512]{1,0:T(8,128)(2,1)S(1)}, bf16[768,512]{1,0:T(8,128)(2,1)...) custom-call(bf16[1024,512]{1,0:T(8,128)(2,1)S(1)} %get-tuple-element.120.refs_0_, ...), custom_call_target="tpu_custom_call" | custom-call | flops 1 | bytes 1 | tf_op jit(solution)/shard_map/mix_back/pallas_call | solution.py:298
  101.7 5.5 %input_back.1 = (f32[1024,512]{1,0:T(8,128)}, bf16[16,512]{1,0:T(8,128)(2,1)S(1)}) custom-call(bf16[1024,512]{1,0:T(8,128)(2,1)S(1)} %copy-done.1, f32[1024,512]{1,0:T(8,128)S(1)} %copy-done.10, bf16[4,512,512]{2,1,0:T(8,128)(2,1)S(1)} %copy-done.9, f32[8,512]{1,0:T(8,128)S(1)} %get-tuple-element.98.norm_ref, f32[8,512]{1,0:T(8,128)S(1)} %get-tuple-element.128.dnorm_ref, ...), custom_call_target="tpu_custom_call" | custom-call | flops 1 | bytes 1 | tf_op jit(solution)/shard_map/input_back/pallas_call | solution.py:569
  107.1 4.2 %weight_back.1 = (bf16[1040,512]{1,0:T(8,128)(2,1)S(1)}, bf16[1040,512]{1,0:T(8,128)(2,1)S(1)}) custom-call(s32[4]{0:T(128)S(1)} %iota_xor_fusion.pos_ref, s32[2,16]{1,0:T(2,128)S(1)} %pad_add_fusion.place_ref, bf16[16,512]{1,0:T(8,128)(2,1)S(1)} %get-tuple-element.136.small_ref, bf16[1024,512]{1,0:T(8,128)(2,1)S(1)} %get-tuple-element.137.n_ref, ...), custom_call_target="tpu_custom_call" | custom-call | flops 1 | bytes 1 | tf_op jit(solution)/shard_map/weight_back/pallas_call | solution.py:511
  113.4 2.3 %collective-permute-done.18 = bf16[1040,512]{1,0:T(8,128)(2,1)S(1)} collective-permute-done((bf16[1040,512]{1,0:T(8,128)(2,1)S(1)}, bf16[1040,512]{1,0:T(8,128)(2,1)S(1)}, u32[]{:S(2)}, u32[]{:S(2)}) %collective-permute-start.18) | collective-permute-done | bytes 1064992 | tf_op jit(solution)/shard_map/ppermute | solution.py:600
  118.6 6.8 %collective-permute-done.19 = bf16[528,512]{1,0:T(8,128)(2,1)S(1)} collective-permute-done((bf16[528,512]{1,0:T(8,128)(2,1)S(1)}, bf16[528,512]{1,0:T(8,128)(2,1)S(1)}, u32[]{:S(2)}, u32[]{:S(2)}) %collective-permute-start.19) | collective-permute-done | bytes 540704 | tf_op jit(solution)/shard_map/ppermute | solution.py:600
  127.1 2.7 %collective-permute-start.20 = (bf16[144,512]{1,0:T(8,128)(2,1)S(1)}, bf16[144,512]{1,0:T(8,128)(2,1)S(1)}, u32[]{:S(2)}, u32[]{:S(2)}) collective-permute-start(bf16[144,512]{1,0:T(8,128)(2,1)S(1)} %add_convert_fusion.6), channel_id=1, source_target_pairs={{0,16},{1,3},{2,18},{3,1},{4,20},{5,7},{6,22},{7,5},{8,24},{9,11},... | collective-permute-start | bytes 442376 | tf_op jit(solution)/shard_map/ppermute | solution.py:600
  129.8 2.3 %collective-permute-done.21 = bf16[272,512]{1,0:T(8,128)(2,1)S(1)} collective-permute-done((bf16[272,512]{1,0:T(8,128)(2,1)S(1)}, bf16[272,512]{1,0:T(8,128)(2,1)S(1)}, u32[]{:S(2)}, u32[]{:S(2)}) %collective-permute-start.21) | collective-permute-done | bytes 278560 | tf_op jit(solution)/shard_map/ppermute | solution.py:600
  133.4 3.1 %collective-permute-done.20 = bf16[144,512]{1,0:T(8,128)(2,1)S(1)} collective-permute-done((bf16[144,512]{1,0:T(8,128)(2,1)S(1)}, bf16[144,512]{1,0:T(8,128)(2,1)S(1)}, u32[]{:S(2)}, u32[]{:S(2)}) %collective-permute-start.20) | collective-permute-done | bytes 147488 | tf_op jit(solution)/shard_map/ppermute | solution.py:600
  137.6 2.5 %collective-permute-start.22 = (bf16[144,512]{1,0:T(8,128)(2,1)S(1)}, bf16[144,512]{1,0:T(8,128)(2,1)S(1)}, u32[]{:S(2)}, u32[]{:S(2)}) collective-permute-start(bf16[144,512]{1,0:T(8,128)(2,1)S(1)} %add_convert_fusion.5), channel_id=1, source_target_pairs={{0,4},{1,17},{2,6},{3,19},{4,0},{5,21},{6,2},{7,23},{8,12},{9,25},... | collective-permute-start | bytes 442376 | tf_op jit(solution)/shard_map/ppermute | solution.py:600
  141.4 1.8 collective-permute-done.22
  143.2 3.0 %collective-permute-done.25 = bf16[80,512]{1,0:T(8,128)(2,1)S(1)} collective-permute-done((bf16[80,512]{1,0:T(8,128)(2,1)S(1)}, bf16[80,512]{1,0:T(8,128)(2,1)S(1)}, u32[]{:S(2)}, u32[]{:S(2)}) %collective-permute-start.25) | collective-permute-done | bytes 81952 | tf_op jit(solution)/shard_map/ppermute | solution.py:600
  147.4 3.1 %collective-permute-done.26 = bf16[64,512]{1,0:T(8,128)(2,1)S(1)} collective-permute-done((bf16[64,512]{1,0:T(8,128)(2,1)S(1)}, bf16[64,512]{1,0:T(8,128)(2,1)S(1)}, u32[]{:S(2)}, u32[]{:S(2)}) %collective-permute-start.26) | collective-permute-done | bytes 65568 | tf_op jit(solution)/shard_map/ppermute | solution.py:600
  151.6 8.5 %collective-permute-done.27 = bf16[128,512]{1,0:T(8,128)(2,1)S(1)} collective-permute-done((bf16[128,512]{1,0:T(8,128)(2,1)S(1)}, bf16[128,512]{1,0:T(8,128)(2,1)S(1)}, u32[]{:S(2)}, u32[]{:S(2)}) %collective-permute-start.27) | collective-permute-done | bytes 131104 | tf_op jit(solution)/shard_map/ppermute | solution.py:600
  162.4 10.5 %collective-permute-done.29.l1 = bf16[256,512]{1,0:T(8,128)(2,1)S(1)} collective-permute-done((bf16[256,512]{1,0:T(8,128)(2,1)S(1)}, bf16[256,512]{1,0:T(8,128)(2,1)S(1)}, u32[]{:S(2)}, u32[]{:S(2)}) %collective-permute-start.29) | collective-permute-done | bytes 262176 | tf_op jit(solution)/shard_map/ppermute | solution.py:600
  176.1 2.2 %collective-permute-done.31.other_ref = f32[8,128]{1,0:T(8,128)S(1)} collective-permute-done((f32[8,128]{1,0:T(8,128)S(1)}, f32[8,128]{1,0:T(8,128)S(1)}, u32[]{:S(2)}, u32[]{:S(2)}) %collective-permute-start.31) | collective-permute-done | bytes 4128 | tf_op jit(solution)/shard_map/ppermute | solution.py:600
  179.0 4.7 %renew_first.1 = bf16[528,512]{1,0:T(8,128)(2,1)} custom-call(s32[1]{0:T(128)} %bitcast.2.half_ref.side_ref, s32[8]{0:T(128)} %add_xor_fusion.index_ref, f32[8,128]{1,0:T(8,128)} %copy-done.19, f32[8,128]{1,0:T(8,128)} %copy-done.21, bf16[576,512]{1,0:T(8,128)(2,1)} %copy-done, bf16[576,512]{1,0:T(8,128)(2,1)} %copy-done.3, bf16[256,512]{1,0:T(8,128)(2,1)} %copy-done.4, ...), custom_call_target="tpu_custom_call" | custom-call | flops 1 | bytes 1 | tf_op jit(solution)/shard_map/renew_first/pallas_call | solution.py:740
  184.4 11.0 %update.1 = (f32[5,128,512]{2,1,0:T(8,128)}, f32[5,128,512]{2,1,0:T(8,128)}, f32[5,128,512]{2,1,0:T(8,128)}, f32[128,2048]{1,0:T(8,128)}, f32[128,2048]{1,0:T(8,...) custom-call(s32[8]{0:T(128)} %add_xor_fusion.index_ref, ...), custom_call_target="tpu_custom_call" | custom-call | flops 1 | bytes 1 | tf_op jit(solution)/shard_map/update/pallas_call | solution.py:819
  195.4 1.7 collective-permute-done.32.p4
  199.2 1.7 collective-permute-done.37
  200.9 2.0 collective-permute-start.33
  206.7 3.0 %unpack_near.1 = (bf16[5,512,512]{2,1,0:T(8,128)(2,1)}, bf16[512,2048]{1,0:T(8,128)(2,1)}, bf16[2048,512]{1,0:T(8,128)(2,1)}) custom-call(s32[4]{0:T(128)S(1)} %iota_xor_fusion.pos_ref, s32[1]{0:T(128)} %bitcast.2.half_ref.side_ref, bf16[1024,512]{1,0:T(8,128)(2,1)S(1)} %copy-done.12, bf16[640,512]{1,0:T(8,128)(2,1)S(1)} %copy-done.13, ...), custom_call_target="tpu_custom_call" | custom-call | flops 1 | bytes 1 | tf_op jit(solution)/shard_map/unpack_near/pallas_call | solution.py:907
  209.7 5.2 %collective-permute-done.39.p2 = bf16[640,512]{1,0:T(8,128)(2,1)S(1)} collective-permute-done((bf16[640,512]{1,0:T(8,128)(2,1)}, bf16[640,512]{1,0:T(8,128)(2,1)S(1)}, u32[]{:S(2)}, u32[]{:S(2)}) %collective-permute-start.39) | collective-permute-done | bytes 655392 | tf_op jit(solution)/shard_map/ppermute | solution.py:600
  219.5 2.7 %unpack_far.1 = (bf16[5,512,512]{2,1,0:T(8,128)(2,1)}, bf16[512,2048]{1,0:T(8,128)(2,1)}, bf16[2048,512]{1,0:T(8,128)(2,1)}) custom-call(s32[4]{0:T(128)S(1)} %iota_xor_fusion.pos_ref, s32[1]{0:T(128)} %bitcast.2.half_ref.side_ref, bf16[528,512]{1,0:T(8,128)(2,1)} %collective-permute-done.33.p0, ...), custom_call_target="tpu_custom_call", output_to_operand_aliasing={{0}: (6, {}), {1}: (7, {}), {2}: (8, {})} | custom-call | flops 1 | bytes 1 | tf_op jit(solution)/shard_map/unpack_far/pallas_call | solution.py:927
  (166 shorter events, 49.8 us)
Async XLA Ops:
  2.4 23.0 %collective-permute-start = (bf16[544,512]{1,0:T(8,128)(2,1)S(1)}, bf16[544,512]{1,0:T(8,128)(2,1)}, u32[]{:S(2)}, u32[]{:S(2)}) collective-permute-start(bf16[544,512]{1,0:T(8,128)(2,1)S(1)} %fusion.5.near0), channel_id=1, source_target_pairs={{0,1},{1,0},{2,3},{3,2},{4,5},{5,4},{6,7},{7,6},{8,9},{9,8},{10,11... | collective-permute-start | bytes 1671176 | tf_op jit(solution)/shard_map/ppermute | solution.py:600
  3.0 10.4 %collective-permute-start.1 = (bf16[272,512]{1,0:T(8,128)(2,1)S(1)}, bf16[272,512]{1,0:T(8,128)(2,1)}, u32[]{:S(2)}, u32[]{:S(2)}) collective-permute-start(bf16[272,512]{1,0:T(8,128)(2,1)S(1)} %constant_dynamic-slice_fusion), channel_id=1, source_target_pairs={{0,2},{1,3},{2,0},{3,1},{4,6},{5,7},{6,4},{7,5},{8,10},{9,11},{10,... | collective-permute-start | bytes 835592 | tf_op jit(solution)/shard_map/ppermute | solution.py:600
  6.2 3.6 %collective-permute-start.2 = (f32[8]{0:T(128)S(1)}, f32[8]{0:T(128)S(1)}, u32[]{:S(2)}, u32[]{:S(2)}) collective-permute-start(f32[8]{0:T(128)S(1)} %compare_convert_fusion), channel_id=1, source_target_pairs={{0,4},{1,5},{2,6},{3,7},{4,0},{5,1},{6,2},{7,3},{8,12},{9,13},{10,... | collective-permute-start | bytes 104 | tf_op jit(solution)/shard_map/ppermute | solution.py:600
  13.4 8.3 %collective-permute-start.4 = (bf16[272,512]{1,0:T(8,128)(2,1)}, bf16[272,512]{1,0:T(8,128)(2,1)}, u32[]{:S(2)}, u32[]{:S(2)}) collective-permute-start(bf16[272,512]{1,0:T(8,128)(2,1)} %collective-permute-done.1.far0), channel_id=1, source_target_pairs={{0,4},{1,5},{2,6},{3,7},{4,0},{5,1},{6,2},{7,3},{8,12},{9,13},{10,... | collective-permute-start | bytes 835592 | tf_op jit(solution)/shard_map/ppermute | solution.py:600
  15.1 4.5 %collective-permute-start.10 = (f32[8]{0:T(128)S(1)}, f32[8]{0:T(128)S(1)}, u32[]{:S(2)}, u32[]{:S(2)}) collective-permute-start(f32[8]{0:T(128)S(1)} %fusion.13), channel_id=1, source_target_pairs={{0,16},{1,17},{2,18},{3,19},{4,20},{5,21},{6,22},{7,23},{8,24},{9,... | collective-permute-start | bytes 104 | tf_op jit(solution)/shard_map/ppermute | solution.py:600
  17.8 26.2 %collective-permute-start.8 = (bf16[640,512]{1,0:T(8,128)(2,1)S(1)}, bf16[640,512]{1,0:T(8,128)(2,1)S(1)}, u32[]{:S(2)}, u32[]{:S(2)}) collective-permute-start(bf16[640,512]{1,0:T(8,128)(2,1)S(1)} %slice_dynamic-update-slice_fusion.p0), channel_id=1, source_target_pairs={{0,2},{1,3},{2,0},{3,1},{4,6},{5,7},{6,4},{7,5},{8,10},{9,11},{10,... | collective-permute-start | bytes 1966088 | tf_op jit(solution)/shard_map/ppermute | solution.py:600
  21.8 23.2 %collective-permute-start.12 = (bf16[528,512]{1,0:T(8,128)(2,1)S(1)}, bf16[528,512]{1,0:T(8,128)(2,1)}, u32[]{:S(2)}, u32[]{:S(2)}) collective-permute-start(bf16[528,512]{1,0:T(8,128)(2,1)S(1)} %fusion.6.t0), channel_id=1, source_target_pairs={{0,2},{1,3},{2,0},{3,1},{4,6},{5,7},{6,4},{7,5},{8,10},{9,11},{10,... | collective-permute-start | bytes 1622024 | tf_op jit(solution)/shard_map/ppermute | solution.py:600
  25.3 19.7 %collective-permute-start.7 = (bf16[640,512]{1,0:T(8,128)(2,1)S(1)}, bf16[640,512]{1,0:T(8,128)(2,1)S(1)}, u32[]{:S(2)}, u32[]{:S(2)}) collective-permute-start(bf16[640,512]{1,0:T(8,128)(2,1)S(1)} %slice_dynamic-update-slice_fusion.p0), channel_id=1, source_target_pairs={{0,1},{1,0},{2,3},{3,2},{4,5},{5,4},{6,7},{7,6},{8,9},{9,8},{10,11... | collective-permute-start | bytes 1966088 | tf_op jit(solution)/shard_map/ppermute | solution.py:600
  73.8 6.2 %collective-permute-start.14 = (bf16[2304,512]{1,0:T(8,128)(2,1)}, bf16[2304,512]{1,0:T(8,128)(2,1)}, u32[]{:S(2)}, u32[]{:S(2)}) collective-permute-start(bf16[2304,512]{1,0:T(8,128)(2,1)} %get-tuple-element.106), channel_id=1, source_target_pairs={{0,1},{1,0},{2,3},{3,2},{4,5},{5,4},{6,7},{7,6},{8,9},{9,8},{10,11... | collective-permute-start | bytes 7077896 | tf_op jit(solution)/shard_map/ppermute | solution.py:600
  81.6 17.0 %collective-permute-start.15 = (bf16[1152,512]{1,0:T(8,128)(2,1)S(1)}, bf16[1152,512]{1,0:T(8,128)(2,1)}, u32[]{:S(2)}, u32[]{:S(2)}) collective-permute-start(bf16[1152,512]{1,0:T(8,128)(2,1)S(1)} %add_convert_fusion), channel_id=1, source_target_pairs={{0,2},{1,5},{2,0},{3,7},{4,6},{5,1},{6,4},{7,3},{8,10},{9,13},{10,... | collective-permute-start | bytes 3538952 | tf_op jit(solution)/shard_map/ppermute | solution.py:600
  100.2 11.0 %collective-permute-start.16 = (bf16[576,512]{1,0:T(8,128)(2,1)S(1)}, bf16[576,512]{1,0:T(8,128)(2,1)S(1)}, u32[]{:S(2)}, u32[]{:S(2)}) collective-permute-start(bf16[576,512]{1,0:T(8,128)(2,1)S(1)} %add_convert_fusion.1), channel_id=1, source_target_pairs={{0,4},{1,9},{2,6},{3,11},{4,0},{5,13},{6,2},{7,15},{8,12},{9,1},{1... | collective-permute-start | bytes 1769480 | tf_op jit(solution)/shard_map/ppermute | solution.py:600
  115.9 9.4 %collective-permute-start.19 = (bf16[528,512]{1,0:T(8,128)(2,1)S(1)}, bf16[528,512]{1,0:T(8,128)(2,1)S(1)}, u32[]{:S(2)}, u32[]{:S(2)}) collective-permute-start(bf16[528,512]{1,0:T(8,128)(2,1)S(1)} %pad_maximum_fusion.1), channel_id=1, source_target_pairs={{0,2},{1,5},{2,0},{3,7},{4,6},{5,1},{6,4},{7,3},{8,10},{9,13},{10,... | collective-permute-start | bytes 1622024 | tf_op jit(solution)/shard_map/ppermute | solution.py:600
  117.0 9.1 %collective-permute-start.17 = (bf16[288,512]{1,0:T(8,128)(2,1)S(1)}, bf16[288,512]{1,0:T(8,128)(2,1)S(1)}, u32[]{:S(2)}, u32[]{:S(2)}) collective-permute-start(bf16[288,512]{1,0:T(8,128)(2,1)S(1)} %add_convert_fusion.3), channel_id=1, source_target_pairs={{0,8},{1,17},{2,10},{3,19},{4,12},{5,21},{6,14},{7,23},{8,0},{9,25... | collective-permute-start | bytes 884744 | tf_op jit(solution)/shard_map/ppermute | solution.py:600
  125.5 6.6 %collective-permute-start.21 = (bf16[272,512]{1,0:T(8,128)(2,1)S(1)}, bf16[272,512]{1,0:T(8,128)(2,1)S(1)}, u32[]{:S(2)}, u32[]{:S(2)}) collective-permute-start(bf16[272,512]{1,0:T(8,128)(2,1)S(1)} %pad_maximum_fusion.3), channel_id=1, source_target_pairs={{0,4},{1,9},{2,6},{3,11},{4,0},{5,13},{6,2},{7,15},{8,12},{9,1},{1... | collective-permute-start | bytes 835592 | tf_op jit(solution)/shard_map/ppermute | solution.py:600
  127.1 9.4 %collective-permute-start.20 = (bf16[144,512]{1,0:T(8,128)(2,1)S(1)}, bf16[144,512]{1,0:T(8,128)(2,1)S(1)}, u32[]{:S(2)}, u32[]{:S(2)}) collective-permute-start(bf16[144,512]{1,0:T(8,128)(2,1)S(1)} %add_convert_fusion.6), channel_id=1, source_target_pairs={{0,16},{1,3},{2,18},{3,1},{4,20},{5,7},{6,22},{7,5},{8,24},{9,11},... | collective-permute-start | bytes 442376 | tf_op jit(solution)/shard_map/ppermute | solution.py:600
  132.2 7.9 %collective-permute-start.23 = (bf16[144,512]{1,0:T(8,128)(2,1)S(1)}, bf16[144,512]{1,0:T(8,128)(2,1)S(1)}, u32[]{:S(2)}, u32[]{:S(2)}) collective-permute-start(bf16[144,512]{1,0:T(8,128)(2,1)S(1)} %pad_maximum_fusion.5), channel_id=1, source_target_pairs={{0,8},{1,17},{2,10},{3,19},{4,12},{5,21},{6,14},{7,23},{8,0},{9,25... | collective-permute-start | bytes 442376 | tf_op jit(solution)/shard_map/ppermute | solution.py:600
  137.6 5.6 %collective-permute-start.22 = (bf16[144,512]{1,0:T(8,128)(2,1)S(1)}, bf16[144,512]{1,0:T(8,128)(2,1)S(1)}, u32[]{:S(2)}, u32[]{:S(2)}) collective-permute-start(bf16[144,512]{1,0:T(8,128)(2,1)S(1)} %add_convert_fusion.5), channel_id=1, source_target_pairs={{0,4},{1,17},{2,6},{3,19},{4,0},{5,21},{6,2},{7,23},{8,12},{9,25},... | collective-permute-start | bytes 442376 | tf_op jit(solution)/shard_map/ppermute | solution.py:600
  140.2 6.0 %collective-permute-start.25 = (bf16[80,512]{1,0:T(8,128)(2,1)S(1)}, bf16[80,512]{1,0:T(8,128)(2,1)S(1)}, u32[]{:S(2)}, u32[]{:S(2)}) collective-permute-start(bf16[80,512]{1,0:T(8,128)(2,1)S(1)} %pad_maximum_fusion.7), channel_id=1, source_target_pairs={{0,16},{1,3},{2,18},{3,1},{4,20},{5,7},{6,22},{7,5},{8,24},{9,11},... | collective-permute-start | bytes 245768 | tf_op jit(solution)/shard_map/ppermute | solution.py:600
  146.3 4.3 %collective-permute-start.26 = (bf16[64,512]{1,0:T(8,128)(2,1)S(1)}, bf16[64,512]{1,0:T(8,128)(2,1)S(1)}, u32[]{:S(2)}, u32[]{:S(2)}) collective-permute-start(bf16[64,512]{1,0:T(8,128)(2,1)S(1)} %add_convert_fusion.8), channel_id=1, source_target_pairs={{0,4},{1,17},{2,6},{3,19},{4,0},{5,21},{6,2},{7,23},{8,12},{9,25},... | collective-permute-start | bytes 196616 | tf_op jit(solution)/shard_map/ppermute | solution.py:600
  146.4 13.7 %collective-permute-start.24 = (bf16[288,512]{1,0:T(8,128)(2,1)S(1)}, bf16[288,512]{1,0:T(8,128)(2,1)S(1)}, u32[]{:S(2)}, u32[]{:S(2)}) collective-permute-start(bf16[288,512]{1,0:T(8,128)(2,1)S(1)} %pad_maximum_fusion.2), channel_id=1, source_target_pairs={{0,16},{1,9},{2,18},{3,11},{4,20},{5,13},{6,22},{7,15},{8,24},{9,1... | collective-permute-start | bytes 884744 | tf_op jit(solution)/shard_map/ppermute | solution.py:600
  150.6 9.5 %collective-permute-start.27 = (bf16[128,512]{1,0:T(8,128)(2,1)S(1)}, bf16[128,512]{1,0:T(8,128)(2,1)S(1)}, u32[]{:S(2)}, u32[]{:S(2)}) collective-permute-start(bf16[128,512]{1,0:T(8,128)(2,1)S(1)} %pad_maximum_fusion.6), channel_id=1, source_target_pairs={{0,16},{1,9},{2,18},{3,11},{4,20},{5,13},{6,22},{7,15},{8,24},{9,1... | collective-permute-start | bytes 393224 | tf_op jit(solution)/shard_map/ppermute | solution.py:600
  160.2 12.8 %collective-permute-start.28 = (bf16[576,512]{1,0:T(8,128)(2,1)S(1)}, bf16[576,512]{1,0:T(8,128)(2,1)S(1)}, u32[]{:S(2)}, u32[]{:S(2)}) collective-permute-start(bf16[576,512]{1,0:T(8,128)(2,1)S(1)} %pad_maximum_fusion.e0), channel_id=1, source_target_pairs={{0,8},{1,5},{2,10},{3,7},{4,12},{5,1},{6,14},{7,3},{8,0},{9,13},{1... | collective-permute-start | bytes 1769480 | tf_op jit(solution)/shard_map/ppermute | solution.py:600
  160.9 12.1 %collective-permute-start.29 = (bf16[256,512]{1,0:T(8,128)(2,1)S(1)}, bf16[256,512]{1,0:T(8,128)(2,1)S(1)}, u32[]{:S(2)}, u32[]{:S(2)}) collective-permute-start(bf16[256,512]{1,0:T(8,128)(2,1)S(1)} %pad_maximum_fusion.4.l0), channel_id=1, source_target_pairs={{0,8},{1,5},{2,10},{3,7},{4,12},{5,1},{6,14},{7,3},{8,0},{9,13},{1... | collective-permute-start | bytes 786440 | tf_op jit(solution)/shard_map/ppermute | solution.py:600
  174.7 3.6 %collective-permute-start.31 = (f32[8,128]{1,0:T(8,128)S(1)}, f32[8,128]{1,0:T(8,128)S(1)}, u32[]{:S(2)}, u32[]{:S(2)}) collective-permute-start(f32[8,128]{1,0:T(8,128)S(1)} %add.283.square_ref), channel_id=1, source_target_pairs={{0,2},{1,3},{2,0},{3,1},{4,6},{5,7},{6,4},{7,5},{8,10},{9,11},{10,... | collective-permute-start | bytes 12296 | tf_op jit(solution)/shard_map/ppermute | solution.py:600
  183.7 13.4 %collective-permute-start.32 = (bf16[528,512]{1,0:T(8,128)(2,1)}, bf16[528,512]{1,0:T(8,128)(2,1)S(1)}, u32[]{:S(2)}, u32[]{:S(2)}) collective-permute-start(bf16[528,512]{1,0:T(8,128)(2,1)} %renew_first.1), channel_id=1, source_target_pairs={{0,2},{1,3},{2,0},{3,1},{4,6},{5,7},{6,4},{7,5},{8,10},{9,11},{10,... | collective-permute-start | bytes 1622024 | tf_op jit(solution)/shard_map/ppermute | solution.py:600
  197.1 7.4 %collective-permute-start.34 = (bf16[1024,512]{1,0:T(8,128)(2,1)}, bf16[1024,512]{1,0:T(8,128)(2,1)S(1)}, u32[]{:S(2)}, u32[]{:S(2)}) collective-permute-start(bf16[1024,512]{1,0:T(8,128)(2,1)} %get-tuple-element.162.p0), channel_id=1, source_target_pairs={{0,1},{1,0},{2,3},{3,2},{4,5},{5,4},{6,7},{7,6},{8,9},{9,8},{10,11... | collective-permute-start | bytes 3145736 | tf_op jit(solution)/shard_map/ppermute | solution.py:600
  197.1 6.1 %collective-permute-start.36 = (bf16[528,512]{1,0:T(8,128)(2,1)S(1)}, bf16[528,512]{1,0:T(8,128)(2,1)S(1)}, u32[]{:S(2)}, u32[]{:S(2)}) collective-permute-start(bf16[528,512]{1,0:T(8,128)(2,1)S(1)} %collective-permute-done.32.p4), channel_id=1, source_target_pairs={{0,1},{1,0},{2,3},{3,2},{4,5},{5,4},{6,7},{7,6},{8,9},{9,8},{10,11... | collective-permute-start | bytes 1622024 | tf_op jit(solution)/shard_map/ppermute | solution.py:600
  197.6 6.8 %collective-permute-start.35 = (bf16[640,512]{1,0:T(8,128)(2,1)}, bf16[640,512]{1,0:T(8,128)(2,1)S(1)}, u32[]{:S(2)}, u32[]{:S(2)}) collective-permute-start(bf16[640,512]{1,0:T(8,128)(2,1)} %get-tuple-element.163.p1), channel_id=1, source_target_pairs={{0,1},{1,0},{2,3},{3,2},{4,5},{5,4},{6,7},{7,6},{8,9},{9,8},{10,11... | collective-permute-start | bytes 1966088 | tf_op jit(solution)/shard_map/ppermute | solution.py:600
  197.6 17.4 %collective-permute-start.39 = (bf16[640,512]{1,0:T(8,128)(2,1)}, bf16[640,512]{1,0:T(8,128)(2,1)S(1)}, u32[]{:S(2)}, u32[]{:S(2)}) collective-permute-start(bf16[640,512]{1,0:T(8,128)(2,1)} %get-tuple-element.163.p1), channel_id=1, source_target_pairs={{0,2},{1,3},{2,0},{3,1},{4,6},{5,7},{6,4},{7,5},{8,10},{9,11},{10,... | collective-permute-start | bytes 1966088 | tf_op jit(solution)/shard_map/ppermute | solution.py:600
  200.9 14.9 %collective-permute-start.33 = (bf16[528,512]{1,0:T(8,128)(2,1)S(1)}, bf16[528,512]{1,0:T(8,128)(2,1)}, u32[]{:S(2)}, u32[]{:S(2)}) collective-permute-start(bf16[528,512]{1,0:T(8,128)(2,1)S(1)} %collective-permute-done.32.p4), channel_id=1, source_target_pairs={{0,4},{1,5},{2,6},{3,7},{4,0},{5,1},{6,2},{7,3},{8,12},{9,13},{10,... | collective-permute-start | bytes 1622024 | tf_op jit(solution)/shard_map/ppermute | solution.py:600
  214.9 4.6 %collective-permute-start.40 = (bf16[640,512]{1,0:T(8,128)(2,1)S(1)}, bf16[640,512]{1,0:T(8,128)(2,1)S(1)}, u32[]{:S(2)}, u32[]{:S(2)}) collective-permute-start(bf16[640,512]{1,0:T(8,128)(2,1)S(1)} %collective-permute-done.39.p2), channel_id=1, source_target_pairs={{0,1},{1,0},{2,3},{3,2},{4,5},{5,4},{6,7},{7,6},{8,9},{9,8},{10,11... | collective-permute-start | bytes 1966088 | tf_op jit(solution)/shard_map/ppermute | solution.py:600
  215.9 3.6 %collective-permute-start.38 = (bf16[528,512]{1,0:T(8,128)(2,1)}, bf16[528,512]{1,0:T(8,128)(2,1)S(1)}, u32[]{:S(2)}, u32[]{:S(2)}) collective-permute-start(bf16[528,512]{1,0:T(8,128)(2,1)} %collective-permute-done.33.p0), channel_id=1, source_target_pairs={{0,1},{1,0},{2,3},{3,2},{4,5},{5,4},{6,7},{7,6},{8,9},{9,8},{10,11... | collective-permute-start | bytes 1622024 | tf_op jit(solution)/shard_map/ppermute | solution.py:600
  (32 other events, 291.2 us)

commit v5 on v4

--- a/solution.py
+++ b/solution.py
@@ -20,6 +20,8 @@
 GROUP = 256
 LANES = 128
 SMALL = 16
+FIRST_UNITS = 7
+DIRECT_UNITS = 3
 CHEAP = pl.CostEstimate(flops=1, bytes_accessed=1, transcendentals=0)
 STEP = 10
 TILE = 512
@@ -317,7 +319,8 @@
     for d in range(count):
         place = place_ref[table, (shard // 2) * count + d]
         where = pl.ds(pl.multiple_of(place * height + unit * rows, rows), rows)
-        target[where, :] = grads[pl.ds(pl.multiple_of(first + d * rows, rows), rows), :]
+        group = d % 2 * (count // 2) + d // 2
+        target[where, :] = grads[pl.ds(pl.multiple_of(first + group * rows, rows), rows), :]
 
 
 def scatter_shards(pos_ref, place_ref, grads, send_ref, keep_ref, unit):
@@ -330,7 +333,7 @@
 def feed_kernel(
     pos_ref, place_ref, domain_ref, x_ref, g_ref, o_ref, norm_ref, p0, p1, p2, p3, t0, t1, t2, t3,
     y_ref, dh_ref, do_ref, send_ref, keep_ref, dnorm_ref,
-    wo, w1, w2, branch, unit_ref, inv_ref, n2, gb, n2_t, gb_t, dn2, grads, u_all, da_all, factor_ref
+    wo, w1, w2, branch, unit_ref, inv_ref, n2, gb, n2_t, dn2, grads, u_all, da_all, factor_ref
 ):
     step = pl.program_id(0)
     last = pl.num_programs(0) - 1
@@ -364,7 +367,6 @@
             n2_t[:, rows] = normed.T
             grad = (g_ref[rows, :].astype(F32) * factor_ref[0:1, 0:1]).astype(BF)
             gb[rows, :] = grad
-            gb_t[:, rows] = grad.T
             dn2[rows, :] = jnp.zeros((256, width), F32)
             return 0
 
@@ -389,7 +391,7 @@
         branch[rows, :] += dot(u, down)
         dn2[rows, :] += dot_nt(da, up)
     up_grad = dot(n2_t[...], da_all[...])
-    down_grad = dot(gb_t[...], u_all[...])
+    down_grad = dot_tn(u_all[...], gb[...])
     grads[...] = up_grad.astype(BF)
     scatter_shards(pos_ref, place_ref, grads, send_ref, keep_ref, step + 1)
     grads[...] = down_grad.astype(BF)
@@ -463,7 +465,6 @@
             pltpu.VMEM((length, width), BF),
             pltpu.VMEM((length, width), BF),
             pltpu.VMEM((width, length), BF),
-            pltpu.VMEM((width, length), BF),
             pltpu.VMEM((length, width), F32),
             pltpu.VMEM((width, block), BF),
             pltpu.VMEM((length, block), BF),
@@ -644,17 +645,13 @@
 
 def gather_plan():
     split = split_bits()
-    even = [split[0]] + split[1:][::-1]
-    odd = split[::-1]
-    return [(("dp", a), ("dp", b)) for a, b in zip(even, odd)]
-
-
-def gather_index():
-    odd = lax.axis_index("shard") % 2
+    even = split[1:] + split[:1]
+    odd = split[1:][::-1] + split[:1]
     mask = jnp.zeros((1,), jnp.int32)
-    for (_, even_bit), (_, odd_bit) in gather_plan():
-        mask = jnp.concatenate([mask, mask | jnp.where(odd == 1, odd_bit, even_bit)])
-    return (lax.axis_index("dp") % mask.shape[0]) ^ mask
+    for a, b in list(zip(even, odd))[:-1]:
+        mask = jnp.concatenate([mask, mask | jnp.where(lax.axis_index("shard") % 2 == 1, b, a)])
+    index = ((lax.axis_index("dp") % 2 ** len(split)) ^ mask) // 2
+    return [(("dp", a), ("dp", b)) for a, b in zip(even, odd)], index
 
 
 def adam(master, first, second, grad, rate, decay):
@@ -665,22 +662,20 @@
     return master - rate * (update + decay * master), first_new, second_new
 
 
-def gather_rows(index_ref, sources, targets):
+def gather_rows(index_ref, source, target, span, base):
     count = index_ref.shape[0]
-    rows = LANES // count
-    for parts, target in zip(sources, targets):
-        units = target.shape[0] // LANES
-        for j in range(count):
-            source = parts[2 * j // count]
-            for u in range(units):
-                place = pl.ds(pl.multiple_of(u * LANES + index_ref[j] * rows, rows), rows)
-                first = (j % (count // 2) * units + u) * rows
-                target[place, :] = source[first : first + rows, :]
-
-
-def squares_kernel(e0, e1, l0, l1, gn_ref, out_ref):
-    total = jnp.sum(jnp.square(gn_ref[...]))
-    for ref in (e0, e1, l0, l1):
+    rows = LANES // 2 // count
+    units = target.shape[0] // span
+    for j in range(count):
+        for u in range(units):
+            place = pl.ds(pl.multiple_of(u * span + base + index_ref[j] * rows, rows), rows)
+            first = (j * units + u) * rows
+            target[place, :] = source[first : first + rows, :]
+
+
+def squares_kernel(early_ref, late_ref, gn_ref, out_ref):
+    total = 0.5 * jnp.sum(jnp.square(gn_ref[...]))
+    for ref in (early_ref, late_ref):
         values = ref[...].astype(F32)
         total += jnp.sum(values * values)
     out_ref[...] = jnp.full(out_ref.shape, total, F32)
@@ -690,13 +685,13 @@
     vmem = pl.BlockSpec(memory_space=pltpu.VMEM)
     return pl.pallas_call(
         squares_kernel,
-        in_specs=[vmem] * 5,
+        in_specs=[vmem] * 3,
         out_specs=vmem,
         out_shape=jax.ShapeDtypeStruct((8, LANES), F32),
         compiler_params=pltpu.CompilerParams(vmem_limit_bytes=VMEM_UNPACK),
         name="squares",
         cost_estimate=CHEAP,
-    )(*early, *late, gn)
+    )(early, late, gn)
 
 
 def clip_factor(square_ref, other_ref):
@@ -704,72 +699,83 @@
     return jnp.minimum(1.0, 1.0 / (norm + 1e-06))
 
 
-def renew_first_kernel(
-    side_ref, index_ref, square_ref, other_ref, e0, e1, l0, l1, gn_ref, nm, nf, ns,
-    am, af, as_, um, uf, us, copy_ref, early, late
+def renew_kernel(
+    side_ref, index_ref, square_ref, other_ref, early_ref, late_ref, gn_ref, nm, nf, ns,
+    am, af, as_, um, uf, us, dm, df, ds, first_ref, second_ref, clip_ref, early, late
 ):
     factor = clip_factor(square_ref, other_ref)
     width = early.shape[1]
-    height = am.shape[1]
-    gather_rows(index_ref, ((e0, e1), (l0, l1)), (early, late))
-
-    def span(unit):
-        return pl.ds(pl.multiple_of(unit * LANES + side_ref[0] * height, height), height)
-
-    for unit in range(8):
+    half = LANES // 2
+    gather_rows(index_ref, early_ref, early, half, 0)
+    gather_rows(index_ref, late_ref, late, half, 0)
+    blocks = um.shape[1] // width
+    middle = FIRST_UNITS
+    for unit in range(5 + blocks + dm.shape[0]):
+        if unit < 4:
+            source = late[unit * half : (unit + 1) * half, :]
+        else:
+            source = early[(unit - 4) * half : (unit - 3) * half, :]
         if unit < 5:
-            source = late[span(unit), :] if unit < 4 else early[span(0), :]
             state = am[unit], af[unit], as_[unit]
-        else:
-            source = early[span(unit - 4), :]
+        elif unit < 5 + blocks:
             cols = slice((unit - 5) * width, (unit - 4) * width)
             state = um[:, cols], uf[:, cols], us[:, cols]
+        else:
+            state = [ref[unit - 5 - blocks] for ref in (dm, df, ds)]
         new = adam(*state, source.astype(F32) * factor, 0.05, 0.01)
-        copy_ref[unit * height : (unit + 1) * height, :] = new[0].astype(BF)
+        target, place = (first_ref, unit) if unit < middle else (second_ref, unit - middle)
+        target[place * half : (place + 1) * half, :] = new[0].astype(BF)
     new = adam(nm[...], nf[...], ns[...], gn_ref[...] * factor, 0.3, 0.0)
-    last = copy_ref.shape[0] - SMALL
-    copy_ref[last:, :] = jnp.zeros((SMALL, width), BF)
-    copy_ref[last : last + 4, 0:LANES] = new[0].astype(BF)
-
-
-def renew_first(side, index, square, early, late, gn, attn, up, norm):
+    last = middle * half
+    first_ref[last:, :] = jnp.zeros((SMALL, width), BF)
+    first_ref[last : last + 4, 0:LANES] = new[0].astype(BF)
+    clip_ref[0] = jnp.sqrt(square_ref[0:1, 0:1] + other_ref[0:1, 0:1])[0, 0]
+
+
+def renew(side, index, square, early, late, gn, attn, up, down, norm):
     five, part, width = attn[0].shape
     hidden = up[0].shape[1]
-    smem = pl.BlockSpec(memory_space=pltpu.SMEM)
-    copy = jax.ShapeDtypeStruct((8 * part // 2 + SMALL, width), BF)
+    half = part // 2
+    down = [a.reshape(a.shape[0] // part, part, width) for a in down]
+    units = five + hidden // width + down[0].shape[0]
+    first = jax.ShapeDtypeStruct((FIRST_UNITS * half + SMALL, width), BF)
+    second = jax.ShapeDtypeStruct(((units - FIRST_UNITS) * half, width), BF)
+    tall = down[0].shape[0]
     return pl.pallas_call(
-        renew_first_kernel,
+        renew_kernel,
         grid_spec=pltpu.PrefetchScalarGridSpec(
             num_scalar_prefetch=1,
             grid=(1,),
-            in_specs=[smem] + [whole(a) for a in (*square, *early, *late, gn, *norm)]
-            + [pl.BlockSpec((five, part // 2, width), lambda i, side: (0, side[0], 0))] * 3
-            + [pl.BlockSpec((part // 2, hidden), lambda i, side: (side[0], 0))] * 3,
-            out_specs=whole(copy),
-            scratch_shapes=[
-                pltpu.VMEM((2 * early[0].shape[0], width), BF),
-                pltpu.VMEM((2 * late[0].shape[0], width), BF),
-            ],
+            in_specs=[pl.BlockSpec(memory_space=pltpu.SMEM)]
+            + [whole(a) for a in (*square, early, late, gn, *norm)]
+            + [pl.BlockSpec((five, half, width), lambda i, side: (0, side[0], 0))] * 3
+            + [pl.BlockSpec((half, hidden), lambda i, side: (side[0], 0))] * 3
+            + [pl.BlockSpec((tall, half, width), lambda i, side: (0, side[0], 0))] * 3,
+            out_specs=[whole(first), whole(second), pl.BlockSpec(memory_space=pltpu.SMEM)],
+            scratch_shapes=[pltpu.VMEM(early.shape, BF), pltpu.VMEM(late.shape, BF)],
         ),
-        out_shape=copy,
+        out_shape=[first, second, jax.ShapeDtypeStruct((1,), F32)],
         compiler_params=pltpu.CompilerParams(
             dimension_semantics=("arbitrary",), vmem_limit_bytes=VMEM_UPDATE
         ),
-        name="renew_first",
+        name="renew",
         cost_estimate=CHEAP,
-    )(side, index, *square, *early, *late, gn, *norm, *attn, *up)
-
-
-def update_kernel(index_ref, square_ref, other_ref, e0, e1, l0, l1, gn_ref, *refs):
+    )(side, index, *square, early, late, gn, *norm, *attn, *up, *down)
+
+
+def update_kernel(
+    side_ref, index_ref, square_ref, other_ref, early_ref, late_ref, got_ref, gn_ref, *refs
+):
     am, af, as_, um, uf, us, dm, df, ds, nm, nf, ns = refs[:12]
     early, late = refs[-2:]
-    outs, copy_low, copy_high = refs[12:-4], refs[-4], refs[-3]
+    outs, copy_low, copy_high, other_half = refs[12:-5], refs[-5], refs[-4], refs[-3]
     step = pl.program_id(0)
     factor = clip_factor(square_ref, other_ref)
     width = early.shape[1]
     part = late.shape[0] // 4
     blocks = um.shape[1] // width
     height = part // pl.num_programs(0)
+    half = LANES // 2
 
     def keep(group, where, unit, size, new):
         for target, value in zip(outs[3 * group : 3 * group + 3], new):
@@ -780,7 +786,12 @@
 
     @pl.when(step == 0)
     def _():
-        gather_rows(index_ref, ((e0, e1), (l0, l1)), (early, late))
+        mine = half * side_ref[0]
+        count = late_ref.shape[0]
+        gather_rows(index_ref, early_ref, early, part, mine)
+        gather_rows(index_ref, late_ref, late, part, mine)
+        gather_rows(index_ref, got_ref.at[:count, :], late, part, half - mine)
+        gather_rows(index_ref, got_ref.at[count:, :], early, part, half - mine)
         new = adam(nm[...], nf[...], ns[...], gn_ref[...] * factor, 0.3, 0.0)
         outs[9][...], outs[10][...], outs[11][...] = new
 
@@ -797,12 +808,20 @@
         new = adam(um[cols], uf[cols], us[cols], source.astype(F32) * factor, 0.05, 0.01)
         keep(1, cols, 5 + j, height, new)
     tall = dm.shape[0]
-    source = early[(blocks + 1) * part :, span(0, tall)].astype(F32).T
-    new = adam(dm[...], df[...], ds[...], source * factor, 0.05, 0.01)
+    source = early[span((blocks + 1) * part, tall), :]
+    new = adam(dm[...], df[...], ds[...], source.astype(F32) * factor, 0.05, 0.01)
     keep(2, (slice(None), slice(None)), 5 + blocks, tall, new)
 
-
-def update(index, square, early, late, gn, attn, up, down, norm):
+    @pl.when(step == pl.num_programs(0) - 1)
+    def _():
+        count = other_half.shape[0] // half
+        base = copy_high.shape[0] - count * part
+        for j in range(count):
+            rows = pl.ds(pl.multiple_of(base + j * part + half - half * side_ref[0], half), half)
+            other_half[j * half : (j + 1) * half, :] = copy_high[rows, :]
+
+
+def update(side, index, square, early, late, got, gn, attn, up, down, norm):
     steps = 4
     smem = pl.BlockSpec(memory_space=pltpu.SMEM)
     five, part, width = attn[0].shape
@@ -814,21 +833,22 @@
     )
     arrays = tuple(attn) + tuple(up) + tuple(down) + tuple(norm)
     low = jax.ShapeDtypeStruct((8 * part, width), BF)
-    tall, short = 2 * early[0].shape[0], 2 * late[0].shape[0]
+    tall, short = 2 * early.shape[0], 2 * late.shape[0]
     high = jax.ShapeDtypeStruct((tall + short - 8 * part, width), BF)
+    other = jax.ShapeDtypeStruct((DIRECT_UNITS * part // 2, width), BF)
     return pl.pallas_call(
         update_kernel,
         grid=(steps,),
-        in_specs=[smem] + [whole(a) for a in (*square, *early, *late, gn)] + specs,
-        out_specs=specs + [whole(low), whole(high)],
-        out_shape=[jax.ShapeDtypeStruct(a.shape, F32) for a in arrays] + [low, high],
+        in_specs=[smem] * 2 + [whole(a) for a in (*square, early, late, got, gn)] + specs,
+        out_specs=specs + [whole(low), whole(high), whole(other)],
+        out_shape=[jax.ShapeDtypeStruct(a.shape, F32) for a in arrays] + [low, high, other],
         scratch_shapes=[pltpu.VMEM((tall, width), BF), pltpu.VMEM((short, width), BF)],
         compiler_params=pltpu.CompilerParams(
             dimension_semantics=("arbitrary",), vmem_limit_bytes=VMEM_UPDATE
         ),
         name="update",
         cost_estimate=CHEAP,
-    )(index, *square, *early, *late, gn, *arrays)
+    )(side, index, *square, early, late, got, gn, *arrays)
 
 
 def place_unit(pos, source, unit, first, count, attn_ref, up_ref, down_ref, sem):
@@ -859,11 +879,13 @@
         copies.append(place_unit(pos, source, unit + j, 0, LANES, *outs, sems.at[len(copies)]))
 
 
-def place_half(pos, side, piece, outs, sems, copies):
+def place_half(pos, side, piece, unit, outs, sems, copies):
     half = LANES // 2
-    for unit in range(8):
-        source = piece.at[pl.ds(unit * half, half), :]
-        copies.append(place_unit(pos, source, unit, half * side, half, *outs, sems.at[len(copies)]))
+    for j in range(piece.shape[0] // half):
+        source = piece.at[pl.ds(j * half, half), :]
+        copies.append(
+            place_unit(pos, source, unit + j, half * side, half, *outs, sems.at[len(copies)])
+        )
 
 
 def unpack_near_kernel(pos_ref, side_ref, p0, p1, p2, p3, p4, p5, attn_ref, up_ref, down_ref, sems):
@@ -873,28 +895,44 @@
         place_whole(pos_ref[index], parts[0], 0, outs, sems, copies)
         place_whole(pos_ref[index], parts[1], 8, outs, sems, copies)
     for index, piece in enumerate((p4, p5)):
-        place_half(pos_ref[2 + index], side_ref[0], piece, outs, sems, copies)
+        place_half(pos_ref[2 + index], side_ref[0], piece, 0, outs, sems, copies)
     run_copies(copies)
 
 
-def unpack_far_kernel(pos_ref, side_ref, p0, p1, p2, p3, *refs):
-    outs, sems = refs[3:6], refs[6]
+def unpack_far_kernel(pos_ref, side_ref, *refs):
+    pieces, outs, sems = refs[:8], refs[11:14], refs[14]
     copies = []
-    for index, piece in enumerate((p0, p1)):
-        place_half(pos_ref[2 + index], side_ref[0] ^ 1, piece, outs, sems, copies)
-    for index, piece in enumerate((p2, p3)):
-        place_whole(pos_ref[2 + index], piece, 8, outs, sems, copies)
+    other = side_ref[0] ^ 1
+    for index in range(2):
+        second, first_other, second_other, direct = pieces[4 * index : 4 * index + 4]
+        pos = pos_ref[2 + index]
+        place_half(pos, side_ref[0], second, FIRST_UNITS, outs, sems, copies)
+        place_half(pos, other, first_other, 0, outs, sems, copies)
+        place_half(pos, other, second_other, FIRST_UNITS, outs, sems, copies)
+        unit = FIRST_UNITS + second_other.shape[0] // (LANES // 2)
+        place_half(pos, other, direct, unit, outs, sems, copies)
     run_copies(copies)
 
 
-def share_copies(pos, side, low, high, first, width, hidden):
+def share_copies(pos, side, first, second, low, high, direct, width, hidden):
     units = (low.shape[0] + high.shape[0]) // LANES
-    ours = swap(first, "shard", 2)
-    other = swap(after(ours, low), "dp", 1)
-    rest = swap(after(high, ours), "shard", 2)
-    near = [swap(after(part, ours), "shard", 1) for part in (low, high)]
-    ours_too = swap(after(ours, low), "shard", 1)
-    first_too = swap(after(first[8 * LANES // 2 :], ours), "shard", 1)
+    half = LANES // 2
+    last_rows = swap(first[FIRST_UNITS * half :], "shard", 1)
+    ours, first_too, low, high, direct = lax.optimization_barrier(
+        (swap(first, "shard", 2), last_rows, low, high, direct)
+    )
+    other = swap(ours, "dp", 1)
+    second_got = swap(after(second, ours), "shard", 2)
+    near = [swap(part, "shard", 1) for part in (low, high)]
+    ours_too = swap(ours, "shard", 1)
+    a, b, c, d = [
+        p[p.shape[0] - SMALL : p.shape[0] - SMALL + 4, :LANES]
+        for p in (first, first_too, ours, ours_too)
+    ]
+    low_bit, high_bit = pos[0] % 2 == 1, pos[0] // 2 == 1
+    a, b, c, d = [jnp.where(low_bit, v, u) for u, v in ((a, b), (b, a), (c, d), (d, c))]
+    a, b, c, d = [jnp.where(high_bit, v, u) for u, v in ((a, c), (b, d), (c, a), (d, b))]
+    norms = jnp.concatenate([a, b, c, d], axis=1)
     hbm = pl.BlockSpec(memory_space=pl.ANY)
     vmem = pl.BlockSpec(memory_space=pltpu.VMEM)
     smem = pl.BlockSpec(memory_space=pltpu.SMEM)
@@ -909,28 +947,23 @@
         in_specs=[smem, smem] + [vmem] * 6,
         out_specs=[hbm] * 3,
         out_shape=shapes,
-        scratch_shapes=[pltpu.SemaphoreType.DMA((2 * (units + 8),))],
+        scratch_shapes=[pltpu.SemaphoreType.DMA((2 * (units + FIRST_UNITS),))],
         compiler_params=params,
         name="unpack_near",
         cost_estimate=CHEAP,
-    )(pos, side, low, high, *near, ours, ours_too)
-    a, b, c, d = [
-        p[p.shape[0] - SMALL : p.shape[0] - SMALL + 4, :LANES]
-        for p in (first, first_too, ours, ours_too)
-    ]
-    low_bit, high_bit = pos[0] % 2 == 1, pos[0] // 2 == 1
-    a, b, c, d = [jnp.where(low_bit, v, u) for u, v in ((a, b), (b, a), (c, d), (d, c))]
-    a, b, c, d = [jnp.where(high_bit, v, u) for u, v in ((a, c), (b, d), (c, a), (d, b))]
-    norms = jnp.concatenate([a, b, c, d], axis=1)
-    far = [other, swap(after(other, begun[0], norms), "shard", 1)]
-    far += [rest, swap(after(rest, begun[0], norms), "shard", 1)]
+    )(pos, side, after(low, norms), high, *near, ours, ours_too)
+    second = after(second_got, begun[0])
+    second_other = swap(second[: -direct.shape[0]], "dp", 1)
+    direct = swap(after(direct, second), "shard", 2)
+    far = [second, other, second_other, direct]
+    far += [swap(after(f, begun[0]), "shard", 1) for f in far]
     done = pl.pallas_call(
         unpack_far_kernel,
-        in_specs=[smem, smem] + [vmem] * 4 + [hbm] * 3,
+        in_specs=[smem, smem] + [vmem] * 8 + [hbm] * 3,
         out_specs=[hbm] * 3,
         out_shape=shapes,
-        scratch_shapes=[pltpu.SemaphoreType.DMA((2 * units,))],
-        input_output_aliases={6: 0, 7: 1, 8: 2},
+        scratch_shapes=[pltpu.SemaphoreType.DMA((4 * units,))],
+        input_output_aliases={10: 0, 11: 1, 12: 2},
         compiler_params=params,
         name="unpack_far",
         cost_estimate=CHEAP,
@@ -998,7 +1031,8 @@
         pos, place, domain_rows, tokens, out_grad, o, norm, second, third
     )
 
-    steps, plan = phases(), gather_plan()
+    steps = phases()
+    plan, index = gather_plan()
     pieces = 2 ** len(steps)
     rows = keep.shape[0] // pieces
 
@@ -1037,17 +1071,18 @@
     small = late_sum(late_got)
     turn, late_got = late_phase(1)
     early.append(after(got, turn))
-    got = exchange(forward_phase(early, 3, rows), *steps[3])
-    small = late_sum(late_got)
+    turn = forward_phase(early, 3, rows)
+    got = exchange(turn, *steps[3])
+    small = late_sum(after(late_got, turn))
     turn, late_got = late_phase(2)
     early.append(after(got, turn))
     early = add_rest(add_up(early, 0, rows))
     got = exchange(early, *plan[0])
-    small = late_sum(late_got)
+    small = late_sum(after(late_got, early))
     turn, late_got = late_phase(3)
     early = jnp.concatenate([early, after(got, turn)])
     got = exchange(early, *plan[1])
-    small = late_sum(late_got)
+    small = late_sum(after(late_got, early))
     late = add_rest(jnp.concatenate([add_up(late, 0, thin), small]))
     late, small = late[:thin], late[thin:]
     late_got = exchange(late, *plan[0])
@@ -1055,24 +1090,23 @@
     late = jnp.concatenate([late, late_got])
     late = jnp.concatenate([late, exchange(late, *plan[1])])
     early = jnp.concatenate([early, after(got, late)])
-    got = exchange(early, *plan[2])
-    late = (late, exchange(late, *plan[2]))
-    early = (early, got)
     square = squares(early, late, norm_grad)
+    square = square + swap(square, "dp", 1)
+    got = exchange(after(jnp.concatenate([late, early]), square), *plan[2])
     square = square + swap(square, "shard", 1)
     square = (square, swap(square, "shard", 2))
-    index = gather_index()
-    clip_norm = jnp.sqrt(square[0][0, 0] + square[1][0, 0])
     attn = (attn_master, attn_first, attn_second)
     up = (up_master, up_first, up_second)
     down = (down_master, down_first, down_second)
     norms = (norm_master, norm_first, norm_second)
-    leaving = renew_first(half, index, square, early, late, norm_grad, attn, up, norms)
-    *new, low, high = update(
-        index, square, early, after(late, leaving), norm_grad, attn, up, down, norms
+    first, second, clip_norm = renew(
+        half, index, square, early, late, norm_grad, attn, up, down, norms
     )
-    copies = share_copies(pos, half, low, high, leaving, width, hidden)
-    return (y, dx) + tuple(new) + (clip_norm,) + tuple(copies)
+    *new, low, high, direct = update(
+        half, index, square, early, late, after(got, first), norm_grad, attn, up, down, norms
+    )
+    copies = share_copies(pos, half, first, second, low, high, direct, width, hidden)
+    return (y, dx) + tuple(new) + (clip_norm.reshape(()),) + tuple(copies)
 
 
 def solution(mesh):

time: 224 us -> 221 us (0.987)
  waiting for transfers between devices: 65.7 us -> 59 us
  starting transfers between devices: 37.9 us -> 44 us
    ppermute x41 -> x45, waiting for transfers between devices: 65.7 us -> 59 us  [exchange(): return lax.ppermute(values, ('dp', 'shard'), perm)]
    ppermute x41 -> x45, starting transfers between devices: 37.9 us -> 44 us  [exchange(): return lax.ppermute(values, ('dp', 'shard'), perm)]
    slice x3 -> x2, local copies, waits for them, and re-layouts: 3.07 us -> 0.77 us  [the longest x1 0.75 us: share_copies(): last_rows = swap(first[FIRST_UNITS * half:], 'shard', 1)]
    unnamed x50 -> x56, local copies, waits for them, and re-layouts: 4.33 us -> 5.24 us
    convert_element_type x14 -> x13, other arithmetic: 7.03 us -> 6.98 us  [add_up(): return total.astype(BF)]
  transfers between devices with their start and end apart: 41 -> 45, of which waited for: 24 -> 26; matrix products, arithmetic and copies ran while one was open for 4% -> 3% of each run, Pallas kernels for 28% -> 31%
where the time goes in v5:
time: 221 us; the launch traced here: 220 us
  Pallas kernels  98 us (44%)
  waiting for transfers between devices  59 us (27%)
  starting transfers between devices  44 us (20%)
  other arithmetic  11 us (5%)
  local copies, waits for them, and re-layouts  6.18 us (3%)
  between operations  2.23 us (1%)
    ppermute x45, waiting for transfers between devices, exchange(): return lax.ppermute(values, ('dp', 'shard'), perm)  59 us
    ppermute x45, starting transfers between devices, exchange(): return lax.ppermute(values, ('dp', 'shard'), perm)  44 us
    pallas_call x1, Pallas kernels, feed(): pl.pallas_call(feed_kernel, grid=(4,), in_specs=[pl.BlockSpec(memory_spac...  26.5 us
    pallas_call x2, Pallas kernels, mix_back(): pl.pallas_call(functools.partial(mix_back_kernel, begun=bool(before)), gr...  22.2 us
    pallas_call x1, Pallas kernels, attend(): pl.pallas_call(attend_kernel, grid=(steps,), in_specs=[pl.BlockSpec(memor...  16.9 us
    pallas_call x1, Pallas kernels, update(): pl.pallas_call(update_kernel, grid=(steps,), in_specs=[smem] * 2 + [whole...  11.2 us
    convert_element_type x13, other arithmetic, add_up(): return total.astype(BF)  6.98 us
    pallas_call x1, Pallas kernels, renew(): pl.pallas_call(renew_kernel, grid_spec=pltpu.PrefetchScalarGridSpec(num_s...  5.74 us
  transfers between devices with their start and end apart: 45, of which 26 were waited for; matrix products, arithmetic and copies ran while one was open for 3% of the time, Pallas kernels for 31%

profile of v5, /device:TPU:0, one launch (start us, length us, event | category | flops | bytes accessed | tf_op | source)
XLA Modules:
  0.0 220.3 jit_solution(8893762138547164923)
XLA Ops:
  3.0 2.6 %collective-permute-start.1 = (bf16[272,512]{1,0:T(8,128)(2,1)S(1)}, bf16[272,512]{1,0:T(8,128)(2,1)}, u32[]{:S(2)}, u32[]{:S(2)}) collective-permute-start(bf16[272,512]{1,0:T(8,128)(2,1)S(1)} %constant_dynamic-slice_fusion), channel_id=1, source_target_pairs={{0,2},{1,3},{2,0},{3,1},{4,6},{5,7},{6,4},{7,5},{8,10},{9,11},{10,... | collective-permute-start | bytes 835592 | tf_op jit(solution)/shard_map/ppermute | solution.py:601
  7.9 1.9 collective-permute-done.2
  11.4 2.0 collective-permute-done.3
  15.1 2.7 %collective-permute-start.10 = (f32[8]{0:T(128)S(1)}, f32[8]{0:T(128)S(1)}, u32[]{:S(2)}, u32[]{:S(2)}) collective-permute-start(f32[8]{0:T(128)S(1)} %fusion.13), channel_id=1, source_target_pairs={{0,16},{1,17},{2,18},{3,19},{4,20},{5,21},{6,22},{7,23},{8,24},{9,... | collective-permute-start | bytes 104 | tf_op jit(solution)/shard_map/ppermute | solution.py:601
  19.6 2.1 collective-permute-done.4.far1
  25.7 16.9 %attend.1 = (bf16[1024,512]{1,0:T(8,128)(2,1)S(1)}, bf16[1024,512]{1,0:T(8,128)(2,1)S(1)}, bf16[1024,512]{1,0:T(8,128)(2,1)S(1)}, bf16[1024,512]{1,0:T(8,128)(2,...) custom-call(s32[4]{0:T(128)S(1)} %iota_xor_fusion.pos_ref, ...), custom_call_target="tpu_custom_call" | custom-call | flops 1 | bytes 1 | tf_op jit(solution)/shard_map/attend/pallas_call | solution.py:217
  45.0 2.4 %collective-permute-done.11.t1 = bf16[528,512]{1,0:T(8,128)(2,1)S(1)} collective-permute-done((bf16[528,512]{1,0:T(8,128)(2,1)S(1)}, bf16[528,512]{1,0:T(8,128)(2,1)S(1)}, u32[]{:S(2)}, u32[]{:S(2)}) %collective-permute-start.11) | collective-permute-done | bytes 540704 | tf_op jit(solution)/shard_map/ppermute | solution.py:601
  47.8 26.5 %feed.1 = (bf16[1024,512]{1,0:T(8,128)(2,1)}, f32[1024,512]{1,0:T(8,128)}, bf16[1024,512]{1,0:T(8,128)(2,1)S(1)}, bf16[2304,512]{1,0:T(8,128)(2,1)}, bf16[2304,512]{1,0:T(8,128)(2,1)}, /*index=5*/f32[8,512]{1,0:T(8,128)S(1)}) custom-call(s32[4]{0:T(128)S(1)} %iota_xor_fusion.pos_ref, s32[2,16]{1,0:T(2,128)S(1)} %pad_add_fusion.place_ref, ...), custom_call_target="tpu_custom_call" | custom-call | flops 1 | bytes 1 | tf_op jit(solution)/shard_map/feed/pallas_call | solution.py:452
  74.5 6.0 %mix_back.2 = (bf16[256,512]{1,0:T(8,128)(2,1)S(1)}, bf16[256,512]{1,0:T(8,128)(2,1)S(1)}, bf16[256,512]{1,0:T(8,128)(2,1)S(1)}, bf16[256,512]{1,0:T(8,128)(2,1)...) custom-call(bf16[1024,512]{1,0:T(8,128)(2,1)S(1)} %get-tuple-element.134.refs_0_, ...), custom_call_target="tpu_custom_call" | custom-call | flops 1 | bytes 1 | tf_op jit(solution)/shard_map/mix_back/pallas_call | solution.py:300
  83.0 16.2 %mix_back.3 = (bf16[768,512]{1,0:T(8,128)(2,1)S(1)}, bf16[768,512]{1,0:T(8,128)(2,1)S(1)}, bf16[768,512]{1,0:T(8,128)(2,1)S(1)}, bf16[768,512]{1,0:T(8,128)(2,1)...) custom-call(bf16[1024,512]{1,0:T(8,128)(2,1)S(1)} %get-tuple-element.134.refs_0_, ...), custom_call_target="tpu_custom_call" | custom-call | flops 1 | bytes 1 | tf_op jit(solution)/shard_map/mix_back/pallas_call | solution.py:300
  102.1 5.5 %input_back.1 = (f32[1024,512]{1,0:T(8,128)}, bf16[16,512]{1,0:T(8,128)(2,1)S(1)}) custom-call(bf16[1024,512]{1,0:T(8,128)(2,1)S(1)} %copy-done.1, f32[1024,512]{1,0:T(8,128)S(1)} %copy-done.8, bf16[4,512,512]{2,1,0:T(8,128)(2,1)S(1)} %copy-done.7, f32[8,512]{1,0:T(8,128)S(1)} %get-tuple-element.112.norm_ref, f32[8,512]{1,0:T(8,128)S(1)} %get-tuple-element.142.dnorm_ref, ...), custom_call_target="tpu_custom_call" | custom-call | flops 1 | bytes 1 | tf_op jit(solution)/shard_map/input_back/pallas_call | solution.py:570
  107.6 4.2 %weight_back.1 = (bf16[1040,512]{1,0:T(8,128)(2,1)S(1)}, bf16[1040,512]{1,0:T(8,128)(2,1)S(1)}) custom-call(s32[4]{0:T(128)S(1)} %iota_xor_fusion.pos_ref, s32[2,16]{1,0:T(2,128)S(1)} %pad_add_fusion.place_ref, bf16[16,512]{1,0:T(8,128)(2,1)S(1)} %get-tuple-element.150.small_ref, bf16[1024,512]{1,0:T(8,128)(2,1)S(1)} %get-tuple-element.151.n_ref, ...), custom_call_target="tpu_custom_call" | custom-call | flops 1 | bytes 1 | tf_op jit(solution)/shard_map/weight_back/pallas_call | solution.py:512
  113.9 2.3 %collective-permute-done.18 = bf16[1040,512]{1,0:T(8,128)(2,1)S(1)} collective-permute-done((bf16[1040,512]{1,0:T(8,128)(2,1)S(1)}, bf16[1040,512]{1,0:T(8,128)(2,1)S(1)}, u32[]{:S(2)}, u32[]{:S(2)}) %collective-permute-start.18) | collective-permute-done | bytes 1064992 | tf_op jit(solution)/shard_map/ppermute | solution.py:601
  119.1 6.8 %collective-permute-done.19 = bf16[528,512]{1,0:T(8,128)(2,1)S(1)} collective-permute-done((bf16[528,512]{1,0:T(8,128)(2,1)S(1)}, bf16[528,512]{1,0:T(8,128)(2,1)S(1)}, u32[]{:S(2)}, u32[]{:S(2)}) %collective-permute-start.19) | collective-permute-done | bytes 540704 | tf_op jit(solution)/shard_map/ppermute | solution.py:601
  127.6 2.6 %collective-permute-start.20 = (bf16[144,512]{1,0:T(8,128)(2,1)S(1)}, bf16[144,512]{1,0:T(8,128)(2,1)S(1)}, u32[]{:S(2)}, u32[]{:S(2)}) collective-permute-start(bf16[144,512]{1,0:T(8,128)(2,1)S(1)} %add_convert_fusion.6), channel_id=1, source_target_pairs={{0,16},{1,3},{2,18},{3,1},{4,20},{5,7},{6,22},{7,5},{8,24},{9,11},... | collective-permute-start | bytes 442376 | tf_op jit(solution)/shard_map/ppermute | solution.py:601
  130.3 2.3 %collective-permute-done.21 = bf16[272,512]{1,0:T(8,128)(2,1)S(1)} collective-permute-done((bf16[272,512]{1,0:T(8,128)(2,1)S(1)}, bf16[272,512]{1,0:T(8,128)(2,1)S(1)}, u32[]{:S(2)}, u32[]{:S(2)}) %collective-permute-start.21) | collective-permute-done | bytes 278560 | tf_op jit(solution)/shard_map/ppermute | solution.py:601
  133.9 3.1 %collective-permute-done.20 = bf16[144,512]{1,0:T(8,128)(2,1)S(1)} collective-permute-done((bf16[144,512]{1,0:T(8,128)(2,1)S(1)}, bf16[144,512]{1,0:T(8,128)(2,1)S(1)}, u32[]{:S(2)}, u32[]{:S(2)}) %collective-permute-start.20) | collective-permute-done | bytes 147488 | tf_op jit(solution)/shard_map/ppermute | solution.py:601
  140.7 3.0 %collective-permute-start.25 = (bf16[80,512]{1,0:T(8,128)(2,1)S(1)}, bf16[80,512]{1,0:T(8,128)(2,1)S(1)}, u32[]{:S(2)}, u32[]{:S(2)}) collective-permute-start(bf16[80,512]{1,0:T(8,128)(2,1)S(1)} %pad_maximum_fusion.7), channel_id=1, source_target_pairs={{0,16},{1,3},{2,18},{3,1},{4,20},{5,7},{6,22},{7,5},{8,24},{9,11},... | collective-permute-start | bytes 245768 | tf_op jit(solution)/shard_map/ppermute | solution.py:601
  143.8 3.8 %collective-permute-done.25 = bf16[80,512]{1,0:T(8,128)(2,1)S(1)} collective-permute-done((bf16[80,512]{1,0:T(8,128)(2,1)S(1)}, bf16[80,512]{1,0:T(8,128)(2,1)S(1)}, u32[]{:S(2)}, u32[]{:S(2)}) %collective-permute-start.25) | collective-permute-done | bytes 81952 | tf_op jit(solution)/shard_map/ppermute | solution.py:601
  147.8 3.1 %collective-permute-start.24 = (bf16[288,512]{1,0:T(8,128)(2,1)S(1)}, bf16[288,512]{1,0:T(8,128)(2,1)S(1)}, u32[]{:S(2)}, u32[]{:S(2)}) collective-permute-start(bf16[288,512]{1,0:T(8,128)(2,1)S(1)} %pad_maximum_fusion.2), channel_id=1, source_target_pairs={{0,16},{1,9},{2,18},{3,11},{4,20},{5,13},{6,22},{7,15},{8,24},{9,1... | collective-permute-start | bytes 884744 | tf_op jit(solution)/shard_map/ppermute | solution.py:601
  150.9 3.2 %collective-permute-done.26 = bf16[64,512]{1,0:T(8,128)(2,1)S(1)} collective-permute-done((bf16[64,512]{1,0:T(8,128)(2,1)S(1)}, bf16[64,512]{1,0:T(8,128)(2,1)S(1)}, u32[]{:S(2)}, u32[]{:S(2)}) %collective-permute-start.26) | collective-permute-done | bytes 65568 | tf_op jit(solution)/shard_map/ppermute | solution.py:601
  154.4 7.2 %collective-permute-done.27 = bf16[128,512]{1,0:T(8,128)(2,1)S(1)} collective-permute-done((bf16[128,512]{1,0:T(8,128)(2,1)S(1)}, bf16[128,512]{1,0:T(8,128)(2,1)S(1)}, u32[]{:S(2)}, u32[]{:S(2)}) %collective-permute-start.27) | collective-permute-done | bytes 131104 | tf_op jit(solution)/shard_map/ppermute | solution.py:601
  162.3 3.1 %collective-permute-start.28 = (f32[8,128]{1,0:T(8,128)S(1)}, f32[8,128]{1,0:T(8,128)S(1)}, u32[]{:S(2)}, u32[]{:S(2)}) collective-permute-start(f32[8,128]{1,0:T(8,128)S(1)} %squares.1), channel_id=1, source_target_pairs={{0,4},{1,5},{2,6},{3,7},{4,0},{5,1},{6,2},{7,3},{8,12},{9,13},{10,... | collective-permute-start | bytes 12296 | tf_op jit(solution)/shard_map/ppermute | solution.py:601
  165.4 1.7 collective-permute-done.28
  167.1 2.0 collective-permute-start.31
  174.5 5.7 %renew.1 = (bf16[464,512]{1,0:T(8,128)(2,1)}, bf16[384,512]{1,0:T(8,128)(2,1)}, f32[1]{0:T(128)}) custom-call(s32[1]{0:T(128)} %bitcast.2.half_ref.side_ref, s32[4]{0:T(128)} %and_select_fusion.index_ref, f32[8,128]{1,0:T(8,128)} %copy-done.18, f32[8,128]{1,0:T(8,128)} %copy-done.20, bf16[576,512]{1,0:T(8,128)(2,1)} %copy-done, bf16[256,512]{1,0:T(8,128)(2,1)} %copy-done.3, ...), custom_call_target="tpu_custom_call" | custom-call | flops 1 | bytes 1 | tf_op jit(solution)/shard_map/renew/pallas_call | solution.py:744
  183.3 11.2 %update.1 = (f32[5,128,512]{2,1,0:T(8,128)}, f32[5,128,512]{2,1,0:T(8,128)}, f32[5,128,512]{2,1,0:T(8,128)}, f32[128,2048]{1,0:T(8,128)}, f32[128,2048]{1,0:T(8,...) custom-call(s32[1]{0:T(128)} %bitcast.2.half_ref.side_ref, ...), custom_call_target="tpu_custom_call" | custom-call | flops 1 | bytes 1 | tf_op jit(solution)/shard_map/update/pallas_call | solution.py:839
  196.6 2.1 collective-permute-done.35.p5
  202.2 2.9 %unpack_near.1 = (bf16[5,512,512]{2,1,0:T(8,128)(2,1)}, bf16[512,2048]{1,0:T(8,128)(2,1)}, bf16[2048,512]{1,0:T(8,128)(2,1)}) custom-call(s32[4]{0:T(128)S(1)} %iota_xor_fusion.pos_ref, s32[1]{0:T(128)} %bitcast.2.half_ref.side_ref, bf16[1024,512]{1,0:T(8,128)(2,1)S(1)} %copy-done.10, bf16[640,512]{1,0:T(8,128)(2,1)S(1)} %copy-done.11, ...), custom_call_target="tpu_custom_call" | custom-call | flops 1 | bytes 1 | tf_op jit(solution)/shard_map/unpack_near/pallas_call | solution.py:945
  205.1 3.3 %collective-permute-done.38.refs_1_ = bf16[464,512]{1,0:T(8,128)(2,1)S(1)} collective-permute-done((bf16[464,512]{1,0:T(8,128)(2,1)S(1)}, bf16[464,512]{1,0:T(8,128)(2,1)S(1)}, u32[]{:S(2)}, u32[]{:S(2)}) %collective-permute-start.38) | collective-permute-done | bytes 475168 | tf_op jit(solution)/shard_map/ppermute | solution.py:601
  209.6 6.2 %collective-permute-done.40.refs_3_ = bf16[192,512]{1,0:T(8,128)(2,1)S(1)} collective-permute-done((bf16[192,512]{1,0:T(8,128)(2,1)S(1)}, bf16[192,512]{1,0:T(8,128)(2,1)S(1)}, u32[]{:S(2)}, u32[]{:S(2)}) %collective-permute-start.40) | collective-permute-done | bytes 196640 | tf_op jit(solution)/shard_map/ppermute | solution.py:601
  217.7 2.4 %unpack_far.1 = (bf16[5,512,512]{2,1,0:T(8,128)(2,1)}, bf16[512,2048]{1,0:T(8,128)(2,1)}, bf16[2048,512]{1,0:T(8,128)(2,1)}) custom-call(s32[4]{0:T(128)S(1)} %iota_xor_fusion.pos_ref, s32[1]{0:T(128)} %bitcast.2.half_ref.side_ref, ...), custom_call_target="tpu_custom_call", output_to_operand_aliasing={{0}: (10, {}), {1}: (11, {}), {2}: (12, {})} | custom-call | flops 1 | bytes 1 | tf_op jit(solution)/shard_map/unpack_far/pallas_call | solution.py:960
  (180 shorter events, 51.2 us)
Async XLA Ops:
  2.4 23.0 %collective-permute-start = (bf16[544,512]{1,0:T(8,128)(2,1)S(1)}, bf16[544,512]{1,0:T(8,128)(2,1)}, u32[]{:S(2)}, u32[]{:S(2)}) collective-permute-start(bf16[544,512]{1,0:T(8,128)(2,1)S(1)} %fusion.5.near0), channel_id=1, source_target_pairs={{0,1},{1,0},{2,3},{3,2},{4,5},{5,4},{6,7},{7,6},{8,9},{9,8},{10,11... | collective-permute-start | bytes 1671176 | tf_op jit(solution)/shard_map/ppermute | solution.py:601
  3.0 10.4 %collective-permute-start.1 = (bf16[272,512]{1,0:T(8,128)(2,1)S(1)}, bf16[272,512]{1,0:T(8,128)(2,1)}, u32[]{:S(2)}, u32[]{:S(2)}) collective-permute-start(bf16[272,512]{1,0:T(8,128)(2,1)S(1)} %constant_dynamic-slice_fusion), channel_id=1, source_target_pairs={{0,2},{1,3},{2,0},{3,1},{4,6},{5,7},{6,4},{7,5},{8,10},{9,11},{10,... | collective-permute-start | bytes 835592 | tf_op jit(solution)/shard_map/ppermute | solution.py:601
  13.4 8.3 %collective-permute-start.4 = (bf16[272,512]{1,0:T(8,128)(2,1)}, bf16[272,512]{1,0:T(8,128)(2,1)}, u32[]{:S(2)}, u32[]{:S(2)}) collective-permute-start(bf16[272,512]{1,0:T(8,128)(2,1)} %collective-permute-done.1.far0), channel_id=1, source_target_pairs={{0,4},{1,5},{2,6},{3,7},{4,0},{5,1},{6,2},{7,3},{8,12},{9,13},{10,... | collective-permute-start | bytes 835592 | tf_op jit(solution)/shard_map/ppermute | solution.py:601
  15.1 4.5 %collective-permute-start.10 = (f32[8]{0:T(128)S(1)}, f32[8]{0:T(128)S(1)}, u32[]{:S(2)}, u32[]{:S(2)}) collective-permute-start(f32[8]{0:T(128)S(1)} %fusion.13), channel_id=1, source_target_pairs={{0,16},{1,17},{2,18},{3,19},{4,20},{5,21},{6,22},{7,23},{8,24},{9,... | collective-permute-start | bytes 104 | tf_op jit(solution)/shard_map/ppermute | solution.py:601
  17.8 26.1 %collective-permute-start.8 = (bf16[640,512]{1,0:T(8,128)(2,1)S(1)}, bf16[640,512]{1,0:T(8,128)(2,1)S(1)}, u32[]{:S(2)}, u32[]{:S(2)}) collective-permute-start(bf16[640,512]{1,0:T(8,128)(2,1)S(1)} %slice_dynamic-update-slice_fusion.p0), channel_id=1, source_target_pairs={{0,2},{1,3},{2,0},{3,1},{4,6},{5,7},{6,4},{7,5},{8,10},{9,11},{10,... | collective-permute-start | bytes 1966088 | tf_op jit(solution)/shard_map/ppermute | solution.py:601
  21.8 23.2 %collective-permute-start.12 = (bf16[528,512]{1,0:T(8,128)(2,1)S(1)}, bf16[528,512]{1,0:T(8,128)(2,1)}, u32[]{:S(2)}, u32[]{:S(2)}) collective-permute-start(bf16[528,512]{1,0:T(8,128)(2,1)S(1)} %fusion.6.t0), channel_id=1, source_target_pairs={{0,2},{1,3},{2,0},{3,1},{4,6},{5,7},{6,4},{7,5},{8,10},{9,11},{10,... | collective-permute-start | bytes 1622024 | tf_op jit(solution)/shard_map/ppermute | solution.py:601
  25.3 19.7 %collective-permute-start.7 = (bf16[640,512]{1,0:T(8,128)(2,1)S(1)}, bf16[640,512]{1,0:T(8,128)(2,1)S(1)}, u32[]{:S(2)}, u32[]{:S(2)}) collective-permute-start(bf16[640,512]{1,0:T(8,128)(2,1)S(1)} %slice_dynamic-update-slice_fusion.p0), channel_id=1, source_target_pairs={{0,1},{1,0},{2,3},{3,2},{4,5},{5,4},{6,7},{7,6},{8,9},{9,8},{10,11... | collective-permute-start | bytes 1966088 | tf_op jit(solution)/shard_map/ppermute | solution.py:601
  74.3 6.2 %collective-permute-start.14 = (bf16[2304,512]{1,0:T(8,128)(2,1)}, bf16[2304,512]{1,0:T(8,128)(2,1)}, u32[]{:S(2)}, u32[]{:S(2)}) collective-permute-start(bf16[2304,512]{1,0:T(8,128)(2,1)} %get-tuple-element.120), channel_id=1, source_target_pairs={{0,1},{1,0},{2,3},{3,2},{4,5},{5,4},{6,7},{7,6},{8,9},{9,8},{10,11... | collective-permute-start | bytes 7077896 | tf_op jit(solution)/shard_map/ppermute | solution.py:601
  82.1 17.0 %collective-permute-start.15 = (bf16[1152,512]{1,0:T(8,128)(2,1)S(1)}, bf16[1152,512]{1,0:T(8,128)(2,1)}, u32[]{:S(2)}, u32[]{:S(2)}) collective-permute-start(bf16[1152,512]{1,0:T(8,128)(2,1)S(1)} %add_convert_fusion), channel_id=1, source_target_pairs={{0,2},{1,5},{2,0},{3,7},{4,6},{5,1},{6,4},{7,3},{8,10},{9,13},{10,... | collective-permute-start | bytes 3538952 | tf_op jit(solution)/shard_map/ppermute | solution.py:601
  100.8 11.0 %collective-permute-start.16 = (bf16[576,512]{1,0:T(8,128)(2,1)S(1)}, bf16[576,512]{1,0:T(8,128)(2,1)S(1)}, u32[]{:S(2)}, u32[]{:S(2)}) collective-permute-start(bf16[576,512]{1,0:T(8,128)(2,1)S(1)} %add_convert_fusion.1), channel_id=1, source_target_pairs={{0,4},{1,9},{2,6},{3,11},{4,0},{5,13},{6,2},{7,15},{8,12},{9,1},{1... | collective-permute-start | bytes 1769480 | tf_op jit(solution)/shard_map/ppermute | solution.py:601
  116.4 9.4 %collective-permute-start.19 = (bf16[528,512]{1,0:T(8,128)(2,1)S(1)}, bf16[528,512]{1,0:T(8,128)(2,1)S(1)}, u32[]{:S(2)}, u32[]{:S(2)}) collective-permute-start(bf16[528,512]{1,0:T(8,128)(2,1)S(1)} %pad_maximum_fusion.1), channel_id=1, source_target_pairs={{0,2},{1,5},{2,0},{3,7},{4,6},{5,1},{6,4},{7,3},{8,10},{9,13},{10,... | collective-permute-start | bytes 1622024 | tf_op jit(solution)/shard_map/ppermute | solution.py:601
  117.5 9.1 %collective-permute-start.17 = (bf16[288,512]{1,0:T(8,128)(2,1)S(1)}, bf16[288,512]{1,0:T(8,128)(2,1)S(1)}, u32[]{:S(2)}, u32[]{:S(2)}) collective-permute-start(bf16[288,512]{1,0:T(8,128)(2,1)S(1)} %add_convert_fusion.3), channel_id=1, source_target_pairs={{0,8},{1,17},{2,10},{3,19},{4,12},{5,21},{6,14},{7,23},{8,0},{9,25... | collective-permute-start | bytes 884744 | tf_op jit(solution)/shard_map/ppermute | solution.py:601
  126.0 6.6 %collective-permute-start.21 = (bf16[272,512]{1,0:T(8,128)(2,1)S(1)}, bf16[272,512]{1,0:T(8,128)(2,1)S(1)}, u32[]{:S(2)}, u32[]{:S(2)}) collective-permute-start(bf16[272,512]{1,0:T(8,128)(2,1)S(1)} %pad_maximum_fusion.3), channel_id=1, source_target_pairs={{0,4},{1,9},{2,6},{3,11},{4,0},{5,13},{6,2},{7,15},{8,12},{9,1},{1... | collective-permute-start | bytes 835592 | tf_op jit(solution)/shard_map/ppermute | solution.py:601
  127.6 9.4 %collective-permute-start.20 = (bf16[144,512]{1,0:T(8,128)(2,1)S(1)}, bf16[144,512]{1,0:T(8,128)(2,1)S(1)}, u32[]{:S(2)}, u32[]{:S(2)}) collective-permute-start(bf16[144,512]{1,0:T(8,128)(2,1)S(1)} %add_convert_fusion.6), channel_id=1, source_target_pairs={{0,16},{1,3},{2,18},{3,1},{4,20},{5,7},{6,22},{7,5},{8,24},{9,11},... | collective-permute-start | bytes 442376 | tf_op jit(solution)/shard_map/ppermute | solution.py:601
  132.7 8.0 %collective-permute-start.23 = (bf16[144,512]{1,0:T(8,128)(2,1)S(1)}, bf16[144,512]{1,0:T(8,128)(2,1)S(1)}, u32[]{:S(2)}, u32[]{:S(2)}) collective-permute-start(bf16[144,512]{1,0:T(8,128)(2,1)S(1)} %pad_maximum_fusion.5), channel_id=1, source_target_pairs={{0,8},{1,17},{2,10},{3,19},{4,12},{5,21},{6,14},{7,23},{8,0},{9,25... | collective-permute-start | bytes 442376 | tf_op jit(solution)/shard_map/ppermute | solution.py:601
  138.1 5.6 %collective-permute-start.22 = (bf16[144,512]{1,0:T(8,128)(2,1)S(1)}, bf16[144,512]{1,0:T(8,128)(2,1)S(1)}, u32[]{:S(2)}, u32[]{:S(2)}) collective-permute-start(bf16[144,512]{1,0:T(8,128)(2,1)S(1)} %add_convert_fusion.5), channel_id=1, source_target_pairs={{0,8},{1,17},{2,10},{3,19},{4,12},{5,21},{6,14},{7,23},{8,0},{9,25... | collective-permute-start | bytes 442376 | tf_op jit(solution)/shard_map/ppermute | solution.py:601
  140.7 6.8 %collective-permute-start.25 = (bf16[80,512]{1,0:T(8,128)(2,1)S(1)}, bf16[80,512]{1,0:T(8,128)(2,1)S(1)}, u32[]{:S(2)}, u32[]{:S(2)}) collective-permute-start(bf16[80,512]{1,0:T(8,128)(2,1)S(1)} %pad_maximum_fusion.7), channel_id=1, source_target_pairs={{0,16},{1,3},{2,18},{3,1},{4,20},{5,7},{6,22},{7,5},{8,24},{9,11},... | collective-permute-start | bytes 245768 | tf_op jit(solution)/shard_map/ppermute | solution.py:601
  147.6 6.5 %collective-permute-start.26 = (bf16[64,512]{1,0:T(8,128)(2,1)S(1)}, bf16[64,512]{1,0:T(8,128)(2,1)S(1)}, u32[]{:S(2)}, u32[]{:S(2)}) collective-permute-start(bf16[64,512]{1,0:T(8,128)(2,1)S(1)} %get-tuple-element.202), channel_id=1, source_target_pairs={{0,8},{1,17},{2,10},{3,19},{4,12},{5,21},{6,14},{7,23},{8,0},{9,25... | collective-permute-start | bytes 196616 | tf_op jit(solution)/shard_map/ppermute | solution.py:601
  147.8 13.9 %collective-permute-start.24 = (bf16[288,512]{1,0:T(8,128)(2,1)S(1)}, bf16[288,512]{1,0:T(8,128)(2,1)S(1)}, u32[]{:S(2)}, u32[]{:S(2)}) collective-permute-start(bf16[288,512]{1,0:T(8,128)(2,1)S(1)} %pad_maximum_fusion.2), channel_id=1, source_target_pairs={{0,16},{1,9},{2,18},{3,11},{4,20},{5,13},{6,22},{7,15},{8,24},{9,1... | collective-permute-start | bytes 884744 | tf_op jit(solution)/shard_map/ppermute | solution.py:601
  154.1 7.5 %collective-permute-start.27 = (bf16[128,512]{1,0:T(8,128)(2,1)S(1)}, bf16[128,512]{1,0:T(8,128)(2,1)S(1)}, u32[]{:S(2)}, u32[]{:S(2)}) collective-permute-start(bf16[128,512]{1,0:T(8,128)(2,1)S(1)} %pad_maximum_fusion.6), channel_id=1, source_target_pairs={{0,16},{1,9},{2,18},{3,11},{4,20},{5,13},{6,22},{7,15},{8,24},{9,1... | collective-permute-start | bytes 393224 | tf_op jit(solution)/shard_map/ppermute | solution.py:601
  162.3 4.8 %collective-permute-start.28 = (f32[8,128]{1,0:T(8,128)S(1)}, f32[8,128]{1,0:T(8,128)S(1)}, u32[]{:S(2)}, u32[]{:S(2)}) collective-permute-start(f32[8,128]{1,0:T(8,128)S(1)} %squares.1), channel_id=1, source_target_pairs={{0,4},{1,5},{2,6},{3,7},{4,0},{5,1},{6,2},{7,3},{8,12},{9,13},{10,... | collective-permute-start | bytes 12296 | tf_op jit(solution)/shard_map/ppermute | solution.py:601
  167.1 15.3 %collective-permute-start.31 = (bf16[832,512]{1,0:T(8,128)(2,1)S(1)}, bf16[832,512]{1,0:T(8,128)(2,1)S(1)}, u32[]{:S(2)}, u32[]{:S(2)}) collective-permute-start(bf16[832,512]{1,0:T(8,128)(2,1)S(1)} %constant_dynamic-update-slice_fusion), channel_id=1, source_target_pairs={{0,4},{1,5},{2,6},{3,7},{4,0},{5,1},{6,2},{7,3},{8,12},{9,13},{10,... | collective-permute-start | bytes 2555912 | tf_op jit(solution)/shard_map/ppermute | solution.py:601
  180.2 14.3 %collective-permute-start.32 = (bf16[464,512]{1,0:T(8,128)(2,1)}, bf16[464,512]{1,0:T(8,128)(2,1)S(1)}, u32[]{:S(2)}, u32[]{:S(2)}) collective-permute-start(bf16[464,512]{1,0:T(8,128)(2,1)} %get-tuple-element.163), channel_id=1, source_target_pairs={{0,2},{1,3},{2,0},{3,1},{4,6},{5,7},{6,4},{7,5},{8,10},{9,11},{10,... | collective-permute-start | bytes 1425416 | tf_op jit(solution)/shard_map/ppermute | solution.py:601
  182.4 12.1 %collective-permute-start.33 = (bf16[16,512]{1,0:T(8,128)(2,1)S(1)}, bf16[16,512]{1,0:T(8,128)(2,1)S(1)}, u32[]{:S(2)}, u32[]{:S(2)}) collective-permute-start(bf16[16,512]{1,0:T(8,128)(2,1)S(1)} %slice.251), channel_id=1, source_target_pairs={{0,1},{1,0},{2,3},{3,2},{4,5},{5,4},{6,7},{7,6},{8,9},{9,8},{10,11... | collective-permute-start | bytes 49160 | tf_op jit(solution)/shard_map/ppermute | solution.py:601
  194.5 5.4 %collective-permute-start.36 = (bf16[1024,512]{1,0:T(8,128)(2,1)}, bf16[1024,512]{1,0:T(8,128)(2,1)S(1)}, u32[]{:S(2)}, u32[]{:S(2)}) collective-permute-start(bf16[1024,512]{1,0:T(8,128)(2,1)} %get-tuple-element.186.p0), channel_id=1, source_target_pairs={{0,1},{1,0},{2,3},{3,2},{4,5},{5,4},{6,7},{7,6},{8,9},{9,8},{10,11... | collective-permute-start | bytes 3145736 | tf_op jit(solution)/shard_map/ppermute | solution.py:601
  195.2 4.7 %collective-permute-start.37 = (bf16[640,512]{1,0:T(8,128)(2,1)}, bf16[640,512]{1,0:T(8,128)(2,1)S(1)}, u32[]{:S(2)}, u32[]{:S(2)}) collective-permute-start(bf16[640,512]{1,0:T(8,128)(2,1)} %get-tuple-element.187.p1), channel_id=1, source_target_pairs={{0,1},{1,0},{2,3},{3,2},{4,5},{5,4},{6,7},{7,6},{8,9},{9,8},{10,11... | collective-permute-start | bytes 1966088 | tf_op jit(solution)/shard_map/ppermute | solution.py:601
  195.6 12.9 %collective-permute-start.38 = (bf16[464,512]{1,0:T(8,128)(2,1)S(1)}, bf16[464,512]{1,0:T(8,128)(2,1)S(1)}, u32[]{:S(2)}, u32[]{:S(2)}) collective-permute-start(bf16[464,512]{1,0:T(8,128)(2,1)S(1)} %collective-permute-done.32.p4), channel_id=1, source_target_pairs={{0,4},{1,5},{2,6},{3,7},{4,0},{5,1},{6,2},{7,3},{8,12},{9,13},{10,... | collective-permute-start | bytes 1425416 | tf_op jit(solution)/shard_map/ppermute | solution.py:601
  195.8 12.7 %collective-permute-start.34 = (bf16[384,512]{1,0:T(8,128)(2,1)S(1)}, bf16[384,512]{1,0:T(8,128)(2,1)S(1)}, u32[]{:S(2)}, u32[]{:S(2)}) collective-permute-start(bf16[384,512]{1,0:T(8,128)(2,1)S(1)} %copy-done.21), channel_id=1, source_target_pairs={{0,2},{1,3},{2,0},{3,1},{4,6},{5,7},{6,4},{7,5},{8,10},{9,11},{10,... | collective-permute-start | bytes 1179656 | tf_op jit(solution)/shard_map/ppermute | solution.py:601
  208.5 9.3 %collective-permute-start.42 = (bf16[464,512]{1,0:T(8,128)(2,1)S(1)}, bf16[464,512]{1,0:T(8,128)(2,1)S(1)}, u32[]{:S(2)}, u32[]{:S(2)}) collective-permute-start(bf16[464,512]{1,0:T(8,128)(2,1)S(1)} %collective-permute-done.38.refs_1_), channel_id=1, source_target_pairs={{0,1},{1,0},{2,3},{3,2},{4,5},{5,4},{6,7},{7,6},{8,9},{9,8},{10,11... | collective-permute-start | bytes 1425416 | tf_op jit(solution)/shard_map/ppermute | solution.py:601
  208.5 7.3 %collective-permute-start.40 = (bf16[192,512]{1,0:T(8,128)(2,1)S(1)}, bf16[192,512]{1,0:T(8,128)(2,1)S(1)}, u32[]{:S(2)}, u32[]{:S(2)}) collective-permute-start(bf16[192,512]{1,0:T(8,128)(2,1)S(1)} %copy-done.22), channel_id=1, source_target_pairs={{0,2},{1,3},{2,0},{3,1},{4,6},{5,7},{6,4},{7,5},{8,10},{9,11},{10,... | collective-permute-start | bytes 589832 | tf_op jit(solution)/shard_map/ppermute | solution.py:601
  209.3 7.0 %collective-permute-start.39 = (bf16[192,512]{1,0:T(8,128)(2,1)S(1)}, bf16[192,512]{1,0:T(8,128)(2,1)S(1)}, u32[]{:S(2)}, u32[]{:S(2)}) collective-permute-start(bf16[192,512]{1,0:T(8,128)(2,1)S(1)} %slice.257), channel_id=1, source_target_pairs={{0,4},{1,5},{2,6},{3,7},{4,0},{5,1},{6,2},{7,3},{8,12},{9,13},{10,... | collective-permute-start | bytes 589832 | tf_op jit(solution)/shard_map/ppermute | solution.py:601
  209.6 8.1 %collective-permute-start.41 = (bf16[384,512]{1,0:T(8,128)(2,1)S(1)}, bf16[384,512]{1,0:T(8,128)(2,1)S(1)}, u32[]{:S(2)}, u32[]{:S(2)}) collective-permute-start(bf16[384,512]{1,0:T(8,128)(2,1)S(1)} %collective-permute-done.34.refs_0_), channel_id=1, source_target_pairs={{0,1},{1,0},{2,3},{3,2},{4,5},{5,4},{6,7},{7,6},{8,9},{9,8},{10,11... | collective-permute-start | bytes 1179656 | tf_op jit(solution)/shard_map/ppermute | solution.py:601
  (37 other events, 289.7 us)

commit v6 on v5

--- a/solution.py
+++ b/solution.py
@@ -21,7 +21,7 @@
 LANES = 128
 SMALL = 16
 FIRST_UNITS = 7
-DIRECT_UNITS = 3
+DIRECT_UNITS = 2
 CHEAP = pl.CostEstimate(flops=1, bytes_accessed=1, transcendentals=0)
 STEP = 10
 TILE = 512
@@ -586,10 +586,6 @@
     return [1 << b for b in range(size.bit_length() - 1)]
 
 
-def split_bits():
-    return bits_of(lax.axis_size("dp"))[:3]
-
-
 def exchange(values, even, odd):
     dp, shard = lax.axis_size("dp"), lax.axis_size("shard")
     perm = []
@@ -610,48 +606,51 @@
 
 
 def places():
-    count = 2 ** len(split_bits())
     dp, shard = lax.axis_index("dp"), lax.axis_index("shard")
-    piece = jnp.arange(2 * count, dtype=jnp.int32)
-    far = (piece // count) ^ (shard // 2)
-    along = (piece % count) ^ (dp % count)
-    order = 0
-    for b in range(len(split_bits())):
-        order = order * 2 + ((along >> b) & 1)
-    even, odd = far * count + order, order * 2 + far
+    piece = jnp.arange(16, dtype=jnp.int32)
+    far = (piece // 8) ^ (shard // 2)
+    along = (piece % 8) ^ (dp % 8)
+    bits = [(along >> b) & 1 for b in range(3)]
+    even = far * 8 + bits[0] * 4 + bits[2] * 2 + (piece >> 1 & 1)
+    odd = bits[0] * 8 + bits[1] * 4 + far * 2 + (piece >> 2 & 1)
     mine = shard % 2
     return jnp.stack(
         [jnp.where(mine == 0, even, odd), jnp.where(mine == 0, odd, even)]
     ).astype(jnp.int32)
 
 
-def phases():
-    split = [("dp", b) for b in split_bits()]
-    return list(zip([("shard", 2)] + split, split + [("shard", 2)]))
+HALVINGS = [
+    (("shard", 2), ("dp", 1)),
+    (("dp", 1), ("dp", 2)),
+    (("dp", 4), ("shard", 2)),
+]
+MIDDLE = (("dp", 2), ("dp", 4))
+GATHERS = [(("dp", 4), ("dp", 2)), (("dp", 1), ("dp", 1))]
+
+
+def quarters():
+    place = lax.axis_index("dp") % 8
+    j = jnp.arange(4, dtype=jnp.int32)
+    even = j % 2 + 2 * ((place // 4) ^ (j // 2))
+    odd = 2 * (j % 2) + ((place // 2 % 2) ^ (j // 2))
+    return jnp.where(lax.axis_index("shard") % 2 == 0, even, odd).astype(jnp.int32)
+
+
+def low_sum(total):
+    return lax.reduce_precision(total, 8, 7).astype(BF)
 
 
 def add_up(parts, low, high):
     total = parts[0][low:high].astype(F32)
     for part in parts[1:]:
         total = total + part[low:high].astype(F32)
-    return total.astype(BF)
+    return low_sum(total)
 
 
 def add_rest(piece):
     for b in bits_of(lax.axis_size("dp"))[3:]:
         piece = add_up([piece, swap(piece, "dp", b)], 0, piece.shape[0])
     return piece
-
-
-def gather_plan():
-    split = split_bits()
-    even = split[1:] + split[:1]
-    odd = split[1:][::-1] + split[:1]
-    mask = jnp.zeros((1,), jnp.int32)
-    for a, b in list(zip(even, odd))[:-1]:
-        mask = jnp.concatenate([mask, mask | jnp.where(lax.axis_index("shard") % 2 == 1, b, a)])
-    index = ((lax.axis_index("dp") % 2 ** len(split)) ^ mask) // 2
-    return [(("dp", a), ("dp", b)) for a, b in zip(even, odd)], index
 
 
 def adam(master, first, second, grad, rate, decay):
@@ -706,15 +705,29 @@
     factor = clip_factor(square_ref, other_ref)
     width = early.shape[1]
     half = LANES // 2
-    gather_rows(index_ref, early_ref, early, half, 0)
-    gather_rows(index_ref, late_ref, late, half, 0)
+    step = pl.program_id(0)
+    height = am.shape[1]
+
+    @pl.when(step == 0)
+    def _():
+        gather_rows(index_ref, early_ref, early, half, 0)
+        gather_rows(index_ref, late_ref, late, half, 0)
+        new = adam(nm[...], nf[...], ns[...], gn_ref[...] * factor, 0.3, 0.0)
+        last = FIRST_UNITS * half
+        first_ref[last:, :] = jnp.zeros((SMALL, width), BF)
+        first_ref[last : last + 4, 0:LANES] = new[0].astype(BF)
+        clip_ref[0] = jnp.sqrt(square_ref[0:1, 0:1] + other_ref[0:1, 0:1])[0, 0]
+
+    def span(unit):
+        return pl.ds(pl.multiple_of(unit * half + step * height, height), height)
+
     blocks = um.shape[1] // width
     middle = FIRST_UNITS
     for unit in range(5 + blocks + dm.shape[0]):
         if unit < 4:
-            source = late[unit * half : (unit + 1) * half, :]
+            source = late[span(unit), :]
         else:
-            source = early[(unit - 4) * half : (unit - 3) * half, :]
+            source = early[span(unit - 4), :]
         if unit < 5:
             state = am[unit], af[unit], as_[unit]
         elif unit < 5 + blocks:
@@ -724,18 +737,15 @@
             state = [ref[unit - 5 - blocks] for ref in (dm, df, ds)]
         new = adam(*state, source.astype(F32) * factor, 0.05, 0.01)
         target, place = (first_ref, unit) if unit < middle else (second_ref, unit - middle)
-        target[place * half : (place + 1) * half, :] = new[0].astype(BF)
-    new = adam(nm[...], nf[...], ns[...], gn_ref[...] * factor, 0.3, 0.0)
-    last = middle * half
-    first_ref[last:, :] = jnp.zeros((SMALL, width), BF)
-    first_ref[last : last + 4, 0:LANES] = new[0].astype(BF)
-    clip_ref[0] = jnp.sqrt(square_ref[0:1, 0:1] + other_ref[0:1, 0:1])[0, 0]
+        target[span(place), :] = new[0].astype(BF)
 
 
 def renew(side, index, square, early, late, gn, attn, up, down, norm):
     five, part, width = attn[0].shape
     hidden = up[0].shape[1]
+    steps = 2
     half = part // 2
+    tile = half // steps
     down = [a.reshape(a.shape[0] // part, part, width) for a in down]
     units = five + hidden // width + down[0].shape[0]
     first = jax.ShapeDtypeStruct((FIRST_UNITS * half + SMALL, width), BF)
@@ -745,12 +755,12 @@
         renew_kernel,
         grid_spec=pltpu.PrefetchScalarGridSpec(
             num_scalar_prefetch=1,
-            grid=(1,),
+            grid=(steps,),
             in_specs=[pl.BlockSpec(memory_space=pltpu.SMEM)]
             + [whole(a) for a in (*square, early, late, gn, *norm)]
-            + [pl.BlockSpec((five, half, width), lambda i, side: (0, side[0], 0))] * 3
-            + [pl.BlockSpec((half, hidden), lambda i, side: (side[0], 0))] * 3
-            + [pl.BlockSpec((tall, half, width), lambda i, side: (0, side[0], 0))] * 3,
+            + [pl.BlockSpec((five, tile, width), lambda i, side: (0, steps * side[0] + i, 0))] * 3
+            + [pl.BlockSpec((tile, hidden), lambda i, side: (steps * side[0] + i, 0))] * 3
+            + [pl.BlockSpec((tall, tile, width), lambda i, side: (0, steps * side[0] + i, 0))] * 3,
             out_specs=[whole(first), whole(second), pl.BlockSpec(memory_space=pltpu.SMEM)],
             scratch_shapes=[pltpu.VMEM(early.shape, BF), pltpu.VMEM(late.shape, BF)],
         ),
@@ -1031,9 +1041,8 @@
         pos, place, domain_rows, tokens, out_grad, o, norm, second, third
     )
 
-    steps = phases()
-    plan, index = gather_plan()
-    pieces = 2 ** len(steps)
+    steps, plan, index = HALVINGS + [MIDDLE], GATHERS, quarters()
+    pieces = 16
     rows = keep.shape[0] // pieces
 
     def forward_phase(parts, phase, rows):
@@ -1071,28 +1080,25 @@
     small = late_sum(late_got)
     turn, late_got = late_phase(1)
     early.append(after(got, turn))
-    turn = forward_phase(early, 3, rows)
+    turn = add_up(early, 0, 2 * rows)
     got = exchange(turn, *steps[3])
     small = late_sum(after(late_got, turn))
+    early = turn
     turn, late_got = late_phase(2)
-    early.append(after(got, turn))
-    early = add_rest(add_up(early, 0, rows))
+    early = add_rest(add_up([early, after(got, turn)], 0, 2 * rows))
     got = exchange(early, *plan[0])
     small = late_sum(after(late_got, early))
-    turn, late_got = late_phase(3)
-    early = jnp.concatenate([early, after(got, turn)])
-    got = exchange(early, *plan[1])
-    small = late_sum(after(late_got, early))
-    late = add_rest(jnp.concatenate([add_up(late, 0, thin), small]))
-    late, small = late[:thin], late[thin:]
+    out = jnp.concatenate([add_up(late, 0, 2 * thin), small])
+    late_got = exchange(out, *steps[3])
+    late = add_rest(add_up([out, late_got], 0, 2 * thin + SMALL))
+    late, small = late[: 2 * thin], late[2 * thin :]
     late_got = exchange(late, *plan[0])
     norm_grad = lax.dynamic_slice(small[:4], (0, shard * part), (4, part)).astype(F32)
-    late = jnp.concatenate([late, late_got])
-    late = jnp.concatenate([late, exchange(late, *plan[1])])
     early = jnp.concatenate([early, after(got, late)])
+    late = jnp.concatenate([late, after(late_got, early)])
     square = squares(early, late, norm_grad)
     square = square + swap(square, "dp", 1)
-    got = exchange(after(jnp.concatenate([late, early]), square), *plan[2])
+    got = exchange(after(jnp.concatenate([late, early]), square), *plan[1])
     square = square + swap(square, "shard", 1)
     square = (square, swap(square, "shard", 2))
     attn = (attn_master, attn_first, attn_second)

time: 221 us -> 216 us (0.977)
  starting transfers between devices: 44 us -> 40.6 us
    ppermute x45 -> x43, starting transfers between devices: 44 us -> 40.6 us  [exchange(): return lax.ppermute(values, ('dp', 'shard'), perm)]
    ppermute x45 -> x43, waiting for transfers between devices: 59 us -> 58.1 us  [exchange(): return lax.ppermute(values, ('dp', 'shard'), perm)]
    convert_element_type x13 -> x14, other arithmetic: 6.98 us -> 6.2 us  [low_sum(): return lax.reduce_precision(total, 8, 7).astype(BF)]
    unnamed x56 -> x50, local copies, waits for them, and re-layouts: 5.24 us -> 5.23 us
  transfers between devices with their start and end apart: 45 -> 43, of which waited for: 26 -> 25; matrix products, arithmetic and copies ran while one was open for 3% -> 3% of each run, Pallas kernels for 31% -> 31%
where the time goes in v6:
time: 216 us; the launch traced here: 215 us
  Pallas kernels  97 us (45%)
  waiting for transfers between devices  58.1 us (27%)
  starting transfers between devices  40.6 us (19%)
  other arithmetic  11 us (5%)
  local copies, waits for them, and re-layouts  6.16 us (3%)
  between operations  2.17 us (1%)
    ppermute x43, waiting for transfers between devices, exchange(): return lax.ppermute(values, ('dp', 'shard'), perm)  58.1 us
    ppermute x43, starting transfers between devices, exchange(): return lax.ppermute(values, ('dp', 'shard'), perm)  40.6 us
    pallas_call x1, Pallas kernels, feed(): pl.pallas_call(feed_kernel, grid=(4,), in_specs=[pl.BlockSpec(memory_spac...  26.5 us
    pallas_call x2, Pallas kernels, mix_back(): pl.pallas_call(functools.partial(mix_back_kernel, begun=bool(before)), gr...  22.2 us
    pallas_call x1, Pallas kernels, attend(): pl.pallas_call(attend_kernel, grid=(steps,), in_specs=[pl.BlockSpec(memor...  16.9 us
    pallas_call x1, Pallas kernels, update(): pl.pallas_call(update_kernel, grid=(steps,), in_specs=[smem] * 2 + [whole...  11.2 us
    convert_element_type x14, other arithmetic, low_sum(): return lax.reduce_precision(total, 8, 7).astype(BF)  6.2 us
    pallas_call x1, Pallas kernels, input_back(): pl.pallas_call(input_back_kernel, grid=(length // tile,), in_specs=[block...  5.45 us
  transfers between devices with their start and end apart: 43, of which 25 were waited for; matrix products, arithmetic and copies ran while one was open for 3% of the time, Pallas kernels for 31%

profile of v6, /device:TPU:0, one launch (start us, length us, event | category | flops | bytes accessed | tf_op | source)
XLA Modules:
  0.0 215.0 jit_solution(8591715515824064350)
XLA Ops:
  3.0 2.6 %collective-permute-start.1 = (bf16[272,512]{1,0:T(8,128)(2,1)S(1)}, bf16[272,512]{1,0:T(8,128)(2,1)}, u32[]{:S(2)}, u32[]{:S(2)}) collective-permute-start(bf16[272,512]{1,0:T(8,128)(2,1)S(1)} %constant_dynamic-slice_fusion), channel_id=1, source_target_pairs={{0,2},{1,3},{2,0},{3,1},{4,6},{5,7},{6,4},{7,5},{8,10},{9,11},{10,... | collective-permute-start | bytes 835592 | tf_op jit(solution)/shard_map/ppermute | solution.py:597
  7.9 1.9 collective-permute-done.2
  11.4 2.0 collective-permute-done.3
  15.1 2.7 %collective-permute-start.10 = (f32[8]{0:T(128)S(1)}, f32[8]{0:T(128)S(1)}, u32[]{:S(2)}, u32[]{:S(2)}) collective-permute-start(f32[8]{0:T(128)S(1)} %fusion.12), channel_id=1, source_target_pairs={{0,16},{1,17},{2,18},{3,19},{4,20},{5,21},{6,22},{7,23},{8,24},{9,... | collective-permute-start | bytes 104 | tf_op jit(solution)/shard_map/ppermute | solution.py:597
  19.6 2.1 collective-permute-done.4.far1
  21.8 1.6 collective-permute-start.12
  25.7 16.9 %attend.1 = (bf16[1024,512]{1,0:T(8,128)(2,1)S(1)}, bf16[1024,512]{1,0:T(8,128)(2,1)S(1)}, bf16[1024,512]{1,0:T(8,128)(2,1)S(1)}, bf16[1024,512]{1,0:T(8,128)(2,...) custom-call(s32[4]{0:T(128)S(1)} %iota_xor_fusion.pos_ref, ...), custom_call_target="tpu_custom_call" | custom-call | flops 1 | bytes 1 | tf_op jit(solution)/shard_map/attend/pallas_call | solution.py:217
  45.0 2.4 %collective-permute-done.11.t1 = bf16[528,512]{1,0:T(8,128)(2,1)S(1)} collective-permute-done((bf16[528,512]{1,0:T(8,128)(2,1)S(1)}, bf16[528,512]{1,0:T(8,128)(2,1)S(1)}, u32[]{:S(2)}, u32[]{:S(2)}) %collective-permute-start.11) | collective-permute-done | bytes 540704 | tf_op jit(solution)/shard_map/ppermute | solution.py:597
  47.8 26.5 %feed.1 = (bf16[1024,512]{1,0:T(8,128)(2,1)}, f32[1024,512]{1,0:T(8,128)}, bf16[1024,512]{1,0:T(8,128)(2,1)S(1)}, bf16[2304,512]{1,0:T(8,128)(2,1)}, bf16[2304,512]{1,0:T(8,128)(2,1)}, /*index=5*/f32[8,512]{1,0:T(8,128)S(1)}) custom-call(s32[4]{0:T(128)S(1)} %iota_xor_fusion.pos_ref, s32[2,16]{1,0:T(2,128)S(1)} %pad_add_fusion.place_ref, ...), custom_call_target="tpu_custom_call" | custom-call | flops 1 | bytes 1 | tf_op jit(solution)/shard_map/feed/pallas_call | solution.py:452
  74.5 6.0 %mix_back.2 = (bf16[256,512]{1,0:T(8,128)(2,1)S(1)}, bf16[256,512]{1,0:T(8,128)(2,1)S(1)}, bf16[256,512]{1,0:T(8,128)(2,1)S(1)}, bf16[256,512]{1,0:T(8,128)(2,1)...) custom-call(bf16[1024,512]{1,0:T(8,128)(2,1)S(1)} %get-tuple-element.133.refs_0_, ...), custom_call_target="tpu_custom_call" | custom-call | flops 1 | bytes 1 | tf_op jit(solution)/shard_map/mix_back/pallas_call | solution.py:300
  83.0 16.2 %mix_back.3 = (bf16[768,512]{1,0:T(8,128)(2,1)S(1)}, bf16[768,512]{1,0:T(8,128)(2,1)S(1)}, bf16[768,512]{1,0:T(8,128)(2,1)S(1)}, bf16[768,512]{1,0:T(8,128)(2,1)...) custom-call(bf16[1024,512]{1,0:T(8,128)(2,1)S(1)} %get-tuple-element.133.refs_0_, ...), custom_call_target="tpu_custom_call" | custom-call | flops 1 | bytes 1 | tf_op jit(solution)/shard_map/mix_back/pallas_call | solution.py:300
  99.1 1.6 reduce-precision_convert_fusion.1
  102.2 5.5 %input_back.1 = (f32[1024,512]{1,0:T(8,128)}, bf16[16,512]{1,0:T(8,128)(2,1)S(1)}) custom-call(bf16[1024,512]{1,0:T(8,128)(2,1)S(1)} %copy-done.1, f32[1024,512]{1,0:T(8,128)S(1)} %copy-done.8, bf16[4,512,512]{2,1,0:T(8,128)(2,1)S(1)} %copy-done.7, f32[8,512]{1,0:T(8,128)S(1)} %get-tuple-element.111.norm_ref, f32[8,512]{1,0:T(8,128)S(1)} %get-tuple-element.141.dnorm_ref, ...), custom_call_target="tpu_custom_call" | custom-call | flops 1 | bytes 1 | tf_op jit(solution)/shard_map/input_back/pallas_call | solution.py:570
  107.6 4.2 %weight_back.1 = (bf16[1040,512]{1,0:T(8,128)(2,1)S(1)}, bf16[1040,512]{1,0:T(8,128)(2,1)S(1)}) custom-call(s32[4]{0:T(128)S(1)} %iota_xor_fusion.pos_ref, s32[2,16]{1,0:T(2,128)S(1)} %pad_add_fusion.place_ref, bf16[16,512]{1,0:T(8,128)(2,1)S(1)} %get-tuple-element.149.small_ref, bf16[1024,512]{1,0:T(8,128)(2,1)S(1)} %get-tuple-element.150.n_ref, ...), custom_call_target="tpu_custom_call" | custom-call | flops 1 | bytes 1 | tf_op jit(solution)/shard_map/weight_back/pallas_call | solution.py:512
  113.9 2.3 %collective-permute-done.18 = bf16[1040,512]{1,0:T(8,128)(2,1)S(1)} collective-permute-done((bf16[1040,512]{1,0:T(8,128)(2,1)S(1)}, bf16[1040,512]{1,0:T(8,128)(2,1)S(1)}, u32[]{:S(2)}, u32[]{:S(2)}) %collective-permute-start.18) | collective-permute-done | bytes 1064992 | tf_op jit(solution)/shard_map/ppermute | solution.py:597
  117.5 2.6 %collective-permute-start.17 = (bf16[288,512]{1,0:T(8,128)(2,1)S(1)}, bf16[288,512]{1,0:T(8,128)(2,1)S(1)}, u32[]{:S(2)}, u32[]{:S(2)}) collective-permute-start(bf16[288,512]{1,0:T(8,128)(2,1)S(1)} %reduce-precision_convert_fusion.5), channel_id=1, source_target_pairs={{0,16},{1,3},{2,18},{3,1},{4,20},{5,7},{6,22},{7,5},{8,24},{9,11},... | collective-permute-start | bytes 884744 | tf_op jit(solution)/shard_map/ppermute | solution.py:597
  120.1 8.5 %collective-permute-done.19 = bf16[528,512]{1,0:T(8,128)(2,1)S(1)} collective-permute-done((bf16[528,512]{1,0:T(8,128)(2,1)S(1)}, bf16[528,512]{1,0:T(8,128)(2,1)S(1)}, u32[]{:S(2)}, u32[]{:S(2)}) %collective-permute-start.19) | collective-permute-done | bytes 540704 | tf_op jit(solution)/shard_map/ppermute | solution.py:597
  132.3 3.0 %collective-permute-done.21 = bf16[272,512]{1,0:T(8,128)(2,1)S(1)} collective-permute-done((bf16[272,512]{1,0:T(8,128)(2,1)S(1)}, bf16[272,512]{1,0:T(8,128)(2,1)S(1)}, u32[]{:S(2)}, u32[]{:S(2)}) %collective-permute-start.21) | collective-permute-done | bytes 278560 | tf_op jit(solution)/shard_map/ppermute | solution.py:597
  135.5 2.7 %collective-permute-start.23 = (bf16[144,512]{1,0:T(8,128)(2,1)S(1)}, bf16[144,512]{1,0:T(8,128)(2,1)S(1)}, u32[]{:S(2)}, u32[]{:S(2)}) collective-permute-start(bf16[144,512]{1,0:T(8,128)(2,1)S(1)} %pad_maximum_fusion.5), channel_id=1, source_target_pairs={{0,16},{1,3},{2,18},{3,1},{4,20},{5,7},{6,22},{7,5},{8,24},{9,11},... | collective-permute-start | bytes 442376 | tf_op jit(solution)/shard_map/ppermute | solution.py:597
  138.7 7.0 %collective-permute-done.23 = bf16[144,512]{1,0:T(8,128)(2,1)S(1)} collective-permute-done((bf16[144,512]{1,0:T(8,128)(2,1)S(1)}, bf16[144,512]{1,0:T(8,128)(2,1)S(1)}, u32[]{:S(2)}, u32[]{:S(2)}) %collective-permute-start.23) | collective-permute-done | bytes 147488 | tf_op jit(solution)/shard_map/ppermute | solution.py:597
  146.5 3.4 %collective-permute-start.22 = (bf16[288,512]{1,0:T(8,128)(2,1)S(1)}, bf16[288,512]{1,0:T(8,128)(2,1)S(1)}, u32[]{:S(2)}, u32[]{:S(2)}) collective-permute-start(bf16[288,512]{1,0:T(8,128)(2,1)S(1)} %reduce-precision_convert_fusion.3), channel_id=1, source_target_pairs={{0,16},{1,9},{2,18},{3,11},{4,20},{5,13},{6,22},{7,15},{8,24},{9,1... | collective-permute-start | bytes 884744 | tf_op jit(solution)/shard_map/ppermute | solution.py:597
  149.9 3.8 %collective-permute-done.24 = bf16[144,512]{1,0:T(8,128)(2,1)S(1)} collective-permute-done((bf16[144,512]{1,0:T(8,128)(2,1)S(1)}, bf16[144,512]{1,0:T(8,128)(2,1)S(1)}, u32[]{:S(2)}, u32[]{:S(2)}) %collective-permute-start.24) | collective-permute-done | bytes 147488 | tf_op jit(solution)/shard_map/ppermute | solution.py:597
  154.6 3.2 %collective-permute-done.22 = bf16[288,512]{1,0:T(8,128)(2,1)S(1)} collective-permute-done((bf16[288,512]{1,0:T(8,128)(2,1)S(1)}, bf16[288,512]{1,0:T(8,128)(2,1)S(1)}, u32[]{:S(2)}, u32[]{:S(2)}) %collective-permute-start.22) | collective-permute-done | bytes 294944 | tf_op jit(solution)/shard_map/ppermute | solution.py:597
  157.9 3.0 %collective-permute-done.25 = bf16[128,512]{1,0:T(8,128)(2,1)S(1)} collective-permute-done((bf16[128,512]{1,0:T(8,128)(2,1)S(1)}, bf16[128,512]{1,0:T(8,128)(2,1)S(1)}, u32[]{:S(2)}, u32[]{:S(2)}) %collective-permute-start.25) | collective-permute-done | bytes 131104 | tf_op jit(solution)/shard_map/ppermute | solution.py:597
  163.2 2.0 collective-permute-done.26
  168.4 2.3 %collective-permute-done.28.other_ref = f32[8,128]{1,0:T(8,128)S(1)} collective-permute-done((f32[8,128]{1,0:T(8,128)S(1)}, f32[8,128]{1,0:T(8,128)S(1)}, u32[]{:S(2)}, u32[]{:S(2)}) %collective-permute-start.28) | collective-permute-done | bytes 4128 | tf_op jit(solution)/shard_map/ppermute | solution.py:597
  171.3 4.8 %renew.1 = (bf16[464,512]{1,0:T(8,128)(2,1)}, bf16[384,512]{1,0:T(8,128)(2,1)}, f32[1]{0:T(128)}) custom-call(s32[1]{0:T(128)} %bitcast.2.half_ref.side_ref, s32[4]{0:T(128)} %broadcast_select_fusion.8.index_ref, f32[8,128]{1,0:T(8,128)} %copy-done.18, f32[8,128]{1,0:T(8,128)} %copy-done.20, bf16[576,512]{1,0:T(8,128)(2,1)} %copy-done, ...), custom_call_target="tpu_custom_call" | custom-call | flops 1 | bytes 1 | tf_op jit(solution)/shard_map/renew/pallas_call | solution.py:754
  179.0 11.2 %update.1 = (f32[5,128,512]{2,1,0:T(8,128)}, f32[5,128,512]{2,1,0:T(8,128)}, f32[5,128,512]{2,1,0:T(8,128)}, f32[128,2048]{1,0:T(8,128)}, f32[128,2048]{1,0:T(8,...) custom-call(s32[1]{0:T(128)} %bitcast.2.half_ref.side_ref, ...), custom_call_target="tpu_custom_call" | custom-call | flops 1 | bytes 1 | tf_op jit(solution)/shard_map/update/pallas_call | solution.py:849
  197.6 2.9 %unpack_near.1 = (bf16[5,512,512]{2,1,0:T(8,128)(2,1)}, bf16[512,2048]{1,0:T(8,128)(2,1)}, bf16[2048,512]{1,0:T(8,128)(2,1)}) custom-call(s32[4]{0:T(128)S(1)} %iota_xor_fusion.pos_ref, s32[1]{0:T(128)} %bitcast.2.half_ref.side_ref, bf16[1024,512]{1,0:T(8,128)(2,1)S(1)} %copy-done.10, bf16[640,512]{1,0:T(8,128)(2,1)S(1)} %copy-done.11, ...), custom_call_target="tpu_custom_call" | custom-call | flops 1 | bytes 1 | tf_op jit(solution)/shard_map/unpack_near/pallas_call | solution.py:955
  200.5 3.0 %collective-permute-done.32.refs_0_ = bf16[384,512]{1,0:T(8,128)(2,1)S(1)} collective-permute-done((bf16[384,512]{1,0:T(8,128)(2,1)}, bf16[384,512]{1,0:T(8,128)(2,1)S(1)}, u32[]{:S(2)}, u32[]{:S(2)}) %collective-permute-start.32) | collective-permute-done | bytes 393248 | tf_op jit(solution)/shard_map/ppermute | solution.py:597
  205.9 4.8 %collective-permute-done.37.refs_2_ = bf16[256,512]{1,0:T(8,128)(2,1)S(1)} collective-permute-done((bf16[256,512]{1,0:T(8,128)(2,1)S(1)}, bf16[256,512]{1,0:T(8,128)(2,1)S(1)}, u32[]{:S(2)}, u32[]{:S(2)}) %collective-permute-start.37) | collective-permute-done | bytes 262176 | tf_op jit(solution)/shard_map/ppermute | solution.py:597
  212.4 2.4 %unpack_far.1 = (bf16[5,512,512]{2,1,0:T(8,128)(2,1)}, bf16[512,2048]{1,0:T(8,128)(2,1)}, bf16[2048,512]{1,0:T(8,128)(2,1)}) custom-call(s32[4]{0:T(128)S(1)} %iota_xor_fusion.pos_ref, s32[1]{0:T(128)} %bitcast.2.half_ref.side_ref, ...), custom_call_target="tpu_custom_call", output_to_operand_aliasing={{0}: (10, {}), {1}: (11, {}), {2}: (12, {})} | custom-call | flops 1 | bytes 1 | tf_op jit(solution)/shard_map/unpack_far/pallas_call | solution.py:970
  (167 shorter events, 47.9 us)
Async XLA Ops:
  2.4 23.0 %collective-permute-start = (bf16[544,512]{1,0:T(8,128)(2,1)S(1)}, bf16[544,512]{1,0:T(8,128)(2,1)}, u32[]{:S(2)}, u32[]{:S(2)}) collective-permute-start(bf16[544,512]{1,0:T(8,128)(2,1)S(1)} %fusion.5.near0), channel_id=1, source_target_pairs={{0,1},{1,0},{2,3},{3,2},{4,5},{5,4},{6,7},{7,6},{8,9},{9,8},{10,11... | collective-permute-start | bytes 1671176 | tf_op jit(solution)/shard_map/ppermute | solution.py:597
  3.0 10.4 %collective-permute-start.1 = (bf16[272,512]{1,0:T(8,128)(2,1)S(1)}, bf16[272,512]{1,0:T(8,128)(2,1)}, u32[]{:S(2)}, u32[]{:S(2)}) collective-permute-start(bf16[272,512]{1,0:T(8,128)(2,1)S(1)} %constant_dynamic-slice_fusion), channel_id=1, source_target_pairs={{0,2},{1,3},{2,0},{3,1},{4,6},{5,7},{6,4},{7,5},{8,10},{9,11},{10,... | collective-permute-start | bytes 835592 | tf_op jit(solution)/shard_map/ppermute | solution.py:597
  13.4 8.3 %collective-permute-start.4 = (bf16[272,512]{1,0:T(8,128)(2,1)}, bf16[272,512]{1,0:T(8,128)(2,1)}, u32[]{:S(2)}, u32[]{:S(2)}) collective-permute-start(bf16[272,512]{1,0:T(8,128)(2,1)} %collective-permute-done.1.far0), channel_id=1, source_target_pairs={{0,4},{1,5},{2,6},{3,7},{4,0},{5,1},{6,2},{7,3},{8,12},{9,13},{10,... | collective-permute-start | bytes 835592 | tf_op jit(solution)/shard_map/ppermute | solution.py:597
  15.1 4.5 %collective-permute-start.10 = (f32[8]{0:T(128)S(1)}, f32[8]{0:T(128)S(1)}, u32[]{:S(2)}, u32[]{:S(2)}) collective-permute-start(f32[8]{0:T(128)S(1)} %fusion.12), channel_id=1, source_target_pairs={{0,16},{1,17},{2,18},{3,19},{4,20},{5,21},{6,22},{7,23},{8,24},{9,... | collective-permute-start | bytes 104 | tf_op jit(solution)/shard_map/ppermute | solution.py:597
  17.8 26.2 %collective-permute-start.8 = (bf16[640,512]{1,0:T(8,128)(2,1)S(1)}, bf16[640,512]{1,0:T(8,128)(2,1)S(1)}, u32[]{:S(2)}, u32[]{:S(2)}) collective-permute-start(bf16[640,512]{1,0:T(8,128)(2,1)S(1)} %slice_dynamic-update-slice_fusion.p0), channel_id=1, source_target_pairs={{0,2},{1,3},{2,0},{3,1},{4,6},{5,7},{6,4},{7,5},{8,10},{9,11},{10,... | collective-permute-start | bytes 1966088 | tf_op jit(solution)/shard_map/ppermute | solution.py:597
  21.8 23.2 %collective-permute-start.12 = (bf16[528,512]{1,0:T(8,128)(2,1)S(1)}, bf16[528,512]{1,0:T(8,128)(2,1)}, u32[]{:S(2)}, u32[]{:S(2)}) collective-permute-start(bf16[528,512]{1,0:T(8,128)(2,1)S(1)} %fusion.6.t0), channel_id=1, source_target_pairs={{0,2},{1,3},{2,0},{3,1},{4,6},{5,7},{6,4},{7,5},{8,10},{9,11},{10,... | collective-permute-start | bytes 1622024 | tf_op jit(solution)/shard_map/ppermute | solution.py:597
  25.3 19.7 %collective-permute-start.7 = (bf16[640,512]{1,0:T(8,128)(2,1)S(1)}, bf16[640,512]{1,0:T(8,128)(2,1)S(1)}, u32[]{:S(2)}, u32[]{:S(2)}) collective-permute-start(bf16[640,512]{1,0:T(8,128)(2,1)S(1)} %slice_dynamic-update-slice_fusion.p0), channel_id=1, source_target_pairs={{0,1},{1,0},{2,3},{3,2},{4,5},{5,4},{6,7},{7,6},{8,9},{9,8},{10,11... | collective-permute-start | bytes 1966088 | tf_op jit(solution)/shard_map/ppermute | solution.py:597
  74.3 6.2 %collective-permute-start.14 = (bf16[2304,512]{1,0:T(8,128)(2,1)}, bf16[2304,512]{1,0:T(8,128)(2,1)}, u32[]{:S(2)}, u32[]{:S(2)}) collective-permute-start(bf16[2304,512]{1,0:T(8,128)(2,1)} %get-tuple-element.119), channel_id=1, source_target_pairs={{0,1},{1,0},{2,3},{3,2},{4,5},{5,4},{6,7},{7,6},{8,9},{9,8},{10,11... | collective-permute-start | bytes 7077896 | tf_op jit(solution)/shard_map/ppermute | solution.py:597
  82.1 17.0 %collective-permute-start.15 = (bf16[1152,512]{1,0:T(8,128)(2,1)S(1)}, bf16[1152,512]{1,0:T(8,128)(2,1)}, u32[]{:S(2)}, u32[]{:S(2)}) collective-permute-start(bf16[1152,512]{1,0:T(8,128)(2,1)S(1)} %reduce-precision_convert_fusion), channel_id=1, source_target_pairs={{0,2},{1,5},{2,0},{3,7},{4,6},{5,1},{6,4},{7,3},{8,10},{9,13},{10,... | collective-permute-start | bytes 3538952 | tf_op jit(solution)/shard_map/ppermute | solution.py:597
  100.8 11.0 %collective-permute-start.16 = (bf16[576,512]{1,0:T(8,128)(2,1)S(1)}, bf16[576,512]{1,0:T(8,128)(2,1)S(1)}, u32[]{:S(2)}, u32[]{:S(2)}) collective-permute-start(bf16[576,512]{1,0:T(8,128)(2,1)S(1)} %reduce-precision_convert_fusion.1), channel_id=1, source_target_pairs={{0,4},{1,9},{2,6},{3,11},{4,0},{5,13},{6,2},{7,15},{8,12},{9,1},{1... | collective-permute-start | bytes 1769480 | tf_op jit(solution)/shard_map/ppermute | solution.py:597
  116.4 12.2 %collective-permute-start.19 = (bf16[528,512]{1,0:T(8,128)(2,1)S(1)}, bf16[528,512]{1,0:T(8,128)(2,1)S(1)}, u32[]{:S(2)}, u32[]{:S(2)}) collective-permute-start(bf16[528,512]{1,0:T(8,128)(2,1)S(1)} %pad_maximum_fusion.2), channel_id=1, source_target_pairs={{0,2},{1,5},{2,0},{3,7},{4,6},{5,1},{6,4},{7,3},{8,10},{9,13},{10,... | collective-permute-start | bytes 1622024 | tf_op jit(solution)/shard_map/ppermute | solution.py:597
  117.5 12.2 %collective-permute-start.17 = (bf16[288,512]{1,0:T(8,128)(2,1)S(1)}, bf16[288,512]{1,0:T(8,128)(2,1)S(1)}, u32[]{:S(2)}, u32[]{:S(2)}) collective-permute-start(bf16[288,512]{1,0:T(8,128)(2,1)S(1)} %reduce-precision_convert_fusion.5), channel_id=1, source_target_pairs={{0,16},{1,3},{2,18},{3,1},{4,20},{5,7},{6,22},{7,5},{8,24},{9,11},... | collective-permute-start | bytes 884744 | tf_op jit(solution)/shard_map/ppermute | solution.py:597
  128.8 6.6 %collective-permute-start.21 = (bf16[272,512]{1,0:T(8,128)(2,1)S(1)}, bf16[272,512]{1,0:T(8,128)(2,1)S(1)}, u32[]{:S(2)}, u32[]{:S(2)}) collective-permute-start(bf16[272,512]{1,0:T(8,128)(2,1)S(1)} %pad_maximum_fusion.3), channel_id=1, source_target_pairs={{0,4},{1,9},{2,6},{3,11},{4,0},{5,13},{6,2},{7,15},{8,12},{9,1},{1... | collective-permute-start | bytes 835592 | tf_op jit(solution)/shard_map/ppermute | solution.py:597
  130.9 7.7 %collective-permute-start.20 = (bf16[288,512]{1,0:T(8,128)(2,1)S(1)}, bf16[288,512]{1,0:T(8,128)(2,1)S(1)}, u32[]{:S(2)}, u32[]{:S(2)}) collective-permute-start(bf16[288,512]{1,0:T(8,128)(2,1)S(1)} %reduce-precision_convert_fusion.4), channel_id=1, source_target_pairs={{0,8},{1,17},{2,10},{3,19},{4,12},{5,21},{6,14},{7,23},{8,0},{9,25... | collective-permute-start | bytes 884744 | tf_op jit(solution)/shard_map/ppermute | solution.py:597
  135.5 10.3 %collective-permute-start.23 = (bf16[144,512]{1,0:T(8,128)(2,1)S(1)}, bf16[144,512]{1,0:T(8,128)(2,1)S(1)}, u32[]{:S(2)}, u32[]{:S(2)}) collective-permute-start(bf16[144,512]{1,0:T(8,128)(2,1)S(1)} %pad_maximum_fusion.5), channel_id=1, source_target_pairs={{0,16},{1,3},{2,18},{3,1},{4,20},{5,7},{6,22},{7,5},{8,24},{9,11},... | collective-permute-start | bytes 442376 | tf_op jit(solution)/shard_map/ppermute | solution.py:597
  145.9 7.9 %collective-permute-start.24 = (bf16[144,512]{1,0:T(8,128)(2,1)S(1)}, bf16[144,512]{1,0:T(8,128)(2,1)S(1)}, u32[]{:S(2)}, u32[]{:S(2)}) collective-permute-start(bf16[144,512]{1,0:T(8,128)(2,1)S(1)} %pad_maximum_fusion.6), channel_id=1, source_target_pairs={{0,8},{1,17},{2,10},{3,19},{4,12},{5,21},{6,14},{7,23},{8,0},{9,25... | collective-permute-start | bytes 442376 | tf_op jit(solution)/shard_map/ppermute | solution.py:597
  146.5 11.3 %collective-permute-start.22 = (bf16[288,512]{1,0:T(8,128)(2,1)S(1)}, bf16[288,512]{1,0:T(8,128)(2,1)S(1)}, u32[]{:S(2)}, u32[]{:S(2)}) collective-permute-start(bf16[288,512]{1,0:T(8,128)(2,1)S(1)} %reduce-precision_convert_fusion.3), channel_id=1, source_target_pairs={{0,16},{1,9},{2,18},{3,11},{4,20},{5,13},{6,22},{7,15},{8,24},{9,1... | collective-permute-start | bytes 884744 | tf_op jit(solution)/shard_map/ppermute | solution.py:597
  153.8 7.1 %collective-permute-start.25 = (bf16[128,512]{1,0:T(8,128)(2,1)S(1)}, bf16[128,512]{1,0:T(8,128)(2,1)S(1)}, u32[]{:S(2)}, u32[]{:S(2)}) collective-permute-start(bf16[128,512]{1,0:T(8,128)(2,1)S(1)} %slice.237), channel_id=1, source_target_pairs={{0,16},{1,9},{2,18},{3,11},{4,20},{5,13},{6,22},{7,15},{8,24},{9,1... | collective-permute-start | bytes 393224 | tf_op jit(solution)/shard_map/ppermute | solution.py:597
  161.4 3.8 %collective-permute-start.26 = (f32[8,128]{1,0:T(8,128)S(1)}, f32[8,128]{1,0:T(8,128)S(1)}, u32[]{:S(2)}, u32[]{:S(2)}) collective-permute-start(f32[8,128]{1,0:T(8,128)S(1)} %squares.1), channel_id=1, source_target_pairs={{0,4},{1,5},{2,6},{3,7},{4,0},{5,1},{6,2},{7,3},{8,12},{9,13},{10,... | collective-permute-start | bytes 12296 | tf_op jit(solution)/shard_map/ppermute | solution.py:597
  165.2 12.9 %collective-permute-start.29 = (bf16[832,512]{1,0:T(8,128)(2,1)}, bf16[832,512]{1,0:T(8,128)(2,1)S(1)}, u32[]{:S(2)}, u32[]{:S(2)}) collective-permute-start(bf16[832,512]{1,0:T(8,128)(2,1)} %pad_maximum_fusion), channel_id=1, source_target_pairs={{0,4},{1,5},{2,6},{3,7},{4,0},{5,1},{6,2},{7,3},{8,12},{9,13},{10,... | collective-permute-start | bytes 2555912 | tf_op jit(solution)/shard_map/ppermute | solution.py:597
  167.1 3.6 %collective-permute-start.28 = (f32[8,128]{1,0:T(8,128)S(1)}, f32[8,128]{1,0:T(8,128)S(1)}, u32[]{:S(2)}, u32[]{:S(2)}) collective-permute-start(f32[8,128]{1,0:T(8,128)S(1)} %add.303.square_ref), channel_id=1, source_target_pairs={{0,2},{1,3},{2,0},{3,1},{4,6},{5,7},{6,4},{7,5},{8,10},{9,11},{10,... | collective-permute-start | bytes 12296 | tf_op jit(solution)/shard_map/ppermute | solution.py:597
  176.1 14.1 %collective-permute-start.30 = (bf16[464,512]{1,0:T(8,128)(2,1)}, bf16[464,512]{1,0:T(8,128)(2,1)S(1)}, u32[]{:S(2)}, u32[]{:S(2)}) collective-permute-start(bf16[464,512]{1,0:T(8,128)(2,1)} %get-tuple-element.161), channel_id=1, source_target_pairs={{0,2},{1,3},{2,0},{3,1},{4,6},{5,7},{6,4},{7,5},{8,10},{9,11},{10,... | collective-permute-start | bytes 1425416 | tf_op jit(solution)/shard_map/ppermute | solution.py:597
  177.7 12.5 %collective-permute-start.31 = (bf16[16,512]{1,0:T(8,128)(2,1)S(1)}, bf16[16,512]{1,0:T(8,128)(2,1)S(1)}, u32[]{:S(2)}, u32[]{:S(2)}) collective-permute-start(bf16[16,512]{1,0:T(8,128)(2,1)S(1)} %slice.205), channel_id=1, source_target_pairs={{0,1},{1,0},{2,3},{3,2},{4,5},{5,4},{6,7},{7,6},{8,9},{9,8},{10,11... | collective-permute-start | bytes 49160 | tf_op jit(solution)/shard_map/ppermute | solution.py:597
  190.2 5.1 %collective-permute-start.34 = (bf16[1024,512]{1,0:T(8,128)(2,1)}, bf16[1024,512]{1,0:T(8,128)(2,1)S(1)}, u32[]{:S(2)}, u32[]{:S(2)}) collective-permute-start(bf16[1024,512]{1,0:T(8,128)(2,1)} %get-tuple-element.184.p0), channel_id=1, source_target_pairs={{0,1},{1,0},{2,3},{3,2},{4,5},{5,4},{6,7},{7,6},{8,9},{9,8},{10,11... | collective-permute-start | bytes 3145736 | tf_op jit(solution)/shard_map/ppermute | solution.py:597
  190.3 3.6 %collective-permute-start.33 = (bf16[464,512]{1,0:T(8,128)(2,1)S(1)}, bf16[464,512]{1,0:T(8,128)(2,1)S(1)}, u32[]{:S(2)}, u32[]{:S(2)}) collective-permute-start(bf16[464,512]{1,0:T(8,128)(2,1)S(1)} %collective-permute-done.30.p4), channel_id=1, source_target_pairs={{0,1},{1,0},{2,3},{3,2},{4,5},{5,4},{6,7},{7,6},{8,9},{9,8},{10,11... | collective-permute-start | bytes 1425416 | tf_op jit(solution)/shard_map/ppermute | solution.py:597
  190.8 4.5 %collective-permute-start.35 = (bf16[640,512]{1,0:T(8,128)(2,1)}, bf16[640,512]{1,0:T(8,128)(2,1)S(1)}, u32[]{:S(2)}, u32[]{:S(2)}) collective-permute-start(bf16[640,512]{1,0:T(8,128)(2,1)} %get-tuple-element.185.p1), channel_id=1, source_target_pairs={{0,1},{1,0},{2,3},{3,2},{4,5},{5,4},{6,7},{7,6},{8,9},{9,8},{10,11... | collective-permute-start | bytes 1966088 | tf_op jit(solution)/shard_map/ppermute | solution.py:597
  190.9 13.5 %collective-permute-start.36 = (bf16[464,512]{1,0:T(8,128)(2,1)S(1)}, bf16[464,512]{1,0:T(8,128)(2,1)S(1)}, u32[]{:S(2)}, u32[]{:S(2)}) collective-permute-start(bf16[464,512]{1,0:T(8,128)(2,1)S(1)} %collective-permute-done.30.p4), channel_id=1, source_target_pairs={{0,4},{1,5},{2,6},{3,7},{4,0},{5,1},{6,2},{7,3},{8,12},{9,13},{10,... | collective-permute-start | bytes 1425416 | tf_op jit(solution)/shard_map/ppermute | solution.py:597
  192.4 11.0 %collective-permute-start.32 = (bf16[384,512]{1,0:T(8,128)(2,1)}, bf16[384,512]{1,0:T(8,128)(2,1)S(1)}, u32[]{:S(2)}, u32[]{:S(2)}) collective-permute-start(bf16[384,512]{1,0:T(8,128)(2,1)} %get-tuple-element.181), channel_id=1, source_target_pairs={{0,2},{1,3},{2,0},{3,1},{4,6},{5,7},{6,4},{7,5},{8,10},{9,11},{10,... | collective-permute-start | bytes 1179656 | tf_op jit(solution)/shard_map/ppermute | solution.py:597
  203.5 7.2 %collective-permute-start.37 = (bf16[256,512]{1,0:T(8,128)(2,1)S(1)}, bf16[256,512]{1,0:T(8,128)(2,1)S(1)}, u32[]{:S(2)}, u32[]{:S(2)}) collective-permute-start(bf16[256,512]{1,0:T(8,128)(2,1)S(1)} %slice.211), channel_id=1, source_target_pairs={{0,4},{1,5},{2,6},{3,7},{4,0},{5,1},{6,2},{7,3},{8,12},{9,13},{10,... | collective-permute-start | bytes 786440 | tf_op jit(solution)/shard_map/ppermute | solution.py:597
  204.4 8.0 %collective-permute-start.40 = (bf16[464,512]{1,0:T(8,128)(2,1)S(1)}, bf16[464,512]{1,0:T(8,128)(2,1)S(1)}, u32[]{:S(2)}, u32[]{:S(2)}) collective-permute-start(bf16[464,512]{1,0:T(8,128)(2,1)S(1)} %collective-permute-done.36.refs_1_), channel_id=1, source_target_pairs={{0,1},{1,0},{2,3},{3,2},{4,5},{5,4},{6,7},{7,6},{8,9},{9,8},{10,11... | collective-permute-start | bytes 1425416 | tf_op jit(solution)/shard_map/ppermute | solution.py:597
  204.4 8.0 %collective-permute-start.39 = (bf16[384,512]{1,0:T(8,128)(2,1)S(1)}, bf16[384,512]{1,0:T(8,128)(2,1)S(1)}, u32[]{:S(2)}, u32[]{:S(2)}) collective-permute-start(bf16[384,512]{1,0:T(8,128)(2,1)S(1)} %collective-permute-done.32.refs_0_), channel_id=1, source_target_pairs={{0,1},{1,0},{2,3},{3,2},{4,5},{5,4},{6,7},{7,6},{8,9},{9,8},{10,11... | collective-permute-start | bytes 1179656 | tf_op jit(solution)/shard_map/ppermute | solution.py:597
  204.9 5.8 %collective-permute-start.38 = (bf16[128,512]{1,0:T(8,128)(2,1)S(1)}, bf16[128,512]{1,0:T(8,128)(2,1)S(1)}, u32[]{:S(2)}, u32[]{:S(2)}) collective-permute-start(bf16[128,512]{1,0:T(8,128)(2,1)S(1)} %copy-done.21), channel_id=1, source_target_pairs={{0,2},{1,3},{2,0},{3,1},{4,6},{5,7},{6,4},{7,5},{8,10},{9,11},{10,... | collective-permute-start | bytes 393224 | tf_op jit(solution)/shard_map/ppermute | solution.py:597
  (34 other events, 261.9 us)

commit v7 on v6

--- a/solution.py
+++ b/solution.py
@@ -356,7 +356,7 @@
         factor_ref[...] = jnp.broadcast_to(jnp.sum(share, axis=1, keepdims=True), factor_ref.shape)
 
         def before(i, _):
-            rows = pl.ds(pl.multiple_of(i * 256, 256), 256)
+            rows = slice(i * 256, (i + 1) * 256)
             h1 = x_ref[rows, :].astype(F32) + dot(o_ref[rows, :], wo[...])
             branch[rows, :] = h1
             unit, inv = normalise(h1)
@@ -370,7 +370,8 @@
             dn2[rows, :] = jnp.zeros((256, width), F32)
             return 0
 
-        lax.fori_loop(0, tiles, before, 0)
+        for i in range(tiles):
+            before(i, 0)
 
     up = w1[step]
     down = w2[step]
@@ -412,7 +413,7 @@
         gain = norm_ref[2:3, :]
 
         def after(i, sums):
-            rows = pl.ds(pl.multiple_of(i * 256, 256), 256)
+            rows = slice(i * 256, (i + 1) * 256)
             y_ref[rows, :] = branch[rows, :].astype(BF)
             grad = dn2[rows, :]
             unit = unit_ref[rows, :]
@@ -429,7 +430,9 @@
             )
 
         empty = jnp.zeros((1, width), F32)
-        sums = lax.fori_loop(0, tiles, after, (empty, empty, jnp.zeros((width, width), F32)))
+        sums = (empty, empty, jnp.zeros((width, width), F32))
+        for i in range(tiles):
+            sums = after(i, sums)
         dnorm_ref[...] = jnp.zeros_like(dnorm_ref)
         dnorm_ref[0:1, :] = sums[0]
         dnorm_ref[1:2, :] = sums[1]
@@ -481,28 +484,21 @@
 
 def weight_back_kernel(pos_ref, place_ref, small_ref, n_ref, *refs):
     grads_in, (send_ref, keep_ref, n_t, grads) = refs[:-4], refs[-4:]
-    step = pl.program_id(0)
-
-    @pl.when(step == 0)
-    def _():
-        n_t[...] = n_ref[...].T
-        for target in (send_ref, keep_ref):
-            target[target.shape[0] - SMALL :, :] = small_ref[...]
-
+    n_t[...] = n_ref[...].T
+    for target in (send_ref, keep_ref):
+        target[target.shape[0] - SMALL :, :] = small_ref[...]
     for m in range(4):
-        @pl.when(step == m)
-        def _():
-            total = None
-            first = 0
-            for j in range(len(grads_in) // 4):
-                part = grads_in[4 * j + m]
-                last = first + part.shape[0]
-                term = dot(n_t[:, first:last], part[...])
-                total = term if total is None else total + term
-                first = last
-            grads[...] = total.astype(BF)
-
-    scatter_shards(pos_ref, place_ref, grads, send_ref, keep_ref, step)
+        total = None
+        first = 0
+        for j in range(len(grads_in) // 4):
+            part = grads_in[4 * j + m]
+            last = first + part.shape[0]
+            term = dot(n_t[:, first:last], part[...])
+            total = term if total is None else total + term
+            first = last
+        grads[m] = total.astype(BF)
+    for m in range(4):
+        scatter_shards(pos_ref, place_ref, grads.at[m], send_ref, keep_ref, m)
 
 
 def weight_back(pos, place, small, n, halves):
@@ -511,11 +507,11 @@
     args = (small, n) + tuple(halves)
     return pl.pallas_call(
         weight_back_kernel,
-        grid=(4,),
+        grid=(1,),
         in_specs=[pl.BlockSpec(memory_space=pltpu.SMEM)] * 2 + [whole(a) for a in args],
         out_specs=[whole(out)] * 2,
         out_shape=[out] * 2,
-        scratch_shapes=[pltpu.VMEM((width, length), BF), pltpu.VMEM((width, width), BF)],
+        scratch_shapes=[pltpu.VMEM((width, length), BF), pltpu.VMEM((4, width, width), BF)],
         compiler_params=pltpu.CompilerParams(
             dimension_semantics=("arbitrary",), vmem_limit_bytes=VMEM_BACK
         ),

time: 216 us -> 213 us (0.986)
  Pallas kernels: 97 us -> 94.1 us
  transfers between devices with their start and end apart: 43 -> 43, of which waited for: 25 -> 25; matrix products, arithmetic and copies ran while one was open for 3% -> 3% of each run, Pallas kernels for 31% -> 32%
where the time goes in v7:
time: 213 us; the launch traced here: 212 us
  Pallas kernels  94.1 us (44%)
  waiting for transfers between devices  56.3 us (26%)
  starting transfers between devices  42.3 us (20%)
  other arithmetic  11 us (5%)
  local copies, waits for them, and re-layouts  6.16 us (3%)
  between operations  2.17 us (1%)
    ppermute x43, waiting for transfers between devices, exchange(): return lax.ppermute(values, ('dp', 'shard'), perm)  56.3 us
    ppermute x43, starting transfers between devices, exchange(): return lax.ppermute(values, ('dp', 'shard'), perm)  42.3 us
    pallas_call x1, Pallas kernels, feed(): pl.pallas_call(feed_kernel, grid=(4,), in_specs=[pl.BlockSpec(memory_spac...  24.4 us
    pallas_call x2, Pallas kernels, mix_back(): pl.pallas_call(functools.partial(mix_back_kernel, begun=bool(before)), gr...  22.2 us
    pallas_call x1, Pallas kernels, attend(): pl.pallas_call(attend_kernel, grid=(steps,), in_specs=[pl.BlockSpec(memor...  16.9 us
    pallas_call x1, Pallas kernels, update(): pl.pallas_call(update_kernel, grid=(steps,), in_specs=[smem] * 2 + [whole...  11.2 us
    convert_element_type x14, other arithmetic, low_sum(): return lax.reduce_precision(total, 8, 7).astype(BF)  6.2 us
    pallas_call x1, Pallas kernels, input_back(): pl.pallas_call(input_back_kernel, grid=(length // tile,), in_specs=[block...  5.45 us
  transfers between devices with their start and end apart: 43, of which 25 were waited for; matrix products, arithmetic and copies ran while one was open for 3% of the time, Pallas kernels for 32%

profile of v7, /device:TPU:0, one launch (start us, length us, event | category | flops | bytes accessed | tf_op | source)
XLA Modules:
  0.0 212.0 jit_solution(11042907011246091927)
XLA Ops:
  3.0 2.6 %collective-permute-start.1 = (bf16[272,512]{1,0:T(8,128)(2,1)S(1)}, bf16[272,512]{1,0:T(8,128)(2,1)}, u32[]{:S(2)}, u32[]{:S(2)}) collective-permute-start(bf16[272,512]{1,0:T(8,128)(2,1)S(1)} %constant_dynamic-slice_fusion), channel_id=1, source_target_pairs={{0,2},{1,3},{2,0},{3,1},{4,6},{5,7},{6,4},{7,5},{8,10},{9,11},{10,... | collective-permute-start | bytes 835592 | tf_op jit(solution)/shard_map/ppermute | solution.py:593
  7.9 1.9 collective-permute-done.2
  11.4 2.0 collective-permute-done.3
  15.1 2.7 %collective-permute-start.10 = (f32[8]{0:T(128)S(1)}, f32[8]{0:T(128)S(1)}, u32[]{:S(2)}, u32[]{:S(2)}) collective-permute-start(f32[8]{0:T(128)S(1)} %fusion.12), channel_id=1, source_target_pairs={{0,16},{1,17},{2,18},{3,19},{4,20},{5,21},{6,22},{7,23},{8,24},{9,... | collective-permute-start | bytes 104 | tf_op jit(solution)/shard_map/ppermute | solution.py:593
  19.6 2.1 collective-permute-done.4.far1
  21.8 1.6 collective-permute-start.12
  25.7 16.9 %attend.1 = (bf16[1024,512]{1,0:T(8,128)(2,1)S(1)}, bf16[1024,512]{1,0:T(8,128)(2,1)S(1)}, bf16[1024,512]{1,0:T(8,128)(2,1)S(1)}, bf16[1024,512]{1,0:T(8,128)(2,...) custom-call(s32[4]{0:T(128)S(1)} %iota_xor_fusion.pos_ref, ...), custom_call_target="tpu_custom_call" | custom-call | flops 1 | bytes 1 | tf_op jit(solution)/shard_map/attend/pallas_call | solution.py:217
  45.0 2.4 %collective-permute-done.11.t1 = bf16[528,512]{1,0:T(8,128)(2,1)S(1)} collective-permute-done((bf16[528,512]{1,0:T(8,128)(2,1)S(1)}, bf16[528,512]{1,0:T(8,128)(2,1)S(1)}, u32[]{:S(2)}, u32[]{:S(2)}) %collective-permute-start.11) | collective-permute-done | bytes 540704 | tf_op jit(solution)/shard_map/ppermute | solution.py:593
  47.8 24.4 %feed.1 = (bf16[1024,512]{1,0:T(8,128)(2,1)}, f32[1024,512]{1,0:T(8,128)}, bf16[1024,512]{1,0:T(8,128)(2,1)S(1)}, bf16[2304,512]{1,0:T(8,128)(2,1)}, bf16[2304,512]{1,0:T(8,128)(2,1)}, /*index=5*/f32[8,512]{1,0:T(8,128)S(1)}) custom-call(s32[4]{0:T(128)S(1)} %iota_xor_fusion.pos_ref, s32[2,16]{1,0:T(2,128)S(1)} %pad_add_fusion.place_ref, ...), custom_call_target="tpu_custom_call" | custom-call | flops 1 | bytes 1 | tf_op jit(solution)/shard_map/feed/pallas_call | solution.py:455
  72.4 6.0 %mix_back.2 = (bf16[256,512]{1,0:T(8,128)(2,1)S(1)}, bf16[256,512]{1,0:T(8,128)(2,1)S(1)}, bf16[256,512]{1,0:T(8,128)(2,1)S(1)}, bf16[256,512]{1,0:T(8,128)(2,1)...) custom-call(bf16[1024,512]{1,0:T(8,128)(2,1)S(1)} %get-tuple-element.133.refs_0_, ...), custom_call_target="tpu_custom_call" | custom-call | flops 1 | bytes 1 | tf_op jit(solution)/shard_map/mix_back/pallas_call | solution.py:300
  80.9 16.2 %mix_back.3 = (bf16[768,512]{1,0:T(8,128)(2,1)S(1)}, bf16[768,512]{1,0:T(8,128)(2,1)S(1)}, bf16[768,512]{1,0:T(8,128)(2,1)S(1)}, bf16[768,512]{1,0:T(8,128)(2,1)...) custom-call(bf16[1024,512]{1,0:T(8,128)(2,1)S(1)} %get-tuple-element.133.refs_0_, ...), custom_call_target="tpu_custom_call" | custom-call | flops 1 | bytes 1 | tf_op jit(solution)/shard_map/mix_back/pallas_call | solution.py:300
  97.1 1.6 reduce-precision_convert_fusion.1
  100.1 5.5 %input_back.1 = (f32[1024,512]{1,0:T(8,128)}, bf16[16,512]{1,0:T(8,128)(2,1)S(1)}) custom-call(bf16[1024,512]{1,0:T(8,128)(2,1)S(1)} %copy-done.1, f32[1024,512]{1,0:T(8,128)S(1)} %copy-done.8, bf16[4,512,512]{2,1,0:T(8,128)(2,1)S(1)} %copy-done.7, f32[8,512]{1,0:T(8,128)S(1)} %get-tuple-element.111.norm_ref, f32[8,512]{1,0:T(8,128)S(1)} %get-tuple-element.141.dnorm_ref, ...), custom_call_target="tpu_custom_call" | custom-call | flops 1 | bytes 1 | tf_op jit(solution)/shard_map/input_back/pallas_call | solution.py:566
  105.5 3.4 %weight_back.1 = (bf16[1040,512]{1,0:T(8,128)(2,1)S(1)}, bf16[1040,512]{1,0:T(8,128)(2,1)S(1)}) custom-call(s32[4]{0:T(128)S(1)} %iota_xor_fusion.pos_ref, s32[2,16]{1,0:T(2,128)S(1)} %pad_add_fusion.place_ref, bf16[16,512]{1,0:T(8,128)(2,1)S(1)} %get-tuple-element.149.small_ref, bf16[1024,512]{1,0:T(8,128)(2,1)S(1)} %get-tuple-element.150.n_ref, ...), custom_call_target="tpu_custom_call" | custom-call | flops 1 | bytes 1 | tf_op jit(solution)/shard_map/weight_back/pallas_call | solution.py:508
  111.0 2.3 %collective-permute-done.18 = bf16[1040,512]{1,0:T(8,128)(2,1)S(1)} collective-permute-done((bf16[1040,512]{1,0:T(8,128)(2,1)S(1)}, bf16[1040,512]{1,0:T(8,128)(2,1)S(1)}, u32[]{:S(2)}, u32[]{:S(2)}) %collective-permute-start.18) | collective-permute-done | bytes 1064992 | tf_op jit(solution)/shard_map/ppermute | solution.py:593
  114.7 2.6 %collective-permute-start.17 = (bf16[288,512]{1,0:T(8,128)(2,1)S(1)}, bf16[288,512]{1,0:T(8,128)(2,1)S(1)}, u32[]{:S(2)}, u32[]{:S(2)}) collective-permute-start(bf16[288,512]{1,0:T(8,128)(2,1)S(1)} %reduce-precision_convert_fusion.5), channel_id=1, source_target_pairs={{0,16},{1,3},{2,18},{3,1},{4,20},{5,7},{6,22},{7,5},{8,24},{9,11},... | collective-permute-start | bytes 884744 | tf_op jit(solution)/shard_map/ppermute | solution.py:593
  117.2 8.6 %collective-permute-done.19 = bf16[528,512]{1,0:T(8,128)(2,1)S(1)} collective-permute-done((bf16[528,512]{1,0:T(8,128)(2,1)S(1)}, bf16[528,512]{1,0:T(8,128)(2,1)S(1)}, u32[]{:S(2)}, u32[]{:S(2)}) %collective-permute-start.19) | collective-permute-done | bytes 540704 | tf_op jit(solution)/shard_map/ppermute | solution.py:593
  129.7 2.9 %collective-permute-done.21 = bf16[272,512]{1,0:T(8,128)(2,1)S(1)} collective-permute-done((bf16[272,512]{1,0:T(8,128)(2,1)S(1)}, bf16[272,512]{1,0:T(8,128)(2,1)S(1)}, u32[]{:S(2)}, u32[]{:S(2)}) %collective-permute-start.21) | collective-permute-done | bytes 278560 | tf_op jit(solution)/shard_map/ppermute | solution.py:593
  132.7 2.6 %collective-permute-start.23 = (bf16[144,512]{1,0:T(8,128)(2,1)S(1)}, bf16[144,512]{1,0:T(8,128)(2,1)S(1)}, u32[]{:S(2)}, u32[]{:S(2)}) collective-permute-start(bf16[144,512]{1,0:T(8,128)(2,1)S(1)} %pad_maximum_fusion.5), channel_id=1, source_target_pairs={{0,16},{1,3},{2,18},{3,1},{4,20},{5,7},{6,22},{7,5},{8,24},{9,11},... | collective-permute-start | bytes 442376 | tf_op jit(solution)/shard_map/ppermute | solution.py:593
  135.9 6.7 %collective-permute-done.23 = bf16[144,512]{1,0:T(8,128)(2,1)S(1)} collective-permute-done((bf16[144,512]{1,0:T(8,128)(2,1)S(1)}, bf16[144,512]{1,0:T(8,128)(2,1)S(1)}, u32[]{:S(2)}, u32[]{:S(2)}) %collective-permute-start.23) | collective-permute-done | bytes 147488 | tf_op jit(solution)/shard_map/ppermute | solution.py:593
  143.8 3.4 %collective-permute-start.22 = (bf16[288,512]{1,0:T(8,128)(2,1)S(1)}, bf16[288,512]{1,0:T(8,128)(2,1)S(1)}, u32[]{:S(2)}, u32[]{:S(2)}) collective-permute-start(bf16[288,512]{1,0:T(8,128)(2,1)S(1)} %reduce-precision_convert_fusion.3), channel_id=1, source_target_pairs={{0,16},{1,9},{2,18},{3,11},{4,20},{5,13},{6,22},{7,15},{8,24},{9,1... | collective-permute-start | bytes 884744 | tf_op jit(solution)/shard_map/ppermute | solution.py:593
  147.2 3.7 %collective-permute-done.24 = bf16[144,512]{1,0:T(8,128)(2,1)S(1)} collective-permute-done((bf16[144,512]{1,0:T(8,128)(2,1)S(1)}, bf16[144,512]{1,0:T(8,128)(2,1)S(1)}, u32[]{:S(2)}, u32[]{:S(2)}) %collective-permute-start.24) | collective-permute-done | bytes 147488 | tf_op jit(solution)/shard_map/ppermute | solution.py:593
  151.9 3.2 %collective-permute-done.22 = bf16[288,512]{1,0:T(8,128)(2,1)S(1)} collective-permute-done((bf16[288,512]{1,0:T(8,128)(2,1)S(1)}, bf16[288,512]{1,0:T(8,128)(2,1)S(1)}, u32[]{:S(2)}, u32[]{:S(2)}) %collective-permute-start.22) | collective-permute-done | bytes 294944 | tf_op jit(solution)/shard_map/ppermute | solution.py:593
  155.2 3.0 %collective-permute-done.25 = bf16[128,512]{1,0:T(8,128)(2,1)S(1)} collective-permute-done((bf16[128,512]{1,0:T(8,128)(2,1)S(1)}, bf16[128,512]{1,0:T(8,128)(2,1)S(1)}, u32[]{:S(2)}, u32[]{:S(2)}) %collective-permute-start.25) | collective-permute-done | bytes 131104 | tf_op jit(solution)/shard_map/ppermute | solution.py:593
  160.5 2.0 collective-permute-done.26
  166.0 2.1 collective-permute-done.28.other_ref
  168.7 4.8 %renew.1 = (bf16[464,512]{1,0:T(8,128)(2,1)}, bf16[384,512]{1,0:T(8,128)(2,1)}, f32[1]{0:T(128)}) custom-call(s32[1]{0:T(128)} %bitcast.2.half_ref.side_ref, s32[4]{0:T(128)} %broadcast_select_fusion.8.index_ref, f32[8,128]{1,0:T(8,128)} %copy-done.18, f32[8,128]{1,0:T(8,128)} %copy-done.20, bf16[576,512]{1,0:T(8,128)(2,1)} %copy-done, ...), custom_call_target="tpu_custom_call" | custom-call | flops 1 | bytes 1 | tf_op jit(solution)/shard_map/renew/pallas_call | solution.py:750
  176.3 11.2 %update.1 = (f32[5,128,512]{2,1,0:T(8,128)}, f32[5,128,512]{2,1,0:T(8,128)}, f32[5,128,512]{2,1,0:T(8,128)}, f32[128,2048]{1,0:T(8,128)}, f32[128,2048]{1,0:T(8,...) custom-call(s32[1]{0:T(128)} %bitcast.2.half_ref.side_ref, ...), custom_call_target="tpu_custom_call" | custom-call | flops 1 | bytes 1 | tf_op jit(solution)/shard_map/update/pallas_call | solution.py:845
  195.2 2.9 %unpack_near.1 = (bf16[5,512,512]{2,1,0:T(8,128)(2,1)}, bf16[512,2048]{1,0:T(8,128)(2,1)}, bf16[2048,512]{1,0:T(8,128)(2,1)}) custom-call(s32[4]{0:T(128)S(1)} %iota_xor_fusion.pos_ref, s32[1]{0:T(128)} %bitcast.2.half_ref.side_ref, bf16[1024,512]{1,0:T(8,128)(2,1)S(1)} %copy-done.10, bf16[640,512]{1,0:T(8,128)(2,1)S(1)} %copy-done.11, ...), custom_call_target="tpu_custom_call" | custom-call | flops 1 | bytes 1 | tf_op jit(solution)/shard_map/unpack_near/pallas_call | solution.py:951
  198.1 2.3 %collective-permute-done.32.refs_0_ = bf16[384,512]{1,0:T(8,128)(2,1)S(1)} collective-permute-done((bf16[384,512]{1,0:T(8,128)(2,1)}, bf16[384,512]{1,0:T(8,128)(2,1)S(1)}, u32[]{:S(2)}, u32[]{:S(2)}) %collective-permute-start.32) | collective-permute-done | bytes 393248 | tf_op jit(solution)/shard_map/ppermute | solution.py:593
  203.3 4.3 %collective-permute-done.37.refs_2_ = bf16[256,512]{1,0:T(8,128)(2,1)S(1)} collective-permute-done((bf16[256,512]{1,0:T(8,128)(2,1)S(1)}, bf16[256,512]{1,0:T(8,128)(2,1)S(1)}, u32[]{:S(2)}, u32[]{:S(2)}) %collective-permute-start.37) | collective-permute-done | bytes 262176 | tf_op jit(solution)/shard_map/ppermute | solution.py:593
  209.4 2.4 %unpack_far.1 = (bf16[5,512,512]{2,1,0:T(8,128)(2,1)}, bf16[512,2048]{1,0:T(8,128)(2,1)}, bf16[2048,512]{1,0:T(8,128)(2,1)}) custom-call(s32[4]{0:T(128)S(1)} %iota_xor_fusion.pos_ref, s32[1]{0:T(128)} %bitcast.2.half_ref.side_ref, ...), custom_call_target="tpu_custom_call", output_to_operand_aliasing={{0}: (10, {}), {1}: (11, {}), {2}: (12, {})} | custom-call | flops 1 | bytes 1 | tf_op jit(solution)/shard_map/unpack_far/pallas_call | solution.py:966
  (167 shorter events, 49.6 us)
Async XLA Ops:
  2.4 23.0 %collective-permute-start = (bf16[544,512]{1,0:T(8,128)(2,1)S(1)}, bf16[544,512]{1,0:T(8,128)(2,1)}, u32[]{:S(2)}, u32[]{:S(2)}) collective-permute-start(bf16[544,512]{1,0:T(8,128)(2,1)S(1)} %fusion.5.near0), channel_id=1, source_target_pairs={{0,1},{1,0},{2,3},{3,2},{4,5},{5,4},{6,7},{7,6},{8,9},{9,8},{10,11... | collective-permute-start | bytes 1671176 | tf_op jit(solution)/shard_map/ppermute | solution.py:593
  3.0 10.4 %collective-permute-start.1 = (bf16[272,512]{1,0:T(8,128)(2,1)S(1)}, bf16[272,512]{1,0:T(8,128)(2,1)}, u32[]{:S(2)}, u32[]{:S(2)}) collective-permute-start(bf16[272,512]{1,0:T(8,128)(2,1)S(1)} %constant_dynamic-slice_fusion), channel_id=1, source_target_pairs={{0,2},{1,3},{2,0},{3,1},{4,6},{5,7},{6,4},{7,5},{8,10},{9,11},{10,... | collective-permute-start | bytes 835592 | tf_op jit(solution)/shard_map/ppermute | solution.py:593
  13.4 8.3 %collective-permute-start.4 = (bf16[272,512]{1,0:T(8,128)(2,1)}, bf16[272,512]{1,0:T(8,128)(2,1)}, u32[]{:S(2)}, u32[]{:S(2)}) collective-permute-start(bf16[272,512]{1,0:T(8,128)(2,1)} %collective-permute-done.1.far0), channel_id=1, source_target_pairs={{0,4},{1,5},{2,6},{3,7},{4,0},{5,1},{6,2},{7,3},{8,12},{9,13},{10,... | collective-permute-start | bytes 835592 | tf_op jit(solution)/shard_map/ppermute | solution.py:593
  15.1 4.5 %collective-permute-start.10 = (f32[8]{0:T(128)S(1)}, f32[8]{0:T(128)S(1)}, u32[]{:S(2)}, u32[]{:S(2)}) collective-permute-start(f32[8]{0:T(128)S(1)} %fusion.12), channel_id=1, source_target_pairs={{0,16},{1,17},{2,18},{3,19},{4,20},{5,21},{6,22},{7,23},{8,24},{9,... | collective-permute-start | bytes 104 | tf_op jit(solution)/shard_map/ppermute | solution.py:593
  17.8 26.2 %collective-permute-start.8 = (bf16[640,512]{1,0:T(8,128)(2,1)S(1)}, bf16[640,512]{1,0:T(8,128)(2,1)S(1)}, u32[]{:S(2)}, u32[]{:S(2)}) collective-permute-start(bf16[640,512]{1,0:T(8,128)(2,1)S(1)} %slice_dynamic-update-slice_fusion.p0), channel_id=1, source_target_pairs={{0,2},{1,3},{2,0},{3,1},{4,6},{5,7},{6,4},{7,5},{8,10},{9,11},{10,... | collective-permute-start | bytes 1966088 | tf_op jit(solution)/shard_map/ppermute | solution.py:593
  21.8 23.2 %collective-permute-start.12 = (bf16[528,512]{1,0:T(8,128)(2,1)S(1)}, bf16[528,512]{1,0:T(8,128)(2,1)}, u32[]{:S(2)}, u32[]{:S(2)}) collective-permute-start(bf16[528,512]{1,0:T(8,128)(2,1)S(1)} %fusion.6.t0), channel_id=1, source_target_pairs={{0,2},{1,3},{2,0},{3,1},{4,6},{5,7},{6,4},{7,5},{8,10},{9,11},{10,... | collective-permute-start | bytes 1622024 | tf_op jit(solution)/shard_map/ppermute | solution.py:593
  25.3 19.7 %collective-permute-start.7 = (bf16[640,512]{1,0:T(8,128)(2,1)S(1)}, bf16[640,512]{1,0:T(8,128)(2,1)S(1)}, u32[]{:S(2)}, u32[]{:S(2)}) collective-permute-start(bf16[640,512]{1,0:T(8,128)(2,1)S(1)} %slice_dynamic-update-slice_fusion.p0), channel_id=1, source_target_pairs={{0,1},{1,0},{2,3},{3,2},{4,5},{5,4},{6,7},{7,6},{8,9},{9,8},{10,11... | collective-permute-start | bytes 1966088 | tf_op jit(solution)/shard_map/ppermute | solution.py:593
  72.3 6.2 %collective-permute-start.14 = (bf16[2304,512]{1,0:T(8,128)(2,1)}, bf16[2304,512]{1,0:T(8,128)(2,1)}, u32[]{:S(2)}, u32[]{:S(2)}) collective-permute-start(bf16[2304,512]{1,0:T(8,128)(2,1)} %get-tuple-element.119), channel_id=1, source_target_pairs={{0,1},{1,0},{2,3},{3,2},{4,5},{5,4},{6,7},{7,6},{8,9},{9,8},{10,11... | collective-permute-start | bytes 7077896 | tf_op jit(solution)/shard_map/ppermute | solution.py:593
  80.1 17.0 %collective-permute-start.15 = (bf16[1152,512]{1,0:T(8,128)(2,1)S(1)}, bf16[1152,512]{1,0:T(8,128)(2,1)}, u32[]{:S(2)}, u32[]{:S(2)}) collective-permute-start(bf16[1152,512]{1,0:T(8,128)(2,1)S(1)} %reduce-precision_convert_fusion), channel_id=1, source_target_pairs={{0,2},{1,5},{2,0},{3,7},{4,6},{5,1},{6,4},{7,3},{8,10},{9,13},{10,... | collective-permute-start | bytes 3538952 | tf_op jit(solution)/shard_map/ppermute | solution.py:593
  98.7 10.2 %collective-permute-start.16 = (bf16[576,512]{1,0:T(8,128)(2,1)S(1)}, bf16[576,512]{1,0:T(8,128)(2,1)S(1)}, u32[]{:S(2)}, u32[]{:S(2)}) collective-permute-start(bf16[576,512]{1,0:T(8,128)(2,1)S(1)} %reduce-precision_convert_fusion.1), channel_id=1, source_target_pairs={{0,4},{1,9},{2,6},{3,11},{4,0},{5,13},{6,2},{7,15},{8,12},{9,1},{1... | collective-permute-start | bytes 1769480 | tf_op jit(solution)/shard_map/ppermute | solution.py:593
  113.6 12.2 %collective-permute-start.19 = (bf16[528,512]{1,0:T(8,128)(2,1)S(1)}, bf16[528,512]{1,0:T(8,128)(2,1)S(1)}, u32[]{:S(2)}, u32[]{:S(2)}) collective-permute-start(bf16[528,512]{1,0:T(8,128)(2,1)S(1)} %pad_maximum_fusion.2), channel_id=1, source_target_pairs={{0,2},{1,5},{2,0},{3,7},{4,6},{5,1},{6,4},{7,3},{8,10},{9,13},{10,... | collective-permute-start | bytes 1622024 | tf_op jit(solution)/shard_map/ppermute | solution.py:593
  114.7 12.3 %collective-permute-start.17 = (bf16[288,512]{1,0:T(8,128)(2,1)S(1)}, bf16[288,512]{1,0:T(8,128)(2,1)S(1)}, u32[]{:S(2)}, u32[]{:S(2)}) collective-permute-start(bf16[288,512]{1,0:T(8,128)(2,1)S(1)} %reduce-precision_convert_fusion.5), channel_id=1, source_target_pairs={{0,16},{1,3},{2,18},{3,1},{4,20},{5,7},{6,22},{7,5},{8,24},{9,11},... | collective-permute-start | bytes 884744 | tf_op jit(solution)/shard_map/ppermute | solution.py:593
  125.9 6.6 %collective-permute-start.21 = (bf16[272,512]{1,0:T(8,128)(2,1)S(1)}, bf16[272,512]{1,0:T(8,128)(2,1)S(1)}, u32[]{:S(2)}, u32[]{:S(2)}) collective-permute-start(bf16[272,512]{1,0:T(8,128)(2,1)S(1)} %pad_maximum_fusion.3), channel_id=1, source_target_pairs={{0,4},{1,9},{2,6},{3,11},{4,0},{5,13},{6,2},{7,15},{8,12},{9,1},{1... | collective-permute-start | bytes 835592 | tf_op jit(solution)/shard_map/ppermute | solution.py:593
  128.2 7.7 %collective-permute-start.20 = (bf16[288,512]{1,0:T(8,128)(2,1)S(1)}, bf16[288,512]{1,0:T(8,128)(2,1)S(1)}, u32[]{:S(2)}, u32[]{:S(2)}) collective-permute-start(bf16[288,512]{1,0:T(8,128)(2,1)S(1)} %reduce-precision_convert_fusion.4), channel_id=1, source_target_pairs={{0,8},{1,17},{2,10},{3,19},{4,12},{5,21},{6,14},{7,23},{8,0},{9,25... | collective-permute-start | bytes 884744 | tf_op jit(solution)/shard_map/ppermute | solution.py:593
  132.7 10.0 %collective-permute-start.23 = (bf16[144,512]{1,0:T(8,128)(2,1)S(1)}, bf16[144,512]{1,0:T(8,128)(2,1)S(1)}, u32[]{:S(2)}, u32[]{:S(2)}) collective-permute-start(bf16[144,512]{1,0:T(8,128)(2,1)S(1)} %pad_maximum_fusion.5), channel_id=1, source_target_pairs={{0,16},{1,3},{2,18},{3,1},{4,20},{5,7},{6,22},{7,5},{8,24},{9,11},... | collective-permute-start | bytes 442376 | tf_op jit(solution)/shard_map/ppermute | solution.py:593
  142.8 8.2 %collective-permute-start.24 = (bf16[144,512]{1,0:T(8,128)(2,1)S(1)}, bf16[144,512]{1,0:T(8,128)(2,1)S(1)}, u32[]{:S(2)}, u32[]{:S(2)}) collective-permute-start(bf16[144,512]{1,0:T(8,128)(2,1)S(1)} %pad_maximum_fusion.6), channel_id=1, source_target_pairs={{0,8},{1,17},{2,10},{3,19},{4,12},{5,21},{6,14},{7,23},{8,0},{9,25... | collective-permute-start | bytes 442376 | tf_op jit(solution)/shard_map/ppermute | solution.py:593
  143.8 11.3 %collective-permute-start.22 = (bf16[288,512]{1,0:T(8,128)(2,1)S(1)}, bf16[288,512]{1,0:T(8,128)(2,1)S(1)}, u32[]{:S(2)}, u32[]{:S(2)}) collective-permute-start(bf16[288,512]{1,0:T(8,128)(2,1)S(1)} %reduce-precision_convert_fusion.3), channel_id=1, source_target_pairs={{0,16},{1,9},{2,18},{3,11},{4,20},{5,13},{6,22},{7,15},{8,24},{9,1... | collective-permute-start | bytes 884744 | tf_op jit(solution)/shard_map/ppermute | solution.py:593
  151.0 7.1 %collective-permute-start.25 = (bf16[128,512]{1,0:T(8,128)(2,1)S(1)}, bf16[128,512]{1,0:T(8,128)(2,1)S(1)}, u32[]{:S(2)}, u32[]{:S(2)}) collective-permute-start(bf16[128,512]{1,0:T(8,128)(2,1)S(1)} %slice.237), channel_id=1, source_target_pairs={{0,16},{1,9},{2,18},{3,11},{4,20},{5,13},{6,22},{7,15},{8,24},{9,1... | collective-permute-start | bytes 393224 | tf_op jit(solution)/shard_map/ppermute | solution.py:593
  158.7 3.8 %collective-permute-start.26 = (f32[8,128]{1,0:T(8,128)S(1)}, f32[8,128]{1,0:T(8,128)S(1)}, u32[]{:S(2)}, u32[]{:S(2)}) collective-permute-start(f32[8,128]{1,0:T(8,128)S(1)} %squares.1), channel_id=1, source_target_pairs={{0,4},{1,5},{2,6},{3,7},{4,0},{5,1},{6,2},{7,3},{8,12},{9,13},{10,... | collective-permute-start | bytes 12296 | tf_op jit(solution)/shard_map/ppermute | solution.py:593
  162.5 12.9 %collective-permute-start.29 = (bf16[832,512]{1,0:T(8,128)(2,1)}, bf16[832,512]{1,0:T(8,128)(2,1)S(1)}, u32[]{:S(2)}, u32[]{:S(2)}) collective-permute-start(bf16[832,512]{1,0:T(8,128)(2,1)} %pad_maximum_fusion), channel_id=1, source_target_pairs={{0,4},{1,5},{2,6},{3,7},{4,0},{5,1},{6,2},{7,3},{8,12},{9,13},{10,... | collective-permute-start | bytes 2555912 | tf_op jit(solution)/shard_map/ppermute | solution.py:593
  164.5 3.6 %collective-permute-start.28 = (f32[8,128]{1,0:T(8,128)S(1)}, f32[8,128]{1,0:T(8,128)S(1)}, u32[]{:S(2)}, u32[]{:S(2)}) collective-permute-start(f32[8,128]{1,0:T(8,128)S(1)} %add.303.square_ref), channel_id=1, source_target_pairs={{0,2},{1,3},{2,0},{3,1},{4,6},{5,7},{6,4},{7,5},{8,10},{9,11},{10,... | collective-permute-start | bytes 12296 | tf_op jit(solution)/shard_map/ppermute | solution.py:593
  173.5 14.0 %collective-permute-start.30 = (bf16[464,512]{1,0:T(8,128)(2,1)}, bf16[464,512]{1,0:T(8,128)(2,1)S(1)}, u32[]{:S(2)}, u32[]{:S(2)}) collective-permute-start(bf16[464,512]{1,0:T(8,128)(2,1)} %get-tuple-element.161), channel_id=1, source_target_pairs={{0,2},{1,3},{2,0},{3,1},{4,6},{5,7},{6,4},{7,5},{8,10},{9,11},{10,... | collective-permute-start | bytes 1425416 | tf_op jit(solution)/shard_map/ppermute | solution.py:593
  175.2 12.2 %collective-permute-start.31 = (bf16[16,512]{1,0:T(8,128)(2,1)S(1)}, bf16[16,512]{1,0:T(8,128)(2,1)S(1)}, u32[]{:S(2)}, u32[]{:S(2)}) collective-permute-start(bf16[16,512]{1,0:T(8,128)(2,1)S(1)} %slice.205), channel_id=1, source_target_pairs={{0,1},{1,0},{2,3},{3,2},{4,5},{5,4},{6,7},{7,6},{8,9},{9,8},{10,11... | collective-permute-start | bytes 49160 | tf_op jit(solution)/shard_map/ppermute | solution.py:593
  187.5 5.4 %collective-permute-start.34 = (bf16[1024,512]{1,0:T(8,128)(2,1)}, bf16[1024,512]{1,0:T(8,128)(2,1)S(1)}, u32[]{:S(2)}, u32[]{:S(2)}) collective-permute-start(bf16[1024,512]{1,0:T(8,128)(2,1)} %get-tuple-element.184.p0), channel_id=1, source_target_pairs={{0,1},{1,0},{2,3},{3,2},{4,5},{5,4},{6,7},{7,6},{8,9},{9,8},{10,11... | collective-permute-start | bytes 3145736 | tf_op jit(solution)/shard_map/ppermute | solution.py:593
  187.9 3.7 %collective-permute-start.33 = (bf16[464,512]{1,0:T(8,128)(2,1)S(1)}, bf16[464,512]{1,0:T(8,128)(2,1)S(1)}, u32[]{:S(2)}, u32[]{:S(2)}) collective-permute-start(bf16[464,512]{1,0:T(8,128)(2,1)S(1)} %collective-permute-done.30.p4), channel_id=1, source_target_pairs={{0,1},{1,0},{2,3},{3,2},{4,5},{5,4},{6,7},{7,6},{8,9},{9,8},{10,11... | collective-permute-start | bytes 1425416 | tf_op jit(solution)/shard_map/ppermute | solution.py:593
  188.1 4.8 %collective-permute-start.35 = (bf16[640,512]{1,0:T(8,128)(2,1)}, bf16[640,512]{1,0:T(8,128)(2,1)S(1)}, u32[]{:S(2)}, u32[]{:S(2)}) collective-permute-start(bf16[640,512]{1,0:T(8,128)(2,1)} %get-tuple-element.185.p1), channel_id=1, source_target_pairs={{0,1},{1,0},{2,3},{3,2},{4,5},{5,4},{6,7},{7,6},{8,9},{9,8},{10,11... | collective-permute-start | bytes 1966088 | tf_op jit(solution)/shard_map/ppermute | solution.py:593
  188.4 13.2 %collective-permute-start.36 = (bf16[464,512]{1,0:T(8,128)(2,1)S(1)}, bf16[464,512]{1,0:T(8,128)(2,1)S(1)}, u32[]{:S(2)}, u32[]{:S(2)}) collective-permute-start(bf16[464,512]{1,0:T(8,128)(2,1)S(1)} %collective-permute-done.30.p4), channel_id=1, source_target_pairs={{0,4},{1,5},{2,6},{3,7},{4,0},{5,1},{6,2},{7,3},{8,12},{9,13},{10,... | collective-permute-start | bytes 1425416 | tf_op jit(solution)/shard_map/ppermute | solution.py:593
  189.4 11.0 %collective-permute-start.32 = (bf16[384,512]{1,0:T(8,128)(2,1)}, bf16[384,512]{1,0:T(8,128)(2,1)S(1)}, u32[]{:S(2)}, u32[]{:S(2)}) collective-permute-start(bf16[384,512]{1,0:T(8,128)(2,1)} %get-tuple-element.181), channel_id=1, source_target_pairs={{0,2},{1,3},{2,0},{3,1},{4,6},{5,7},{6,4},{7,5},{8,10},{9,11},{10,... | collective-permute-start | bytes 1179656 | tf_op jit(solution)/shard_map/ppermute | solution.py:593
  200.4 7.2 %collective-permute-start.37 = (bf16[256,512]{1,0:T(8,128)(2,1)S(1)}, bf16[256,512]{1,0:T(8,128)(2,1)S(1)}, u32[]{:S(2)}, u32[]{:S(2)}) collective-permute-start(bf16[256,512]{1,0:T(8,128)(2,1)S(1)} %slice.211), channel_id=1, source_target_pairs={{0,4},{1,5},{2,6},{3,7},{4,0},{5,1},{6,2},{7,3},{8,12},{9,13},{10,... | collective-permute-start | bytes 786440 | tf_op jit(solution)/shard_map/ppermute | solution.py:593
  201.6 7.7 %collective-permute-start.40 = (bf16[464,512]{1,0:T(8,128)(2,1)S(1)}, bf16[464,512]{1,0:T(8,128)(2,1)S(1)}, u32[]{:S(2)}, u32[]{:S(2)}) collective-permute-start(bf16[464,512]{1,0:T(8,128)(2,1)S(1)} %collective-permute-done.36.refs_1_), channel_id=1, source_target_pairs={{0,1},{1,0},{2,3},{3,2},{4,5},{5,4},{6,7},{7,6},{8,9},{9,8},{10,11... | collective-permute-start | bytes 1425416 | tf_op jit(solution)/shard_map/ppermute | solution.py:593
  201.6 7.7 %collective-permute-start.39 = (bf16[384,512]{1,0:T(8,128)(2,1)S(1)}, bf16[384,512]{1,0:T(8,128)(2,1)S(1)}, u32[]{:S(2)}, u32[]{:S(2)}) collective-permute-start(bf16[384,512]{1,0:T(8,128)(2,1)S(1)} %collective-permute-done.32.refs_0_), channel_id=1, source_target_pairs={{0,1},{1,0},{2,3},{3,2},{4,5},{5,4},{6,7},{7,6},{8,9},{9,8},{10,11... | collective-permute-start | bytes 1179656 | tf_op jit(solution)/shard_map/ppermute | solution.py:593
  202.2 5.5 %collective-permute-start.38 = (bf16[128,512]{1,0:T(8,128)(2,1)S(1)}, bf16[128,512]{1,0:T(8,128)(2,1)S(1)}, u32[]{:S(2)}, u32[]{:S(2)}) collective-permute-start(bf16[128,512]{1,0:T(8,128)(2,1)S(1)} %copy-done.21), channel_id=1, source_target_pairs={{0,2},{1,3},{2,0},{3,1},{4,6},{5,7},{6,4},{7,5},{8,10},{9,11},{10,... | collective-permute-start | bytes 393224 | tf_op jit(solution)/shard_map/ppermute | solution.py:593
  (34 other events, 255.5 us)

commit v8 on v7

--- a/solution.py
+++ b/solution.py
@@ -9,7 +9,7 @@
 BF = jnp.bfloat16
 F32 = jnp.float32
 MIB = 1024 * 1024
-VMEM_ATTEND = 40 * MIB
+VMEM_ATTEND = 48 * MIB
 VMEM_MIX = 44 * MIB
 VMEM_FEED = 44 * MIB
 VMEM_BACK = 24 * MIB
@@ -521,13 +521,24 @@
 
 
 def input_back_kernel(x_ref, dh_ref, w_ref, norm_ref, dnorm_ref, *refs):
-    grads_in, (dx_ref, small_ref, sums, dn_ref) = refs[:-4], refs[-4:]
+    grads_in, (dx_ref, small_ref, sums) = refs[:-3], refs[-3:]
     step = pl.program_id(0)
     tile = x_ref.shape[0]
 
     @pl.when(step == 0)
     def _():
         sums[...] = jnp.zeros_like(sums)
+
+    def rows_back(parts, first):
+        rows = pl.ds(pl.multiple_of(first, tile), tile)
+        dn = None
+        for m in range(4):
+            term = dot_nt(parts[m][rows, :], w_ref[m])
+            dn = term if dn is None else dn + term
+        unit, inv = normalise(x_ref[...].astype(F32))
+        dx_ref[...] = dh_ref[...] + normalise_back(dn, unit, inv, norm_ref[0:1, :])
+        sums[0:1, :] += jnp.sum(dn * unit, axis=0, keepdims=True)
+        sums[1:2, :] += jnp.sum(dn, axis=0, keepdims=True)
 
     first = 0
     for j in range(len(grads_in) // 4):
@@ -536,20 +547,9 @@
 
         @pl.when((step >= begin) & (step < begin + count))
         def _():
-            rows = pl.ds(pl.multiple_of((step - begin) * tile, tile), tile)
-            dn = None
-            for m in range(4):
-                term = dot_nt(grads_in[4 * j + m][rows, :], w_ref[m])
-                dn = term if dn is None else dn + term
-            dn_ref[...] = dn
+            rows_back(grads_in[4 * j : 4 * j + 4], (step - begin) * tile)
 
         first += count
-
-    dn = dn_ref[...]
-    unit, inv = normalise(x_ref[...].astype(F32))
-    dx_ref[...] = dh_ref[...] + normalise_back(dn, unit, inv, norm_ref[0:1, :])
-    sums[0:1, :] += jnp.sum(dn * unit, axis=0, keepdims=True)
-    sums[1:2, :] += jnp.sum(dn, axis=0, keepdims=True)
 
     @pl.when(step == pl.num_programs(0) - 1)
     def _():
@@ -569,7 +569,7 @@
         in_specs=[block] * 2 + [whole(w), whole(norm), whole(dnorm)] + [whole(a) for a in halves],
         out_specs=[block, whole(small)],
         out_shape=[jax.ShapeDtypeStruct((length, width), F32), small],
-        scratch_shapes=[pltpu.VMEM((8, width), F32), pltpu.VMEM((tile, width), F32)],
+        scratch_shapes=[pltpu.VMEM((8, width), F32)],
         compiler_params=pltpu.CompilerParams(
             dimension_semantics=("arbitrary",), vmem_limit_bytes=VMEM_BACK
         ),

time: 213 us -> 212 us (level)
  other arithmetic: 11 us -> 8.36 us
    unnamed x50 -> x54, local copies, waits for them, and re-layouts: 5.23 us -> 6.8 us
  transfers between devices with their start and end apart: 43 -> 43, of which waited for: 25 -> 25; matrix products, arithmetic and copies ran while one was open for 3% -> 2% of each run, Pallas kernels for 32% -> 31%
where the time goes in v8:
time: 212 us; the launch traced here: 211 us
  Pallas kernels  93.3 us (44%)
  waiting for transfers between devices  57.6 us (27%)
  starting transfers between devices  42.2 us (20%)
  other arithmetic  8.36 us (4%)
  local copies, waits for them, and re-layouts  7.73 us (4%)
  between operations  2.18 us (1%)
    ppermute x43, waiting for transfers between devices, exchange(): return lax.ppermute(values, ('dp', 'shard'), perm)  57.6 us
    ppermute x43, starting transfers between devices, exchange(): return lax.ppermute(values, ('dp', 'shard'), perm)  42.2 us
    pallas_call x1, Pallas kernels, feed(): pl.pallas_call(feed_kernel, grid=(4,), in_specs=[pl.BlockSpec(memory_spac...  24.6 us
    pallas_call x2, Pallas kernels, mix_back(): pl.pallas_call(functools.partial(mix_back_kernel, begun=bool(before)), gr...  22.2 us
    pallas_call x1, Pallas kernels, attend(): pl.pallas_call(attend_kernel, grid=(steps,), in_specs=[pl.BlockSpec(memor...  16.8 us
    pallas_call x1, Pallas kernels, update(): pl.pallas_call(update_kernel, grid=(steps,), in_specs=[smem] * 2 + [whole...  11.2 us
    unnamed x54, local copies, waits for them, and re-layouts  6.8 us
    pallas_call x1, Pallas kernels, renew(): pl.pallas_call(renew_kernel, grid_spec=pltpu.PrefetchScalarGridSpec(num_s...  4.79 us
  transfers between devices with their start and end apart: 43, of which 25 were waited for; matrix products, arithmetic and copies ran while one was open for 2% of the time, Pallas kernels for 31%

profile of v8, /device:TPU:0, one launch (start us, length us, event | category | flops | bytes accessed | tf_op | source)
XLA Modules:
  0.0 211.4 jit_solution(14678401453473427267)
XLA Ops:
  3.0 2.6 %collective-permute-start.1 = (bf16[272,512]{1,0:T(8,128)(2,1)S(1)}, bf16[272,512]{1,0:T(8,128)(2,1)S(1)}, u32[]{:S(2)}, u32[]{:S(2)}) collective-permute-start(bf16[272,512]{1,0:T(8,128)(2,1)S(1)} %constant_dynamic-slice_fusion), channel_id=1, source_target_pairs={{0,2},{1,3},{2,0},{3,1},{4,6},{5,7},{6,4},{7,5},{8,10},{9,11},{10,... | collective-permute-start | bytes 835592 | tf_op jit(solution)/shard_map/ppermute | solution.py:593
  7.9 1.9 collective-permute-done.2
  11.4 2.0 collective-permute-done.3
  15.1 2.7 %collective-permute-start.10 = (f32[8]{0:T(128)S(1)}, f32[8]{0:T(128)S(1)}, u32[]{:S(2)}, u32[]{:S(2)}) collective-permute-start(f32[8]{0:T(128)S(1)} %fusion.12), channel_id=1, source_target_pairs={{0,16},{1,17},{2,18},{3,19},{4,20},{5,21},{6,22},{7,23},{8,24},{9,... | collective-permute-start | bytes 104 | tf_op jit(solution)/shard_map/ppermute | solution.py:593
  19.6 1.8 collective-permute-done.4.far1
  26.8 16.8 %attend.1 = (bf16[1024,512]{1,0:T(8,128)(2,1)S(1)}, bf16[1024,512]{1,0:T(8,128)(2,1)S(1)}, bf16[1024,512]{1,0:T(8,128)(2,1)S(1)}, bf16[1024,512]{1,0:T(8,128)(2,...) custom-call(s32[4]{0:T(128)S(1)} %iota_xor_fusion.pos_ref, ...), custom_call_target="tpu_custom_call" | custom-call | flops 1 | bytes 1 | tf_op jit(solution)/shard_map/attend/pallas_call | solution.py:217
  44.9 2.5 %collective-permute-done.11.t1 = bf16[528,512]{1,0:T(8,128)(2,1)S(1)} collective-permute-done((bf16[528,512]{1,0:T(8,128)(2,1)S(1)}, bf16[528,512]{1,0:T(8,128)(2,1)S(1)}, u32[]{:S(2)}, u32[]{:S(2)}) %collective-permute-start.11) | collective-permute-done | bytes 540704 | tf_op jit(solution)/shard_map/ppermute | solution.py:593
  48.8 24.6 %feed.1 = (bf16[1024,512]{1,0:T(8,128)(2,1)}, f32[1024,512]{1,0:T(8,128)}, bf16[1024,512]{1,0:T(8,128)(2,1)S(1)}, bf16[2304,512]{1,0:T(8,128)(2,1)}, bf16[2304,512]{1,0:T(8,128)(2,1)}, /*index=5*/f32[8,512]{1,0:T(8,128)S(1)}) custom-call(s32[4]{0:T(128)S(1)} %iota_xor_fusion.pos_ref, s32[2,16]{1,0:T(2,128)S(1)} %pad_add_fusion.place_ref, ...), custom_call_target="tpu_custom_call" | custom-call | flops 1 | bytes 1 | tf_op jit(solution)/shard_map/feed/pallas_call | solution.py:455
  73.7 6.0 %mix_back.2 = (bf16[256,512]{1,0:T(8,128)(2,1)S(1)}, bf16[256,512]{1,0:T(8,128)(2,1)S(1)}, bf16[256,512]{1,0:T(8,128)(2,1)S(1)}, bf16[256,512]{1,0:T(8,128)(2,1)...) custom-call(bf16[1024,512]{1,0:T(8,128)(2,1)S(1)} %get-tuple-element.133.refs_0_, ...), custom_call_target="tpu_custom_call" | custom-call | flops 1 | bytes 1 | tf_op jit(solution)/shard_map/mix_back/pallas_call | solution.py:300
  80.9 16.2 %mix_back.3 = (bf16[768,512]{1,0:T(8,128)(2,1)S(1)}, bf16[768,512]{1,0:T(8,128)(2,1)S(1)}, bf16[768,512]{1,0:T(8,128)(2,1)S(1)}, bf16[768,512]{1,0:T(8,128)(2,1)...) custom-call(bf16[1024,512]{1,0:T(8,128)(2,1)S(1)} %get-tuple-element.133.refs_0_, ...), custom_call_target="tpu_custom_call" | custom-call | flops 1 | bytes 1 | tf_op jit(solution)/shard_map/mix_back/pallas_call | solution.py:300
  99.9 4.5 %input_back.1 = (f32[1024,512]{1,0:T(8,128)}, bf16[16,512]{1,0:T(8,128)(2,1)S(1)}) custom-call(bf16[1024,512]{1,0:T(8,128)(2,1)S(1)} %copy-done.1, f32[1024,512]{1,0:T(8,128)S(1)} %copy-done.7, bf16[4,512,512]{2,1,0:T(8,128)(2,1)S(1)} %copy-done.6, f32[8,512]{1,0:T(8,128)S(1)} %get-tuple-element.111.norm_ref, f32[8,512]{1,0:T(8,128)S(1)} %get-tuple-element.141.dnorm_ref, ...), custom_call_target="tpu_custom_call" | custom-call | flops 1 | bytes 1 | tf_op jit(solution)/shard_map/input_back/pallas_call | solution.py:566
  104.5 3.4 %weight_back.1 = (bf16[1040,512]{1,0:T(8,128)(2,1)S(1)}, bf16[1040,512]{1,0:T(8,128)(2,1)S(1)}) custom-call(s32[4]{0:T(128)S(1)} %iota_xor_fusion.pos_ref, s32[2,16]{1,0:T(2,128)S(1)} %pad_add_fusion.place_ref, bf16[16,512]{1,0:T(8,128)(2,1)S(1)} %get-tuple-element.149.small_ref, bf16[1024,512]{1,0:T(8,128)(2,1)S(1)} %copy-done.11, ...), custom_call_target="tpu_custom_call" | custom-call | flops 1 | bytes 1 | tf_op jit(solution)/shard_map/weight_back/pallas_call | solution.py:508
  109.7 2.6 %collective-permute-done.18 = bf16[1040,512]{1,0:T(8,128)(2,1)S(1)} collective-permute-done((bf16[1040,512]{1,0:T(8,128)(2,1)S(1)}, bf16[1040,512]{1,0:T(8,128)(2,1)S(1)}, u32[]{:S(2)}, u32[]{:S(2)}) %collective-permute-start.18) | collective-permute-done | bytes 1064992 | tf_op jit(solution)/shard_map/ppermute | solution.py:593
  113.9 2.6 %collective-permute-start.17 = (bf16[288,512]{1,0:T(8,128)(2,1)S(1)}, bf16[288,512]{1,0:T(8,128)(2,1)S(1)}, u32[]{:S(2)}, u32[]{:S(2)}) collective-permute-start(bf16[288,512]{1,0:T(8,128)(2,1)S(1)} %reduce-precision_convert_fusion.5), channel_id=1, source_target_pairs={{0,16},{1,3},{2,18},{3,1},{4,20},{5,7},{6,22},{7,5},{8,24},{9,11},... | collective-permute-start | bytes 884744 | tf_op jit(solution)/shard_map/ppermute | solution.py:593
  116.5 8.6 %collective-permute-done.19 = bf16[528,512]{1,0:T(8,128)(2,1)S(1)} collective-permute-done((bf16[528,512]{1,0:T(8,128)(2,1)S(1)}, bf16[528,512]{1,0:T(8,128)(2,1)S(1)}, u32[]{:S(2)}, u32[]{:S(2)}) %collective-permute-start.19) | collective-permute-done | bytes 540704 | tf_op jit(solution)/shard_map/ppermute | solution.py:593
  129.0 2.8 %collective-permute-done.21 = bf16[272,512]{1,0:T(8,128)(2,1)S(1)} collective-permute-done((bf16[272,512]{1,0:T(8,128)(2,1)S(1)}, bf16[272,512]{1,0:T(8,128)(2,1)S(1)}, u32[]{:S(2)}, u32[]{:S(2)}) %collective-permute-start.21) | collective-permute-done | bytes 278560 | tf_op jit(solution)/shard_map/ppermute | solution.py:593
  132.0 2.5 %collective-permute-start.23 = (bf16[144,512]{1,0:T(8,128)(2,1)S(1)}, bf16[144,512]{1,0:T(8,128)(2,1)S(1)}, u32[]{:S(2)}, u32[]{:S(2)}) collective-permute-start(bf16[144,512]{1,0:T(8,128)(2,1)S(1)} %pad_maximum_fusion.5), channel_id=1, source_target_pairs={{0,16},{1,3},{2,18},{3,1},{4,20},{5,7},{6,22},{7,5},{8,24},{9,11},... | collective-permute-start | bytes 442376 | tf_op jit(solution)/shard_map/ppermute | solution.py:593
  135.9 5.9 %collective-permute-done.23 = bf16[144,512]{1,0:T(8,128)(2,1)S(1)} collective-permute-done((bf16[144,512]{1,0:T(8,128)(2,1)S(1)}, bf16[144,512]{1,0:T(8,128)(2,1)S(1)}, u32[]{:S(2)}, u32[]{:S(2)}) %collective-permute-start.23) | collective-permute-done | bytes 147488 | tf_op jit(solution)/shard_map/ppermute | solution.py:593
  142.4 3.4 %collective-permute-start.22 = (bf16[288,512]{1,0:T(8,128)(2,1)S(1)}, bf16[288,512]{1,0:T(8,128)(2,1)S(1)}, u32[]{:S(2)}, u32[]{:S(2)}) collective-permute-start(bf16[288,512]{1,0:T(8,128)(2,1)S(1)} %reduce-precision_convert_fusion.3), channel_id=1, source_target_pairs={{0,16},{1,9},{2,18},{3,11},{4,20},{5,13},{6,22},{7,15},{8,24},{9,1... | collective-permute-start | bytes 884744 | tf_op jit(solution)/shard_map/ppermute | solution.py:593
  145.9 4.4 %collective-permute-done.24 = bf16[144,512]{1,0:T(8,128)(2,1)S(1)} collective-permute-done((bf16[144,512]{1,0:T(8,128)(2,1)S(1)}, bf16[144,512]{1,0:T(8,128)(2,1)S(1)}, u32[]{:S(2)}, u32[]{:S(2)}) %collective-permute-start.24) | collective-permute-done | bytes 147488 | tf_op jit(solution)/shard_map/ppermute | solution.py:593
  150.6 3.2 %collective-permute-done.22 = bf16[288,512]{1,0:T(8,128)(2,1)S(1)} collective-permute-done((bf16[288,512]{1,0:T(8,128)(2,1)S(1)}, bf16[288,512]{1,0:T(8,128)(2,1)S(1)}, u32[]{:S(2)}, u32[]{:S(2)}) %collective-permute-start.22) | collective-permute-done | bytes 294944 | tf_op jit(solution)/shard_map/ppermute | solution.py:593
  153.8 3.0 %collective-permute-done.25 = bf16[128,512]{1,0:T(8,128)(2,1)S(1)} collective-permute-done((bf16[128,512]{1,0:T(8,128)(2,1)S(1)}, bf16[128,512]{1,0:T(8,128)(2,1)S(1)}, u32[]{:S(2)}, u32[]{:S(2)}) %collective-permute-start.25) | collective-permute-done | bytes 131104 | tf_op jit(solution)/shard_map/ppermute | solution.py:593
  157.4 1.8 collective-permute-start.26
  159.3 1.9 collective-permute-done.26
  161.1 1.8 collective-permute-start.29
  165.8 1.8 collective-permute-done.28.other_ref
  168.3 4.8 %renew.1 = (bf16[464,512]{1,0:T(8,128)(2,1)}, bf16[384,512]{1,0:T(8,128)(2,1)}, f32[1]{0:T(128)}) custom-call(s32[1]{0:T(128)} %bitcast.2.half_ref.side_ref, s32[4]{0:T(128)} %broadcast_select_fusion.8.index_ref, f32[8,128]{1,0:T(8,128)} %copy-done.20, f32[8,128]{1,0:T(8,128)} %copy-done.22, bf16[576,512]{1,0:T(8,128)(2,1)} %copy-done, ...), custom_call_target="tpu_custom_call" | custom-call | flops 1 | bytes 1 | tf_op jit(solution)/shard_map/renew/pallas_call | solution.py:750
  176.1 11.2 %update.1 = (f32[5,128,512]{2,1,0:T(8,128)}, f32[5,128,512]{2,1,0:T(8,128)}, f32[5,128,512]{2,1,0:T(8,128)}, f32[128,2048]{1,0:T(8,128)}, f32[128,2048]{1,0:T(8,...) custom-call(s32[1]{0:T(128)} %bitcast.2.half_ref.side_ref, ...), custom_call_target="tpu_custom_call" | custom-call | flops 1 | bytes 1 | tf_op jit(solution)/shard_map/update/pallas_call | solution.py:845
  195.0 2.9 %unpack_near.1 = (bf16[5,512,512]{2,1,0:T(8,128)(2,1)}, bf16[512,2048]{1,0:T(8,128)(2,1)}, bf16[2048,512]{1,0:T(8,128)(2,1)}) custom-call(s32[4]{0:T(128)S(1)} %iota_xor_fusion.pos_ref, s32[1]{0:T(128)} %bitcast.2.half_ref.side_ref, bf16[1024,512]{1,0:T(8,128)(2,1)S(1)} %copy-done.9, bf16[640,512]{1,0:T(8,128)(2,1)S(1)} %copy-done.12, ...), custom_call_target="tpu_custom_call" | custom-call | flops 1 | bytes 1 | tf_op jit(solution)/shard_map/unpack_near/pallas_call | solution.py:951
  197.9 1.9 collective-permute-done.32.refs_0_
  202.8 4.2 %collective-permute-done.37.refs_2_ = bf16[256,512]{1,0:T(8,128)(2,1)S(1)} collective-permute-done((bf16[256,512]{1,0:T(8,128)(2,1)S(1)}, bf16[256,512]{1,0:T(8,128)(2,1)S(1)}, u32[]{:S(2)}, u32[]{:S(2)}) %collective-permute-start.37) | collective-permute-done | bytes 262176 | tf_op jit(solution)/shard_map/ppermute | solution.py:593
  208.8 2.4 %unpack_far.1 = (bf16[5,512,512]{2,1,0:T(8,128)(2,1)}, bf16[512,2048]{1,0:T(8,128)(2,1)}, bf16[2048,512]{1,0:T(8,128)(2,1)}) custom-call(s32[4]{0:T(128)S(1)} %iota_xor_fusion.pos_ref, s32[1]{0:T(128)} %bitcast.2.half_ref.side_ref, ...), custom_call_target="tpu_custom_call", output_to_operand_aliasing={{0}: (10, {}), {1}: (11, {}), {2}: (12, {})} | custom-call | flops 1 | bytes 1 | tf_op jit(solution)/shard_map/unpack_far/pallas_call | solution.py:966
  (171 shorter events, 50.7 us)
Async XLA Ops:
  2.4 23.4 %collective-permute-start = (bf16[544,512]{1,0:T(8,128)(2,1)S(1)}, bf16[544,512]{1,0:T(8,128)(2,1)}, u32[]{:S(2)}, u32[]{:S(2)}) collective-permute-start(bf16[544,512]{1,0:T(8,128)(2,1)S(1)} %fusion.5.near0), channel_id=1, source_target_pairs={{0,1},{1,0},{2,3},{3,2},{4,5},{5,4},{6,7},{7,6},{8,9},{9,8},{10,11... | collective-permute-start | bytes 1671176 | tf_op jit(solution)/shard_map/ppermute | solution.py:593
  3.0 10.4 %collective-permute-start.1 = (bf16[272,512]{1,0:T(8,128)(2,1)S(1)}, bf16[272,512]{1,0:T(8,128)(2,1)S(1)}, u32[]{:S(2)}, u32[]{:S(2)}) collective-permute-start(bf16[272,512]{1,0:T(8,128)(2,1)S(1)} %constant_dynamic-slice_fusion), channel_id=1, source_target_pairs={{0,2},{1,3},{2,0},{3,1},{4,6},{5,7},{6,4},{7,5},{8,10},{9,11},{10,... | collective-permute-start | bytes 835592 | tf_op jit(solution)/shard_map/ppermute | solution.py:593
  13.4 8.0 %collective-permute-start.4 = (bf16[272,512]{1,0:T(8,128)(2,1)S(1)}, bf16[272,512]{1,0:T(8,128)(2,1)}, u32[]{:S(2)}, u32[]{:S(2)}) collective-permute-start(bf16[272,512]{1,0:T(8,128)(2,1)S(1)} %collective-permute-done.1.far0), channel_id=1, source_target_pairs={{0,4},{1,5},{2,6},{3,7},{4,0},{5,1},{6,2},{7,3},{8,12},{9,13},{10,... | collective-permute-start | bytes 835592 | tf_op jit(solution)/shard_map/ppermute | solution.py:593
  15.1 4.5 %collective-permute-start.10 = (f32[8]{0:T(128)S(1)}, f32[8]{0:T(128)S(1)}, u32[]{:S(2)}, u32[]{:S(2)}) collective-permute-start(f32[8]{0:T(128)S(1)} %fusion.12), channel_id=1, source_target_pairs={{0,16},{1,17},{2,18},{3,19},{4,20},{5,21},{6,22},{7,23},{8,24},{9,... | collective-permute-start | bytes 104 | tf_op jit(solution)/shard_map/ppermute | solution.py:593
  17.7 25.9 %collective-permute-start.8 = (bf16[640,512]{1,0:T(8,128)(2,1)S(1)}, bf16[640,512]{1,0:T(8,128)(2,1)S(1)}, u32[]{:S(2)}, u32[]{:S(2)}) collective-permute-start(bf16[640,512]{1,0:T(8,128)(2,1)S(1)} %slice_dynamic-update-slice_fusion.p0), channel_id=1, source_target_pairs={{0,2},{1,3},{2,0},{3,1},{4,6},{5,7},{6,4},{7,5},{8,10},{9,11},{10,... | collective-permute-start | bytes 1966088 | tf_op jit(solution)/shard_map/ppermute | solution.py:593
  21.5 23.4 %collective-permute-start.12 = (bf16[528,512]{1,0:T(8,128)(2,1)S(1)}, bf16[528,512]{1,0:T(8,128)(2,1)}, u32[]{:S(2)}, u32[]{:S(2)}) collective-permute-start(bf16[528,512]{1,0:T(8,128)(2,1)S(1)} %fusion.6.t0), channel_id=1, source_target_pairs={{0,2},{1,3},{2,0},{3,1},{4,6},{5,7},{6,4},{7,5},{8,10},{9,11},{10,... | collective-permute-start | bytes 1622024 | tf_op jit(solution)/shard_map/ppermute | solution.py:593
  25.7 19.2 %collective-permute-start.7 = (bf16[640,512]{1,0:T(8,128)(2,1)S(1)}, bf16[640,512]{1,0:T(8,128)(2,1)S(1)}, u32[]{:S(2)}, u32[]{:S(2)}) collective-permute-start(bf16[640,512]{1,0:T(8,128)(2,1)S(1)} %slice_dynamic-update-slice_fusion.p0), channel_id=1, source_target_pairs={{0,1},{1,0},{2,3},{3,2},{4,5},{5,4},{6,7},{7,6},{8,9},{9,8},{10,11... | collective-permute-start | bytes 1966088 | tf_op jit(solution)/shard_map/ppermute | solution.py:593
  43.6 3.7 %collective-permute-start.9 = (bf16[640,512]{1,0:T(8,128)(2,1)S(1)}, bf16[640,512]{1,0:T(8,128)(2,1)S(1)}, u32[]{:S(2)}, u32[]{:S(2)}) collective-permute-start(bf16[640,512]{1,0:T(8,128)(2,1)S(1)} %collective-permute-done.8.p2), channel_id=1, source_target_pairs={{0,1},{1,0},{2,3},{3,2},{4,5},{5,4},{6,7},{7,6},{8,9},{9,8},{10,11... | collective-permute-start | bytes 1966088 | tf_op jit(solution)/shard_map/ppermute | solution.py:593
  73.4 6.4 %collective-permute-start.14 = (bf16[2304,512]{1,0:T(8,128)(2,1)}, bf16[2304,512]{1,0:T(8,128)(2,1)S(1)}, u32[]{:S(2)}, u32[]{:S(2)}) collective-permute-start(bf16[2304,512]{1,0:T(8,128)(2,1)} %get-tuple-element.119), channel_id=1, source_target_pairs={{0,1},{1,0},{2,3},{3,2},{4,5},{5,4},{6,7},{7,6},{8,9},{9,8},{10,11... | collective-permute-start | bytes 7077896 | tf_op jit(solution)/shard_map/ppermute | solution.py:593
  80.1 16.9 %collective-permute-start.15 = (bf16[1152,512]{1,0:T(8,128)(2,1)S(1)}, bf16[1152,512]{1,0:T(8,128)(2,1)}, u32[]{:S(2)}, u32[]{:S(2)}) collective-permute-start(bf16[1152,512]{1,0:T(8,128)(2,1)S(1)} %reduce-precision_convert_fusion), channel_id=1, source_target_pairs={{0,2},{1,5},{2,0},{3,7},{4,6},{5,1},{6,4},{7,3},{8,10},{9,13},{10,... | collective-permute-start | bytes 3538952 | tf_op jit(solution)/shard_map/ppermute | solution.py:593
  98.5 9.9 %collective-permute-start.16 = (bf16[576,512]{1,0:T(8,128)(2,1)S(1)}, bf16[576,512]{1,0:T(8,128)(2,1)S(1)}, u32[]{:S(2)}, u32[]{:S(2)}) collective-permute-start(bf16[576,512]{1,0:T(8,128)(2,1)S(1)} %reduce-precision_convert_fusion.1), channel_id=1, source_target_pairs={{0,4},{1,9},{2,6},{3,11},{4,0},{5,13},{6,2},{7,15},{8,12},{9,1},{1... | collective-permute-start | bytes 1769480 | tf_op jit(solution)/shard_map/ppermute | solution.py:593
  112.5 12.6 %collective-permute-start.19 = (bf16[528,512]{1,0:T(8,128)(2,1)S(1)}, bf16[528,512]{1,0:T(8,128)(2,1)S(1)}, u32[]{:S(2)}, u32[]{:S(2)}) collective-permute-start(bf16[528,512]{1,0:T(8,128)(2,1)S(1)} %pad_maximum_fusion.2), channel_id=1, source_target_pairs={{0,2},{1,5},{2,0},{3,7},{4,6},{5,1},{6,4},{7,3},{8,10},{9,13},{10,... | collective-permute-start | bytes 1622024 | tf_op jit(solution)/shard_map/ppermute | solution.py:593
  113.9 12.3 %collective-permute-start.17 = (bf16[288,512]{1,0:T(8,128)(2,1)S(1)}, bf16[288,512]{1,0:T(8,128)(2,1)S(1)}, u32[]{:S(2)}, u32[]{:S(2)}) collective-permute-start(bf16[288,512]{1,0:T(8,128)(2,1)S(1)} %reduce-precision_convert_fusion.5), channel_id=1, source_target_pairs={{0,16},{1,3},{2,18},{3,1},{4,20},{5,7},{6,22},{7,5},{8,24},{9,11},... | collective-permute-start | bytes 884744 | tf_op jit(solution)/shard_map/ppermute | solution.py:593
  125.2 6.6 %collective-permute-start.21 = (bf16[272,512]{1,0:T(8,128)(2,1)S(1)}, bf16[272,512]{1,0:T(8,128)(2,1)S(1)}, u32[]{:S(2)}, u32[]{:S(2)}) collective-permute-start(bf16[272,512]{1,0:T(8,128)(2,1)S(1)} %pad_maximum_fusion.3), channel_id=1, source_target_pairs={{0,4},{1,9},{2,6},{3,11},{4,0},{5,13},{6,2},{7,15},{8,12},{9,1},{1... | collective-permute-start | bytes 835592 | tf_op jit(solution)/shard_map/ppermute | solution.py:593
  127.4 8.5 %collective-permute-start.20 = (bf16[288,512]{1,0:T(8,128)(2,1)S(1)}, bf16[288,512]{1,0:T(8,128)(2,1)S(1)}, u32[]{:S(2)}, u32[]{:S(2)}) collective-permute-start(bf16[288,512]{1,0:T(8,128)(2,1)S(1)} %reduce-precision_convert_fusion.4), channel_id=1, source_target_pairs={{0,8},{1,17},{2,10},{3,19},{4,12},{5,21},{6,14},{7,23},{8,0},{9,25... | collective-permute-start | bytes 884744 | tf_op jit(solution)/shard_map/ppermute | solution.py:593
  132.0 9.8 %collective-permute-start.23 = (bf16[144,512]{1,0:T(8,128)(2,1)S(1)}, bf16[144,512]{1,0:T(8,128)(2,1)S(1)}, u32[]{:S(2)}, u32[]{:S(2)}) collective-permute-start(bf16[144,512]{1,0:T(8,128)(2,1)S(1)} %pad_maximum_fusion.5), channel_id=1, source_target_pairs={{0,16},{1,3},{2,18},{3,1},{4,20},{5,7},{6,22},{7,5},{8,24},{9,11},... | collective-permute-start | bytes 442376 | tf_op jit(solution)/shard_map/ppermute | solution.py:593
  141.9 8.3 %collective-permute-start.24 = (bf16[144,512]{1,0:T(8,128)(2,1)S(1)}, bf16[144,512]{1,0:T(8,128)(2,1)S(1)}, u32[]{:S(2)}, u32[]{:S(2)}) collective-permute-start(bf16[144,512]{1,0:T(8,128)(2,1)S(1)} %pad_maximum_fusion.6), channel_id=1, source_target_pairs={{0,8},{1,17},{2,10},{3,19},{4,12},{5,21},{6,14},{7,23},{8,0},{9,25... | collective-permute-start | bytes 442376 | tf_op jit(solution)/shard_map/ppermute | solution.py:593
  142.4 11.3 %collective-permute-start.22 = (bf16[288,512]{1,0:T(8,128)(2,1)S(1)}, bf16[288,512]{1,0:T(8,128)(2,1)S(1)}, u32[]{:S(2)}, u32[]{:S(2)}) collective-permute-start(bf16[288,512]{1,0:T(8,128)(2,1)S(1)} %reduce-precision_convert_fusion.3), channel_id=1, source_target_pairs={{0,16},{1,9},{2,18},{3,11},{4,20},{5,13},{6,22},{7,15},{8,24},{9,1... | collective-permute-start | bytes 884744 | tf_op jit(solution)/shard_map/ppermute | solution.py:593
  150.3 6.5 %collective-permute-start.25 = (bf16[128,512]{1,0:T(8,128)(2,1)S(1)}, bf16[128,512]{1,0:T(8,128)(2,1)S(1)}, u32[]{:S(2)}, u32[]{:S(2)}) collective-permute-start(bf16[128,512]{1,0:T(8,128)(2,1)S(1)} %slice.237), channel_id=1, source_target_pairs={{0,16},{1,9},{2,18},{3,11},{4,20},{5,13},{6,22},{7,15},{8,24},{9,1... | collective-permute-start | bytes 393224 | tf_op jit(solution)/shard_map/ppermute | solution.py:593
  157.4 3.8 %collective-permute-start.26 = (f32[8,128]{1,0:T(8,128)S(1)}, f32[8,128]{1,0:T(8,128)S(1)}, u32[]{:S(2)}, u32[]{:S(2)}) collective-permute-start(f32[8,128]{1,0:T(8,128)S(1)} %squares.1), channel_id=1, source_target_pairs={{0,4},{1,5},{2,6},{3,7},{4,0},{5,1},{6,2},{7,3},{8,12},{9,13},{10,... | collective-permute-start | bytes 12296 | tf_op jit(solution)/shard_map/ppermute | solution.py:593
  161.1 14.0 %collective-permute-start.29 = (bf16[832,512]{1,0:T(8,128)(2,1)S(1)}, bf16[832,512]{1,0:T(8,128)(2,1)S(1)}, u32[]{:S(2)}, u32[]{:S(2)}) collective-permute-start(bf16[832,512]{1,0:T(8,128)(2,1)S(1)} %pad_maximum_fusion), channel_id=1, source_target_pairs={{0,4},{1,5},{2,6},{3,7},{4,0},{5,1},{6,2},{7,3},{8,12},{9,13},{10,... | collective-permute-start | bytes 2555912 | tf_op jit(solution)/shard_map/ppermute | solution.py:593
  164.1 3.6 %collective-permute-start.28 = (f32[8,128]{1,0:T(8,128)S(1)}, f32[8,128]{1,0:T(8,128)S(1)}, u32[]{:S(2)}, u32[]{:S(2)}) collective-permute-start(f32[8,128]{1,0:T(8,128)S(1)} %add.303.square_ref), channel_id=1, source_target_pairs={{0,2},{1,3},{2,0},{3,1},{4,6},{5,7},{6,4},{7,5},{8,10},{9,11},{10,... | collective-permute-start | bytes 12296 | tf_op jit(solution)/shard_map/ppermute | solution.py:593
  173.1 14.2 %collective-permute-start.30 = (bf16[464,512]{1,0:T(8,128)(2,1)}, bf16[464,512]{1,0:T(8,128)(2,1)S(1)}, u32[]{:S(2)}, u32[]{:S(2)}) collective-permute-start(bf16[464,512]{1,0:T(8,128)(2,1)} %get-tuple-element.161), channel_id=1, source_target_pairs={{0,2},{1,3},{2,0},{3,1},{4,6},{5,7},{6,4},{7,5},{8,10},{9,11},{10,... | collective-permute-start | bytes 1425416 | tf_op jit(solution)/shard_map/ppermute | solution.py:593
  175.2 12.1 %collective-permute-start.31 = (bf16[16,512]{1,0:T(8,128)(2,1)S(1)}, bf16[16,512]{1,0:T(8,128)(2,1)S(1)}, u32[]{:S(2)}, u32[]{:S(2)}) collective-permute-start(bf16[16,512]{1,0:T(8,128)(2,1)S(1)} %slice.205), channel_id=1, source_target_pairs={{0,1},{1,0},{2,3},{3,2},{4,5},{5,4},{6,7},{7,6},{8,9},{9,8},{10,11... | collective-permute-start | bytes 49160 | tf_op jit(solution)/shard_map/ppermute | solution.py:593
  187.3 5.4 %collective-permute-start.34 = (bf16[1024,512]{1,0:T(8,128)(2,1)}, bf16[1024,512]{1,0:T(8,128)(2,1)S(1)}, u32[]{:S(2)}, u32[]{:S(2)}) collective-permute-start(bf16[1024,512]{1,0:T(8,128)(2,1)} %get-tuple-element.184.p0), channel_id=1, source_target_pairs={{0,1},{1,0},{2,3},{3,2},{4,5},{5,4},{6,7},{7,6},{8,9},{9,8},{10,11... | collective-permute-start | bytes 3145736 | tf_op jit(solution)/shard_map/ppermute | solution.py:593
  187.9 4.7 %collective-permute-start.35 = (bf16[640,512]{1,0:T(8,128)(2,1)}, bf16[640,512]{1,0:T(8,128)(2,1)S(1)}, u32[]{:S(2)}, u32[]{:S(2)}) collective-permute-start(bf16[640,512]{1,0:T(8,128)(2,1)} %get-tuple-element.185.p1), channel_id=1, source_target_pairs={{0,1},{1,0},{2,3},{3,2},{4,5},{5,4},{6,7},{7,6},{8,9},{9,8},{10,11... | collective-permute-start | bytes 1966088 | tf_op jit(solution)/shard_map/ppermute | solution.py:593
  188.3 13.1 %collective-permute-start.36 = (bf16[464,512]{1,0:T(8,128)(2,1)S(1)}, bf16[464,512]{1,0:T(8,128)(2,1)S(1)}, u32[]{:S(2)}, u32[]{:S(2)}) collective-permute-start(bf16[464,512]{1,0:T(8,128)(2,1)S(1)} %collective-permute-done.30.p4), channel_id=1, source_target_pairs={{0,4},{1,5},{2,6},{3,7},{4,0},{5,1},{6,2},{7,3},{8,12},{9,13},{10,... | collective-permute-start | bytes 1425416 | tf_op jit(solution)/shard_map/ppermute | solution.py:593
  188.7 11.0 %collective-permute-start.32 = (bf16[384,512]{1,0:T(8,128)(2,1)}, bf16[384,512]{1,0:T(8,128)(2,1)S(1)}, u32[]{:S(2)}, u32[]{:S(2)}) collective-permute-start(bf16[384,512]{1,0:T(8,128)(2,1)} %get-tuple-element.181), channel_id=1, source_target_pairs={{0,2},{1,3},{2,0},{3,1},{4,6},{5,7},{6,4},{7,5},{8,10},{9,11},{10,... | collective-permute-start | bytes 1179656 | tf_op jit(solution)/shard_map/ppermute | solution.py:593
  199.8 7.2 %collective-permute-start.37 = (bf16[256,512]{1,0:T(8,128)(2,1)S(1)}, bf16[256,512]{1,0:T(8,128)(2,1)S(1)}, u32[]{:S(2)}, u32[]{:S(2)}) collective-permute-start(bf16[256,512]{1,0:T(8,128)(2,1)S(1)} %slice.211), channel_id=1, source_target_pairs={{0,4},{1,5},{2,6},{3,7},{4,0},{5,1},{6,2},{7,3},{8,12},{9,13},{10,... | collective-permute-start | bytes 786440 | tf_op jit(solution)/shard_map/ppermute | solution.py:593
  201.5 7.3 %collective-permute-start.40 = (bf16[464,512]{1,0:T(8,128)(2,1)S(1)}, bf16[464,512]{1,0:T(8,128)(2,1)S(1)}, u32[]{:S(2)}, u32[]{:S(2)}) collective-permute-start(bf16[464,512]{1,0:T(8,128)(2,1)S(1)} %collective-permute-done.36.refs_1_), channel_id=1, source_target_pairs={{0,1},{1,0},{2,3},{3,2},{4,5},{5,4},{6,7},{7,6},{8,9},{9,8},{10,11... | collective-permute-start | bytes 1425416 | tf_op jit(solution)/shard_map/ppermute | solution.py:593
  201.5 7.3 %collective-permute-start.39 = (bf16[384,512]{1,0:T(8,128)(2,1)S(1)}, bf16[384,512]{1,0:T(8,128)(2,1)S(1)}, u32[]{:S(2)}, u32[]{:S(2)}) collective-permute-start(bf16[384,512]{1,0:T(8,128)(2,1)S(1)} %collective-permute-done.32.refs_0_), channel_id=1, source_target_pairs={{0,1},{1,0},{2,3},{3,2},{4,5},{5,4},{6,7},{7,6},{8,9},{9,8},{10,11... | collective-permute-start | bytes 1179656 | tf_op jit(solution)/shard_map/ppermute | solution.py:593
  202.0 5.4 %collective-permute-start.38 = (bf16[128,512]{1,0:T(8,128)(2,1)S(1)}, bf16[128,512]{1,0:T(8,128)(2,1)S(1)}, u32[]{:S(2)}, u32[]{:S(2)}) collective-permute-start(bf16[128,512]{1,0:T(8,128)(2,1)S(1)} %copy-done.23), channel_id=1, source_target_pairs={{0,2},{1,3},{2,0},{3,1},{4,6},{5,7},{6,4},{7,5},{8,10},{9,11},{10,... | collective-permute-start | bytes 393224 | tf_op jit(solution)/shard_map/ppermute | solution.py:593
  (36 other events, 241.8 us)
